TPU v7x, 32 devices: a whole 2x2x4 slice. The times are simulated.
32 devices in a mesh: parts: 2 (over x), tok: 16 (over z, y, core).
Axes of the slice: x: 2, y: 2, z: 4, core: 2. Of those that a mesh axis runs over, the one named last changes fastest.
Arguments:
- queries: bfloat16 [4096, 4096], P(('parts', 'tok')), parts along dimension 0, may hold values from -30 to 30
- keys: bfloat16 [4096, 512], P(('parts', 'tok')), parts along dimension 0, may hold values from -4 to 4
- values: bfloat16 [4096, 512], P(('parts', 'tok')), parts along dimension 0, may hold values from -5 to 5
- outputs: bfloat16 [4096, 4096], P(('parts', 'tok')), parts along dimension 0, may hold values from -3 to 3
- out_grad: bfloat16 [4096, 4096], P(('parts', 'tok')), parts along dimension 0, may hold values from -6 to 6
- ancestors: int32 [32, 10], P('parts'), parts along dimension 0, may hold values from -1 to 14, as said below
Outputs:
- query_grad: bfloat16 [4096, 4096], P(('parts', 'tok')), parts along dimension 0
- key_grad: bfloat16 [4096, 512], P(('parts', 'tok')), parts along dimension 0
- value_grad: bfloat16 [4096, 512], P(('parts', 'tok')), parts along dimension 0
There are 2 independent parts, one for each index of `parts`. A program takes and returns all parts, laid end to end along the dimension named above; each array names one. Nothing has to cross between parts.
Inputs may be any that keep to these rules, and one draw needn't show every extreme that they name: Row t lists the ancestor tiles of tile t, from its parent up to tile 0, each once, then -1 to the end. Every listed tile is earlier than t; tile 0 is an ancestor of every other tile and has none; some tile has exactly 10 ancestors.
All inputs are finite; a program needn't handle non-finite values.
Results may differ from a plain program's by a relative error of at most 0.0053.
Values may be sent and summed in bfloat16 or wider, within the bound.
No kernel may reach another device: no remote copies, remote signals or barrier semaphores. Data moves between devices by JAX's collectives and lax.ppermute only.
A program may use at most 128 MiB of HBM per device.

v0:
```python
import jax
import jax.numpy as jnp
from jax import lax
from jax.sharding import PartitionSpec as P

QH = 32
KVH = 4
HD = 128
TILE = 128


def pair_lists(ancestor_rows, query_tiles, block_pairs):
    query_count, depth_count = ancestor_rows.shape
    slot_count = depth_count + 1
    key_list = jnp.concatenate([ancestor_rows, query_tiles[:, None]], axis=1).reshape(-1)
    query_slot = jnp.broadcast_to(
        jnp.arange(query_count, dtype=jnp.int32)[:, None], (query_count, slot_count)
    ).reshape(-1)
    self_flag = jnp.broadcast_to(
        jnp.arange(slot_count) == slot_count - 1, (query_count, slot_count)
    ).reshape(-1)
    is_live = key_list >= 0
    ranking = jnp.argsort(1 - is_live.astype(jnp.int32), stable=True)
    pair_total = query_count * slot_count
    padded = -(-pair_total // block_pairs) * block_pairs
    padding_count = padded - pair_total

    def arrange(entries, filler):
        return jnp.concatenate(
            [entries[ranking], jnp.full((padding_count,), filler, entries.dtype)]
        )

    live_pairs = jnp.sum(is_live.astype(jnp.int32))
    return (
        arrange(query_slot, 0),
        arrange(jnp.maximum(key_list, 0), 0),
        arrange(self_flag, False),
        arrange(is_live, False),
        live_pairs,
        padded,
    )


def tree_backward(queries, outputs, out_grad, keys, values, ancestor_rows, query_tiles):
    query_count, tile_len, kv_count, group_len, head_dim = queries.shape
    softmax_scale = head_dim ** (-0.5)
    block_pairs = max(1, 64 // (kv_count * group_len))
    pair_query, pair_key, pair_self, pair_live, live_pairs, padded = pair_lists(
        ancestor_rows, query_tiles, block_pairs
    )
    block_total = (live_pairs + block_pairs - 1) // block_pairs
    causal = jnp.arange(tile_len)[:, None] >= jnp.arange(tile_len)[None, :]

    def take_block(index):
        start = index * block_pairs
        return tuple(
            (
                lax.dynamic_slice_in_dim(entry, start, block_pairs)
                for entry in (pair_query, pair_key, pair_self, pair_live)
            )
        )

    def masked_scores(query_block, key_block, self_ids, live_ids):
        raw_scores = (
            jnp.einsum(
                "bikgd,bjkd->bkgij", query_block, key_block, preferred_element_type=jnp.float32
            )
            * softmax_scale
        )
        key_mask = live_ids[:, None, None] & (
            jnp.logical_not(self_ids)[:, None, None] | causal[None]
        )
        return jnp.where(key_mask[:, None, None], raw_scores, -1e30)

    stat_shape = (padded, kv_count, group_len, tile_len)

    def first_sweep(index, state):
        max_rows, sum_rows = state
        query_ids, key_ids, self_ids, live_ids = take_block(index)
        masked = masked_scores(queries[query_ids], keys[key_ids], self_ids, live_ids)
        block_max = jnp.max(masked, axis=-1)
        block_sum = (
            jnp.sum(jnp.exp(masked - block_max[..., None]), axis=-1)
            * live_ids.astype(jnp.float32)[:, None, None, None]
        )
        start = index * block_pairs
        return (
            lax.dynamic_update_slice_in_dim(max_rows, block_max, start, 0),
            lax.dynamic_update_slice_in_dim(sum_rows, block_sum, start, 0),
        )

    max_rows, sum_rows = lax.fori_loop(
        0,
        block_total,
        first_sweep,
        (jnp.full(stat_shape, -1e30, jnp.float32), jnp.zeros(stat_shape, jnp.float32)),
    )
    row_shape = (query_count, kv_count, group_len, tile_len)
    row_max = jnp.full(row_shape, -1e30, jnp.float32).at[pair_query].max(max_rows)
    row_total = (
        jnp.zeros(row_shape, jnp.float32)
        .at[pair_query]
        .add(sum_rows * jnp.exp(max_rows - row_max[pair_query]))
    )
    log_total = row_max + jnp.log(row_total)
    row_delta = jnp.transpose(
        jnp.sum(out_grad.astype(jnp.float32) * outputs.astype(jnp.float32), axis=-1), (0, 2, 3, 1)
    )

    def second_sweep(index, state):
        query_acc, key_acc, value_acc = state
        query_ids, key_ids, self_ids, live_ids = take_block(index)
        query_block = queries[query_ids]
        key_block = keys[key_ids]
        value_block = values[key_ids]
        grad_block = out_grad[query_ids]
        masked = masked_scores(query_block, key_block, self_ids, live_ids)
        attn_probs = jnp.exp(masked - log_total[query_ids][..., None])
        grad_probs = jnp.einsum(
            "bikgd,bjkd->bkgij", grad_block, value_block, preferred_element_type=jnp.float32
        )
        grad_scores = (attn_probs * (grad_probs - row_delta[query_ids][..., None])).astype(
            jnp.bfloat16
        )
        probs_low = attn_probs.astype(jnp.bfloat16)
        query_acc = query_acc.at[query_ids].add(
            jnp.einsum(
                "bkgij,bjkd->bikgd", grad_scores, key_block, preferred_element_type=jnp.float32
            )
        )
        key_acc = key_acc.at[key_ids].add(
            jnp.einsum(
                "bkgij,bikgd->bjkd", grad_scores, query_block, preferred_element_type=jnp.float32
            )
        )
        value_acc = value_acc.at[key_ids].add(
            jnp.einsum(
                "bkgij,bikgd->bjkd", probs_low, grad_block, preferred_element_type=jnp.float32
            )
        )
        return (query_acc, key_acc, value_acc)

    start_state = (
        jnp.zeros(queries.shape, jnp.float32),
        jnp.zeros(keys.shape, jnp.float32),
        jnp.zeros(keys.shape, jnp.float32),
    )
    query_acc, key_acc, value_acc = lax.fori_loop(0, block_total, second_sweep, start_state)
    return ((query_acc * softmax_scale).astype(jnp.bfloat16), key_acc, value_acc)


def per_device(queries, keys, values, outputs, out_grad, ancestors):
    tile_count = ancestors.shape[0]
    groups = QH // KVH
    row_count = queries.shape[0]
    tiles_here = row_count // TILE
    softmax_scale = HD ** (-0.5)
    gathered_keys, gathered_values = (
        lax.all_gather(keys, "tok", axis=0, tiled=True),
        lax.all_gather(values, "tok", axis=0, tiled=True),
    )
    first_tile = lax.axis_index("tok") * tiles_here
    query_tiles = first_tile + jnp.arange(tiles_here, dtype=jnp.int32)
    ancestor_rows = lax.dynamic_slice_in_dim(ancestors, first_tile, tiles_here, 0)
    query_shape = (tiles_here, TILE, KVH, groups, HD)
    key_shape = (tile_count, TILE, KVH, HD)
    query_grad, key_acc, value_acc = tree_backward(
        queries.reshape(query_shape),
        outputs.reshape(query_shape),
        out_grad.reshape(query_shape),
        gathered_keys.reshape(key_shape),
        gathered_values.reshape(key_shape),
        ancestor_rows,
        query_tiles,
    )
    all_rows = tile_count * TILE
    key_sum, value_sum = (
        lax.psum_scatter(
            key_acc.reshape(all_rows, KVH * HD), "tok", scatter_dimension=0, tiled=True
        ),
        lax.psum_scatter(
            value_acc.reshape(all_rows, KVH * HD), "tok", scatter_dimension=0, tiled=True
        ),
    )
    return (
        query_grad.reshape(row_count, QH * HD),
        (key_sum * softmax_scale).astype(jnp.bfloat16),
        value_sum.astype(jnp.bfloat16),
    )


def solution(mesh):
    return jax.shard_map(
        per_device,
        mesh=mesh,
        in_specs=(
            P(("parts", "tok"), None),
            P(("parts", "tok"), None),
            P(("parts", "tok"), None),
            P(("parts", "tok"), None),
            P(("parts", "tok"), None),
            P("parts", None),
        ),
        out_specs=(P(("parts", "tok"), None), P(("parts", "tok"), None), P(("parts", "tok"), None)),
        check_vma=False,
    )
```

profile of v0, /device:TPU:0, one launch (start us, length us, event | category | flops | bytes accessed | tf_op | source)
XLA Modules:
  0.0 461.1 jit_solution(17456207643026106930)
XLA Ops:
  7.2 0.7 all-gather.3.cloned.1.call-update
  8.0 0.7 all-gather.5.cloned.1.call-update
  8.7 0.1 maximum_bitcast_fusion
  8.8 0.1 convert_subtract_fusion
  8.9 0.6 convert_reduce_fusion
  10.2 1.3 sort.17
  11.5 0.7 gather_fusion.5
  12.2 0.7 gather_fusion.3
  12.8 0.7 gather_fusion.6
  13.5 0.7 gather_fusion.4
  14.2 1.6 copy.23
  15.8 0.7 copy.27
  16.5 1.6 copy.26
  18.1 1.6 copy.25
  19.7 1.3 copy.28
  21.0 0.4 fusion.27
  21.4 0.1 fusion.28
  21.6 0.1 pad_add_fusion
  21.7 32.6 %all-gather.3.cloned.1.call-done = bf16[2048,512]{1,0:T(8,128)(2,1)} async-done(((bf16[128,512]{1,0:T(8,128)(2,1)}), bf16[2048,512]{1,0:T(8,128)(2,1)}) %all-gather.3.cloned.1.call-update) | async-done | bytes 2097168 | tf_op jit(solution)/shard_map/all_gather | solution.py:159
  54.3 2.5 reshape.152
  56.8 0.7 broadcast_in_dim.52
  57.5 0.7 broadcast_in_dim.51
  58.2 3.8 while.30
  58.3 0.1 dynamic-slice_not_fusion.3
  58.5 0.1 or_and_fusion.5
  58.6 0.8 gather_fusion.2
  59.4 0.8 fusion.63
  60.2 1.2 exponential_reduce_fusion.2
  61.3 0.7 multiply_dynamic-update-slice_fusion.2
  62.0 2.1 scatter_fusion.3
  64.1 1.1 exponential_multiply_fusion
  65.2 1.0 scatter_fusion.4
  66.2 30.4 %all-gather.5.cloned.1.call-done = bf16[2048,512]{1,0:T(8,128)(2,1)} async-done(((bf16[128,512]{1,0:T(8,128)(2,1)}), bf16[2048,512]{1,0:T(8,128)(2,1)}) %all-gather.5.cloned.1.call-update) | async-done | bytes 2097168 | tf_op jit(solution)/shard_map/all_gather | solution.py:160
  96.6 4.0 reshape.154
  100.6 0.2 broadcast_in_dim.48
  100.9 2.4 broadcast.103.clone
  103.3 2.5 broadcast.103
  105.8 31.9 %while.29 = (s32[]{:T(128)}, f32[1,128,4,8,128]{4,3,2,1,0:T(8,128)S(1)}, f32[16,128,4,128]{3,1,2,0:T(8,128)}, f32[16,128,4,128]{3,1,2,0:T(8,128)}, s32[]{:T(128)...) while((s32[]{:T(128)}, ...), condition=%wide.region_13.14_spmd.clone, body=%wide.region_9.13_spmd.clone.sunk | while | flops 1354056704 | bytes 60215672 | solution.py:148
  106.0 0.1 not_convert_fusion.3
  106.1 0.1 or_and_fusion.4
  106.2 3.1 gather_fusion.1
  109.2 3.1 gather_fusion
  112.3 1.1 copy.63
  113.4 0.8 fusion.59
  114.2 0.5 copy-done.4
  114.7 1.9 fusion.61
  116.6 1.5 fusion.60
  118.0 1.6 convolution_bitcast_fusion.5
  119.6 2.7 convolution_bitcast_fusion.4
  122.3 5.5 %copy.64 = f32[2,128,4,8,128]{4,3,2,1,0:T(8,128)} copy(f32[2,128,4,8,128]{1,4,3,2,0:T(8,128)} %convolution_bitcast_fusion.4) | data formatting | bytes 8388608 | tf_op jit(solution)/shard_map/while/body/bkgij,bjkd->bikgd/transpose | solution.py:127
  127.7 4.8 %scatter_fusion = f32[128,4,8,128,1]{3,2,4,1,0:T(8,128)S(1)} fusion(f32[128,4,8,128,1]{3,2,4,1,0:T(8,128)S(1)} %bitcast.130, s32[2]{0:T(128)S(1)} %get-tuple-element.464, f32[2,128,4,8,128]{4,3,2,1,0:T(8,128)} %copy.64), kind=kCustom, calls=%fused_computation.7.clone.clone.1 | custom fusion | flops 1048576 | bytes 12582920 | tf_op jit(solution)/shard_map/while/body/scatter-add | solution.py:126
  132.5 2.6 scatter_fusion.1
  135.1 2.6 scatter_fusion.2
  137.7 5.0 %copy.30 = f32[16,128,4,128]{3,2,1,0:T(4,128)S(1)} copy(f32[16,128,4,128]{3,1,2,0:T(8,128)} %get-tuple-element.153) | data formatting | bytes 8388608 | tf_op jit(solution)/shard_map/while | solution.py:148
  142.7 2.4 copy.56
  145.1 0.3 reduce-scatter.3.cloned.1.call-start
  145.4 5.0 %copy.29 = f32[16,128,4,128]{3,2,1,0:T(4,128)S(1)} copy(f32[16,128,4,128]{3,1,2,0:T(8,128)} %get-tuple-element.152) | data formatting | bytes 8388608 | tf_op jit(solution)/shard_map/while | solution.py:148
  150.4 2.4 copy.57
  152.8 0.3 multiply_convert_fusion
  153.1 1.3 reshape.156
  154.3 223.0 %reduce-scatter.5.cloned.1.call-done = f32[128,512]{1,0:T(8,128)} async-done(((f32[2048,512]{1,0:T(8,128)}), f32[128,512]{1,0:T(8,128)}) %reduce-scatter.5.cloned.1.call-update) | async-done | bytes 262160 | tf_op jit(solution)/shard_map/reduce_scatter | solution.py:181
  377.3 1.6 convert_element_type.53
  378.9 74.0 %reduce-scatter.3.cloned.1.call-done = f32[128,512]{1,0:T(8,128)} async-done(((f32[2048,512]{1,0:T(8,128)}), f32[128,512]{1,0:T(8,128)}) %reduce-scatter.3.cloned.1.call-update) | async-done | bytes 262160 | tf_op jit(solution)/shard_map/reduce_scatter | solution.py:178
  453.0 1.6 multiply_convert_fusion.1
  (32 shorter events, 0.6 us)
Async XLA Ops:
  7.2 1.6 copy-start
  7.2 47.1 %all-gather.3.cloned.1.call-start = ((), (), s32[]{:S(2)}) async-start(), calls=%async_computation.2 | async-start | bytes 2228224 | tf_op jit(solution)/shard_map/all_gather | solution.py:159
  7.9 88.7 %all-gather.5.cloned.1.call-start = ((), (), s32[]{:S(2)}) async-start(), calls=%async_computation.3 | async-start | bytes 2228224 | tf_op jit(solution)/shard_map/all_gather | solution.py:160
  8.7 368.6 %reduce-scatter.5.cloned.1.call-start = ((), (), s32[]{:S(2)}) async-start(), calls=%async_computation.5 | async-start | bytes 4456448 | tf_op jit(solution)/shard_map/reduce_scatter | solution.py:181
  62.0 38.6 %copy-start.2 = (bf16[16,128,4,128]{3,2,1,0:T(4,128)(2,1)}, bf16[16,128,4,128]{3,2,1,0:T(4,128)(2,1)S(1)}, u32[]{:S(2)}) copy-start(bf16[16,128,4,128]{3,2,1,0:T(4,128)(2,1)S(1)} %get-tuple-element.586) | copy-start | bytes 6291460
  113.4 1.2 copy-start.4
  114.7 1.9 copy-start.3
  145.1 307.8 %reduce-scatter.3.cloned.1.call-start = ((), (), s32[]{:S(2)}) async-start(), calls=%async_computation.4 | async-start | bytes 4456448 | tf_op jit(solution)/shard_map/reduce_scatter | solution.py:178
  152.8 301.8 %copy-start.1 = (s32[16,10]{1,0:T(8,128)S(1)}, s32[16,10]{1,0:T(8,128)}, u32[]{:S(2)}) copy-start(s32[16,10]{1,0:T(8,128)} %param.15) | copy-start | bytes 1924
Sparse Core Ops, SparseCore 0:
  10.2 44.0 all-gather.2
  56.4 40.1 all-gather.4
  145.2 232.0 reduce-scatter.4
  381.5 71.3 reduce-scatter.2
where the time goes:
time: 464 us; the launch traced here: 461 us
  waiting for transfers between devices  361 us (78%)
  local copies, waits for them, and re-layouts  52.7 us (11%)
  other arithmetic  22.8 us (5%)
  between operations  14.6 us (3%)
  matrix products  9.12 us (2%)
    reduce_scatter x1, waiting for transfers between devices, per_device(): lax.psum_scatter(value_acc.reshape(all_rows, KVH * HD), 'tok', scatter_di...  223 us
    reduce_scatter x1, waiting for transfers between devices, per_device(): lax.psum_scatter(key_acc.reshape(all_rows, KVH * HD), 'tok', scatter_dime...  74 us
    all_gather x1, waiting for transfers between devices, per_device(): lax.all_gather(keys, 'tok', axis=0, tiled=True)  32.6 us
    all_gather x1, waiting for transfers between devices, per_device(): lax.all_gather(values, 'tok', axis=0, tiled=True)  30.4 us
    unnamed x13, local copies, waits for them, and re-layouts  11.6 us
    while x2, local copies, waits for them, and re-layouts, tree_backward(): lax.fori_loop(0, block_total, second_sweep, start_state)  9.95 us
  transfers between devices with their start and end apart: 4, of which 4 were waited for; matrix products, arithmetic and copies ran while one was open for 8% of the time, Pallas kernels for 0%

commit v1 on v0

v1 whole, which is shorter than its diff:
```python
import functools
import math

import jax
import jax.numpy as jnp
from jax import lax
from jax.experimental import pallas as pl
from jax.experimental.pallas import tpu as pltpu
from jax.sharding import PartitionSpec as P

QH = 32
KVH = 4
HD = 128
TILE = 128
GROUP = QH // KVH
LOCAL = KVH // 2
ROWS = GROUP * TILE
PAIR = 2 * TILE
COLS = 2
SCALE = HD ** (-0.5)
LOG2E = 1.0 / math.log(2.0)
MASKED = -1e30
NT_DIMS = (((1,), (1,)), ((), ()))


def delta_kernel(out_ref, grad_ref, delta_ref):
    for head in range(QH):
        cols = slice(head * HD, (head + 1) * HD)
        product = out_ref[:, cols].astype(jnp.float32) * grad_ref[:, cols].astype(jnp.float32)
        delta_ref[head : head + 1, :] = jnp.sum(product.T, axis=0, keepdims=True)


def row_deltas(outputs, out_grad):
    return pl.pallas_call(
        delta_kernel,
        out_shape=jax.ShapeDtypeStruct((QH, TILE), jnp.float32),
        name="row_deltas",
    )(outputs, out_grad)


def backward_kernel(depth, steps, me_ref, anc_ref, q_own, q_peer, g_own, g_peer, d_own, d_peer, *rest):
    arrivals = rest[: 2 * steps]
    dq_own, dq_peer, near_ref, far_ref = rest[2 * steps : 2 * steps + 4]
    (k_all, v_all, q_all, g_all, delta, probs, chunk_max, total, dk_acc, dv_acc, dq_acc) = rest[
        2 * steps + 4 :
    ]
    me = me_ref[0]
    core = me & 1
    chip = me >> 1
    level = chip // COLS
    column = chip % COLS

    for index, arrival in enumerate(arrivals):
        for half in range(2):
            rows = slice(half * TILE, (half + 1) * TILE)
            k_all[2 * index + half] = arrival[rows, :HD]
            v_all[2 * index + half] = arrival[rows, HD:]
    for u, (q_ref, g_ref, d_ref) in enumerate(((q_own, g_own, d_own), (q_peer, g_peer, d_peer))):
        for head in range(GROUP):
            rows = slice(head * TILE, (head + 1) * TILE)
            cols = slice(head * HD, (head + 1) * HD)
            q_all[u, rows, :] = q_ref[:, cols]
            g_all[u, rows, :] = g_ref[:, cols]
            delta[u, :, rows] = d_ref[head : head + 1, :]
    dk_acc[...] = jnp.zeros_like(dk_acc)
    dv_acc[...] = jnp.zeros_like(dv_acc)

    def slot_of(tile):
        other = tile >> 1
        shift = level - other // COLS
        beside = column ^ (other % COLS)
        return (shift * COLS + beside) * 2 + ((tile & 1) ^ core)

    def one_tile(u, carry):
        tile = 2 * chip + (core ^ u)
        live = jnp.int32(1)
        for slot in range(depth):
            live += (anc_ref[tile, slot] >= 0).astype(jnp.int32)
        own_slot = slot_of(tile)
        chunks = (live + 1) // 2

        def slots(chunk):
            if isinstance(chunk, int) and chunk == 0:
                first = own_slot
            else:
                first = slot_of(anc_ref[tile, 2 * chunk - 1])
            good = 2 * chunk + 1 < live
            second = jnp.where(
                good, slot_of(anc_ref[tile, jnp.minimum(2 * chunk, depth - 1)]), own_slot
            )
            return first, second, good

        def scores_chunk(chunk):
            is_first = isinstance(chunk, int) and chunk == 0
            first, second, good = slots(chunk)
            key_block = jnp.concatenate([k_all[first], k_all[second]], axis=0)
            for pair in range(GROUP // 2):
                rows = slice(pair * PAIR, (pair + 1) * PAIR)
                raw = lax.dot_general(
                    key_block, q_all[u, rows, :], NT_DIMS, preferred_element_type=jnp.float32
                ) * (SCALE * LOG2E)
                top, low = raw[:TILE], raw[TILE:]
                if is_first:
                    key_pos = lax.broadcasted_iota(jnp.int32, (TILE, PAIR), 0)
                    query_pos = lax.broadcasted_iota(jnp.int32, (TILE, PAIR), 1) & (TILE - 1)
                    top = jnp.where(key_pos <= query_pos, top, MASKED)
                low = jnp.where(good, low, MASKED)
                block_max = jnp.maximum(
                    jnp.max(top, axis=0, keepdims=True), jnp.max(low, axis=0, keepdims=True)
                )
                if is_first:
                    new_max = block_max
                else:
                    old_max = chunk_max[chunk - 1, :, rows]
                    new_max = jnp.maximum(old_max, block_max)
                top = jnp.exp2(top - new_max)
                low = jnp.exp2(low - new_max)
                block_sum = jnp.sum(top, axis=0, keepdims=True) + jnp.sum(
                    low, axis=0, keepdims=True
                )
                if not is_first:
                    block_sum += total[:, rows] * jnp.exp2(old_max - new_max)
                total[:, rows] = block_sum
                chunk_max[chunk, :, rows] = new_max
                probs[chunk, :TILE, rows] = top
                probs[chunk, TILE:, rows] = low

        scores_chunk(0)

        def scores_loop(chunk, carry):
            scores_chunk(chunk)
            return carry

        lax.fori_loop(1, chunks, scores_loop, 0)
        final_max = chunk_max[chunks - 1]
        inverse = 1.0 / total[...]
        dq_acc[...] = jnp.zeros_like(dq_acc)

        def grads_loop(chunk, carry):
            first = jnp.where(
                chunk == 0, own_slot, slot_of(anc_ref[tile, jnp.maximum(2 * chunk - 1, 0)])
            )
            good = 2 * chunk + 1 < live
            second = jnp.where(
                good, slot_of(anc_ref[tile, jnp.minimum(2 * chunk, depth - 1)]), own_slot
            )
            key_block = jnp.concatenate([k_all[first], k_all[second]], axis=0)
            value_block = jnp.concatenate([v_all[first], v_all[second]], axis=0)
            key_turned = key_block.T
            factor = jnp.exp2(chunk_max[chunk] - final_max) * inverse
            dk = jnp.zeros((PAIR, HD), jnp.float32)
            dv = jnp.zeros((PAIR, HD), jnp.float32)
            for pair in range(GROUP // 2):
                rows = slice(pair * PAIR, (pair + 1) * PAIR)
                query_block = q_all[u, rows, :]
                grad_block = g_all[u, rows, :]
                grad_probs = lax.dot_general(
                    value_block, grad_block, NT_DIMS, preferred_element_type=jnp.float32
                )
                attn = probs[chunk, :, rows] * factor[:, rows]
                attn_low = attn.astype(jnp.bfloat16)
                grad_scores = (attn * (grad_probs - delta[u, :, rows])).astype(jnp.bfloat16)
                dv += jnp.dot(attn_low, grad_block, preferred_element_type=jnp.float32)
                dk += jnp.dot(grad_scores, query_block, preferred_element_type=jnp.float32)
                dq_acc[:, rows] += jnp.dot(
                    key_turned, grad_scores, preferred_element_type=jnp.float32
                )
            dk_acc[first] += dk[:TILE]
            dk_acc[second] += dk[TILE:]
            dv_acc[first] += dv[:TILE]
            dv_acc[second] += dv[TILE:]
            return carry

        lax.fori_loop(0, chunks, grads_loop, 0)

        def put(dq_ref):
            for head in range(GROUP):
                cols = slice(head * TILE, (head + 1) * TILE)
                dq_ref[:, cols] = (dq_acc[:, cols] * SCALE).T.astype(jnp.bfloat16)

        @pl.when(u == 0)
        def _():
            put(dq_own)

        @pl.when(u == 1)
        def _():
            put(dq_peer)

        return carry

    lax.fori_loop(0, 2, one_tile, 0)

    for shift in range(steps):
        for half in range(2):
            rows = slice(half * TILE, (half + 1) * TILE)
            slot = shift * 4 + half
            near_ref[shift, rows, :HD] = dk_acc[slot]
            near_ref[shift, rows, HD:] = dv_acc[slot]
            far_ref[shift, rows, :HD] = dk_acc[slot + 2].astype(jnp.bfloat16)
            far_ref[shift, rows, HD:] = dv_acc[slot + 2].astype(jnp.bfloat16)


def head_backward(local, me, ancestors, q_pair, g_pair, d_pair, arrivals):
    steps = len(arrivals) // 2
    depth = ancestors.shape[1]
    max_chunks = (depth + 2) // 2
    slots = 4 * steps

    def pick(me_ref):
        return (me_ref[0] & 1) * LOCAL + local

    wide = pl.BlockSpec((TILE, ROWS), lambda i, me_ref, anc_ref: (0, pick(me_ref)))
    small = pl.BlockSpec((GROUP, TILE), lambda i, me_ref, anc_ref: (pick(me_ref), 0))
    whole = pl.BlockSpec((PAIR, 2 * HD), lambda i, *_: (0, 0))
    return pl.pallas_call(
        functools.partial(backward_kernel, depth, steps),
        grid_spec=pltpu.PrefetchScalarGridSpec(
            num_scalar_prefetch=2,
            grid=(1,),
            in_specs=[wide] * 4 + [small] * 2 + [whole] * len(arrivals),
            out_specs=[
                pl.BlockSpec((TILE, ROWS), lambda i, *_: (0, 0)),
                pl.BlockSpec((TILE, ROWS), lambda i, *_: (0, 0)),
                pl.BlockSpec((steps, PAIR, 2 * HD), lambda i, *_: (0, 0, 0)),
                pl.BlockSpec((steps, PAIR, 2 * HD), lambda i, *_: (0, 0, 0)),
            ],
            scratch_shapes=[
                pltpu.VMEM((slots, TILE, HD), jnp.bfloat16),
                pltpu.VMEM((slots, TILE, HD), jnp.bfloat16),
                pltpu.VMEM((2, ROWS, HD), jnp.bfloat16),
                pltpu.VMEM((2, ROWS, HD), jnp.bfloat16),
                pltpu.VMEM((2, 1, ROWS), jnp.float32),
                pltpu.VMEM((max_chunks, PAIR, ROWS), jnp.float32),
                pltpu.VMEM((max_chunks, 1, ROWS), jnp.float32),
                pltpu.VMEM((1, ROWS), jnp.float32),
                pltpu.VMEM((slots, TILE, HD), jnp.float32),
                pltpu.VMEM((slots, TILE, HD), jnp.float32),
                pltpu.VMEM((HD, ROWS), jnp.float32),
            ],
        ),
        out_shape=[
            jax.ShapeDtypeStruct((TILE, ROWS), jnp.bfloat16),
            jax.ShapeDtypeStruct((TILE, ROWS), jnp.bfloat16),
            jax.ShapeDtypeStruct((steps, PAIR, 2 * HD), jnp.float32),
            jax.ShapeDtypeStruct((steps, PAIR, 2 * HD), jnp.bfloat16),
        ],
        compiler_params=pltpu.CompilerParams(vmem_limit_bytes=48 * 1024 * 1024),
        name="tree_backward",
    )(me, ancestors, *q_pair, *g_pair, *d_pair, *arrivals)


def per_device(tok_count, queries, keys, values, outputs, out_grad, ancestors):
    steps = tok_count // (2 * COLS)
    width = 2 * COLS
    index = lax.axis_index("tok")
    core = index % 2
    me = index.reshape(1).astype(jnp.int32)

    swap = [(t, t ^ 1) for t in range(tok_count)]

    def to_peer(x):
        return lax.ppermute(x, "tok", swap)

    def up(x, shift):
        return lax.ppermute(
            x, "tok", [(t, t + shift * width) for t in range(tok_count - shift * width)]
        )

    def down(x, shift):
        return lax.ppermute(
            x, "tok", [(t + shift * width, t) for t in range(tok_count - shift * width)]
        )

    def beside(x, lowest, first=0, last=1):
        return lax.ppermute(
            x,
            "tok",
            [
                (t, t ^ 2)
                for t in range(lowest * width, tok_count)
                if first <= (t >> 1) % COLS <= last
            ],
        )

    def columns(x, who, count):
        return lax.dynamic_slice_in_dim(x, who * count, count, 1)

    half_cols = LOCAL * HD
    kv_peer = to_peer(
        jnp.concatenate(
            [columns(keys, 1 - core, half_cols), columns(values, 1 - core, half_cols)], axis=1
        )
    )
    kv_own = jnp.concatenate([columns(keys, core, half_cols), columns(values, core, half_cols)], axis=1)
    q_pair = (queries, to_peer(queries))
    g_pair = (out_grad, to_peer(out_grad))
    deltas = row_deltas(outputs, out_grad)
    d_pair = (deltas, to_peer(deltas))

    gathered = []
    for local in range(LOCAL):
        payload = jnp.concatenate(
            [
                jnp.concatenate(
                    [
                        part[:, local * HD : (local + 1) * HD],
                        part[:, half_cols + local * HD : half_cols + (local + 1) * HD],
                    ],
                    axis=1,
                )
                for part in (kv_own, kv_peer)
            ],
            axis=0,
        )
        arrivals = [payload, beside(payload, 0, 0, 0)]
        for shift in range(1, steps):
            moved = up(payload, shift)
            arrivals += [moved, beside(moved, shift)]
        gathered.append(arrivals)

    dq_own, dq_peer, sums = [], [], []
    for local in range(LOCAL):
        own, peer, near, far = head_backward(
            local, me, ancestors, q_pair, g_pair, d_pair, gathered[local]
        )
        dq_own.append(own)
        dq_peer.append(to_peer(peer))
        acc = near[0] + beside(far[0], 0, 1, 1).astype(jnp.float32)
        for shift in range(steps - 1, 0, -1):
            joint = near[shift] + beside(far[shift], shift).astype(jnp.float32)
            acc += down(joint.astype(jnp.bfloat16), shift).astype(jnp.float32)
        scaled = jnp.concatenate([acc[:, :HD] * SCALE, acc[:, HD:]], axis=1).astype(jnp.bfloat16)
        sums.append((scaled[:TILE], to_peer(scaled[TILE:])))

    def in_order(own, other):
        return jnp.where(
            core == 0,
            jnp.concatenate(own + other, axis=1),
            jnp.concatenate(other + own, axis=1),
        )

    return (
        in_order(dq_own, dq_peer),
        in_order([s[0][:, :HD] for s in sums], [s[1][:, :HD] for s in sums]),
        in_order([s[0][:, HD:] for s in sums], [s[1][:, HD:] for s in sums]),
    )


def solution(mesh):
    return jax.shard_map(
        functools.partial(per_device, mesh.shape["tok"]),
        mesh=mesh,
        in_specs=(
            P(("parts", "tok"), None),
            P(("parts", "tok"), None),
            P(("parts", "tok"), None),
            P(("parts", "tok"), None),
            P(("parts", "tok"), None),
            P("parts", None),
        ),
        out_specs=(P(("parts", "tok"), None), P(("parts", "tok"), None), P(("parts", "tok"), None)),
        check_vma=False,
    )
```

time: 464 us -> 142 us (0.31)
  the two profiles are of different devices: /device:TPU:0 before, /device:TPU:15 now
where the time goes in v1:
time: 142 us; the launch traced here: 141 us
  starting transfers between devices  60.1 us (42%)
  waiting for transfers between devices  49.9 us (35%)
  Pallas kernels  23.7 us (17%)
  local copies, waits for them, and re-layouts  3.27 us (2%)
  other arithmetic  3.04 us (2%)
    ppermute x6, waiting for transfers between devices, down(): lax.ppermute(x, 'tok', [(t + shift * width, t) for t in range(tok_count -...  36.7 us
    ppermute x16, starting transfers between devices, beside(): lax.ppermute(x, 'tok', [(t, t ^ 2) for t in range(lowest * width, tok_cou...  23.6 us
    pallas_call x2, Pallas kernels, head_backward(): pl.pallas_call(functools.partial(backward_kernel, depth, steps), grid_spe...  20.9 us
    ppermute x6, starting transfers between devices, up(): lax.ppermute(x, 'tok', [(t, t + shift * width) for t in range(tok_count -...  14.5 us
    ppermute x8, starting transfers between devices, to_peer(): return lax.ppermute(x, 'tok', swap)  13.2 us
    ppermute x6, waiting for transfers between devices, up(): lax.ppermute(x, 'tok', [(t, t + shift * width) for t in range(tok_count -...  9.96 us
    ppermute x6, starting transfers between devices, down(): lax.ppermute(x, 'tok', [(t + shift * width, t) for t in range(tok_count -...  8.82 us
  transfers between devices with their start and end apart: 36, of which 7 were waited for; matrix products, arithmetic and copies ran while one was open for 2% of the time, Pallas kernels for 17%

profile of v1, /device:TPU:15, one launch (start us, length us, event | category | flops | bytes accessed | tf_op | source)
XLA Modules:
  0.0 141.3 jit_solution(8275310163696192178)
XLA Ops:
  0.6 0.7 collective-permute-start
  1.4 0.1 collective-permute-start.1
  1.5 0.9 constant_dynamic-slice_fusion.2
  2.4 0.5 collective-permute-start.3
  2.8 0.8 constant_dynamic-slice_fusion
  3.7 1.5 %collective-permute-done.3 = bf16[128,512]{1,0:T(8,128)(2,1)S(1)} collective-permute-done((bf16[128,512]{1,0:T(8,128)(2,1)S(1)}, bf16[128,512]{1,0:T(8,128)(2,1)S(1)}, u32[]{:S(2)}, u32[]{:S(2)}) %collective-permute-start.3) | collective-permute-done | bytes 131104 | tf_op jit(solution)/shard_map/ppermute | solution.py:262
  5.3 0.0 copy-start
  5.3 0.8 collective-permute-start.9
  6.1 2.8 %row_deltas.1.d_own = f32[32,128]{1,0:T(8,128)} custom-call(bf16[128,4096]{1,0:T(8,128)(2,1)} %out_ref.1, bf16[128,4096]{1,0:T(8,128)(2,1)} %g_own.3), custom_call_target="tpu_custom_call" | custom-call | tf_op jit(solution)/shard_map/row_deltas/pallas_call | solution.py:34
  8.9 0.1 collective-permute-start.2
  9.0 3.2 %collective-permute-start.5 = (bf16[256,256]{1,0:T(8,128)(2,1)S(1)}, bf16[256,256]{1,0:T(8,128)(2,1)S(1)}, u32[]{:S(2)}, u32[]{:S(2)}) collective-permute-start(bf16[256,256]{1,0:T(8,128)(2,1)S(1)} %maximum_maximum_fusion.rest_0_), channel_id=1, source_target_pairs={{0,4},{1,5},{2,6},{3,7},{4,8},{5,9},{6,10},{7,11},{8,12},{9,13},{1... | collective-permute-start | bytes 393224 | tf_op jit(solution)/shard_map/ppermute | solution.py:265
  12.2 0.0 collective-permute-done.2.d_peer
  12.2 2.9 %collective-permute-start.7 = (bf16[256,256]{1,0:T(8,128)(2,1)S(1)}, bf16[256,256]{1,0:T(8,128)(2,1)S(1)}, u32[]{:S(2)}, u32[]{:S(2)}) collective-permute-start(bf16[256,256]{1,0:T(8,128)(2,1)S(1)} %maximum_maximum_fusion.rest_0_), channel_id=1, source_target_pairs={{0,8},{1,9},{2,10},{3,11},{4,12},{5,13},{6,14},{7,15},{16,24},{17,... | collective-permute-start | bytes 393224 | tf_op jit(solution)/shard_map/ppermute | solution.py:265
  15.1 0.0 collective-permute-done.9.rest_6_
  15.2 1.3 collective-permute-start.4
  16.5 2.6 %collective-permute-done.5.rest_2_ = bf16[256,256]{1,0:T(8,128)(2,1)S(1)} collective-permute-done((bf16[256,256]{1,0:T(8,128)(2,1)S(1)}, bf16[256,256]{1,0:T(8,128)(2,1)S(1)}, u32[]{:S(2)}, u32[]{:S(2)}) %collective-permute-start.5) | collective-permute-done | bytes 131104 | tf_op jit(solution)/shard_map/ppermute | solution.py:265
  19.1 1.9 %collective-permute-start.12 = (bf16[256,256]{1,0:T(8,128)(2,1)S(1)}, bf16[256,256]{1,0:T(8,128)(2,1)S(1)}, u32[]{:S(2)}, u32[]{:S(2)}) collective-permute-start(bf16[256,256]{1,0:T(8,128)(2,1)S(1)} %maximum_maximum_fusion.1.rest_0_), channel_id=1, source_target_pairs={{0,4},{1,5},{2,6},{3,7},{4,8},{5,9},{6,10},{7,11},{8,12},{9,13},{1... | collective-permute-start | bytes 393224 | tf_op jit(solution)/shard_map/ppermute | solution.py:265
  21.0 1.2 collective-permute-done.7.rest_4_
  22.2 5.0 %collective-permute-start.14 = (bf16[256,256]{1,0:T(8,128)(2,1)S(1)}, bf16[256,256]{1,0:T(8,128)(2,1)S(1)}, u32[]{:S(2)}, u32[]{:S(2)}) collective-permute-start(bf16[256,256]{1,0:T(8,128)(2,1)S(1)} %maximum_maximum_fusion.1.rest_0_), channel_id=1, source_target_pairs={{0,8},{1,9},{2,10},{3,11},{4,12},{5,13},{6,14},{7,15},{16,24},{17,... | collective-permute-start | bytes 393224 | tf_op jit(solution)/shard_map/ppermute | solution.py:265
  27.2 0.7 collective-permute-start.16
  27.9 0.0 collective-permute-done.12.rest_2_
  27.9 0.7 collective-permute-start.10
  28.6 6.2 %collective-permute-done.14.rest_4_ = bf16[256,256]{1,0:T(8,128)(2,1)S(1)} collective-permute-done((bf16[256,256]{1,0:T(8,128)(2,1)S(1)}, bf16[256,256]{1,0:T(8,128)(2,1)S(1)}, u32[]{:S(2)}, u32[]{:S(2)}) %collective-permute-start.14) | collective-permute-done | bytes 131104 | tf_op jit(solution)/shard_map/ppermute | solution.py:265
  34.7 2.1 %collective-permute-start.6 = (bf16[256,256]{1,0:T(8,128)(2,1)S(1)}, bf16[256,256]{1,0:T(8,128)(2,1)S(1)}, u32[]{:S(2)}, u32[]{:S(2)}) collective-permute-start(bf16[256,256]{1,0:T(8,128)(2,1)S(1)} %collective-permute-done.5.rest_2_), channel_id=1, source_target_pairs={{4,6},{5,7},{6,4},{7,5},{8,10},{9,11},{10,8},{11,9},{12,14},{13,15... | collective-permute-start | bytes 393224 | tf_op jit(solution)/shard_map/ppermute | solution.py:275
  36.9 1.3 collective-permute-start.8
  38.2 1.3 collective-permute-start.11
  39.5 1.7 %collective-permute-done.6.rest_3_ = bf16[256,256]{1,0:T(8,128)(2,1)S(1)} collective-permute-done((bf16[256,256]{1,0:T(8,128)(2,1)S(1)}, bf16[256,256]{1,0:T(8,128)(2,1)S(1)}, u32[]{:S(2)}, u32[]{:S(2)}) %collective-permute-start.6) | collective-permute-done | bytes 131104 | tf_op jit(solution)/shard_map/ppermute | solution.py:275
  41.2 2.3 %collective-permute-start.13 = (bf16[256,256]{1,0:T(8,128)(2,1)S(1)}, bf16[256,256]{1,0:T(8,128)(2,1)S(1)}, u32[]{:S(2)}, u32[]{:S(2)}) collective-permute-start(bf16[256,256]{1,0:T(8,128)(2,1)S(1)} %collective-permute-done.12.rest_2_), channel_id=1, source_target_pairs={{4,6},{5,7},{6,4},{7,5},{8,10},{9,11},{10,8},{11,9},{12,14},{13,15... | collective-permute-start | bytes 393224 | tf_op jit(solution)/shard_map/ppermute | solution.py:275
  43.5 0.7 collective-permute-start.15
  44.2 0.7 collective-permute-start.17
  44.9 0.0 copy-start.1
  44.9 0.7 copy-done.1
  45.6 0.7 copy-done.3
  46.3 10.4 %tree_backward.2 = (bf16[128,1024]{1,0:T(8,128)(2,1)S(1)}, bf16[128,1024]{1,0:T(8,128)(2,1)S(1)}, f32[4,256,256]{2,1,0:T(8,128)S(1)}, bf16[4,256,256]{2,1,0:T(8,128)(2,1)S(1)}) custom-call(s32[1]{0:T(128)} %bitcast.me_ref, s32[16,10]{1,0:T(8,128)S(1)} %copy-done.3, bf16[128,4096]{1,0:T(8,128)(2,1)S(1)} %copy-done, ...), custom_call_target="tpu_custom_call" | custom-call | tf_op jit(solution)/shard_map/tree_backward/pallas_call | solution.py:215
  56.8 0.0 copy-start.2
  56.8 0.0 copy-start.4
  56.8 0.7 collective-permute-start.21
  57.5 0.7 collective-permute-start.23
  58.2 1.9 %collective-permute-start.25 = (bf16[256,256]{1,0:T(8,128)(2,1)S(1)}, bf16[256,256]{1,0:T(8,128)(2,1)S(1)}, u32[]{:S(2)}, u32[]{:S(2)}) collective-permute-start(bf16[256,256]{1,0:T(8,128)(2,1)S(1)} %get-tuple-element.30), channel_id=1, source_target_pairs={{4,6},{5,7},{6,4},{7,5},{8,10},{9,11},{10,8},{11,9},{12,14},{13,15... | collective-permute-start | bytes 393224 | tf_op jit(solution)/shard_map/ppermute | solution.py:275
  60.2 3.4 %collective-permute-start.20 = (bf16[256,256]{1,0:T(8,128)(2,1)S(1)}, bf16[256,256]{1,0:T(8,128)(2,1)S(1)}, u32[]{:S(2)}, u32[]{:S(2)}) collective-permute-start(bf16[256,256]{1,0:T(8,128)(2,1)S(1)} %get-tuple-element.29), channel_id=1, source_target_pairs={{2,0},{3,1},{6,4},{7,5},{10,8},{11,9},{14,12},{15,13},{18,16},{19,... | collective-permute-start | bytes 393224 | tf_op jit(solution)/shard_map/ppermute | solution.py:275
  63.6 10.5 %tree_backward.3 = (bf16[128,1024]{1,0:T(8,128)(2,1)S(1)}, bf16[128,1024]{1,0:T(8,128)(2,1)S(1)}, f32[4,256,256]{2,1,0:T(8,128)S(1)}, bf16[4,256,256]{2,1,0:T(8,128)(2,1)S(1)}) custom-call(s32[1]{0:T(128)} %bitcast.me_ref, s32[16,10]{1,0:T(8,128)S(1)} %copy-done.4, bf16[128,4096]{1,0:T(8,128)(2,1)S(1)} %copy-done, ...), custom_call_target="tpu_custom_call" | custom-call | tf_op jit(solution)/shard_map/tree_backward/pallas_call | solution.py:215
  74.1 0.7 collective-permute-start.28
  74.7 0.7 collective-permute-start.30
  75.4 1.9 %collective-permute-start.32 = (bf16[256,256]{1,0:T(8,128)(2,1)S(1)}, bf16[256,256]{1,0:T(8,128)(2,1)S(1)}, u32[]{:S(2)}, u32[]{:S(2)}) collective-permute-start(bf16[256,256]{1,0:T(8,128)(2,1)S(1)} %get-tuple-element.34), channel_id=1, source_target_pairs={{4,6},{5,7},{6,4},{7,5},{8,10},{9,11},{10,8},{11,9},{12,14},{13,15... | collective-permute-start | bytes 393224 | tf_op jit(solution)/shard_map/ppermute | solution.py:275
  77.4 3.4 %collective-permute-start.27 = (bf16[256,256]{1,0:T(8,128)(2,1)S(1)}, bf16[256,256]{1,0:T(8,128)(2,1)S(1)}, u32[]{:S(2)}, u32[]{:S(2)}) collective-permute-start(bf16[256,256]{1,0:T(8,128)(2,1)S(1)} %get-tuple-element.33), channel_id=1, source_target_pairs={{2,0},{3,1},{6,4},{7,5},{10,8},{11,9},{14,12},{15,13},{18,16},{19,... | collective-permute-start | bytes 393224 | tf_op jit(solution)/shard_map/ppermute | solution.py:275
  80.7 0.1 fusion.8
  80.9 0.7 collective-permute-start.22
  81.5 1.3 collective-permute-start.24
  82.9 1.9 %collective-permute-start.26 = (bf16[256,256]{1,0:T(8,128)(2,1)S(1)}, bf16[256,256]{1,0:T(8,128)(2,1)S(1)}, u32[]{:S(2)}, u32[]{:S(2)}) collective-permute-start(bf16[256,256]{1,0:T(8,128)(2,1)S(1)} %get-tuple-element.24), channel_id=1, source_target_pairs={{4,0},{5,1},{6,2},{7,3},{8,4},{9,5},{10,6},{11,7},{12,8},{13,9},{1... | collective-permute-start | bytes 393224 | tf_op jit(solution)/shard_map/ppermute | solution.py:270
  84.8 0.1 fusion.2
  84.9 2.6 %collective-permute-start.18 = (bf16[128,1024]{1,0:T(8,128)(2,1)S(1)}, bf16[128,1024]{1,0:T(8,128)(2,1)S(1)}, u32[]{:S(2)}, u32[]{:S(2)}) collective-permute-start(bf16[128,1024]{1,0:T(8,128)(2,1)S(1)} %get-tuple-element.13), channel_id=1, source_target_pairs={{0,1},{1,0},{2,3},{3,2},{4,5},{5,4},{6,7},{7,6},{8,9},{9,8},{10,11... | collective-permute-start | bytes 786440 | tf_op jit(solution)/shard_map/ppermute | solution.py:262
  87.5 0.7 collective-permute-start.29
  88.2 33.0 %collective-permute-done.24 = bf16[256,256]{1,0:T(8,128)(2,1)S(1)} collective-permute-done((bf16[256,256]{1,0:T(8,128)(2,1)S(1)}, bf16[256,256]{1,0:T(8,128)(2,1)S(1)}, u32[]{:S(2)}, u32[]{:S(2)}) %collective-permute-start.24) | collective-permute-done | bytes 131104 | tf_op jit(solution)/shard_map/ppermute | solution.py:270
  121.2 1.3 collective-permute-start.31
  122.5 3.0 %collective-permute-start.33 = (bf16[256,256]{1,0:T(8,128)(2,1)S(1)}, bf16[256,256]{1,0:T(8,128)(2,1)S(1)}, u32[]{:S(2)}, u32[]{:S(2)}) collective-permute-start(bf16[256,256]{1,0:T(8,128)(2,1)S(1)} %get-tuple-element.27), channel_id=1, source_target_pairs={{4,0},{5,1},{6,2},{7,3},{8,4},{9,5},{10,6},{11,7},{12,8},{13,9},{1... | collective-permute-start | bytes 393224 | tf_op jit(solution)/shard_map/ppermute | solution.py:270
  125.5 0.1 fusion.14
  125.6 5.6 %collective-permute-start.19 = (bf16[128,1024]{1,0:T(8,128)(2,1)S(1)}, bf16[128,1024]{1,0:T(8,128)(2,1)S(1)}, u32[]{:S(2)}, u32[]{:S(2)}) collective-permute-start(bf16[128,1024]{1,0:T(8,128)(2,1)S(1)} %get-tuple-element.14), channel_id=1, source_target_pairs={{0,1},{1,0},{2,3},{3,2},{4,5},{5,4},{6,7},{7,6},{8,9},{9,8},{10,11... | collective-permute-start | bytes 786440 | tf_op jit(solution)/shard_map/ppermute | solution.py:262
  131.2 3.7 %collective-permute-done.33 = bf16[256,256]{1,0:T(8,128)(2,1)S(1)} collective-permute-done((bf16[256,256]{1,0:T(8,128)(2,1)S(1)}, bf16[256,256]{1,0:T(8,128)(2,1)S(1)}, u32[]{:S(2)}, u32[]{:S(2)}) %collective-permute-start.33) | collective-permute-done | bytes 131104 | tf_op jit(solution)/shard_map/ppermute | solution.py:270
  134.9 0.1 fusion.16
  135.1 3.4 %collective-permute-start.34 = (bf16[128,256]{1,0:T(8,128)(2,1)S(1)}, bf16[128,256]{1,0:T(8,128)(2,1)S(1)}, u32[]{:S(2)}, u32[]{:S(2)}) collective-permute-start(bf16[128,256]{1,0:T(8,128)(2,1)S(1)} %pad_maximum_fusion.2), channel_id=1, source_target_pairs={{0,1},{1,0},{2,3},{3,2},{4,5},{5,4},{6,7},{7,6},{8,9},{9,8},{10,11... | collective-permute-start | bytes 196616 | tf_op jit(solution)/shard_map/ppermute | solution.py:262
  138.5 0.1 collective-permute-start.35
  138.6 1.2 maximum_select_fusion
  139.9 0.7 maximum_select_fusion.2
  140.6 0.7 maximum_select_fusion.1
  (48 shorter events, 0.3 us)
Async XLA Ops:
  0.6 43.6 %collective-permute-start = (bf16[128,4096]{1,0:T(8,128)(2,1)}, bf16[128,4096]{1,0:T(8,128)(2,1)S(1)}, u32[]{:S(2)}, u32[]{:S(2)}) collective-permute-start(bf16[128,4096]{1,0:T(8,128)(2,1)} %q_own.3), channel_id=1, source_target_pairs={{0,1},{1,0},{2,3},{3,2},{4,5},{5,4},{6,7},{7,6},{8,9},{9,8},{10,11... | collective-permute-start | bytes 3145736 | tf_op jit(solution)/shard_map/ppermute | solution.py:262
  1.4 43.5 %collective-permute-start.1 = (bf16[128,4096]{1,0:T(8,128)(2,1)}, bf16[128,4096]{1,0:T(8,128)(2,1)}, u32[]{:S(2)}, u32[]{:S(2)}) collective-permute-start(bf16[128,4096]{1,0:T(8,128)(2,1)} %g_own.3), channel_id=1, source_target_pairs={{0,1},{1,0},{2,3},{3,2},{4,5},{5,4},{6,7},{7,6},{8,9},{9,8},{10,11... | collective-permute-start | bytes 3145736 | tf_op jit(solution)/shard_map/ppermute | solution.py:262
  2.4 2.9 %collective-permute-start.3 = (bf16[128,512]{1,0:T(8,128)(2,1)S(1)}, bf16[128,512]{1,0:T(8,128)(2,1)S(1)}, u32[]{:S(2)}, u32[]{:S(2)}) collective-permute-start(bf16[128,512]{1,0:T(8,128)(2,1)S(1)} %pad_maximum_fusion), channel_id=1, source_target_pairs={{0,1},{1,0},{2,3},{3,2},{4,5},{5,4},{6,7},{7,6},{8,9},{9,8},{10,11... | collective-permute-start | bytes 393224 | tf_op jit(solution)/shard_map/ppermute | solution.py:262
  5.3 39.6 %copy-start = (bf16[128,4096]{1,0:T(8,128)(2,1)S(1)}, bf16[128,4096]{1,0:T(8,128)(2,1)}, u32[]{:S(2)}) copy-start(bf16[128,4096]{1,0:T(8,128)(2,1)} %q_own.3) | copy-start | bytes 3145732
  5.3 9.9 %collective-permute-start.9 = (bf16[256,256]{1,0:T(8,128)(2,1)S(1)}, bf16[256,256]{1,0:T(8,128)(2,1)S(1)}, u32[]{:S(2)}, u32[]{:S(2)}) collective-permute-start(bf16[256,256]{1,0:T(8,128)(2,1)S(1)} %maximum_maximum_fusion.rest_0_), channel_id=1, source_target_pairs={{0,12},{1,13},{2,14},{3,15},{16,28},{17,29},{18,30},{19,31}} | collective-permute-start | bytes 393224 | tf_op jit(solution)/shard_map/ppermute | solution.py:265
  8.9 3.3 %collective-permute-start.2 = (f32[32,128]{1,0:T(8,128)}, f32[32,128]{1,0:T(8,128)S(1)}, u32[]{:S(2)}, u32[]{:S(2)}) collective-permute-start(f32[32,128]{1,0:T(8,128)} %row_deltas.1.d_own), channel_id=1, source_target_pairs={{0,1},{1,0},{2,3},{3,2},{4,5},{5,4},{6,7},{7,6},{8,9},{9,8},{10,11... | collective-permute-start | bytes 49160 | tf_op jit(solution)/shard_map/ppermute | solution.py:262
  9.0 10.1 %collective-permute-start.5 = (bf16[256,256]{1,0:T(8,128)(2,1)S(1)}, bf16[256,256]{1,0:T(8,128)(2,1)S(1)}, u32[]{:S(2)}, u32[]{:S(2)}) collective-permute-start(bf16[256,256]{1,0:T(8,128)(2,1)S(1)} %maximum_maximum_fusion.rest_0_), channel_id=1, source_target_pairs={{0,4},{1,5},{2,6},{3,7},{4,8},{5,9},{6,10},{7,11},{8,12},{9,13},{1... | collective-permute-start | bytes 393224 | tf_op jit(solution)/shard_map/ppermute | solution.py:265
  12.2 10.0 %collective-permute-start.7 = (bf16[256,256]{1,0:T(8,128)(2,1)S(1)}, bf16[256,256]{1,0:T(8,128)(2,1)S(1)}, u32[]{:S(2)}, u32[]{:S(2)}) collective-permute-start(bf16[256,256]{1,0:T(8,128)(2,1)S(1)} %maximum_maximum_fusion.rest_0_), channel_id=1, source_target_pairs={{0,8},{1,9},{2,10},{3,11},{4,12},{5,13},{6,14},{7,15},{16,24},{17,... | collective-permute-start | bytes 393224 | tf_op jit(solution)/shard_map/ppermute | solution.py:265
  15.2 12.0 %collective-permute-start.4 = (bf16[256,256]{1,0:T(8,128)(2,1)S(1)}, bf16[256,256]{1,0:T(8,128)(2,1)S(1)}, u32[]{:S(2)}, u32[]{:S(2)}) collective-permute-start(bf16[256,256]{1,0:T(8,128)(2,1)S(1)} %maximum_maximum_fusion.rest_0_), channel_id=1, source_target_pairs={{0,2},{1,3},{4,6},{5,7},{8,10},{9,11},{12,14},{13,15},{16,18},{17,... | collective-permute-start | bytes 393224 | tf_op jit(solution)/shard_map/ppermute | solution.py:275
  19.1 8.8 %collective-permute-start.12 = (bf16[256,256]{1,0:T(8,128)(2,1)S(1)}, bf16[256,256]{1,0:T(8,128)(2,1)S(1)}, u32[]{:S(2)}, u32[]{:S(2)}) collective-permute-start(bf16[256,256]{1,0:T(8,128)(2,1)S(1)} %maximum_maximum_fusion.1.rest_0_), channel_id=1, source_target_pairs={{0,4},{1,5},{2,6},{3,7},{4,8},{5,9},{6,10},{7,11},{8,12},{9,13},{1... | collective-permute-start | bytes 393224 | tf_op jit(solution)/shard_map/ppermute | solution.py:265
  22.2 12.5 %collective-permute-start.14 = (bf16[256,256]{1,0:T(8,128)(2,1)S(1)}, bf16[256,256]{1,0:T(8,128)(2,1)S(1)}, u32[]{:S(2)}, u32[]{:S(2)}) collective-permute-start(bf16[256,256]{1,0:T(8,128)(2,1)S(1)} %maximum_maximum_fusion.1.rest_0_), channel_id=1, source_target_pairs={{0,8},{1,9},{2,10},{3,11},{4,12},{5,13},{6,14},{7,15},{16,24},{17,... | collective-permute-start | bytes 393224 | tf_op jit(solution)/shard_map/ppermute | solution.py:265
  27.2 9.7 %collective-permute-start.16 = (bf16[256,256]{1,0:T(8,128)(2,1)S(1)}, bf16[256,256]{1,0:T(8,128)(2,1)S(1)}, u32[]{:S(2)}, u32[]{:S(2)}) collective-permute-start(bf16[256,256]{1,0:T(8,128)(2,1)S(1)} %maximum_maximum_fusion.1.rest_0_), channel_id=1, source_target_pairs={{0,12},{1,13},{2,14},{3,15},{16,28},{17,29},{18,30},{19,31}} | collective-permute-start | bytes 393224 | tf_op jit(solution)/shard_map/ppermute | solution.py:265
  27.9 10.3 %collective-permute-start.10 = (bf16[256,256]{1,0:T(8,128)(2,1)S(1)}, bf16[256,256]{1,0:T(8,128)(2,1)S(1)}, u32[]{:S(2)}, u32[]{:S(2)}) collective-permute-start(bf16[256,256]{1,0:T(8,128)(2,1)S(1)} %collective-permute-done.9.rest_6_), channel_id=1, source_target_pairs={{12,14},{13,15},{14,12},{15,13},{28,30},{29,31},{30,28},{31,29}} | collective-permute-start | bytes 393224 | tf_op jit(solution)/shard_map/ppermute | solution.py:275
  34.7 6.5 %collective-permute-start.6 = (bf16[256,256]{1,0:T(8,128)(2,1)S(1)}, bf16[256,256]{1,0:T(8,128)(2,1)S(1)}, u32[]{:S(2)}, u32[]{:S(2)}) collective-permute-start(bf16[256,256]{1,0:T(8,128)(2,1)S(1)} %collective-permute-done.5.rest_2_), channel_id=1, source_target_pairs={{4,6},{5,7},{6,4},{7,5},{8,10},{9,11},{10,8},{11,9},{12,14},{13,15... | collective-permute-start | bytes 393224 | tf_op jit(solution)/shard_map/ppermute | solution.py:275
  36.9 6.6 %collective-permute-start.8 = (bf16[256,256]{1,0:T(8,128)(2,1)S(1)}, bf16[256,256]{1,0:T(8,128)(2,1)}, u32[]{:S(2)}, u32[]{:S(2)}) collective-permute-start(bf16[256,256]{1,0:T(8,128)(2,1)S(1)} %collective-permute-done.7.rest_4_), channel_id=1, source_target_pairs={{8,10},{9,11},{10,8},{11,9},{12,14},{13,15},{14,12},{15,13},{24,26... | collective-permute-start | bytes 393224 | tf_op jit(solution)/shard_map/ppermute | solution.py:275
  38.2 19.3 %collective-permute-start.11 = (bf16[256,256]{1,0:T(8,128)(2,1)S(1)}, bf16[256,256]{1,0:T(8,128)(2,1)S(1)}, u32[]{:S(2)}, u32[]{:S(2)}) collective-permute-start(bf16[256,256]{1,0:T(8,128)(2,1)S(1)} %maximum_maximum_fusion.1.rest_0_), channel_id=1, source_target_pairs={{0,2},{1,3},{4,6},{5,7},{8,10},{9,11},{12,14},{13,15},{16,18},{17,... | collective-permute-start | bytes 393224 | tf_op jit(solution)/shard_map/ppermute | solution.py:275
  41.2 17.0 %collective-permute-start.13 = (bf16[256,256]{1,0:T(8,128)(2,1)S(1)}, bf16[256,256]{1,0:T(8,128)(2,1)S(1)}, u32[]{:S(2)}, u32[]{:S(2)}) collective-permute-start(bf16[256,256]{1,0:T(8,128)(2,1)S(1)} %collective-permute-done.12.rest_2_), channel_id=1, source_target_pairs={{4,6},{5,7},{6,4},{7,5},{8,10},{9,11},{10,8},{11,9},{12,14},{13,15... | collective-permute-start | bytes 393224 | tf_op jit(solution)/shard_map/ppermute | solution.py:275
  43.5 16.6 %collective-permute-start.15 = (bf16[256,256]{1,0:T(8,128)(2,1)S(1)}, bf16[256,256]{1,0:T(8,128)(2,1)S(1)}, u32[]{:S(2)}, u32[]{:S(2)}) collective-permute-start(bf16[256,256]{1,0:T(8,128)(2,1)S(1)} %collective-permute-done.14.rest_4_), channel_id=1, source_target_pairs={{8,10},{9,11},{10,8},{11,9},{12,14},{13,15},{14,12},{15,13},{24,26... | collective-permute-start | bytes 393224 | tf_op jit(solution)/shard_map/ppermute | solution.py:275
  44.2 19.3 %collective-permute-start.17 = (bf16[256,256]{1,0:T(8,128)(2,1)S(1)}, bf16[256,256]{1,0:T(8,128)(2,1)S(1)}, u32[]{:S(2)}, u32[]{:S(2)}) collective-permute-start(bf16[256,256]{1,0:T(8,128)(2,1)S(1)} %collective-permute-done.16.rest_6_), channel_id=1, source_target_pairs={{12,14},{13,15},{14,12},{15,13},{28,30},{29,31},{30,28},{31,29}} | collective-permute-start | bytes 393224 | tf_op jit(solution)/shard_map/ppermute | solution.py:275
  44.9 0.7 copy-start.1
  45.6 0.7 copy-start.3
  56.8 6.8 %copy-start.2 = (f32[32,128]{1,0:T(8,128)S(1)}, f32[32,128]{1,0:T(8,128)}, u32[]{:S(2)}) copy-start(f32[32,128]{1,0:T(8,128)} %row_deltas.1.d_own) | copy-start | bytes 49156
  56.8 6.8 %copy-start.4 = (s32[16,10]{1,0:T(8,128)S(1)}, s32[16,10]{1,0:T(8,128)}, u32[]{:S(2)}) copy-start(s32[16,10]{1,0:T(8,128)} %anc_ref.3) | copy-start | bytes 1924
  56.8 17.9 %collective-permute-start.21 = (bf16[256,256]{1,0:T(8,128)(2,1)S(1)}, bf16[256,256]{1,0:T(8,128)(2,1)S(1)}, u32[]{:S(2)}, u32[]{:S(2)}) collective-permute-start(bf16[256,256]{1,0:T(8,128)(2,1)S(1)} %get-tuple-element.32), channel_id=1, source_target_pairs={{12,14},{13,15},{14,12},{15,13},{28,30},{29,31},{30,28},{31,29}} | collective-permute-start | bytes 393224 | tf_op jit(solution)/shard_map/ppermute | solution.py:275
  57.5 17.9 %collective-permute-start.23 = (bf16[256,256]{1,0:T(8,128)(2,1)S(1)}, bf16[256,256]{1,0:T(8,128)(2,1)S(1)}, u32[]{:S(2)}, u32[]{:S(2)}) collective-permute-start(bf16[256,256]{1,0:T(8,128)(2,1)S(1)} %get-tuple-element.31), channel_id=1, source_target_pairs={{8,10},{9,11},{10,8},{11,9},{12,14},{13,15},{14,12},{15,13},{24,26... | collective-permute-start | bytes 393224 | tf_op jit(solution)/shard_map/ppermute | solution.py:275
  58.2 19.2 %collective-permute-start.25 = (bf16[256,256]{1,0:T(8,128)(2,1)S(1)}, bf16[256,256]{1,0:T(8,128)(2,1)S(1)}, u32[]{:S(2)}, u32[]{:S(2)}) collective-permute-start(bf16[256,256]{1,0:T(8,128)(2,1)S(1)} %get-tuple-element.30), channel_id=1, source_target_pairs={{4,6},{5,7},{6,4},{7,5},{8,10},{9,11},{10,8},{11,9},{12,14},{13,15... | collective-permute-start | bytes 393224 | tf_op jit(solution)/shard_map/ppermute | solution.py:275
  60.2 24.7 %collective-permute-start.20 = (bf16[256,256]{1,0:T(8,128)(2,1)S(1)}, bf16[256,256]{1,0:T(8,128)(2,1)S(1)}, u32[]{:S(2)}, u32[]{:S(2)}) collective-permute-start(bf16[256,256]{1,0:T(8,128)(2,1)S(1)} %get-tuple-element.29), channel_id=1, source_target_pairs={{2,0},{3,1},{6,4},{7,5},{10,8},{11,9},{14,12},{15,13},{18,16},{19,... | collective-permute-start | bytes 393224 | tf_op jit(solution)/shard_map/ppermute | solution.py:275
  74.1 6.8 %collective-permute-start.28 = (bf16[256,256]{1,0:T(8,128)(2,1)S(1)}, bf16[256,256]{1,0:T(8,128)(2,1)S(1)}, u32[]{:S(2)}, u32[]{:S(2)}) collective-permute-start(bf16[256,256]{1,0:T(8,128)(2,1)S(1)} %get-tuple-element.36), channel_id=1, source_target_pairs={{12,14},{13,15},{14,12},{15,13},{28,30},{29,31},{30,28},{31,29}} | collective-permute-start | bytes 393224 | tf_op jit(solution)/shard_map/ppermute | solution.py:275
  74.7 6.8 %collective-permute-start.30 = (bf16[256,256]{1,0:T(8,128)(2,1)S(1)}, bf16[256,256]{1,0:T(8,128)(2,1)S(1)}, u32[]{:S(2)}, u32[]{:S(2)}) collective-permute-start(bf16[256,256]{1,0:T(8,128)(2,1)S(1)} %get-tuple-element.35), channel_id=1, source_target_pairs={{8,10},{9,11},{10,8},{11,9},{12,14},{13,15},{14,12},{15,13},{24,26... | collective-permute-start | bytes 393224 | tf_op jit(solution)/shard_map/ppermute | solution.py:275
  75.4 7.4 %collective-permute-start.32 = (bf16[256,256]{1,0:T(8,128)(2,1)S(1)}, bf16[256,256]{1,0:T(8,128)(2,1)S(1)}, u32[]{:S(2)}, u32[]{:S(2)}) collective-permute-start(bf16[256,256]{1,0:T(8,128)(2,1)S(1)} %get-tuple-element.34), channel_id=1, source_target_pairs={{4,6},{5,7},{6,4},{7,5},{8,10},{9,11},{10,8},{11,9},{12,14},{13,15... | collective-permute-start | bytes 393224 | tf_op jit(solution)/shard_map/ppermute | solution.py:275
  77.4 48.2 %collective-permute-start.27 = (bf16[256,256]{1,0:T(8,128)(2,1)S(1)}, bf16[256,256]{1,0:T(8,128)(2,1)S(1)}, u32[]{:S(2)}, u32[]{:S(2)}) collective-permute-start(bf16[256,256]{1,0:T(8,128)(2,1)S(1)} %get-tuple-element.33), channel_id=1, source_target_pairs={{2,0},{3,1},{6,4},{7,5},{10,8},{11,9},{14,12},{15,13},{18,16},{19,... | collective-permute-start | bytes 393224 | tf_op jit(solution)/shard_map/ppermute | solution.py:275
  80.9 6.7 %collective-permute-start.22 = (bf16[256,256]{1,0:T(8,128)(2,1)S(1)}, bf16[256,256]{1,0:T(8,128)(2,1)S(1)}, u32[]{:S(2)}, u32[]{:S(2)}) collective-permute-start(bf16[256,256]{1,0:T(8,128)(2,1)S(1)} %get-tuple-element.23), channel_id=1, source_target_pairs={{12,0},{13,1},{14,2},{15,3},{28,16},{29,17},{30,18},{31,19}} | collective-permute-start | bytes 393224 | tf_op jit(solution)/shard_map/ppermute | solution.py:270
  81.5 39.6 %collective-permute-start.24 = (bf16[256,256]{1,0:T(8,128)(2,1)S(1)}, bf16[256,256]{1,0:T(8,128)(2,1)S(1)}, u32[]{:S(2)}, u32[]{:S(2)}) collective-permute-start(bf16[256,256]{1,0:T(8,128)(2,1)S(1)} %get-tuple-element.25), channel_id=1, source_target_pairs={{8,0},{9,1},{10,2},{11,3},{12,4},{13,5},{14,6},{15,7},{24,16},{25,... | collective-permute-start | bytes 393224 | tf_op jit(solution)/shard_map/ppermute | solution.py:270
  82.9 39.6 %collective-permute-start.26 = (bf16[256,256]{1,0:T(8,128)(2,1)S(1)}, bf16[256,256]{1,0:T(8,128)(2,1)S(1)}, u32[]{:S(2)}, u32[]{:S(2)}) collective-permute-start(bf16[256,256]{1,0:T(8,128)(2,1)S(1)} %get-tuple-element.24), channel_id=1, source_target_pairs={{4,0},{5,1},{6,2},{7,3},{8,4},{9,5},{10,6},{11,7},{12,8},{13,9},{1... | collective-permute-start | bytes 393224 | tf_op jit(solution)/shard_map/ppermute | solution.py:270
  84.9 53.7 %collective-permute-start.18 = (bf16[128,1024]{1,0:T(8,128)(2,1)S(1)}, bf16[128,1024]{1,0:T(8,128)(2,1)S(1)}, u32[]{:S(2)}, u32[]{:S(2)}) collective-permute-start(bf16[128,1024]{1,0:T(8,128)(2,1)S(1)} %get-tuple-element.13), channel_id=1, source_target_pairs={{0,1},{1,0},{2,3},{3,2},{4,5},{5,4},{6,7},{7,6},{8,9},{9,8},{10,11... | collective-permute-start | bytes 786440 | tf_op jit(solution)/shard_map/ppermute | solution.py:262
  87.5 43.7 %collective-permute-start.29 = (bf16[256,256]{1,0:T(8,128)(2,1)S(1)}, bf16[256,256]{1,0:T(8,128)(2,1)S(1)}, u32[]{:S(2)}, u32[]{:S(2)}) collective-permute-start(bf16[256,256]{1,0:T(8,128)(2,1)S(1)} %get-tuple-element.26), channel_id=1, source_target_pairs={{12,0},{13,1},{14,2},{15,3},{28,16},{29,17},{30,18},{31,19}} | collective-permute-start | bytes 393224 | tf_op jit(solution)/shard_map/ppermute | solution.py:270
  121.2 10.1 %collective-permute-start.31 = (bf16[256,256]{1,0:T(8,128)(2,1)S(1)}, bf16[256,256]{1,0:T(8,128)(2,1)S(1)}, u32[]{:S(2)}, u32[]{:S(2)}) collective-permute-start(bf16[256,256]{1,0:T(8,128)(2,1)S(1)} %get-tuple-element.28), channel_id=1, source_target_pairs={{8,0},{9,1},{10,2},{11,3},{12,4},{13,5},{14,6},{15,7},{24,16},{25,... | collective-permute-start | bytes 393224 | tf_op jit(solution)/shard_map/ppermute | solution.py:270
  122.5 12.4 %collective-permute-start.33 = (bf16[256,256]{1,0:T(8,128)(2,1)S(1)}, bf16[256,256]{1,0:T(8,128)(2,1)S(1)}, u32[]{:S(2)}, u32[]{:S(2)}) collective-permute-start(bf16[256,256]{1,0:T(8,128)(2,1)S(1)} %get-tuple-element.27), channel_id=1, source_target_pairs={{4,0},{5,1},{6,2},{7,3},{8,4},{9,5},{10,6},{11,7},{12,8},{13,9},{1... | collective-permute-start | bytes 393224 | tf_op jit(solution)/shard_map/ppermute | solution.py:270
  125.6 13.0 %collective-permute-start.19 = (bf16[128,1024]{1,0:T(8,128)(2,1)S(1)}, bf16[128,1024]{1,0:T(8,128)(2,1)S(1)}, u32[]{:S(2)}, u32[]{:S(2)}) collective-permute-start(bf16[128,1024]{1,0:T(8,128)(2,1)S(1)} %get-tuple-element.14), channel_id=1, source_target_pairs={{0,1},{1,0},{2,3},{3,2},{4,5},{5,4},{6,7},{7,6},{8,9},{9,8},{10,11... | collective-permute-start | bytes 786440 | tf_op jit(solution)/shard_map/ppermute | solution.py:262
  135.1 4.8 %collective-permute-start.34 = (bf16[128,256]{1,0:T(8,128)(2,1)S(1)}, bf16[128,256]{1,0:T(8,128)(2,1)S(1)}, u32[]{:S(2)}, u32[]{:S(2)}) collective-permute-start(bf16[128,256]{1,0:T(8,128)(2,1)S(1)} %pad_maximum_fusion.2), channel_id=1, source_target_pairs={{0,1},{1,0},{2,3},{3,2},{4,5},{5,4},{6,7},{7,6},{8,9},{9,8},{10,11... | collective-permute-start | bytes 196616 | tf_op jit(solution)/shard_map/ppermute | solution.py:262
  138.5 1.3 collective-permute-start.35

commit v2 on v0

v2 whole, which is shorter than its diff:
```python
import functools
import math

import jax
import jax.numpy as jnp
from jax import lax
from jax.experimental import pallas as pl
from jax.experimental.pallas import tpu as pltpu
from jax.sharding import Mesh
from jax.sharding import PartitionSpec as P

QH = 32
KVH = 4
HD = 128
TILE = 128
GROUP = QH // KVH
ROWS = GROUP * TILE
PAIR = 2 * TILE
QUAD = 4
LEVEL = QUAD * TILE
SCALE = HD ** (-0.5)
SCALE2 = SCALE / math.log(2.0)
MASKED = -1e30
NT_DIMS = (((1,), (1,)), ((), ()))
PARAMS = pltpu.CompilerParams(vmem_limit_bytes=48 * 1024 * 1024)


def delta_kernel(out_ref, grad_ref, delta_ref):
    for head in range(QH):
        cols = slice(head * HD, (head + 1) * HD)
        product = out_ref[:, cols].astype(jnp.float32) * grad_ref[:, cols].astype(jnp.float32)
        delta_ref[head : head + 1, :] = jnp.sum(product.T, axis=0, keepdims=True)


def row_deltas(outputs, out_grad):
    return pl.pallas_call(
        delta_kernel,
        out_shape=jax.ShapeDtypeStruct((QH, TILE), jnp.float32),
        name="row_deltas",
    )(outputs, out_grad)


def live_counts(anc_ref, me, u, depth):
    tile = me ^ u
    cut = ((me >> 2) - 1) * QUAD
    near, live = jnp.int32(1), jnp.int32(1)
    for slot in range(depth):
        entry = anc_ref[tile, slot]
        live += (entry >= 0).astype(jnp.int32)
        near += ((entry >= 0) & (entry >= cut)).astype(jnp.int32)
    return tile, near, live


def chunk_slots(anc_ref, me, tile, depth, start, stop, lowest):
    def slot_of(entry):
        seen = jnp.where(entry == 0, tile, anc_ref[tile, jnp.clip(entry - 1, 0, depth - 1)])
        return ((me >> 2) - (seen >> 2) - lowest) * QUAD + ((seen ^ me) & (QUAD - 1))

    good = start + 1 < stop
    first = slot_of(start)
    return first, jnp.where(good, slot_of(start + 1), first), good


def slot_rows(slot):
    return pl.ds(pl.multiple_of(slot * TILE, TILE), TILE)


def two_tiles(ref, first, second):
    return jnp.concatenate([ref[slot_rows(first), :], ref[slot_rows(second), :]], axis=0)


def two_heads(ref, u, pair):
    left = ref[u, :, 2 * pair * HD : (2 * pair + 1) * HD]
    right = ref[u, :, (2 * pair + 1) * HD : (2 * pair + 2) * HD]
    return jnp.concatenate([left, right], axis=0)


def causal_mask():
    key_pos = lax.broadcasted_iota(jnp.int32, (TILE, PAIR), 0)
    query_pos = lax.broadcasted_iota(jnp.int32, (TILE, PAIR), 1) & (TILE - 1)
    return key_pos <= query_pos


def gather_queries(scratch, own, peer, side):
    scratch[0] = own[...]
    scratch[1] = peer[...]
    scratch[2] = side[:TILE, :]
    scratch[3] = side[TILE:, :]


def stats_kernel(depth, steps, me_ref, anc_ref, q_own, q_peer, q_side, *rest):
    k_refs = rest[:steps]
    lse_ref, q_all, k_all, top_max, total = rest[steps:]
    me = me_ref[0]
    gather_queries(q_all, q_own, q_peer, q_side)
    for shift, k_ref in enumerate(k_refs):
        k_all[shift * LEVEL : (shift + 1) * LEVEL, :] = k_ref[...]

    def one_tile(u, carry):
        tile, _, live = live_counts(anc_ref, me, u, depth)

        def chunk_stats(index, is_first):
            first, second, good = chunk_slots(anc_ref, me, tile, depth, 2 * index, live, 0)
            key_block = two_tiles(k_all, first, second)
            for pair in range(GROUP // 2):
                rows = slice(pair * PAIR, (pair + 1) * PAIR)
                raw = lax.dot_general(
                    key_block,
                    two_heads(q_all, u, pair),
                    NT_DIMS,
                    preferred_element_type=jnp.float32,
                )
                top, low = raw[:TILE], raw[TILE:]
                if is_first:
                    top = jnp.where(causal_mask(), top, MASKED)
                low_max = jnp.max(low, axis=0, keepdims=True)
                new_max = jnp.maximum(
                    jnp.max(top, axis=0, keepdims=True), jnp.where(good, low_max, MASKED)
                )
                if not is_first:
                    old_max = top_max[:, rows]
                    new_max = jnp.maximum(old_max, new_max)
                low_base = jnp.where(good, new_max, -MASKED)
                new_sum = jnp.sum(
                    jnp.exp2((top - new_max) * SCALE2), axis=0, keepdims=True
                ) + jnp.sum(jnp.exp2((low - low_base) * SCALE2), axis=0, keepdims=True)
                if not is_first:
                    new_sum += total[:, rows] * jnp.exp2((old_max - new_max) * SCALE2)
                top_max[:, rows] = new_max
                total[:, rows] = new_sum

        chunk_stats(0, True)

        def step(index, carry):
            chunk_stats(index, False)
            return carry

        lax.fori_loop(1, (live + 1) // 2, step, 0)
        lse_ref[u] = top_max[...] * SCALE2 + jnp.log2(total[...])
        return carry

    lax.fori_loop(0, QUAD, one_tile, 0)


def grads_kernel(depth, near_part, steps, me_ref, anc_ref, q_own, q_peer, q_side, g_own, g_peer, g_side, d_own, d_peer, d_side, lse_ref, *rest):
    kv_refs = rest[: 2 * steps]
    rest = rest[2 * steps :]
    if near_part:
        dq_in, dq_own, dq_peer, dq_side = rest[:4]
        rest = rest[4:]
    else:
        dq_acc = rest[0]
        rest = rest[1:]
    partial_refs = rest[:steps]
    q_all, g_all, delta, k_all, v_all, dk_acc, dv_acc = rest[steps : steps + 7]
    if near_part:
        dq_acc = rest[steps + 7]
    lowest = 0 if near_part else 2
    me = me_ref[0]
    gather_queries(q_all, q_own, q_peer, q_side)
    gather_queries(g_all, g_own, g_peer, g_side)
    for head in range(GROUP):
        cols = slice(head * TILE, (head + 1) * TILE)
        delta[0, :, cols] = d_own[head : head + 1, :]
        delta[1, :, cols] = d_peer[head : head + 1, :]
        delta[2, :, cols] = d_side[head : head + 1, :]
        delta[3, :, cols] = d_side[GROUP + head : GROUP + head + 1, :]
    for shift in range(steps):
        k_all[shift * LEVEL : (shift + 1) * LEVEL, :] = kv_refs[shift][...]
        v_all[shift * LEVEL : (shift + 1) * LEVEL, :] = kv_refs[steps + shift][...]
    dk_acc[...] = jnp.zeros_like(dk_acc)
    dv_acc[...] = jnp.zeros_like(dv_acc)

    def one_tile(u, carry):
        tile, near, live = live_counts(anc_ref, me, u, depth)
        start, stop = (0, near) if near_part else (near, live)
        if near_part:
            dq_acc[u] = dq_in[u]
        else:
            dq_acc[u] = jnp.zeros((HD, ROWS), jnp.float32)

        def chunk_grads(index, is_first):
            first, second, good = chunk_slots(
                anc_ref, me, tile, depth, start + 2 * index, stop, lowest
            )
            key_block = two_tiles(k_all, first, second)
            value_block = two_tiles(v_all, first, second)
            key_turned = key_block.T
            dk = jnp.zeros((PAIR, HD), jnp.float32)
            dv = jnp.zeros((PAIR, HD), jnp.float32)
            for pair in range(GROUP // 2):
                rows = slice(pair * PAIR, (pair + 1) * PAIR)
                query_block = two_heads(q_all, u, pair)
                grad_block = two_heads(g_all, u, pair)
                raw = lax.dot_general(
                    key_block, query_block, NT_DIMS, preferred_element_type=jnp.float32
                )
                grad_probs = lax.dot_general(
                    value_block, grad_block, NT_DIMS, preferred_element_type=jnp.float32
                )
                lse = lse_ref[u, :, rows]
                away = delta[u, :, rows]
                lows, scores = [], []
                for part in range(2):
                    half = slice(part * TILE, (part + 1) * TILE)
                    base = lse if part == 0 else jnp.where(good, lse, -MASKED)
                    attn = jnp.exp2(raw[half] * SCALE2 - base)
                    if is_first and part == 0:
                        attn = jnp.where(causal_mask(), attn, 0.0)
                    lows.append(attn.astype(jnp.bfloat16))
                    scores.append((attn * (grad_probs[half] - away)).astype(jnp.bfloat16))
                attn_low = jnp.concatenate(lows, axis=0)
                grad_scores = jnp.concatenate(scores, axis=0)
                dv += jnp.dot(attn_low, grad_block, preferred_element_type=jnp.float32)
                dk += jnp.dot(grad_scores, query_block, preferred_element_type=jnp.float32)
                dq_acc[u, :, rows] += jnp.dot(
                    key_turned, grad_scores, preferred_element_type=jnp.float32
                )
            dk_acc[slot_rows(first), :] += dk[:TILE]
            dk_acc[slot_rows(second), :] += dk[TILE:]
            dv_acc[slot_rows(first), :] += dv[:TILE]
            dv_acc[slot_rows(second), :] += dv[TILE:]

        def step(index, carry):
            chunk_grads(index, False)
            return carry

        if near_part:
            chunk_grads(0, True)
        lax.fori_loop(1 if near_part else 0, (stop - start + 1) // 2, step, 0)
        return carry

    lax.fori_loop(0, QUAD, one_tile, 0)

    if near_part:
        for u in range(QUAD):
            for head in range(GROUP):
                cols = slice(head * HD, (head + 1) * HD)
                turned = (dq_acc[u, :, cols] * SCALE).T.astype(jnp.bfloat16)
                if u == 0:
                    dq_own[:, cols] = turned
                elif u == 1:
                    dq_peer[:, cols] = turned
                else:
                    dq_side[(u - 2) * TILE : (u - 1) * TILE, cols] = turned
    for shift, out_ref in enumerate(partial_refs):
        rows = slice(shift * LEVEL, (shift + 1) * LEVEL)
        out_ref[:, :HD] = dk_acc[rows, :].astype(out_ref.dtype)
        out_ref[:, HD:] = dv_acc[rows, :].astype(out_ref.dtype)


def fixed(shape):
    return pl.BlockSpec(shape, lambda i, *_: (0,) * len(shape))


def own_head(me_ref):
    return ((me_ref[0] & 1) << 1) | ((me_ref[0] >> 1) & 1)


WIDE = pl.BlockSpec((TILE, ROWS), lambda i, me_ref, anc_ref: (0, own_head(me_ref)))
SMALL = pl.BlockSpec((GROUP, TILE), lambda i, me_ref, anc_ref: (own_head(me_ref), 0))
SIDE = fixed((PAIR, ROWS))
LSE = fixed((QUAD, 1, ROWS))
KEYS = fixed((LEVEL, HD))
SUMS = fixed((LEVEL, 2 * HD))
DQ = fixed((QUAD, HD, ROWS))


def statistics(me, ancestors, q_set, k_list):
    steps = len(k_list)
    return pl.pallas_call(
        functools.partial(stats_kernel, ancestors.shape[1], steps),
        grid_spec=pltpu.PrefetchScalarGridSpec(
            num_scalar_prefetch=2,
            grid=(1,),
            in_specs=[WIDE, WIDE, SIDE] + [KEYS] * steps,
            out_specs=LSE,
            scratch_shapes=[
                pltpu.VMEM((QUAD, TILE, ROWS), jnp.bfloat16),
                pltpu.VMEM((steps * LEVEL, HD), jnp.bfloat16),
                pltpu.VMEM((1, ROWS), jnp.float32),
                pltpu.VMEM((1, ROWS), jnp.float32),
            ],
        ),
        out_shape=jax.ShapeDtypeStruct((QUAD, 1, ROWS), jnp.float32),
        compiler_params=PARAMS,
        name="statistics",
    )(me, ancestors, *q_set, *k_list)


def gradients(me, ancestors, q_set, g_set, d_set, lse, k_list, v_list, dq_far=None):
    steps = len(k_list)
    near_part = dq_far is not None
    if near_part:
        dq_specs = [WIDE_OUT, WIDE_OUT, SIDE]
        dq_shapes = [
            jax.ShapeDtypeStruct((TILE, ROWS), jnp.bfloat16),
            jax.ShapeDtypeStruct((TILE, ROWS), jnp.bfloat16),
            jax.ShapeDtypeStruct((PAIR, ROWS), jnp.bfloat16),
        ]
        kinds = [jnp.float32] + [jnp.bfloat16] * (steps - 1)
    else:
        dq_specs = [DQ]
        dq_shapes = [jax.ShapeDtypeStruct((QUAD, HD, ROWS), jnp.float32)]
        kinds = [jnp.bfloat16] * steps
    scratch = [
        pltpu.VMEM((QUAD, TILE, ROWS), jnp.bfloat16),
        pltpu.VMEM((QUAD, TILE, ROWS), jnp.bfloat16),
        pltpu.VMEM((QUAD, 1, ROWS), jnp.float32),
        pltpu.VMEM((steps * LEVEL, HD), jnp.bfloat16),
        pltpu.VMEM((steps * LEVEL, HD), jnp.bfloat16),
        pltpu.VMEM((steps * LEVEL, HD), jnp.float32),
        pltpu.VMEM((steps * LEVEL, HD), jnp.float32),
    ]
    if near_part:
        scratch.append(pltpu.VMEM((QUAD, HD, ROWS), jnp.float32))
    return pl.pallas_call(
        functools.partial(grads_kernel, ancestors.shape[1], near_part, steps),
        grid_spec=pltpu.PrefetchScalarGridSpec(
            num_scalar_prefetch=2,
            grid=(1,),
            in_specs=[WIDE, WIDE, SIDE, WIDE, WIDE, SIDE, SMALL, SMALL, fixed((2 * GROUP, TILE)), LSE]
            + [KEYS] * (2 * steps)
            + ([DQ] if near_part else []),
            out_specs=dq_specs + [SUMS] * steps,
            scratch_shapes=scratch,
        ),
        out_shape=dq_shapes + [jax.ShapeDtypeStruct((LEVEL, 2 * HD), kind) for kind in kinds],
        compiler_params=PARAMS,
        name="near_grads" if near_part else "far_grads",
    )(
        me,
        ancestors,
        *q_set,
        *g_set,
        *d_set,
        lse,
        *k_list,
        *v_list,
        *([dq_far] if near_part else []),
    )


WIDE_OUT = fixed((TILE, ROWS))


def per_device(steps, queries, keys, values, outputs, out_grad, ancestors):
    level, side, core = (lax.axis_index(name) for name in ("level", "side", "core"))
    me = (QUAD * level + 2 * side + core).reshape(1).astype(jnp.int32)

    def to_peer(x):
        return lax.ppermute(x, "core", [(0, 1), (1, 0)])

    def to_side(x):
        return lax.ppermute(x, "side", [(0, 1), (1, 0)])

    def up(x, shift):
        return lax.ppermute(x, "level", [(z, z + shift) for z in range(steps - shift)])

    def down(x, shift):
        return lax.ppermute(x, "level", [(z + shift, z) for z in range(steps - shift)])

    def columns(x, who, count):
        return lax.dynamic_slice_in_dim(x, who * count, count, 1)

    def head_rows(x, who):
        return lax.dynamic_slice_in_dim(x, who * GROUP, GROUP, 0)

    side_head = 2 * core + 1 - side
    half = 2 * HD
    kv_peer = to_peer(
        jnp.concatenate([columns(keys, 1 - core, half), columns(values, 1 - core, half)], axis=1)
    )
    q_peer = to_peer(queries)
    g_peer = to_peer(out_grad)
    k_chip = jnp.concatenate([columns(keys, core, half), kv_peer[:, :half]], axis=0)
    v_chip = jnp.concatenate([columns(values, core, half), kv_peer[:, half:]], axis=0)
    kv_side = to_side(
        jnp.concatenate([columns(k_chip, 1 - side, HD), columns(v_chip, 1 - side, HD)], axis=1)
    )
    k_level = jnp.concatenate([columns(k_chip, side, HD), kv_side[:, :HD]], axis=0)
    v_level = jnp.concatenate([columns(v_chip, side, HD), kv_side[:, HD:]], axis=0)
    k_list = [k_level] + [up(k_level, shift) for shift in range(1, steps)]

    def both(own, peer):
        return jnp.concatenate([columns(own, side_head, ROWS), columns(peer, side_head, ROWS)], axis=0)

    q_set = (queries, q_peer, to_side(both(queries, q_peer)))
    v_list = [v_level] + [up(v_level, shift) for shift in range(1, steps)]
    g_set = (out_grad, g_peer, to_side(both(out_grad, g_peer)))
    deltas = row_deltas(outputs, out_grad)
    d_peer = to_peer(deltas)
    d_side = to_side(
        jnp.concatenate([head_rows(deltas, side_head), head_rows(d_peer, side_head)], axis=0)
    )
    d_set = (deltas, d_peer, d_side)

    lse = statistics(me, ancestors, q_set, k_list)
    dq_far, *far = gradients(me, ancestors, q_set, g_set, d_set, lse, k_list[2:], v_list[2:])
    back = [down(far[shift - 2], shift) for shift in range(2, steps)]
    dq_own, dq_peer, dq_side, total, near = gradients(
        me, ancestors, q_set, g_set, d_set, lse, k_list[:2], v_list[:2], dq_far
    )
    back.append(down(near, 1))
    dq_side = to_side(dq_side)
    dq_diag = to_peer(dq_side[TILE:])
    dq_peer = to_peer(dq_peer)

    for part in back:
        total += part.astype(jnp.float32)
    scaled = jnp.concatenate([total[:, :HD] * SCALE, total[:, HD:]], axis=1).astype(jnp.bfloat16)
    kv_side = to_side(scaled[PAIR:])
    kv_peer = to_peer(jnp.concatenate([scaled[TILE:PAIR], kv_side[TILE:]], axis=1))

    def in_order(own, beside, peer, diagonal):
        here = jnp.where(
            side == 0,
            jnp.concatenate([own, beside], axis=1),
            jnp.concatenate([beside, own], axis=1),
        )
        there = jnp.where(
            side == 0,
            jnp.concatenate([peer, diagonal], axis=1),
            jnp.concatenate([diagonal, peer], axis=1),
        )
        return jnp.where(
            core == 0,
            jnp.concatenate([here, there], axis=1),
            jnp.concatenate([there, here], axis=1),
        )

    return (
        in_order(dq_own, dq_side[:TILE], dq_peer, dq_diag),
        in_order(scaled[:TILE, :HD], kv_side[:TILE, :HD], kv_peer[:, :HD], kv_peer[:, half : half + HD]),
        in_order(scaled[:TILE, HD:], kv_side[:TILE, HD:], kv_peer[:, HD:half], kv_peer[:, half + HD :]),
    )


def solution(mesh):
    parts, tok = mesh.shape["parts"], mesh.shape["tok"]
    quads = Mesh(
        mesh.devices.reshape(parts, tok // QUAD, 2, 2), ("parts", "level", "side", "core")
    )
    rows = P(("parts", "level", "side", "core"), None)
    return jax.shard_map(
        functools.partial(per_device, tok // QUAD),
        mesh=quads,
        in_specs=(rows, rows, rows, rows, rows, P("parts", None)),
        out_specs=(rows, rows, rows),
        check_vma=False,
    )
```

time: 464 us -> 131 us (0.28)
  waiting for transfers between devices: 361 us -> 58.2 us
  local copies, waits for them, and re-layouts: 52.7 us -> 10.3 us
  starting transfers between devices: 0.38 us -> 36.5 us
  Pallas kernels: 0 us -> 20 us
  other arithmetic: 22.8 us -> 5.96 us
  between operations: 14.6 us -> 1.09 us
  matrix products: 9.12 us -> 0 us
    reduce_scatter x2 -> x0, waiting for transfers between devices: 297 us -> none  [the longest x1 223 us: per_device(): lax.psum_scatter(value_acc.reshape(all_rows, KVH * HD), 'tok', scatter_di...]
    all_gather x2 -> x0, waiting for transfers between devices: 63 us -> none  [the longest x1 32.6 us: per_device(): lax.all_gather(keys, 'tok', axis=0, tiled=True)]
    ppermute x0 -> x22, waiting for transfers between devices: none -> 58.2 us  [the longest x3 40.2 us: down(): lax.ppermute(x, 'level', [(z + shift, z) for z in range(steps - shift)])]
    ppermute x0 -> x22, starting transfers between devices: none -> 36.5 us  [the longest x6 22.7 us: up(): lax.ppermute(x, 'level', [(z, z + shift) for z in range(steps - shift)])]
    pallas_call x0 -> x4, Pallas kernels: none -> 20 us  [the longest x2 13.7 us: gradients(): pl.pallas_call(functools.partial(grads_kernel, ancestors.shape[1], near_p...]
    scatter-add x4 -> x0, other arithmetic: 11.1 us -> none  [the longest x1 4.79 us: second_sweep(): query_acc.at[query_ids]]
    gather x8 -> x0, local copies, waits for them, and re-layouts: 10.7 us -> none  [the longest x2 4.19 us: second_sweep(): key_block = keys[key_ids]]
    while x6 -> x0, local copies, waits for them, and re-layouts: 10.4 us -> none  [the longest x2 9.95 us: tree_backward(): lax.fori_loop(0, block_total, second_sweep, start_state)]
  transfers between devices with their start and end apart: 4 -> 22, of which waited for: 4 -> 5; matrix products, arithmetic and copies ran while one was open for 8% -> 5% of each run, Pallas kernels for 0% -> 8%
where the time goes in v2:
time: 131 us; the launch traced here: 132 us
  waiting for transfers between devices  58.2 us (44%)
  starting transfers between devices  36.5 us (28%)
  Pallas kernels  20 us (15%)
  local copies, waits for them, and re-layouts  10.3 us (8%)
  other arithmetic  5.96 us (5%)
    ppermute x3, waiting for transfers between devices, down(): lax.ppermute(x, 'level', [(z + shift, z) for z in range(steps - shift)])  40.2 us
    ppermute x6, starting transfers between devices, up(): lax.ppermute(x, 'level', [(z, z + shift) for z in range(steps - shift)])  22.7 us
    ppermute x6, waiting for transfers between devices, to_side(): return lax.ppermute(x, 'side', [(0, 1), (1, 0)])  18 us
    pallas_call x2, Pallas kernels, gradients(): pl.pallas_call(functools.partial(grads_kernel, ancestors.shape[1], near_p...  13.7 us
    ppermute x6, starting transfers between devices, to_side(): return lax.ppermute(x, 'side', [(0, 1), (1, 0)])  8.65 us
    unnamed x28, local copies, waits for them, and re-layouts  5.68 us
    ppermute x3, starting transfers between devices, down(): lax.ppermute(x, 'level', [(z + shift, z) for z in range(steps - shift)])  3.88 us
    pallas_call x1, Pallas kernels, statistics(): pl.pallas_call(functools.partial(stats_kernel, ancestors.shape[1], steps)...  3.56 us
  transfers between devices with their start and end apart: 22, of which 5 were waited for; matrix products, arithmetic and copies ran while one was open for 5% of the time, Pallas kernels for 8%

profile of v2, /device:TPU:0, one launch (start us, length us, event | category | flops | bytes accessed | tf_op | source)
XLA Modules:
  0.0 132.1 jit_solution(1028504022197918025)
XLA Ops:
  0.6 0.0 copy-start
  0.6 1.0 constant_dynamic-slice_fusion.3
  1.6 0.0 copy-start.1
  1.6 1.0 constant_dynamic-slice_fusion.1
  2.6 0.5 collective-permute-start.6
  3.2 0.1 collective-permute-start
  3.2 0.4 collective-permute-start.2
  3.7 2.8 %row_deltas.1.d_own = f32[32,128]{1,0:T(8,128)} custom-call(bf16[128,4096]{1,0:T(8,128)(2,1)} %out_ref.1, bf16[128,4096]{1,0:T(8,128)(2,1)} %g_own.3), custom_call_target="tpu_custom_call" | custom-call | tf_op jit(solution)/shard_map/row_deltas/pallas_call | solution.py:36
  6.4 0.1 collective-permute-start.4
  6.5 0.7 fusion.3
  7.2 0.7 pad_maximum_fusion.4
  7.9 2.9 %collective-permute-start.7 = (bf16[256,256]{1,0:T(8,128)(2,1)}, bf16[256,256]{1,0:T(8,128)(2,1)}, u32[]{:S(2)}, u32[]{:S(2)}) collective-permute-start(bf16[256,256]{1,0:T(8,128)(2,1)} %pad_maximum_fusion.4), channel_id=1, source_target_pairs={{0,2},{2,0},{1,3},{3,1},{4,6},{6,4},{5,7},{7,5},{8,10},{10,8},{9,1... | collective-permute-start | bytes 393224 | tf_op jit(solution)/shard_map/ppermute | solution.py:355
  10.9 0.0 copy-start.9
  10.9 0.0 copy-start.13
  10.9 4.0 %collective-permute-done.7 = bf16[256,256]{1,0:T(8,128)(2,1)} collective-permute-done((bf16[256,256]{1,0:T(8,128)(2,1)}, bf16[256,256]{1,0:T(8,128)(2,1)}, u32[]{:S(2)}, u32[]{:S(2)}) %collective-permute-start.7) | collective-permute-done | bytes 131104 | tf_op jit(solution)/shard_map/ppermute | solution.py:355
  14.9 0.9 fusion.11
  15.8 0.0 collective-permute-done.q_peer
  15.8 1.8 %collective-permute-start.1 = (bf16[256,1024]{1,0:T(8,128)(2,1)S(1)}, bf16[256,1024]{1,0:T(8,128)(2,1)S(1)}, u32[]{:S(2)}, u32[]{:S(2)}) collective-permute-start(bf16[256,1024]{1,0:T(8,128)(2,1)S(1)} %pad_maximum_fusion), channel_id=1, source_target_pairs={{0,2},{2,0},{1,3},{3,1},{4,6},{6,4},{5,7},{7,5},{8,10},{10,8},{9,1... | collective-permute-start | bytes 1572872 | tf_op jit(solution)/shard_map/ppermute | solution.py:355
  17.7 1.0 constant_dynamic-slice_fusion.6
  18.6 0.8 pad_maximum_fusion.1
  19.5 0.3 collective-permute-start.3
  19.8 5.7 %collective-permute-start.10 = (bf16[512,128]{1,0:T(8,128)(2,1)S(1)}, bf16[512,128]{1,0:T(8,128)(2,1)S(1)}, u32[]{:S(2)}, u32[]{:S(2)}) collective-permute-start(bf16[512,128]{1,0:T(8,128)(2,1)S(1)} %pad_maximum_fusion.5.rest_0_), channel_id=1, source_target_pairs={{0,12},{1,13},{2,14},{3,15},{16,28},{17,29},{18,30},{19,31}} | collective-permute-start | bytes 393224 | tf_op jit(solution)/shard_map/ppermute | solution.py:358
  25.5 1.3 collective-permute-start.9
  26.8 2.5 %collective-permute-start.8 = (bf16[512,128]{1,0:T(8,128)(2,1)S(1)}, bf16[512,128]{1,0:T(8,128)(2,1)S(1)}, u32[]{:S(2)}, u32[]{:S(2)}) collective-permute-start(bf16[512,128]{1,0:T(8,128)(2,1)S(1)} %pad_maximum_fusion.5.rest_0_), channel_id=1, source_target_pairs={{0,4},{4,8},{8,12},{1,5},{5,9},{9,13},{2,6},{6,10},{10,14},{3,7},{... | collective-permute-start | bytes 393224 | tf_op jit(solution)/shard_map/ppermute | solution.py:358
  29.4 0.0 collective-permute-done.10.rest_3_.rest_1_
  29.4 0.0 copy-start.5
  29.4 0.6 copy-done.5
  30.0 6.8 %collective-permute-start.13 = (bf16[512,128]{1,0:T(8,128)(2,1)S(1)}, bf16[512,128]{1,0:T(8,128)(2,1)}, u32[]{:S(2)}, u32[]{:S(2)}) collective-permute-start(bf16[512,128]{1,0:T(8,128)(2,1)S(1)} %pad_maximum_fusion.6.rest_2_), channel_id=1, source_target_pairs={{0,12},{1,13},{2,14},{3,15},{16,28},{17,29},{18,30},{19,31}} | collective-permute-start | bytes 393224 | tf_op jit(solution)/shard_map/ppermute | solution.py:358
  36.8 0.7 copy-done.7
  37.5 2.0 %collective-permute-start.12 = (bf16[512,128]{1,0:T(8,128)(2,1)S(1)}, bf16[512,128]{1,0:T(8,128)(2,1)}, u32[]{:S(2)}, u32[]{:S(2)}) collective-permute-start(bf16[512,128]{1,0:T(8,128)(2,1)S(1)} %pad_maximum_fusion.6.rest_2_), channel_id=1, source_target_pairs={{0,8},{4,12},{1,9},{5,13},{2,10},{6,14},{3,11},{7,15},{16,24},{20,... | collective-permute-start | bytes 393224 | tf_op jit(solution)/shard_map/ppermute | solution.py:358
  39.4 4.5 %collective-permute-start.11 = (bf16[512,128]{1,0:T(8,128)(2,1)S(1)}, bf16[512,128]{1,0:T(8,128)(2,1)}, u32[]{:S(2)}, u32[]{:S(2)}) collective-permute-start(bf16[512,128]{1,0:T(8,128)(2,1)S(1)} %pad_maximum_fusion.6.rest_2_), channel_id=1, source_target_pairs={{0,4},{4,8},{8,12},{1,5},{5,9},{9,13},{2,6},{6,10},{10,14},{3,7},{... | collective-permute-start | bytes 393224 | tf_op jit(solution)/shard_map/ppermute | solution.py:358
  43.9 0.7 constant_dynamic-slice_fusion.4
  44.6 0.6 pad_maximum_fusion.7
  45.2 0.8 copy-done.2
  46.0 1.5 %collective-permute-start.5 = (f32[16,128]{1,0:T(8,128)}, f32[16,128]{1,0:T(8,128)}, u32[]{:S(2)}, u32[]{:S(2)}) collective-permute-start(f32[16,128]{1,0:T(8,128)} %pad_maximum_fusion.7), channel_id=1, source_target_pairs={{0,2},{2,0},{1,3},{3,1},{4,6},{6,4},{5,7},{7,5},{8,10},{10,8},{9,1... | collective-permute-start | bytes 24584 | tf_op jit(solution)/shard_map/ppermute | solution.py:355
  47.5 1.0 copy-done.3
  48.5 0.9 copy-done.6
  49.4 0.9 copy-done.8
  50.3 0.7 copy-done.10
  51.0 3.6 %statistics.1.lse_ref = f32[4,1,1024]{2,1,0:T(1,128)S(1)} custom-call(s32[1]{0:T(128)} %bitcast.me_ref, s32[16,10]{1,0:T(8,128)S(1)} %copy-done.10, bf16[128,4096]{1,0:T(8,128)(2,1)S(1)} %copy-done, bf16[128,4096]{1,0:T(8,128)(2,1)S(1)} %collective-permute-done.q_peer, bf16[256,1024]{1,0:T(8,128)(2,1)S(1)} %copy-done.3, ...), custom_call_target="tpu_custom_call" | custom-call | tf_op jit(solution)/shard_map/statistics/pallas_call | solution.py:271
  54.6 0.0 copy-start.4
  54.6 0.0 collective-permute-done.12.rest_2_
  54.7 3.7 %far_grads.1 = (f32[4,128,1024]{2,1,0:T(8,128)}, bf16[512,256]{1,0:T(8,128)(2,1)S(1)}, bf16[512,256]{1,0:T(8,128)(2,1)S(1)}) custom-call(s32[1]{0:T(128)} %bitcast.me_ref, s32[16,10]{1,0:T(8,128)S(1)} %copy-done.11, bf16[128,4096]{1,0:T(8,128)(2,1)S(1)} %copy-done, bf16[128,4096]{1,0:T(8,128)(2,1)S(1)} %collective-permute-done.q_peer, ...), custom_call_target="tpu_custom_call" | custom-call | tf_op jit(solution)/shard_map/far_grads/pallas_call | solution.py:317
  58.4 0.0 collective-permute-done.11.rest_3_
  58.4 10.0 %near_grads.1 = (bf16[128,1024]{1,0:T(8,128)(2,1)S(1)}, bf16[128,1024]{1,0:T(8,128)(2,1)S(1)}, bf16[256,1024]{1,0:T(8,128)(2,1)S(1)}, f32[512,256]{1,0:T(8,128)S(1)}, bf16[512,256]{1,0:T(8,128)(2,1)S(1)}) custom-call(s32[1]{0:T(128)} %bitcast.me_ref, s32[16,10]{1,0:T(8,128)S(1)} %copy-done.11, bf16[128,4096]{1,0:T(8,128)(2,1)S(1)} %copy-done, ...), custom_call_target="tpu_custom_call" | custom-call | tf_op jit(solution)/shard_map/near_grads/pallas_call | solution.py:317
  68.4 0.0 copy-start.12
  68.4 1.3 collective-permute-start.19
  69.7 1.3 collective-permute-start.17
  71.0 1.3 collective-permute-start.18
  72.3 15.1 %collective-permute-done.19 = bf16[512,256]{1,0:T(8,128)(2,1)S(1)} collective-permute-done((bf16[512,256]{1,0:T(8,128)(2,1)S(1)}, bf16[512,256]{1,0:T(8,128)(2,1)S(1)}, u32[]{:S(2)}, u32[]{:S(2)}) %collective-permute-start.19) | collective-permute-done | bytes 262176 | tf_op jit(solution)/shard_map/ppermute | solution.py:361
  87.4 25.1 %collective-permute-done.17 = bf16[512,256]{1,0:T(8,128)(2,1)S(1)} collective-permute-done((bf16[512,256]{1,0:T(8,128)(2,1)S(1)}, bf16[512,256]{1,0:T(8,128)(2,1)S(1)}, u32[]{:S(2)}, u32[]{:S(2)}) %collective-permute-start.17) | collective-permute-done | bytes 262176 | tf_op jit(solution)/shard_map/ppermute | solution.py:361
  112.5 0.1 fusion.7
  112.7 0.5 collective-permute-start.20
  113.3 0.0 collective-permute-start.15
  113.3 1.5 %collective-permute-start.14 = (bf16[256,1024]{1,0:T(8,128)(2,1)}, bf16[256,1024]{1,0:T(8,128)(2,1)S(1)}, u32[]{:S(2)}, u32[]{:S(2)}) collective-permute-start(bf16[256,1024]{1,0:T(8,128)(2,1)} %copy-done.12), channel_id=1, source_target_pairs={{0,2},{2,0},{1,3},{3,1},{4,6},{6,4},{5,7},{7,5},{8,10},{10,8},{9,1... | collective-permute-start | bytes 1572872 | tf_op jit(solution)/shard_map/ppermute | solution.py:355
  114.8 4.1 %collective-permute-done.20 = bf16[256,256]{1,0:T(8,128)(2,1)S(1)} collective-permute-done((bf16[256,256]{1,0:T(8,128)(2,1)S(1)}, bf16[256,256]{1,0:T(8,128)(2,1)S(1)}, u32[]{:S(2)}, u32[]{:S(2)}) %collective-permute-start.20) | collective-permute-done | bytes 131104 | tf_op jit(solution)/shard_map/ppermute | solution.py:355
  118.9 0.1 collective-permute-start.21
  119.1 9.9 %collective-permute-done.14 = bf16[256,1024]{1,0:T(8,128)(2,1)S(1)} collective-permute-done((bf16[256,1024]{1,0:T(8,128)(2,1)}, bf16[256,1024]{1,0:T(8,128)(2,1)S(1)}, u32[]{:S(2)}, u32[]{:S(2)}) %collective-permute-start.14) | collective-permute-done | bytes 524320 | tf_op jit(solution)/shard_map/ppermute | solution.py:355
  129.0 0.1 collective-permute-start.16
  129.2 0.7 maximum_select_fusion.4
  129.9 0.7 maximum_select_fusion.3
  130.6 0.1 maximum_select_fusion.1
  130.7 0.1 maximum_select_fusion.2
  130.9 1.2 maximum_select_fusion
  (50 shorter events, 0.4 us)
Async XLA Ops:
  0.6 10.2 %copy-start = (bf16[128,4096]{1,0:T(8,128)(2,1)S(1)}, bf16[128,4096]{1,0:T(8,128)(2,1)}, u32[]{:S(2)}) copy-start(bf16[128,4096]{1,0:T(8,128)(2,1)} %q_own.5) | copy-start | bytes 3145732
  1.6 9.2 %copy-start.1 = (bf16[128,4096]{1,0:T(8,128)(2,1)S(1)}, bf16[128,4096]{1,0:T(8,128)(2,1)}, u32[]{:S(2)}) copy-start(bf16[128,4096]{1,0:T(8,128)(2,1)} %g_own.3) | copy-start | bytes 3145732
  2.6 3.9 %collective-permute-start.6 = (bf16[128,512]{1,0:T(8,128)(2,1)S(1)}, bf16[128,512]{1,0:T(8,128)(2,1)S(1)}, u32[]{:S(2)}, u32[]{:S(2)}) collective-permute-start(bf16[128,512]{1,0:T(8,128)(2,1)S(1)} %pad_maximum_fusion.3), channel_id=1, source_target_pairs={{0,1},{1,0},{2,3},{3,2},{4,5},{5,4},{6,7},{7,6},{8,9},{9,8},{10,11... | collective-permute-start | bytes 393224 | tf_op jit(solution)/shard_map/ppermute | solution.py:352
  3.2 12.6 %collective-permute-start = (bf16[128,4096]{1,0:T(8,128)(2,1)}, bf16[128,4096]{1,0:T(8,128)(2,1)S(1)}, u32[]{:S(2)}, u32[]{:S(2)}) collective-permute-start(bf16[128,4096]{1,0:T(8,128)(2,1)} %q_own.5), channel_id=1, source_target_pairs={{0,1},{1,0},{2,3},{3,2},{4,5},{5,4},{6,7},{7,6},{8,9},{9,8},{10,11... | collective-permute-start | bytes 3145736 | tf_op jit(solution)/shard_map/ppermute | solution.py:352
  3.2 14.4 %collective-permute-start.2 = (bf16[128,4096]{1,0:T(8,128)(2,1)}, bf16[128,4096]{1,0:T(8,128)(2,1)}, u32[]{:S(2)}, u32[]{:S(2)}) collective-permute-start(bf16[128,4096]{1,0:T(8,128)(2,1)} %g_own.3), channel_id=1, source_target_pairs={{0,1},{1,0},{2,3},{3,2},{4,5},{5,4},{6,7},{7,6},{8,9},{9,8},{10,11... | collective-permute-start | bytes 3145736 | tf_op jit(solution)/shard_map/ppermute | solution.py:352
  6.4 20.4 %collective-permute-start.4 = (f32[32,128]{1,0:T(8,128)}, f32[32,128]{1,0:T(8,128)}, u32[]{:S(2)}, u32[]{:S(2)}) collective-permute-start(f32[32,128]{1,0:T(8,128)} %row_deltas.1.d_own), channel_id=1, source_target_pairs={{0,1},{1,0},{2,3},{3,2},{4,5},{5,4},{6,7},{7,6},{8,9},{9,8},{10,11... | collective-permute-start | bytes 49160 | tf_op jit(solution)/shard_map/ppermute | solution.py:352
  7.9 7.0 %collective-permute-start.7 = (bf16[256,256]{1,0:T(8,128)(2,1)}, bf16[256,256]{1,0:T(8,128)(2,1)}, u32[]{:S(2)}, u32[]{:S(2)}) collective-permute-start(bf16[256,256]{1,0:T(8,128)(2,1)} %pad_maximum_fusion.4), channel_id=1, source_target_pairs={{0,2},{2,0},{1,3},{3,1},{4,6},{6,4},{5,7},{7,5},{8,10},{10,8},{9,1... | collective-permute-start | bytes 393224 | tf_op jit(solution)/shard_map/ppermute | solution.py:355
  10.9 18.4 %copy-start.9 = (f32[32,128]{1,0:T(8,128)S(1)}, f32[32,128]{1,0:T(8,128)}, u32[]{:S(2)}) copy-start(f32[32,128]{1,0:T(8,128)} %row_deltas.1.d_own) | copy-start | bytes 49156
  10.9 18.5 %copy-start.13 = (bf16[256,128]{1,0:T(8,128)(2,1)S(1)}, bf16[256,128]{1,0:T(8,128)(2,1)}, u32[]{:S(2)}) copy-start(bf16[256,128]{1,0:T(8,128)(2,1)} %get-tuple-element.29) | copy-start | bytes 196612
  15.8 29.3 %collective-permute-start.1 = (bf16[256,1024]{1,0:T(8,128)(2,1)S(1)}, bf16[256,1024]{1,0:T(8,128)(2,1)S(1)}, u32[]{:S(2)}, u32[]{:S(2)}) collective-permute-start(bf16[256,1024]{1,0:T(8,128)(2,1)S(1)} %pad_maximum_fusion), channel_id=1, source_target_pairs={{0,2},{2,0},{1,3},{3,1},{4,6},{6,4},{5,7},{7,5},{8,10},{10,8},{9,1... | collective-permute-start | bytes 1572872 | tf_op jit(solution)/shard_map/ppermute | solution.py:355
  19.5 35.2 %collective-permute-start.3 = (bf16[256,1024]{1,0:T(8,128)(2,1)}, bf16[256,1024]{1,0:T(8,128)(2,1)}, u32[]{:S(2)}, u32[]{:S(2)}) collective-permute-start(bf16[256,1024]{1,0:T(8,128)(2,1)} %pad_maximum_fusion.1), channel_id=1, source_target_pairs={{0,2},{2,0},{1,3},{3,1},{4,6},{6,4},{5,7},{7,5},{8,10},{10,8},{9,1... | collective-permute-start | bytes 1572872 | tf_op jit(solution)/shard_map/ppermute | solution.py:355
  19.8 9.6 %collective-permute-start.10 = (bf16[512,128]{1,0:T(8,128)(2,1)S(1)}, bf16[512,128]{1,0:T(8,128)(2,1)S(1)}, u32[]{:S(2)}, u32[]{:S(2)}) collective-permute-start(bf16[512,128]{1,0:T(8,128)(2,1)S(1)} %pad_maximum_fusion.5.rest_0_), channel_id=1, source_target_pairs={{0,12},{1,13},{2,14},{3,15},{16,28},{17,29},{18,30},{19,31}} | collective-permute-start | bytes 393224 | tf_op jit(solution)/shard_map/ppermute | solution.py:358
  25.5 11.3 %collective-permute-start.9 = (bf16[512,128]{1,0:T(8,128)(2,1)S(1)}, bf16[512,128]{1,0:T(8,128)(2,1)S(1)}, u32[]{:S(2)}, u32[]{:S(2)}) collective-permute-start(bf16[512,128]{1,0:T(8,128)(2,1)S(1)} %pad_maximum_fusion.5.rest_0_), channel_id=1, source_target_pairs={{0,8},{4,12},{1,9},{5,13},{2,10},{6,14},{3,11},{7,15},{16,24},{20,... | collective-permute-start | bytes 393224 | tf_op jit(solution)/shard_map/ppermute | solution.py:358
  26.8 12.6 %collective-permute-start.8 = (bf16[512,128]{1,0:T(8,128)(2,1)S(1)}, bf16[512,128]{1,0:T(8,128)(2,1)S(1)}, u32[]{:S(2)}, u32[]{:S(2)}) collective-permute-start(bf16[512,128]{1,0:T(8,128)(2,1)S(1)} %pad_maximum_fusion.5.rest_0_), channel_id=1, source_target_pairs={{0,4},{4,8},{8,12},{1,5},{5,9},{9,13},{2,6},{6,10},{10,14},{3,7},{... | collective-permute-start | bytes 393224 | tf_op jit(solution)/shard_map/ppermute | solution.py:358
  29.4 0.7 copy-start.5
  30.0 24.6 %collective-permute-start.13 = (bf16[512,128]{1,0:T(8,128)(2,1)S(1)}, bf16[512,128]{1,0:T(8,128)(2,1)}, u32[]{:S(2)}, u32[]{:S(2)}) collective-permute-start(bf16[512,128]{1,0:T(8,128)(2,1)S(1)} %pad_maximum_fusion.6.rest_2_), channel_id=1, source_target_pairs={{0,12},{1,13},{2,14},{3,15},{16,28},{17,29},{18,30},{19,31}} | collective-permute-start | bytes 393224 | tf_op jit(solution)/shard_map/ppermute | solution.py:358
  36.8 0.7 copy-start.7
  37.5 17.2 %collective-permute-start.12 = (bf16[512,128]{1,0:T(8,128)(2,1)S(1)}, bf16[512,128]{1,0:T(8,128)(2,1)}, u32[]{:S(2)}, u32[]{:S(2)}) collective-permute-start(bf16[512,128]{1,0:T(8,128)(2,1)S(1)} %pad_maximum_fusion.6.rest_2_), channel_id=1, source_target_pairs={{0,8},{4,12},{1,9},{5,13},{2,10},{6,14},{3,11},{7,15},{16,24},{20,... | collective-permute-start | bytes 393224 | tf_op jit(solution)/shard_map/ppermute | solution.py:358
  39.4 19.0 %collective-permute-start.11 = (bf16[512,128]{1,0:T(8,128)(2,1)S(1)}, bf16[512,128]{1,0:T(8,128)(2,1)}, u32[]{:S(2)}, u32[]{:S(2)}) collective-permute-start(bf16[512,128]{1,0:T(8,128)(2,1)S(1)} %pad_maximum_fusion.6.rest_2_), channel_id=1, source_target_pairs={{0,4},{4,8},{8,12},{1,5},{5,9},{9,13},{2,6},{6,10},{10,14},{3,7},{... | collective-permute-start | bytes 393224 | tf_op jit(solution)/shard_map/ppermute | solution.py:358
  45.2 0.8 copy-start.2
  46.0 8.6 %collective-permute-start.5 = (f32[16,128]{1,0:T(8,128)}, f32[16,128]{1,0:T(8,128)}, u32[]{:S(2)}, u32[]{:S(2)}) collective-permute-start(f32[16,128]{1,0:T(8,128)} %pad_maximum_fusion.7), channel_id=1, source_target_pairs={{0,2},{2,0},{1,3},{3,1},{4,6},{6,4},{5,7},{7,5},{8,10},{10,8},{9,1... | collective-permute-start | bytes 24584 | tf_op jit(solution)/shard_map/ppermute | solution.py:355
  47.5 1.0 copy-start.3
  48.5 0.9 copy-start.6
  49.4 0.9 copy-start.8
  50.3 0.7 copy-start.10
  51.0 3.6 %copy-start.11 = (s32[16,10]{1,0:T(8,128)S(1)}, s32[16,10]{1,0:T(8,128)}, u32[]{:S(2)}) copy-start(s32[16,10]{1,0:T(8,128)} %anc_ref.5) | copy-start | bytes 1924
  54.6 3.8 %copy-start.4 = (bf16[256,1024]{1,0:T(8,128)(2,1)S(1)}, bf16[256,1024]{1,0:T(8,128)(2,1)}, u32[]{:S(2)}) copy-start(bf16[256,1024]{1,0:T(8,128)(2,1)} %copy-done.2) | copy-start | bytes 1572868
  68.4 44.3 %copy-start.12 = (bf16[256,1024]{1,0:T(8,128)(2,1)}, bf16[256,1024]{1,0:T(8,128)(2,1)S(1)}, u32[]{:S(2)}) copy-start(bf16[256,1024]{1,0:T(8,128)(2,1)S(1)} %get-tuple-element.13) | copy-start | bytes 1572868
  68.4 19.0 %collective-permute-start.19 = (bf16[512,256]{1,0:T(8,128)(2,1)S(1)}, bf16[512,256]{1,0:T(8,128)(2,1)S(1)}, u32[]{:S(2)}, u32[]{:S(2)}) collective-permute-start(bf16[512,256]{1,0:T(8,128)(2,1)S(1)} %get-tuple-element.18), channel_id=1, source_target_pairs={{4,0},{8,4},{12,8},{5,1},{9,5},{13,9},{6,2},{10,6},{14,10},{7,3},{... | collective-permute-start | bytes 786440 | tf_op jit(solution)/shard_map/ppermute | solution.py:361
  69.7 42.8 %collective-permute-start.17 = (bf16[512,256]{1,0:T(8,128)(2,1)S(1)}, bf16[512,256]{1,0:T(8,128)(2,1)S(1)}, u32[]{:S(2)}, u32[]{:S(2)}) collective-permute-start(bf16[512,256]{1,0:T(8,128)(2,1)S(1)} %get-tuple-element.16), channel_id=1, source_target_pairs={{8,0},{12,4},{9,1},{13,5},{10,2},{14,6},{11,3},{15,7},{24,16},{28,... | collective-permute-start | bytes 786440 | tf_op jit(solution)/shard_map/ppermute | solution.py:361
  71.0 41.5 %collective-permute-start.18 = (bf16[512,256]{1,0:T(8,128)(2,1)S(1)}, bf16[512,256]{1,0:T(8,128)(2,1)S(1)}, u32[]{:S(2)}, u32[]{:S(2)}) collective-permute-start(bf16[512,256]{1,0:T(8,128)(2,1)S(1)} %get-tuple-element.17), channel_id=1, source_target_pairs={{12,0},{13,1},{14,2},{15,3},{28,16},{29,17},{30,18},{31,19}} | collective-permute-start | bytes 786440 | tf_op jit(solution)/shard_map/ppermute | solution.py:361
  112.7 6.2 %collective-permute-start.20 = (bf16[256,256]{1,0:T(8,128)(2,1)S(1)}, bf16[256,256]{1,0:T(8,128)(2,1)S(1)}, u32[]{:S(2)}, u32[]{:S(2)}) collective-permute-start(bf16[256,256]{1,0:T(8,128)(2,1)S(1)} %fusion.1), channel_id=1, source_target_pairs={{0,2},{2,0},{1,3},{3,1},{4,6},{6,4},{5,7},{7,5},{8,10},{10,8},{9,1... | collective-permute-start | bytes 393224 | tf_op jit(solution)/shard_map/ppermute | solution.py:355
  113.3 17.4 %collective-permute-start.15 = (bf16[128,1024]{1,0:T(8,128)(2,1)S(1)}, bf16[128,1024]{1,0:T(8,128)(2,1)S(1)}, u32[]{:S(2)}, u32[]{:S(2)}) collective-permute-start(bf16[128,1024]{1,0:T(8,128)(2,1)S(1)} %get-tuple-element.14), channel_id=1, source_target_pairs={{0,1},{1,0},{2,3},{3,2},{4,5},{5,4},{6,7},{7,6},{8,9},{9,8},{10,11... | collective-permute-start | bytes 786440 | tf_op jit(solution)/shard_map/ppermute | solution.py:352
  113.3 15.7 %collective-permute-start.14 = (bf16[256,1024]{1,0:T(8,128)(2,1)}, bf16[256,1024]{1,0:T(8,128)(2,1)S(1)}, u32[]{:S(2)}, u32[]{:S(2)}) collective-permute-start(bf16[256,1024]{1,0:T(8,128)(2,1)} %copy-done.12), channel_id=1, source_target_pairs={{0,2},{2,0},{1,3},{3,1},{4,6},{6,4},{5,7},{7,5},{8,10},{10,8},{9,1... | collective-permute-start | bytes 1572872 | tf_op jit(solution)/shard_map/ppermute | solution.py:355
  118.9 10.2 %collective-permute-start.21 = (bf16[128,512]{1,0:T(8,128)(2,1)S(1)}, bf16[128,512]{1,0:T(8,128)(2,1)S(1)}, u32[]{:S(2)}, u32[]{:S(2)}) collective-permute-start(bf16[128,512]{1,0:T(8,128)(2,1)S(1)} %fusion.2), channel_id=1, source_target_pairs={{0,1},{1,0},{2,3},{3,2},{4,5},{5,4},{6,7},{7,6},{8,9},{9,8},{10,11... | collective-permute-start | bytes 393224 | tf_op jit(solution)/shard_map/ppermute | solution.py:352
  129.0 1.7 %collective-permute-start.16 = (bf16[128,1024]{1,0:T(8,128)(2,1)S(1)}, bf16[128,1024]{1,0:T(8,128)(2,1)S(1)}, u32[]{:S(2)}, u32[]{:S(2)}) collective-permute-start(bf16[128,1024]{1,0:T(8,128)(2,1)S(1)} %get-tuple-element.22), channel_id=1, source_target_pairs={{0,1},{1,0},{2,3},{3,2},{4,5},{5,4},{6,7},{7,6},{8,9},{9,8},{10,11... | collective-permute-start | bytes 786440 | tf_op jit(solution)/shard_map/ppermute | solution.py:352

commit v3 on v2

--- a/solution.py
+++ b/solution.py
@@ -22,7 +22,7 @@
 SCALE2 = SCALE / math.log(2.0)
 MASKED = -1e30
 NT_DIMS = (((1,), (1,)), ((), ()))
-PARAMS = pltpu.CompilerParams(vmem_limit_bytes=48 * 1024 * 1024)
+PARAMS = pltpu.CompilerParams(vmem_limit_bytes=28 * 1024 * 1024)
 
 
 def delta_kernel(out_ref, grad_ref, delta_ref):
@@ -249,6 +249,15 @@
         out_ref[:, HD:] = dv_acc[rows, :].astype(out_ref.dtype)
 
 
+def work(ancestors, products):
+    pairs = QUAD * (ancestors.shape[1] + 1)
+    return pl.CostEstimate(
+        flops=2 * products * pairs * GROUP * TILE * TILE * 2 * HD,
+        transcendentals=pairs * GROUP * TILE * TILE,
+        bytes_accessed=16 * 1024 * 1024,
+    )
+
+
 def fixed(shape):
     return pl.BlockSpec(shape, lambda i, *_: (0,) * len(shape))
 
@@ -284,6 +293,7 @@
         ),
         out_shape=jax.ShapeDtypeStruct((QUAD, 1, ROWS), jnp.float32),
         compiler_params=PARAMS,
+        cost_estimate=work(ancestors, 1),
         name="statistics",
     )(me, ancestors, *q_set, *k_list)
 
@@ -327,6 +337,7 @@
         ),
         out_shape=dq_shapes + [jax.ShapeDtypeStruct((LEVEL, 2 * HD), kind) for kind in kinds],
         compiler_params=PARAMS,
+        cost_estimate=work(ancestors, 5),
         name="near_grads" if near_part else "far_grads",
     )(
         me,
@@ -344,6 +355,155 @@
 WIDE_OUT = fixed((TILE, ROWS))
 
 
+def pack_keys_kernel(me_ref, k_own, v_own, k_peer, v_peer, k_away, v_away, k_far, v_far, mine_ref, send_ref):
+    mine_ref[:TILE, :HD] = k_own[...]
+    mine_ref[:TILE, HD:] = v_own[...]
+    mine_ref[TILE:, :HD] = k_peer[...]
+    mine_ref[TILE:, HD:] = v_peer[...]
+    send_ref[:TILE, :HD] = k_away[...]
+    send_ref[:TILE, HD:] = v_away[...]
+    send_ref[TILE:, :HD] = k_far[...]
+    send_ref[TILE:, HD:] = v_far[...]
+
+
+def side_head(me_ref):
+    return own_head(me_ref) ^ 1
+
+
+def pack_keys(me, keys, values, k_peer, v_peer):
+    mine = pl.BlockSpec((TILE, HD), lambda i, me_ref: (0, own_head(me_ref)))
+    away = pl.BlockSpec((TILE, HD), lambda i, me_ref: (0, side_head(me_ref)))
+    return pl.pallas_call(
+        pack_keys_kernel,
+        grid_spec=pltpu.PrefetchScalarGridSpec(
+            num_scalar_prefetch=1,
+            grid=(1,),
+            in_specs=[mine] * 4 + [away] * 4,
+            out_specs=[fixed((PAIR, 2 * HD))] * 2,
+        ),
+        out_shape=[jax.ShapeDtypeStruct((PAIR, 2 * HD), jnp.bfloat16)] * 2,
+        name="pack_keys",
+    )(me, keys, values, k_peer, v_peer, keys, values, k_peer, v_peer)
+
+
+def pack_queries_kernel(me_ref, q_own, q_peer, g_own, g_peer, q_ref, g_ref):
+    q_ref[:TILE, :] = q_own[...]
+    q_ref[TILE:, :] = q_peer[...]
+    g_ref[:TILE, :] = g_own[...]
+    g_ref[TILE:, :] = g_peer[...]
+
+
+def pack_queries(me, queries, q_peer, out_grad, g_peer):
+    away = pl.BlockSpec((TILE, ROWS), lambda i, me_ref: (0, side_head(me_ref)))
+    return pl.pallas_call(
+        pack_queries_kernel,
+        grid_spec=pltpu.PrefetchScalarGridSpec(
+            num_scalar_prefetch=1,
+            grid=(1,),
+            in_specs=[away] * 4,
+            out_specs=[SIDE] * 2,
+        ),
+        out_shape=[jax.ShapeDtypeStruct((PAIR, ROWS), jnp.bfloat16)] * 2,
+        name="pack_queries",
+    )(me, queries, q_peer, out_grad, g_peer)
+
+
+def pack_deltas_kernel(me_ref, d_own, d_peer, send_ref):
+    send_ref[:GROUP, :] = d_own[...]
+    send_ref[GROUP:, :] = d_peer[...]
+
+
+def pack_deltas(me, deltas, d_peer):
+    away = pl.BlockSpec((GROUP, TILE), lambda i, me_ref: (side_head(me_ref), 0))
+    return pl.pallas_call(
+        pack_deltas_kernel,
+        grid_spec=pltpu.PrefetchScalarGridSpec(
+            num_scalar_prefetch=1,
+            grid=(1,),
+            in_specs=[away] * 2,
+            out_specs=fixed((2 * GROUP, TILE)),
+        ),
+        out_shape=jax.ShapeDtypeStruct((2 * GROUP, TILE), jnp.float32),
+        name="pack_deltas",
+    )(me, deltas, d_peer)
+
+
+def add_sums_kernel(count, *refs):
+    total_ref, parts = refs[0], refs[1 : 1 + count]
+    own_ref, peer_ref, send_ref = refs[-3:]
+    total = total_ref[...]
+    for part in parts:
+        total += part[...].astype(jnp.float32)
+    scaled = jnp.concatenate([total[:, :HD] * SCALE, total[:, HD:]], axis=1).astype(jnp.bfloat16)
+    own_ref[...] = scaled[:TILE]
+    peer_ref[...] = scaled[TILE:PAIR]
+    send_ref[...] = scaled[PAIR:]
+
+
+def add_sums(total, parts, first_needed):
+    here = pl.BlockSpec(memory_space=pltpu.VMEM)
+    return pl.pallas_call(
+        functools.partial(add_sums_kernel, len(parts)),
+        in_specs=[here] * (1 + len(parts)) + [pl.BlockSpec(memory_space=pl.ANY)],
+        out_specs=[here] * 3,
+        out_shape=[
+            jax.ShapeDtypeStruct((TILE, 2 * HD), jnp.bfloat16),
+            jax.ShapeDtypeStruct((TILE, 2 * HD), jnp.bfloat16),
+            jax.ShapeDtypeStruct((PAIR, 2 * HD), jnp.bfloat16),
+        ],
+        name="add_sums",
+    )(total, *parts, first_needed)
+
+
+def placed(me_ref, width):
+    head = own_head(me_ref)
+    return [pl.ds(pl.multiple_of((head ^ flip) * width, width), width) for flip in range(4)]
+
+
+def place_queries_kernel(me_ref, own, side, peer, far, dq_ref):
+    at = placed(me_ref, ROWS)
+    dq_ref[:, at[0]] = own[...]
+    dq_ref[:, at[1]] = side[:TILE, :]
+    dq_ref[:, at[2]] = peer[...]
+    dq_ref[:, at[3]] = far[...]
+
+
+def place_queries(me, own, side, peer, far):
+    return pl.pallas_call(
+        place_queries_kernel,
+        grid_spec=pltpu.PrefetchScalarGridSpec(
+            num_scalar_prefetch=1,
+            grid=(1,),
+            in_specs=[WIDE_OUT, SIDE, WIDE_OUT, WIDE_OUT],
+            out_specs=fixed((TILE, QH * HD)),
+        ),
+        out_shape=jax.ShapeDtypeStruct((TILE, QH * HD), jnp.bfloat16),
+        name="place_queries",
+    )(me, own, side, peer, far)
+
+
+def place_keys_kernel(me_ref, own, side, peer, far, dk_ref, dv_ref):
+    at = placed(me_ref, HD)
+    for spot, part in zip(at, (own[...], side[:TILE, :], peer[...], far[...])):
+        dk_ref[:, spot] = part[:, :HD]
+        dv_ref[:, spot] = part[:, HD:]
+
+
+def place_keys(me, own, side, peer, far):
+    piece = fixed((TILE, 2 * HD))
+    return pl.pallas_call(
+        place_keys_kernel,
+        grid_spec=pltpu.PrefetchScalarGridSpec(
+            num_scalar_prefetch=1,
+            grid=(1,),
+            in_specs=[piece, fixed((PAIR, 2 * HD)), piece, piece],
+            out_specs=[fixed((TILE, KVH * HD))] * 2,
+        ),
+        out_shape=[jax.ShapeDtypeStruct((TILE, KVH * HD), jnp.bfloat16)] * 2,
+        name="place_keys",
+    )(me, own, side, peer, far)
+
+
 def per_device(steps, queries, keys, values, outputs, out_grad, ancestors):
     level, side, core = (lax.axis_index(name) for name in ("level", "side", "core"))
     me = (QUAD * level + 2 * side + core).reshape(1).astype(jnp.int32)
@@ -360,40 +520,19 @@
     def down(x, shift):
         return lax.ppermute(x, "level", [(z + shift, z) for z in range(steps - shift)])
 
-    def columns(x, who, count):
-        return lax.dynamic_slice_in_dim(x, who * count, count, 1)
-
-    def head_rows(x, who):
-        return lax.dynamic_slice_in_dim(x, who * GROUP, GROUP, 0)
-
-    side_head = 2 * core + 1 - side
-    half = 2 * HD
-    kv_peer = to_peer(
-        jnp.concatenate([columns(keys, 1 - core, half), columns(values, 1 - core, half)], axis=1)
-    )
-    q_peer = to_peer(queries)
-    g_peer = to_peer(out_grad)
-    k_chip = jnp.concatenate([columns(keys, core, half), kv_peer[:, :half]], axis=0)
-    v_chip = jnp.concatenate([columns(values, core, half), kv_peer[:, half:]], axis=0)
-    kv_side = to_side(
-        jnp.concatenate([columns(k_chip, 1 - side, HD), columns(v_chip, 1 - side, HD)], axis=1)
-    )
-    k_level = jnp.concatenate([columns(k_chip, side, HD), kv_side[:, :HD]], axis=0)
-    v_level = jnp.concatenate([columns(v_chip, side, HD), kv_side[:, HD:]], axis=0)
+    kv_chip, kv_send = pack_keys(me, keys, values, to_peer(keys), to_peer(values))
+    kv_side = to_side(kv_send)
+    k_level = jnp.concatenate([kv_chip[:, :HD], kv_side[:, :HD]], axis=0)
+    v_level = jnp.concatenate([kv_chip[:, HD:], kv_side[:, HD:]], axis=0)
     k_list = [k_level] + [up(k_level, shift) for shift in range(1, steps)]
-
-    def both(own, peer):
-        return jnp.concatenate([columns(own, side_head, ROWS), columns(peer, side_head, ROWS)], axis=0)
-
-    q_set = (queries, q_peer, to_side(both(queries, q_peer)))
+    q_peer, g_peer = to_peer(queries), to_peer(out_grad)
+    q_send, g_send = pack_queries(me, queries, q_peer, out_grad, g_peer)
+    q_set = (queries, q_peer, to_side(q_send))
     v_list = [v_level] + [up(v_level, shift) for shift in range(1, steps)]
-    g_set = (out_grad, g_peer, to_side(both(out_grad, g_peer)))
+    g_set = (out_grad, g_peer, to_side(g_send))
     deltas = row_deltas(outputs, out_grad)
     d_peer = to_peer(deltas)
-    d_side = to_side(
-        jnp.concatenate([head_rows(deltas, side_head), head_rows(d_peer, side_head)], axis=0)
-    )
-    d_set = (deltas, d_peer, d_side)
+    d_set = (deltas, d_peer, to_side(pack_deltas(me, deltas, d_peer)))
 
     lse = statistics(me, ancestors, q_set, k_list)
     dq_far, *far = gradients(me, ancestors, q_set, g_set, d_set, lse, k_list[2:], v_list[2:])
@@ -401,38 +540,18 @@
     dq_own, dq_peer, dq_side, total, near = gradients(
         me, ancestors, q_set, g_set, d_set, lse, k_list[:2], v_list[:2], dq_far
     )
+    dq_side = to_side(dq_side)
     back.append(down(near, 1))
-    dq_side = to_side(dq_side)
-    dq_diag = to_peer(dq_side[TILE:])
     dq_peer = to_peer(dq_peer)
 
-    for part in back:
-        total += part.astype(jnp.float32)
-    scaled = jnp.concatenate([total[:, :HD] * SCALE, total[:, HD:]], axis=1).astype(jnp.bfloat16)
-    kv_side = to_side(scaled[PAIR:])
-    kv_peer = to_peer(jnp.concatenate([scaled[TILE:PAIR], kv_side[TILE:]], axis=1))
-
-    def in_order(own, beside, peer, diagonal):
-        here = jnp.where(
-            side == 0,
-            jnp.concatenate([own, beside], axis=1),
-            jnp.concatenate([beside, own], axis=1),
-        )
-        there = jnp.where(
-            side == 0,
-            jnp.concatenate([peer, diagonal], axis=1),
-            jnp.concatenate([diagonal, peer], axis=1),
-        )
-        return jnp.where(
-            core == 0,
-            jnp.concatenate([here, there], axis=1),
-            jnp.concatenate([there, here], axis=1),
-        )
-
+    sum_own, sum_peer, sum_side = add_sums(total, back, dq_side)
+    dq_far = to_peer(dq_side[TILE:])
+    sum_peer = to_peer(sum_peer)
+    sum_side = to_side(sum_side)
+    sum_far = to_peer(sum_side[TILE:])
     return (
-        in_order(dq_own, dq_side[:TILE], dq_peer, dq_diag),
-        in_order(scaled[:TILE, :HD], kv_side[:TILE, :HD], kv_peer[:, :HD], kv_peer[:, half : half + HD]),
-        in_order(scaled[:TILE, HD:], kv_side[:TILE, HD:], kv_peer[:, HD:half], kv_peer[:, half + HD :]),
+        place_queries(me, dq_own, dq_side, dq_peer, dq_far),
+        *place_keys(me, sum_own, sum_side, sum_peer, sum_far),
     )
 
 

time: 131 us -> 113 us (0.86)
  the two profiles are of different devices: /device:TPU:0 before, /device:TPU:3 now
where the time goes in v3:
time: 113 us; the launch traced here: 112 us
  starting transfers between devices  40.6 us (36%)
  waiting for transfers between devices  37.7 us (33%)
  Pallas kernels  25.1 us (22%)
  local copies, waits for them, and re-layouts  7.5 us (7%)
    ppermute x3, waiting for transfers between devices, down(): lax.ppermute(x, 'level', [(z + shift, z) for z in range(steps - shift)])  28.7 us
    ppermute x6, starting transfers between devices, up(): lax.ppermute(x, 'level', [(z, z + shift) for z in range(steps - shift)])  21.8 us
    ppermute x9, starting transfers between devices, to_peer(): return lax.ppermute(x, 'core', [(0, 1), (1, 0)])  10.5 us
    pallas_call x2, Pallas kernels, gradients(): pl.pallas_call(functools.partial(grads_kernel, ancestors.shape[1], near_p...  8.06 us
    unnamed x48, local copies, waits for them, and re-layouts  7.46 us
    ppermute x6, waiting for transfers between devices, to_side(): return lax.ppermute(x, 'side', [(0, 1), (1, 0)])  7.42 us
    ppermute x6, starting transfers between devices, to_side(): return lax.ppermute(x, 'side', [(0, 1), (1, 0)])  4.56 us
    ppermute x3, starting transfers between devices, down(): lax.ppermute(x, 'level', [(z + shift, z) for z in range(steps - shift)])  3.86 us
  transfers between devices with their start and end apart: 24, of which 8 were waited for; matrix products, arithmetic and copies ran while one was open for 0% of the time, Pallas kernels for 14%

profile of v3, /device:TPU:3, one launch (start us, length us, event | category | flops | bytes accessed | tf_op | source)
XLA Modules:
  0.0 111.9 jit_solution(9149786144461043430)
XLA Ops:
  0.6 0.7 collective-permute-start
  1.4 0.1 collective-permute-start.1
  1.5 0.4 collective-permute-start.6
  1.9 0.1 collective-permute-start.7
  2.0 2.8 %row_deltas.1.d_own = f32[32,128]{1,0:T(8,128)} custom-call(bf16[128,4096]{1,0:T(8,128)(2,1)} %out_ref.1, bf16[128,4096]{1,0:T(8,128)(2,1)} %g_own.5), custom_call_target="tpu_custom_call" | custom-call | tf_op jit(solution)/shard_map/row_deltas/pallas_call | solution.py:36
  4.7 0.4 collective-permute-start.4
  5.1 0.4 collective-permute-done.6.k_peer.k_far
  5.6 0.2 collective-permute-done.7.v_peer.v_far
  5.7 0.5 copy-done.13
  6.2 0.2 copy-done.14
  6.4 1.6 %pack_keys.1 = (bf16[256,256]{1,0:T(8,128)(2,1)}, bf16[256,256]{1,0:T(8,128)(2,1)}) custom-call(s32[1]{0:T(128)} %bitcast.me_ref, bf16[128,512]{1,0:T(8,128)(2,1)} %k_away.1, bf16[128,512]{1,0:T(8,128)(2,1)} %v_away.1, bf16[128,512]{1,0:T(8,128)(2,1)} %copy-done.13, bf16[128,512]{1,0:T(8,128)(2,1)} %copy-done.14, bf16[128,512]{1,0:T(8,128)(2,1)} %k_away.1, ...), custom_call_target="tpu_custom_call" | custom-call | tf_op jit(solution)/shard_map/pack_keys/pallas_call | solution.py:376
  8.0 1.3 %collective-permute-start.8 = (bf16[256,256]{1,0:T(8,128)(2,1)}, bf16[256,256]{1,0:T(8,128)(2,1)S(1)}, u32[]{:S(2)}, u32[]{:S(2)}) collective-permute-start(bf16[256,256]{1,0:T(8,128)(2,1)} %get-tuple-element.23), channel_id=1, source_target_pairs={{0,2},{2,0},{1,3},{3,1},{4,6},{6,4},{5,7},{7,5},{8,10},{10,8},{9,1... | collective-permute-start | bytes 393224 | tf_op jit(solution)/shard_map/ppermute | solution.py:515
  9.4 0.0 collective-permute-done.q_peer
  9.4 0.0 collective-permute-done.1.g_peer
  9.4 1.0 copy-done.2
  10.3 1.0 copy-done.4
  11.3 2.2 %pack_queries.1 = (bf16[256,1024]{1,0:T(8,128)(2,1)}, bf16[256,1024]{1,0:T(8,128)(2,1)}) custom-call(s32[1]{0:T(128)} %bitcast.me_ref, bf16[128,4096]{1,0:T(8,128)(2,1)} %q_own.7, bf16[128,4096]{1,0:T(8,128)(2,1)} %copy-done.2, bf16[128,4096]{1,0:T(8,128)(2,1)} %g_own.5, bf16[128,4096]{1,0:T(8,128)(2,1)} %copy-done.4), custom_call_target="tpu_custom_call" | custom-call | tf_op jit(solution)/shard_map/pack_queries/pallas_call | solution.py:398
  13.5 0.2 collective-permute-start.2
  13.8 1.3 %collective-permute-start.3 = (bf16[256,1024]{1,0:T(8,128)(2,1)}, bf16[256,1024]{1,0:T(8,128)(2,1)S(1)}, u32[]{:S(2)}, u32[]{:S(2)}) collective-permute-start(bf16[256,1024]{1,0:T(8,128)(2,1)} %get-tuple-element.21), channel_id=1, source_target_pairs={{0,2},{2,0},{1,3},{3,1},{4,6},{6,4},{5,7},{7,5},{8,10},{10,8},{9,1... | collective-permute-start | bytes 1572872 | tf_op jit(solution)/shard_map/ppermute | solution.py:515
  15.1 5.2 %collective-permute-start.11 = (bf16[512,128]{1,0:T(8,128)(2,1)S(1)}, bf16[512,128]{1,0:T(8,128)(2,1)S(1)}, u32[]{:S(2)}, u32[]{:S(2)}) collective-permute-start(bf16[512,128]{1,0:T(8,128)(2,1)S(1)} %pad_maximum_fusion.rest_0_), channel_id=1, source_target_pairs={{0,12},{1,13},{2,14},{3,15},{16,28},{17,29},{18,30},{19,31}} | collective-permute-start | bytes 393224 | tf_op jit(solution)/shard_map/ppermute | solution.py:518
  20.4 1.3 %collective-permute-start.10 = (bf16[512,128]{1,0:T(8,128)(2,1)S(1)}, bf16[512,128]{1,0:T(8,128)(2,1)S(1)}, u32[]{:S(2)}, u32[]{:S(2)}) collective-permute-start(bf16[512,128]{1,0:T(8,128)(2,1)S(1)} %pad_maximum_fusion.rest_0_), channel_id=1, source_target_pairs={{0,8},{4,12},{1,9},{5,13},{2,10},{6,14},{3,11},{7,15},{16,24},{20,... | collective-permute-start | bytes 393224 | tf_op jit(solution)/shard_map/ppermute | solution.py:518
  21.7 0.0 collective-permute-done.4.d_peer
  21.7 0.0 copy-start.9
  21.7 2.2 %collective-permute-start.9 = (bf16[512,128]{1,0:T(8,128)(2,1)S(1)}, bf16[512,128]{1,0:T(8,128)(2,1)S(1)}, u32[]{:S(2)}, u32[]{:S(2)}) collective-permute-start(bf16[512,128]{1,0:T(8,128)(2,1)S(1)} %pad_maximum_fusion.rest_0_), channel_id=1, source_target_pairs={{0,4},{4,8},{8,12},{1,5},{5,9},{9,13},{2,6},{6,10},{10,14},{3,7},{... | collective-permute-start | bytes 393224 | tf_op jit(solution)/shard_map/ppermute | solution.py:518
  23.9 1.3 %pack_deltas.1 = f32[16,128]{1,0:T(8,128)} custom-call(s32[1]{0:T(128)} %bitcast.me_ref, f32[32,128]{1,0:T(8,128)} %row_deltas.1.d_own, f32[32,128]{1,0:T(8,128)} %copy-done.9), custom_call_target="tpu_custom_call" | custom-call | tf_op jit(solution)/shard_map/pack_deltas/pallas_call | solution.py:418
  25.2 0.0 copy-start
  25.2 0.3 collective-permute-start.5
  25.5 0.0 collective-permute-done.10.rest_2_.rest_0_
  25.5 9.5 %collective-permute-start.14 = (bf16[512,128]{1,0:T(8,128)(2,1)S(1)}, bf16[512,128]{1,0:T(8,128)(2,1)S(1)}, u32[]{:S(2)}, u32[]{:S(2)}) collective-permute-start(bf16[512,128]{1,0:T(8,128)(2,1)S(1)} %pad_maximum_fusion.1.rest_2_), channel_id=1, source_target_pairs={{0,12},{1,13},{2,14},{3,15},{16,28},{17,29},{18,30},{19,31}} | collective-permute-start | bytes 393224 | tf_op jit(solution)/shard_map/ppermute | solution.py:518
  35.1 0.0 collective-permute-done.9.rest_1_
  35.1 1.9 %collective-permute-start.13 = (bf16[512,128]{1,0:T(8,128)(2,1)S(1)}, bf16[512,128]{1,0:T(8,128)(2,1)S(1)}, u32[]{:S(2)}, u32[]{:S(2)}) collective-permute-start(bf16[512,128]{1,0:T(8,128)(2,1)S(1)} %pad_maximum_fusion.1.rest_2_), channel_id=1, source_target_pairs={{0,8},{4,12},{1,9},{5,13},{2,10},{6,14},{3,11},{7,15},{16,24},{20,... | collective-permute-start | bytes 393224 | tf_op jit(solution)/shard_map/ppermute | solution.py:518
  37.0 0.0 collective-permute-done.2.q_side
  37.0 1.6 %collective-permute-start.12 = (bf16[512,128]{1,0:T(8,128)(2,1)S(1)}, bf16[512,128]{1,0:T(8,128)(2,1)S(1)}, u32[]{:S(2)}, u32[]{:S(2)}) collective-permute-start(bf16[512,128]{1,0:T(8,128)(2,1)S(1)} %pad_maximum_fusion.1.rest_2_), channel_id=1, source_target_pairs={{0,4},{4,8},{8,12},{1,5},{5,9},{9,13},{2,6},{6,10},{10,14},{3,7},{... | collective-permute-start | bytes 393224 | tf_op jit(solution)/shard_map/ppermute | solution.py:518
  38.6 0.0 copy-start.3
  38.6 1.2 %copy-done.3 = bf16[128,4096]{1,0:T(8,128)(2,1)S(1)} copy-done((bf16[128,4096]{1,0:T(8,128)(2,1)S(1)}, bf16[128,4096]{1,0:T(8,128)(2,1)}, u32[]{:S(2)}) %copy-start.3) | copy-done | bytes 1048600
  39.8 3.1 %statistics.1.lse_ref = f32[4,1,1024]{2,1,0:T(1,128)S(1)} custom-call(s32[1]{0:T(128)} %bitcast.me_ref, s32[16,10]{1,0:T(8,128)S(1)} %copy-done.11, bf16[128,4096]{1,0:T(8,128)(2,1)S(1)} %copy-done.1, bf16[128,4096]{1,0:T(8,128)(2,1)S(1)} %copy-done.3, bf16[256,1024]{1,0:T(8,128)(2,1)S(1)} %collective-permute-done.2.q_side, ...), custom_call_target="tpu_custom_call" | custom-call | flops 2952790016 | bytes 16777216 | tf_op jit(solution)/shard_map/statistics/pallas_call | solution.py:280
  43.0 0.0 collective-permute-done.14.rest_3_
  43.0 1.2 %far_grads.1 = (f32[4,128,1024]{2,1,0:T(8,128)S(1)}, bf16[512,256]{1,0:T(8,128)(2,1)S(1)}, bf16[512,256]{1,0:T(8,128)(2,1)S(1)}) custom-call(s32[1]{0:T(128)} %bitcast.me_ref, s32[16,10]{1,0:T(8,128)S(1)} %copy-done.11, bf16[128,4096]{1,0:T(8,128)(2,1)S(1)} %copy-done.1, bf16[128,4096]{1,0:T(8,128)(2,1)S(1)} %copy-done.3, ...), custom_call_target="tpu_custom_call" | custom-call | flops 14763950080 | bytes 16777216 | tf_op jit(solution)/shard_map/far_grads/pallas_call | solution.py:327
  44.3 6.8 %near_grads.1 = (bf16[128,1024]{1,0:T(8,128)(2,1)S(1)}, bf16[128,1024]{1,0:T(8,128)(2,1)S(1)}, bf16[256,1024]{1,0:T(8,128)(2,1)S(1)}, f32[512,256]{1,0:T(8,128)S(1)}, bf16[512,256]{1,0:T(8,128)(2,1)S(1)}) custom-call(s32[1]{0:T(128)} %bitcast.me_ref, s32[16,10]{1,0:T(8,128)S(1)} %copy-done.11, bf16[128,4096]{1,0:T(8,128)(2,1)S(1)} %copy-done.1, ...), custom_call_target="tpu_custom_call" | custom-call | flops 14763950080 | bytes 16777216 | tf_op jit(solution)/shard_map/near_grads/pallas_call | solution.py:327
  51.1 0.0 copy-start.6
  51.1 0.8 copy-done.6
  51.9 0.7 copy-done.7
  52.6 0.2 collective-permute-start.15
  52.8 1.3 %collective-permute-start.20 = (bf16[512,256]{1,0:T(8,128)(2,1)S(1)}, bf16[512,256]{1,0:T(8,128)(2,1)S(1)}, u32[]{:S(2)}, u32[]{:S(2)}) collective-permute-start(bf16[512,256]{1,0:T(8,128)(2,1)S(1)} %get-tuple-element.31), channel_id=1, source_target_pairs={{4,0},{8,4},{12,8},{5,1},{9,5},{13,9},{6,2},{10,6},{14,10},{7,3},{... | collective-permute-start | bytes 786440 | tf_op jit(solution)/shard_map/ppermute | solution.py:521
  54.1 1.3 %collective-permute-start.18 = (bf16[512,256]{1,0:T(8,128)(2,1)S(1)}, bf16[512,256]{1,0:T(8,128)(2,1)S(1)}, u32[]{:S(2)}, u32[]{:S(2)}) collective-permute-start(bf16[512,256]{1,0:T(8,128)(2,1)S(1)} %get-tuple-element.29), channel_id=1, source_target_pairs={{8,0},{12,4},{9,1},{13,5},{10,2},{14,6},{11,3},{15,7},{24,16},{28,... | collective-permute-start | bytes 786440 | tf_op jit(solution)/shard_map/ppermute | solution.py:521
  55.4 1.3 %collective-permute-start.19 = (bf16[512,256]{1,0:T(8,128)(2,1)S(1)}, bf16[512,256]{1,0:T(8,128)(2,1)S(1)}, u32[]{:S(2)}, u32[]{:S(2)}) collective-permute-start(bf16[512,256]{1,0:T(8,128)(2,1)S(1)} %get-tuple-element.30), channel_id=1, source_target_pairs={{12,0},{13,1},{14,2},{15,3},{28,16},{29,17},{30,18},{31,19}} | collective-permute-start | bytes 786440 | tf_op jit(solution)/shard_map/ppermute | solution.py:521
  56.7 1.5 %collective-permute-start.16 = (bf16[128,1024]{1,0:T(8,128)(2,1)S(1)}, bf16[128,1024]{1,0:T(8,128)(2,1)S(1)}, u32[]{:S(2)}, u32[]{:S(2)}) collective-permute-start(bf16[128,1024]{1,0:T(8,128)(2,1)S(1)} %get-tuple-element.27), channel_id=1, source_target_pairs={{0,1},{1,0},{2,3},{3,2},{4,5},{5,4},{6,7},{7,6},{8,9},{9,8},{10,11... | collective-permute-start | bytes 786440 | tf_op jit(solution)/shard_map/ppermute | solution.py:512
  58.2 6.7 %collective-permute-done.15.side.refs_4_ = bf16[256,1024]{1,0:T(8,128)(2,1)S(1)} collective-permute-done((bf16[256,1024]{1,0:T(8,128)(2,1)S(1)}, bf16[256,1024]{1,0:T(8,128)(2,1)S(1)}, u32[]{:S(2)}, u32[]{:S(2)}) %collective-permute-start.15) | collective-permute-done | bytes 524320 | tf_op jit(solution)/shard_map/ppermute | solution.py:515
  64.9 2.1 %collective-permute-start.17 = (bf16[128,1024]{1,0:T(8,128)(2,1)S(1)}, bf16[128,1024]{1,0:T(8,128)(2,1)S(1)}, u32[]{:S(2)}, u32[]{:S(2)}) collective-permute-start(bf16[128,1024]{1,0:T(8,128)(2,1)S(1)} %slice.26), channel_id=1, source_target_pairs={{0,1},{1,0},{2,3},{3,2},{4,5},{5,4},{6,7},{7,6},{8,9},{9,8},{10,11... | collective-permute-start | bytes 786440 | tf_op jit(solution)/shard_map/ppermute | solution.py:512
  67.0 1.5 %collective-permute-done.20.refs_3_ = bf16[512,256]{1,0:T(8,128)(2,1)S(1)} collective-permute-done((bf16[512,256]{1,0:T(8,128)(2,1)S(1)}, bf16[512,256]{1,0:T(8,128)(2,1)S(1)}, u32[]{:S(2)}, u32[]{:S(2)}) %collective-permute-start.20) | collective-permute-done | bytes 262176 | tf_op jit(solution)/shard_map/ppermute | solution.py:521
  68.6 16.6 %collective-permute-done.18.refs_1_ = bf16[512,256]{1,0:T(8,128)(2,1)S(1)} collective-permute-done((bf16[512,256]{1,0:T(8,128)(2,1)S(1)}, bf16[512,256]{1,0:T(8,128)(2,1)S(1)}, u32[]{:S(2)}, u32[]{:S(2)}) %collective-permute-start.18) | collective-permute-done | bytes 262176 | tf_op jit(solution)/shard_map/ppermute | solution.py:521
  85.1 10.6 %collective-permute-done.19.refs_2_ = bf16[512,256]{1,0:T(8,128)(2,1)S(1)} collective-permute-done((bf16[512,256]{1,0:T(8,128)(2,1)S(1)}, bf16[512,256]{1,0:T(8,128)(2,1)S(1)}, u32[]{:S(2)}, u32[]{:S(2)}) %collective-permute-start.19) | collective-permute-done | bytes 262176 | tf_op jit(solution)/shard_map/ppermute | solution.py:521
  95.8 0.7 copy-done.20
  96.5 2.0 %add_sums.1 = (bf16[128,256]{1,0:T(8,128)(2,1)}, bf16[128,256]{1,0:T(8,128)(2,1)}, bf16[256,256]{1,0:T(8,128)(2,1)}) custom-call(f32[512,256]{1,0:T(8,128)} %copy-done.6, bf16[512,256]{1,0:T(8,128)(2,1)} %copy-done.19, bf16[512,256]{1,0:T(8,128)(2,1)} %copy-done.20, bf16[512,256]{1,0:T(8,128)(2,1)} %copy-done.18, bf16[256,1024]{1,0:T(8,128)(2,1)} %copy-done.12), custom_call_target="tpu_custom_call" | custom-call | tf_op jit(solution)/shard_map/add_sums/pallas_call | solution.py:445
  98.5 1.2 %collective-permute-start.21 = (bf16[256,256]{1,0:T(8,128)(2,1)}, bf16[256,256]{1,0:T(8,128)(2,1)S(1)}, u32[]{:S(2)}, u32[]{:S(2)}) collective-permute-start(bf16[256,256]{1,0:T(8,128)(2,1)} %get-tuple-element.33), channel_id=1, source_target_pairs={{0,2},{2,0},{1,3},{3,1},{4,6},{6,4},{5,7},{7,5},{8,10},{10,8},{9,1... | collective-permute-start | bytes 393224 | tf_op jit(solution)/shard_map/ppermute | solution.py:515
  99.7 2.1 %collective-permute-start.22 = (bf16[128,256]{1,0:T(8,128)(2,1)}, bf16[128,256]{1,0:T(8,128)(2,1)S(1)}, u32[]{:S(2)}, u32[]{:S(2)}) collective-permute-start(bf16[128,256]{1,0:T(8,128)(2,1)} %get-tuple-element.34), channel_id=1, source_target_pairs={{0,1},{1,0},{2,3},{3,2},{4,5},{5,4},{6,7},{7,6},{8,9},{9,8},{10,11... | collective-permute-start | bytes 196616 | tf_op jit(solution)/shard_map/ppermute | solution.py:512
  101.8 0.7 collective-permute-done.21.side
  102.5 3.0 %collective-permute-start.23 = (bf16[128,256]{1,0:T(8,128)(2,1)S(1)}, bf16[128,256]{1,0:T(8,128)(2,1)S(1)}, u32[]{:S(2)}, u32[]{:S(2)}) collective-permute-start(bf16[128,256]{1,0:T(8,128)(2,1)S(1)} %slice.27), channel_id=1, source_target_pairs={{0,1},{1,0},{2,3},{3,2},{4,5},{5,4},{6,7},{7,6},{8,9},{9,8},{10,11... | collective-permute-start | bytes 196616 | tf_op jit(solution)/shard_map/ppermute | solution.py:512
  105.5 0.9 collective-permute-done.23.far
  106.4 0.6 copy-done.23
  107.1 1.7 %place_keys.1 = (bf16[128,512]{1,0:T(8,128)(2,1)}, bf16[128,512]{1,0:T(8,128)(2,1)}) custom-call(s32[1]{0:T(128)} %bitcast.me_ref, bf16[128,256]{1,0:T(8,128)(2,1)} %get-tuple-element.32.own, bf16[256,256]{1,0:T(8,128)(2,1)} %copy-done.15, bf16[128,256]{1,0:T(8,128)(2,1)} %copy-done.22, bf16[128,256]{1,0:T(8,128)(2,1)} %copy-done.23), custom_call_target="tpu_custom_call" | custom-call | tf_op jit(solution)/shard_map/place_keys/pallas_call | solution.py:494
  108.8 0.7 copy-done.16
  109.5 0.1 copy-done.17
  109.6 2.3 %place_queries.1 = bf16[128,4096]{1,0:T(8,128)(2,1)} custom-call(s32[1]{0:T(128)} %bitcast.me_ref, bf16[128,1024]{1,0:T(8,128)(2,1)} %copy-done.7, bf16[256,1024]{1,0:T(8,128)(2,1)} %copy-done.12, bf16[128,1024]{1,0:T(8,128)(2,1)} %copy-done.16, bf16[128,1024]{1,0:T(8,128)(2,1)} %copy-done.17), custom_call_target="tpu_custom_call" | custom-call | tf_op jit(solution)/shard_map/place_queries/pallas_call | solution.py:472
  (48 shorter events, 0.1 us)
Async XLA Ops:
  0.6 8.7 %collective-permute-start = (bf16[128,4096]{1,0:T(8,128)(2,1)}, bf16[128,4096]{1,0:T(8,128)(2,1)S(1)}, u32[]{:S(2)}, u32[]{:S(2)}) collective-permute-start(bf16[128,4096]{1,0:T(8,128)(2,1)} %q_own.7), channel_id=1, source_target_pairs={{0,1},{1,0},{2,3},{3,2},{4,5},{5,4},{6,7},{7,6},{8,9},{9,8},{10,11... | collective-permute-start | bytes 3145736 | tf_op jit(solution)/shard_map/ppermute | solution.py:512
  1.4 8.0 %collective-permute-start.1 = (bf16[128,4096]{1,0:T(8,128)(2,1)}, bf16[128,4096]{1,0:T(8,128)(2,1)S(1)}, u32[]{:S(2)}, u32[]{:S(2)}) collective-permute-start(bf16[128,4096]{1,0:T(8,128)(2,1)} %g_own.5), channel_id=1, source_target_pairs={{0,1},{1,0},{2,3},{3,2},{4,5},{5,4},{6,7},{7,6},{8,9},{9,8},{10,11... | collective-permute-start | bytes 3145736 | tf_op jit(solution)/shard_map/ppermute | solution.py:512
  1.5 4.1 %collective-permute-start.6 = (bf16[128,512]{1,0:T(8,128)(2,1)}, bf16[128,512]{1,0:T(8,128)(2,1)S(1)}, u32[]{:S(2)}, u32[]{:S(2)}) collective-permute-start(bf16[128,512]{1,0:T(8,128)(2,1)} %k_away.1), channel_id=1, source_target_pairs={{0,1},{1,0},{2,3},{3,2},{4,5},{5,4},{6,7},{7,6},{8,9},{9,8},{10,11... | collective-permute-start | bytes 393224 | tf_op jit(solution)/shard_map/ppermute | solution.py:512
  1.9 3.9 %collective-permute-start.7 = (bf16[128,512]{1,0:T(8,128)(2,1)}, bf16[128,512]{1,0:T(8,128)(2,1)S(1)}, u32[]{:S(2)}, u32[]{:S(2)}) collective-permute-start(bf16[128,512]{1,0:T(8,128)(2,1)} %v_away.1), channel_id=1, source_target_pairs={{0,1},{1,0},{2,3},{3,2},{4,5},{5,4},{6,7},{7,6},{8,9},{9,8},{10,11... | collective-permute-start | bytes 393224 | tf_op jit(solution)/shard_map/ppermute | solution.py:512
  4.7 16.9 %collective-permute-start.4 = (f32[32,128]{1,0:T(8,128)}, f32[32,128]{1,0:T(8,128)S(1)}, u32[]{:S(2)}, u32[]{:S(2)}) collective-permute-start(f32[32,128]{1,0:T(8,128)} %row_deltas.1.d_own), channel_id=1, source_target_pairs={{0,1},{1,0},{2,3},{3,2},{4,5},{5,4},{6,7},{7,6},{8,9},{9,8},{10,11... | collective-permute-start | bytes 49160 | tf_op jit(solution)/shard_map/ppermute | solution.py:512
  5.6 0.7 copy-start.13
  5.7 0.7 copy-start.14
  8.0 5.7 %copy-start.21 = (bf16[256,256]{1,0:T(8,128)(2,1)S(1)}, bf16[256,256]{1,0:T(8,128)(2,1)}, u32[]{:S(2)}) copy-start(bf16[256,256]{1,0:T(8,128)(2,1)} %get-tuple-element.22) | copy-start | bytes 393220
  8.0 30.6 %copy-start.1 = (bf16[128,4096]{1,0:T(8,128)(2,1)S(1)}, bf16[128,4096]{1,0:T(8,128)(2,1)}, u32[]{:S(2)}) copy-start(bf16[128,4096]{1,0:T(8,128)(2,1)} %q_own.7) | copy-start | bytes 3145732
  8.0 30.6 %copy-start.11 = (s32[16,10]{1,0:T(8,128)S(1)}, s32[16,10]{1,0:T(8,128)}, u32[]{:S(2)}) copy-start(s32[16,10]{1,0:T(8,128)} %anc_ref.5) | copy-start | bytes 1924
  8.0 7.0 %collective-permute-start.8 = (bf16[256,256]{1,0:T(8,128)(2,1)}, bf16[256,256]{1,0:T(8,128)(2,1)S(1)}, u32[]{:S(2)}, u32[]{:S(2)}) collective-permute-start(bf16[256,256]{1,0:T(8,128)(2,1)} %get-tuple-element.23), channel_id=1, source_target_pairs={{0,2},{2,0},{1,3},{3,1},{4,6},{6,4},{5,7},{7,5},{8,10},{10,8},{9,1... | collective-permute-start | bytes 393224 | tf_op jit(solution)/shard_map/ppermute | solution.py:515
  9.4 1.0 copy-start.2
  10.3 1.0 copy-start.4
  13.5 23.5 %collective-permute-start.2 = (bf16[256,1024]{1,0:T(8,128)(2,1)}, bf16[256,1024]{1,0:T(8,128)(2,1)S(1)}, u32[]{:S(2)}, u32[]{:S(2)}) collective-permute-start(bf16[256,1024]{1,0:T(8,128)(2,1)} %get-tuple-element.20), channel_id=1, source_target_pairs={{0,2},{2,0},{1,3},{3,1},{4,6},{6,4},{5,7},{7,5},{8,10},{10,8},{9,1... | collective-permute-start | bytes 1572872 | tf_op jit(solution)/shard_map/ppermute | solution.py:515
  13.8 29.2 %collective-permute-start.3 = (bf16[256,1024]{1,0:T(8,128)(2,1)}, bf16[256,1024]{1,0:T(8,128)(2,1)S(1)}, u32[]{:S(2)}, u32[]{:S(2)}) collective-permute-start(bf16[256,1024]{1,0:T(8,128)(2,1)} %get-tuple-element.21), channel_id=1, source_target_pairs={{0,2},{2,0},{1,3},{3,1},{4,6},{6,4},{5,7},{7,5},{8,10},{10,8},{9,1... | collective-permute-start | bytes 1572872 | tf_op jit(solution)/shard_map/ppermute | solution.py:515
  15.1 10.1 %collective-permute-start.11 = (bf16[512,128]{1,0:T(8,128)(2,1)S(1)}, bf16[512,128]{1,0:T(8,128)(2,1)S(1)}, u32[]{:S(2)}, u32[]{:S(2)}) collective-permute-start(bf16[512,128]{1,0:T(8,128)(2,1)S(1)} %pad_maximum_fusion.rest_0_), channel_id=1, source_target_pairs={{0,12},{1,13},{2,14},{3,15},{16,28},{17,29},{18,30},{19,31}} | collective-permute-start | bytes 393224 | tf_op jit(solution)/shard_map/ppermute | solution.py:518
  20.4 5.2 %collective-permute-start.10 = (bf16[512,128]{1,0:T(8,128)(2,1)S(1)}, bf16[512,128]{1,0:T(8,128)(2,1)S(1)}, u32[]{:S(2)}, u32[]{:S(2)}) collective-permute-start(bf16[512,128]{1,0:T(8,128)(2,1)S(1)} %pad_maximum_fusion.rest_0_), channel_id=1, source_target_pairs={{0,8},{4,12},{1,9},{5,13},{2,10},{6,14},{3,11},{7,15},{16,24},{20,... | collective-permute-start | bytes 393224 | tf_op jit(solution)/shard_map/ppermute | solution.py:518
  21.7 2.2 %copy-start.9 = (f32[32,128]{1,0:T(8,128)}, f32[32,128]{1,0:T(8,128)S(1)}, u32[]{:S(2)}) copy-start(f32[32,128]{1,0:T(8,128)S(1)} %collective-permute-done.4.d_peer) | copy-start | bytes 49156
  21.7 13.4 %collective-permute-start.9 = (bf16[512,128]{1,0:T(8,128)(2,1)S(1)}, bf16[512,128]{1,0:T(8,128)(2,1)S(1)}, u32[]{:S(2)}, u32[]{:S(2)}) collective-permute-start(bf16[512,128]{1,0:T(8,128)(2,1)S(1)} %pad_maximum_fusion.rest_0_), channel_id=1, source_target_pairs={{0,4},{4,8},{8,12},{1,5},{5,9},{9,13},{2,6},{6,10},{10,14},{3,7},{... | collective-permute-start | bytes 393224 | tf_op jit(solution)/shard_map/ppermute | solution.py:518
  25.2 17.8 %copy-start.8 = (f32[32,128]{1,0:T(8,128)S(1)}, f32[32,128]{1,0:T(8,128)}, u32[]{:S(2)}) copy-start(f32[32,128]{1,0:T(8,128)} %row_deltas.1.d_own) | copy-start | bytes 49156
  25.2 17.8 %copy-start.10 = (f32[32,128]{1,0:T(8,128)S(1)}, f32[32,128]{1,0:T(8,128)}, u32[]{:S(2)}) copy-start(f32[32,128]{1,0:T(8,128)} %copy-done.9) | copy-start | bytes 49156
  25.2 17.8 %copy-start = (bf16[128,4096]{1,0:T(8,128)(2,1)S(1)}, bf16[128,4096]{1,0:T(8,128)(2,1)}, u32[]{:S(2)}) copy-start(bf16[128,4096]{1,0:T(8,128)(2,1)} %g_own.5) | copy-start | bytes 3145732
  25.2 17.7 %collective-permute-start.5 = (f32[16,128]{1,0:T(8,128)}, f32[16,128]{1,0:T(8,128)S(1)}, u32[]{:S(2)}, u32[]{:S(2)}) collective-permute-start(f32[16,128]{1,0:T(8,128)} %pack_deltas.1), channel_id=1, source_target_pairs={{0,2},{2,0},{1,3},{3,1},{4,6},{6,4},{5,7},{7,5},{8,10},{10,8},{9,1... | collective-permute-start | bytes 24584 | tf_op jit(solution)/shard_map/ppermute | solution.py:515
  25.5 17.4 %collective-permute-start.14 = (bf16[512,128]{1,0:T(8,128)(2,1)S(1)}, bf16[512,128]{1,0:T(8,128)(2,1)S(1)}, u32[]{:S(2)}, u32[]{:S(2)}) collective-permute-start(bf16[512,128]{1,0:T(8,128)(2,1)S(1)} %pad_maximum_fusion.1.rest_2_), channel_id=1, source_target_pairs={{0,12},{1,13},{2,14},{3,15},{16,28},{17,29},{18,30},{19,31}} | collective-permute-start | bytes 393224 | tf_op jit(solution)/shard_map/ppermute | solution.py:518
  35.1 7.9 %collective-permute-start.13 = (bf16[512,128]{1,0:T(8,128)(2,1)S(1)}, bf16[512,128]{1,0:T(8,128)(2,1)S(1)}, u32[]{:S(2)}, u32[]{:S(2)}) collective-permute-start(bf16[512,128]{1,0:T(8,128)(2,1)S(1)} %pad_maximum_fusion.1.rest_2_), channel_id=1, source_target_pairs={{0,8},{4,12},{1,9},{5,13},{2,10},{6,14},{3,11},{7,15},{16,24},{20,... | collective-permute-start | bytes 393224 | tf_op jit(solution)/shard_map/ppermute | solution.py:518
  37.0 7.3 %collective-permute-start.12 = (bf16[512,128]{1,0:T(8,128)(2,1)S(1)}, bf16[512,128]{1,0:T(8,128)(2,1)S(1)}, u32[]{:S(2)}, u32[]{:S(2)}) collective-permute-start(bf16[512,128]{1,0:T(8,128)(2,1)S(1)} %pad_maximum_fusion.1.rest_2_), channel_id=1, source_target_pairs={{0,4},{4,8},{8,12},{1,5},{5,9},{9,13},{2,6},{6,10},{10,14},{3,7},{... | collective-permute-start | bytes 393224 | tf_op jit(solution)/shard_map/ppermute | solution.py:518
  38.6 1.2 %copy-start.3 = (bf16[128,4096]{1,0:T(8,128)(2,1)S(1)}, bf16[128,4096]{1,0:T(8,128)(2,1)}, u32[]{:S(2)}) copy-start(bf16[128,4096]{1,0:T(8,128)(2,1)} %copy-done.2) | copy-start | bytes 3145732
  39.8 3.2 %copy-start.5 = (bf16[128,4096]{1,0:T(8,128)(2,1)S(1)}, bf16[128,4096]{1,0:T(8,128)(2,1)}, u32[]{:S(2)}) copy-start(bf16[128,4096]{1,0:T(8,128)(2,1)} %copy-done.4) | copy-start | bytes 3145732
  51.1 0.8 copy-start.6
  51.9 0.7 copy-start.7
  52.6 12.3 %collective-permute-start.15 = (bf16[256,1024]{1,0:T(8,128)(2,1)S(1)}, bf16[256,1024]{1,0:T(8,128)(2,1)S(1)}, u32[]{:S(2)}, u32[]{:S(2)}) collective-permute-start(bf16[256,1024]{1,0:T(8,128)(2,1)S(1)} %get-tuple-element.26), channel_id=1, source_target_pairs={{0,2},{2,0},{1,3},{3,1},{4,6},{6,4},{5,7},{7,5},{8,10},{10,8},{9,1... | collective-permute-start | bytes 1572872 | tf_op jit(solution)/shard_map/ppermute | solution.py:515
  52.8 15.8 %collective-permute-start.20 = (bf16[512,256]{1,0:T(8,128)(2,1)S(1)}, bf16[512,256]{1,0:T(8,128)(2,1)S(1)}, u32[]{:S(2)}, u32[]{:S(2)}) collective-permute-start(bf16[512,256]{1,0:T(8,128)(2,1)S(1)} %get-tuple-element.31), channel_id=1, source_target_pairs={{4,0},{8,4},{12,8},{5,1},{9,5},{13,9},{6,2},{10,6},{14,10},{7,3},{... | collective-permute-start | bytes 786440 | tf_op jit(solution)/shard_map/ppermute | solution.py:521
  54.1 31.0 %collective-permute-start.18 = (bf16[512,256]{1,0:T(8,128)(2,1)S(1)}, bf16[512,256]{1,0:T(8,128)(2,1)S(1)}, u32[]{:S(2)}, u32[]{:S(2)}) collective-permute-start(bf16[512,256]{1,0:T(8,128)(2,1)S(1)} %get-tuple-element.29), channel_id=1, source_target_pairs={{8,0},{12,4},{9,1},{13,5},{10,2},{14,6},{11,3},{15,7},{24,16},{28,... | collective-permute-start | bytes 786440 | tf_op jit(solution)/shard_map/ppermute | solution.py:521
  55.4 40.3 %collective-permute-start.19 = (bf16[512,256]{1,0:T(8,128)(2,1)S(1)}, bf16[512,256]{1,0:T(8,128)(2,1)S(1)}, u32[]{:S(2)}, u32[]{:S(2)}) collective-permute-start(bf16[512,256]{1,0:T(8,128)(2,1)S(1)} %get-tuple-element.30), channel_id=1, source_target_pairs={{12,0},{13,1},{14,2},{15,3},{28,16},{29,17},{30,18},{31,19}} | collective-permute-start | bytes 786440 | tf_op jit(solution)/shard_map/ppermute | solution.py:521
  56.7 52.1 %collective-permute-start.16 = (bf16[128,1024]{1,0:T(8,128)(2,1)S(1)}, bf16[128,1024]{1,0:T(8,128)(2,1)S(1)}, u32[]{:S(2)}, u32[]{:S(2)}) collective-permute-start(bf16[128,1024]{1,0:T(8,128)(2,1)S(1)} %get-tuple-element.27), channel_id=1, source_target_pairs={{0,1},{1,0},{2,3},{3,2},{4,5},{5,4},{6,7},{7,6},{8,9},{9,8},{10,11... | collective-permute-start | bytes 786440 | tf_op jit(solution)/shard_map/ppermute | solution.py:512
  64.9 30.9 %copy-start.12 = (bf16[256,1024]{1,0:T(8,128)(2,1)}, bf16[256,1024]{1,0:T(8,128)(2,1)S(1)}, u32[]{:S(2)}) copy-start(bf16[256,1024]{1,0:T(8,128)(2,1)S(1)} %collective-permute-done.15.side.refs_4_) | copy-start | bytes 1572868
  64.9 43.9 %collective-permute-start.17 = (bf16[128,1024]{1,0:T(8,128)(2,1)S(1)}, bf16[128,1024]{1,0:T(8,128)(2,1)S(1)}, u32[]{:S(2)}, u32[]{:S(2)}) collective-permute-start(bf16[128,1024]{1,0:T(8,128)(2,1)S(1)} %slice.26), channel_id=1, source_target_pairs={{0,1},{1,0},{2,3},{3,2},{4,5},{5,4},{6,7},{7,6},{8,9},{9,8},{10,11... | collective-permute-start | bytes 786440 | tf_op jit(solution)/shard_map/ppermute | solution.py:512
  68.6 27.2 %copy-start.18 = (bf16[512,256]{1,0:T(8,128)(2,1)}, bf16[512,256]{1,0:T(8,128)(2,1)S(1)}, u32[]{:S(2)}) copy-start(bf16[512,256]{1,0:T(8,128)(2,1)S(1)} %collective-permute-done.20.refs_3_) | copy-start | bytes 786436
  85.1 10.6 %copy-start.19 = (bf16[512,256]{1,0:T(8,128)(2,1)}, bf16[512,256]{1,0:T(8,128)(2,1)S(1)}, u32[]{:S(2)}) copy-start(bf16[512,256]{1,0:T(8,128)(2,1)S(1)} %collective-permute-done.18.refs_1_) | copy-start | bytes 786436
  95.8 0.7 copy-start.20
  98.5 4.0 %collective-permute-start.21 = (bf16[256,256]{1,0:T(8,128)(2,1)}, bf16[256,256]{1,0:T(8,128)(2,1)S(1)}, u32[]{:S(2)}, u32[]{:S(2)}) collective-permute-start(bf16[256,256]{1,0:T(8,128)(2,1)} %get-tuple-element.33), channel_id=1, source_target_pairs={{0,2},{2,0},{1,3},{3,1},{4,6},{6,4},{5,7},{7,5},{8,10},{10,8},{9,1... | collective-permute-start | bytes 393224 | tf_op jit(solution)/shard_map/ppermute | solution.py:515
  99.7 5.8 %collective-permute-start.22 = (bf16[128,256]{1,0:T(8,128)(2,1)}, bf16[128,256]{1,0:T(8,128)(2,1)S(1)}, u32[]{:S(2)}, u32[]{:S(2)}) collective-permute-start(bf16[128,256]{1,0:T(8,128)(2,1)} %get-tuple-element.34), channel_id=1, source_target_pairs={{0,1},{1,0},{2,3},{3,2},{4,5},{5,4},{6,7},{7,6},{8,9},{9,8},{10,11... | collective-permute-start | bytes 196616 | tf_op jit(solution)/shard_map/ppermute | solution.py:512
  102.5 3.9 %copy-start.15 = (bf16[256,256]{1,0:T(8,128)(2,1)}, bf16[256,256]{1,0:T(8,128)(2,1)S(1)}, u32[]{:S(2)}) copy-start(bf16[256,256]{1,0:T(8,128)(2,1)S(1)} %collective-permute-done.21.side) | copy-start | bytes 393220
  102.5 3.9 %collective-permute-start.23 = (bf16[128,256]{1,0:T(8,128)(2,1)S(1)}, bf16[128,256]{1,0:T(8,128)(2,1)S(1)}, u32[]{:S(2)}, u32[]{:S(2)}) collective-permute-start(bf16[128,256]{1,0:T(8,128)(2,1)S(1)} %slice.27), channel_id=1, source_target_pairs={{0,1},{1,0},{2,3},{3,2},{4,5},{5,4},{6,7},{7,6},{8,9},{9,8},{10,11... | collective-permute-start | bytes 196616 | tf_op jit(solution)/shard_map/ppermute | solution.py:512
  105.5 0.9 copy-start.22
  106.4 0.6 copy-start.23
  108.8 0.7 copy-start.16
  108.8 0.8 copy-start.17

commit v4 on v3

--- a/solution.py
+++ b/solution.py
@@ -23,21 +23,24 @@
 MASKED = -1e30
 NT_DIMS = (((1,), (1,)), ((), ()))
 PARAMS = pltpu.CompilerParams(vmem_limit_bytes=28 * 1024 * 1024)
-
-
-def delta_kernel(out_ref, grad_ref, delta_ref):
+SMALL_PARAMS = pltpu.CompilerParams(vmem_limit_bytes=16 * 1024 * 1024)
+
+
+def delta_kernel(out_ref, grad_ref, after_ref, delta_ref):
     for head in range(QH):
         cols = slice(head * HD, (head + 1) * HD)
         product = out_ref[:, cols].astype(jnp.float32) * grad_ref[:, cols].astype(jnp.float32)
         delta_ref[head : head + 1, :] = jnp.sum(product.T, axis=0, keepdims=True)
 
 
-def row_deltas(outputs, out_grad):
+def row_deltas(outputs, out_grad, after):
     return pl.pallas_call(
         delta_kernel,
+        in_specs=[pl.BlockSpec(memory_space=pltpu.VMEM)] * 2 + [pl.BlockSpec(memory_space=pl.ANY)],
         out_shape=jax.ShapeDtypeStruct((QH, TILE), jnp.float32),
+        compiler_params=SMALL_PARAMS,
         name="row_deltas",
-    )(outputs, out_grad)
+    )(outputs, out_grad, after)
 
 
 def live_counts(anc_ref, me, u, depth):
@@ -142,42 +145,56 @@
     lax.fori_loop(0, QUAD, one_tile, 0)
 
 
-def grads_kernel(depth, near_part, steps, me_ref, anc_ref, q_own, q_peer, q_side, g_own, g_peer, g_side, d_own, d_peer, d_side, lse_ref, *rest):
-    kv_refs = rest[: 2 * steps]
-    rest = rest[2 * steps :]
-    if near_part:
-        dq_in, dq_own, dq_peer, dq_side = rest[:4]
-        rest = rest[4:]
+def grads_kernel(depth, stage, steps, me_ref, anc_ref, q_own, q_peer, q_side, g_own, g_peer, g_side, d_own, d_peer, d_side, lse_ref, *rest):
+    kv_refs, rest = rest[: 2 * steps], rest[2 * steps :]
+    if stage != "far":
+        dq_in, rest = rest[0], rest[1:]
+    if stage == "own":
+        dk_in, dv_in, rest = rest[0], rest[1], rest[2:]
+    tiles = {"far": (0, 1, 2, 3), "side": (2, 3), "own": (0, 1)}[stage]
+    lowest = 2 if stage == "far" else 0
+    if stage == "far":
+        dq_acc, partial_refs, rest = rest[0], rest[1 : 1 + steps], rest[1 + steps :]
+    elif stage == "side":
+        dq_side, dk_acc, dv_acc, rest = rest[0], rest[1], rest[2], rest[3:]
     else:
+        dq_own, dq_peer, partial_refs, rest = rest[0], rest[1], rest[2 : 2 + steps], rest[2 + steps :]
+    q_all, g_all, delta, k_all, v_all, rest = *rest[:5], rest[5:]
+    if stage != "side":
+        dk_acc, dv_acc, rest = rest[0], rest[1], rest[2:]
+    if stage != "far":
         dq_acc = rest[0]
-        rest = rest[1:]
-    partial_refs = rest[:steps]
-    q_all, g_all, delta, k_all, v_all, dk_acc, dv_acc = rest[steps : steps + 7]
-    if near_part:
-        dq_acc = rest[steps + 7]
-    lowest = 0 if near_part else 2
     me = me_ref[0]
-    gather_queries(q_all, q_own, q_peer, q_side)
-    gather_queries(g_all, g_own, g_peer, g_side)
-    for head in range(GROUP):
-        cols = slice(head * TILE, (head + 1) * TILE)
-        delta[0, :, cols] = d_own[head : head + 1, :]
-        delta[1, :, cols] = d_peer[head : head + 1, :]
-        delta[2, :, cols] = d_side[head : head + 1, :]
-        delta[3, :, cols] = d_side[GROUP + head : GROUP + head + 1, :]
+    for place, u in enumerate(tiles):
+        if u < 2:
+            q_all[place] = (q_own, q_peer)[u][...]
+            g_all[place] = (g_own, g_peer)[u][...]
+        else:
+            rows = slice((u - 2) * TILE, (u - 1) * TILE)
+            q_all[place] = q_side[rows, :]
+            g_all[place] = g_side[rows, :]
+        for head in range(GROUP):
+            cols = slice(head * TILE, (head + 1) * TILE)
+            d_ref, row = ((d_own, 0), (d_peer, 0), (d_side, 0), (d_side, GROUP))[u]
+            delta[place, :, cols] = d_ref[row + head : row + head + 1, :]
     for shift in range(steps):
         k_all[shift * LEVEL : (shift + 1) * LEVEL, :] = kv_refs[shift][...]
         v_all[shift * LEVEL : (shift + 1) * LEVEL, :] = kv_refs[steps + shift][...]
-    dk_acc[...] = jnp.zeros_like(dk_acc)
-    dv_acc[...] = jnp.zeros_like(dv_acc)
-
-    def one_tile(u, carry):
+    if stage == "own":
+        dk_acc[...] = dk_in[...]
+        dv_acc[...] = dv_in[...]
+    else:
+        dk_acc[...] = jnp.zeros_like(dk_acc)
+        dv_acc[...] = jnp.zeros_like(dv_acc)
+
+    def one_tile(place, carry):
+        u = tiles[0] + place
         tile, near, live = live_counts(anc_ref, me, u, depth)
-        start, stop = (0, near) if near_part else (near, live)
-        if near_part:
-            dq_acc[u] = dq_in[u]
+        start, stop = (near, live) if stage == "far" else (0, near)
+        if stage == "far":
+            dq_acc[place] = jnp.zeros((HD, ROWS), jnp.float32)
         else:
-            dq_acc[u] = jnp.zeros((HD, ROWS), jnp.float32)
+            dq_acc[place] = dq_in[place]
 
         def chunk_grads(index, is_first):
             first, second, good = chunk_slots(
@@ -190,8 +207,8 @@
             dv = jnp.zeros((PAIR, HD), jnp.float32)
             for pair in range(GROUP // 2):
                 rows = slice(pair * PAIR, (pair + 1) * PAIR)
-                query_block = two_heads(q_all, u, pair)
-                grad_block = two_heads(g_all, u, pair)
+                query_block = two_heads(q_all, place, pair)
+                grad_block = two_heads(g_all, place, pair)
                 raw = lax.dot_general(
                     key_block, query_block, NT_DIMS, preferred_element_type=jnp.float32
                 )
@@ -199,7 +216,7 @@
                     value_block, grad_block, NT_DIMS, preferred_element_type=jnp.float32
                 )
                 lse = lse_ref[u, :, rows]
-                away = delta[u, :, rows]
+                away = delta[place, :, rows]
                 lows, scores = [], []
                 for part in range(2):
                     half = slice(part * TILE, (part + 1) * TILE)
@@ -213,7 +230,7 @@
                 grad_scores = jnp.concatenate(scores, axis=0)
                 dv += jnp.dot(attn_low, grad_block, preferred_element_type=jnp.float32)
                 dk += jnp.dot(grad_scores, query_block, preferred_element_type=jnp.float32)
-                dq_acc[u, :, rows] += jnp.dot(
+                dq_acc[place, :, rows] += jnp.dot(
                     key_turned, grad_scores, preferred_element_type=jnp.float32
                 )
             dk_acc[slot_rows(first), :] += dk[:TILE]
@@ -225,28 +242,27 @@
             chunk_grads(index, False)
             return carry
 
-        if near_part:
+        if stage != "far":
             chunk_grads(0, True)
-        lax.fori_loop(1 if near_part else 0, (stop - start + 1) // 2, step, 0)
+        lax.fori_loop(0 if stage == "far" else 1, (stop - start + 1) // 2, step, 0)
         return carry
 
-    lax.fori_loop(0, QUAD, one_tile, 0)
-
-    if near_part:
-        for u in range(QUAD):
+    lax.fori_loop(0, len(tiles), one_tile, 0)
+
+    if stage != "far":
+        for place in range(2):
             for head in range(GROUP):
                 cols = slice(head * HD, (head + 1) * HD)
-                turned = (dq_acc[u, :, cols] * SCALE).T.astype(jnp.bfloat16)
-                if u == 0:
-                    dq_own[:, cols] = turned
-                elif u == 1:
-                    dq_peer[:, cols] = turned
+                turned = (dq_acc[place, :, cols] * SCALE).T.astype(jnp.bfloat16)
+                if stage == "side":
+                    dq_side[place * TILE : (place + 1) * TILE, cols] = turned
                 else:
-                    dq_side[(u - 2) * TILE : (u - 1) * TILE, cols] = turned
-    for shift, out_ref in enumerate(partial_refs):
-        rows = slice(shift * LEVEL, (shift + 1) * LEVEL)
-        out_ref[:, :HD] = dk_acc[rows, :].astype(out_ref.dtype)
-        out_ref[:, HD:] = dv_acc[rows, :].astype(out_ref.dtype)
+                    (dq_own, dq_peer)[place][:, cols] = turned
+    if stage != "side":
+        for shift, out_ref in enumerate(partial_refs):
+            rows = slice(shift * LEVEL, (shift + 1) * LEVEL)
+            out_ref[:, :HD] = dk_acc[rows, :].astype(out_ref.dtype)
+            out_ref[:, HD:] = dv_acc[rows, :].astype(out_ref.dtype)
 
 
 def work(ancestors, products):
@@ -273,6 +289,7 @@
 KEYS = fixed((LEVEL, HD))
 SUMS = fixed((LEVEL, 2 * HD))
 DQ = fixed((QUAD, HD, ROWS))
+WIDE_OUT = fixed((TILE, ROWS))
 
 
 def statistics(me, ancestors, q_set, k_list):
@@ -298,114 +315,103 @@
     )(me, ancestors, *q_set, *k_list)
 
 
-def gradients(me, ancestors, q_set, g_set, d_set, lse, k_list, v_list, dq_far=None):
+def gradients(stage, me, ancestors, q_set, g_set, d_set, lse, k_list, v_list, *carried):
     steps = len(k_list)
-    near_part = dq_far is not None
-    if near_part:
-        dq_specs = [WIDE_OUT, WIDE_OUT, SIDE]
-        dq_shapes = [
-            jax.ShapeDtypeStruct((TILE, ROWS), jnp.bfloat16),
-            jax.ShapeDtypeStruct((TILE, ROWS), jnp.bfloat16),
-            jax.ShapeDtypeStruct((PAIR, ROWS), jnp.bfloat16),
-        ]
-        kinds = [jnp.float32] + [jnp.bfloat16] * (steps - 1)
+    tiles = QUAD if stage == "far" else 2
+    acc = (steps * LEVEL, HD)
+    wide = jax.ShapeDtypeStruct((TILE, ROWS), jnp.bfloat16)
+    sums = [jax.ShapeDtypeStruct((LEVEL, 2 * HD), jnp.bfloat16)] * steps
+    accs = [jax.ShapeDtypeStruct(acc, jnp.float32)] * 2
+    dq_half = pl.BlockSpec((2, HD, ROWS), lambda i, *_: (1 if stage == "side" else 0, 0, 0))
+    extra_specs = [dq_half, fixed(acc), fixed(acc)][: len(carried)]
+    if stage == "far":
+        out_specs = [DQ] + [SUMS] * steps
+        out_shape = [jax.ShapeDtypeStruct((QUAD, HD, ROWS), jnp.float32)] + sums
+    elif stage == "side":
+        out_specs = [SIDE, fixed(acc), fixed(acc)]
+        out_shape = [jax.ShapeDtypeStruct((PAIR, ROWS), jnp.bfloat16)] + accs
     else:
-        dq_specs = [DQ]
-        dq_shapes = [jax.ShapeDtypeStruct((QUAD, HD, ROWS), jnp.float32)]
-        kinds = [jnp.bfloat16] * steps
+        sums[0] = jax.ShapeDtypeStruct((LEVEL, 2 * HD), jnp.float32)
+        out_specs = [WIDE_OUT, WIDE_OUT] + [SUMS] * steps
+        out_shape = [wide, wide] + sums
     scratch = [
-        pltpu.VMEM((QUAD, TILE, ROWS), jnp.bfloat16),
-        pltpu.VMEM((QUAD, TILE, ROWS), jnp.bfloat16),
-        pltpu.VMEM((QUAD, 1, ROWS), jnp.float32),
-        pltpu.VMEM((steps * LEVEL, HD), jnp.bfloat16),
-        pltpu.VMEM((steps * LEVEL, HD), jnp.bfloat16),
-        pltpu.VMEM((steps * LEVEL, HD), jnp.float32),
-        pltpu.VMEM((steps * LEVEL, HD), jnp.float32),
+        pltpu.VMEM((tiles, TILE, ROWS), jnp.bfloat16),
+        pltpu.VMEM((tiles, TILE, ROWS), jnp.bfloat16),
+        pltpu.VMEM((tiles, 1, ROWS), jnp.float32),
+        pltpu.VMEM(acc, jnp.bfloat16),
+        pltpu.VMEM(acc, jnp.bfloat16),
     ]
-    if near_part:
-        scratch.append(pltpu.VMEM((QUAD, HD, ROWS), jnp.float32))
-    return pl.pallas_call(
-        functools.partial(grads_kernel, ancestors.shape[1], near_part, steps),
+    if stage != "side":
+        scratch += [pltpu.VMEM(acc, jnp.float32)] * 2
+    if stage != "far":
+        scratch.append(pltpu.VMEM((tiles, HD, ROWS), jnp.float32))
+    return pl.pallas_call(
+        functools.partial(grads_kernel, ancestors.shape[1], stage, steps),
         grid_spec=pltpu.PrefetchScalarGridSpec(
             num_scalar_prefetch=2,
             grid=(1,),
             in_specs=[WIDE, WIDE, SIDE, WIDE, WIDE, SIDE, SMALL, SMALL, fixed((2 * GROUP, TILE)), LSE]
             + [KEYS] * (2 * steps)
-            + ([DQ] if near_part else []),
-            out_specs=dq_specs + [SUMS] * steps,
+            + extra_specs,
+            out_specs=out_specs,
             scratch_shapes=scratch,
         ),
-        out_shape=dq_shapes + [jax.ShapeDtypeStruct((LEVEL, 2 * HD), kind) for kind in kinds],
+        out_shape=out_shape,
         compiler_params=PARAMS,
         cost_estimate=work(ancestors, 5),
-        name="near_grads" if near_part else "far_grads",
-    )(
-        me,
-        ancestors,
-        *q_set,
-        *g_set,
-        *d_set,
-        lse,
-        *k_list,
-        *v_list,
-        *([dq_far] if near_part else []),
-    )
-
-
-WIDE_OUT = fixed((TILE, ROWS))
-
-
-def pack_keys_kernel(me_ref, k_own, v_own, k_peer, v_peer, k_away, v_away, k_far, v_far, mine_ref, send_ref):
-    mine_ref[:TILE, :HD] = k_own[...]
-    mine_ref[:TILE, HD:] = v_own[...]
-    mine_ref[TILE:, :HD] = k_peer[...]
-    mine_ref[TILE:, HD:] = v_peer[...]
-    send_ref[:TILE, :HD] = k_away[...]
-    send_ref[:TILE, HD:] = v_away[...]
-    send_ref[TILE:, :HD] = k_far[...]
-    send_ref[TILE:, HD:] = v_far[...]
+        name=stage + "_grads",
+    )(me, ancestors, *q_set, *g_set, *d_set, lse, *k_list, *v_list, *carried)
 
 
 def side_head(me_ref):
     return own_head(me_ref) ^ 1
 
 
-def pack_keys(me, keys, values, k_peer, v_peer):
-    mine = pl.BlockSpec((TILE, HD), lambda i, me_ref: (0, own_head(me_ref)))
-    away = pl.BlockSpec((TILE, HD), lambda i, me_ref: (0, side_head(me_ref)))
+def head_columns(head, width):
+    return pl.ds(pl.multiple_of(head * width, width), width)
+
+
+def pack_keys_kernel(me_ref, k_own, v_own, k_peer, v_peer, mine_ref, send_ref):
+    for head, out_ref in ((own_head(me_ref), mine_ref), (side_head(me_ref), send_ref)):
+        at = head_columns(head, HD)
+        out_ref[:TILE, :HD] = k_own[:, at]
+        out_ref[:TILE, HD:] = v_own[:, at]
+        out_ref[TILE:, :HD] = k_peer[:, at]
+        out_ref[TILE:, HD:] = v_peer[:, at]
+
+
+SCALARS = pl.BlockSpec(memory_space=pltpu.SMEM)
+HERE = pl.BlockSpec(memory_space=pltpu.VMEM)
+
+
+def pack_keys(me, *arrays):
     return pl.pallas_call(
         pack_keys_kernel,
-        grid_spec=pltpu.PrefetchScalarGridSpec(
-            num_scalar_prefetch=1,
-            grid=(1,),
-            in_specs=[mine] * 4 + [away] * 4,
-            out_specs=[fixed((PAIR, 2 * HD))] * 2,
-        ),
+        in_specs=[SCALARS] + [HERE] * 4,
+        out_specs=[HERE] * 2,
         out_shape=[jax.ShapeDtypeStruct((PAIR, 2 * HD), jnp.bfloat16)] * 2,
+        compiler_params=SMALL_PARAMS,
         name="pack_keys",
-    )(me, keys, values, k_peer, v_peer, keys, values, k_peer, v_peer)
+    )(me, *arrays)
 
 
 def pack_queries_kernel(me_ref, q_own, q_peer, g_own, g_peer, q_ref, g_ref):
-    q_ref[:TILE, :] = q_own[...]
-    q_ref[TILE:, :] = q_peer[...]
-    g_ref[:TILE, :] = g_own[...]
-    g_ref[TILE:, :] = g_peer[...]
-
-
-def pack_queries(me, queries, q_peer, out_grad, g_peer):
-    away = pl.BlockSpec((TILE, ROWS), lambda i, me_ref: (0, side_head(me_ref)))
+    at = head_columns(side_head(me_ref), ROWS)
+    q_ref[:TILE, :] = q_own[:, at]
+    q_ref[TILE:, :] = q_peer[:, at]
+    g_ref[:TILE, :] = g_own[:, at]
+    g_ref[TILE:, :] = g_peer[:, at]
+
+
+def pack_queries(me, *arrays):
     return pl.pallas_call(
         pack_queries_kernel,
-        grid_spec=pltpu.PrefetchScalarGridSpec(
-            num_scalar_prefetch=1,
-            grid=(1,),
-            in_specs=[away] * 4,
-            out_specs=[SIDE] * 2,
-        ),
+        in_specs=[SCALARS] + [HERE] * 4,
+        out_specs=[HERE] * 2,
         out_shape=[jax.ShapeDtypeStruct((PAIR, ROWS), jnp.bfloat16)] * 2,
+        compiler_params=SMALL_PARAMS,
         name="pack_queries",
-    )(me, queries, q_peer, out_grad, g_peer)
+    )(me, *arrays)
 
 
 def pack_deltas_kernel(me_ref, d_own, d_peer, send_ref):
@@ -424,40 +430,63 @@
             out_specs=fixed((2 * GROUP, TILE)),
         ),
         out_shape=jax.ShapeDtypeStruct((2 * GROUP, TILE), jnp.float32),
+        compiler_params=SMALL_PARAMS,
         name="pack_deltas",
     )(me, deltas, d_peer)
 
 
-def add_sums_kernel(count, *refs):
-    total_ref, parts = refs[0], refs[1 : 1 + count]
-    own_ref, peer_ref, send_ref = refs[-3:]
+def add_far_kernel(total_ref, *refs):
+    parts, out_ref = refs[:-3], refs[-2]
     total = total_ref[...]
     for part in parts:
         total += part[...].astype(jnp.float32)
+    out_ref[...] = total
+
+
+def add_far(acc, parts, passing):
+    here = pl.BlockSpec(memory_space=pltpu.VMEM)
+    anywhere = pl.BlockSpec(memory_space=pl.ANY)
+    return pl.pallas_call(
+        add_far_kernel,
+        in_specs=[here] * (1 + len(parts)) + [anywhere],
+        out_specs=[here, anywhere],
+        out_shape=[
+            jax.ShapeDtypeStruct(acc.shape, jnp.float32),
+            jax.ShapeDtypeStruct(passing.shape, passing.dtype),
+        ],
+        input_output_aliases={1 + len(parts): 1},
+        compiler_params=SMALL_PARAMS,
+        name="add_far",
+    )(acc, *parts, passing)
+
+
+def add_sums_kernel(total_ref, near_ref, own_ref, peer_ref, send_ref):
+    total = total_ref[...] + near_ref[...].astype(jnp.float32)
     scaled = jnp.concatenate([total[:, :HD] * SCALE, total[:, HD:]], axis=1).astype(jnp.bfloat16)
     own_ref[...] = scaled[:TILE]
     peer_ref[...] = scaled[TILE:PAIR]
     send_ref[...] = scaled[PAIR:]
 
 
-def add_sums(total, parts, first_needed):
+def add_sums(total, near):
     here = pl.BlockSpec(memory_space=pltpu.VMEM)
     return pl.pallas_call(
-        functools.partial(add_sums_kernel, len(parts)),
-        in_specs=[here] * (1 + len(parts)) + [pl.BlockSpec(memory_space=pl.ANY)],
+        add_sums_kernel,
+        in_specs=[here] * 2,
         out_specs=[here] * 3,
         out_shape=[
             jax.ShapeDtypeStruct((TILE, 2 * HD), jnp.bfloat16),
             jax.ShapeDtypeStruct((TILE, 2 * HD), jnp.bfloat16),
             jax.ShapeDtypeStruct((PAIR, 2 * HD), jnp.bfloat16),
         ],
+        compiler_params=SMALL_PARAMS,
         name="add_sums",
-    )(total, *parts, first_needed)
+    )(total, near)
 
 
 def placed(me_ref, width):
     head = own_head(me_ref)
-    return [pl.ds(pl.multiple_of((head ^ flip) * width, width), width) for flip in range(4)]
+    return [head_columns(head ^ flip, width) for flip in range(4)]
 
 
 def place_queries_kernel(me_ref, own, side, peer, far, dq_ref):
@@ -468,18 +497,15 @@
     dq_ref[:, at[3]] = far[...]
 
 
-def place_queries(me, own, side, peer, far):
+def place_queries(me, *pieces):
     return pl.pallas_call(
         place_queries_kernel,
-        grid_spec=pltpu.PrefetchScalarGridSpec(
-            num_scalar_prefetch=1,
-            grid=(1,),
-            in_specs=[WIDE_OUT, SIDE, WIDE_OUT, WIDE_OUT],
-            out_specs=fixed((TILE, QH * HD)),
-        ),
+        in_specs=[SCALARS] + [HERE] * 4,
+        out_specs=HERE,
         out_shape=jax.ShapeDtypeStruct((TILE, QH * HD), jnp.bfloat16),
+        compiler_params=SMALL_PARAMS,
         name="place_queries",
-    )(me, own, side, peer, far)
+    )(me, *pieces)
 
 
 def place_keys_kernel(me_ref, own, side, peer, far, dk_ref, dv_ref):
@@ -489,19 +515,15 @@
         dv_ref[:, spot] = part[:, HD:]
 
 
-def place_keys(me, own, side, peer, far):
-    piece = fixed((TILE, 2 * HD))
+def place_keys(me, *pieces):
     return pl.pallas_call(
         place_keys_kernel,
-        grid_spec=pltpu.PrefetchScalarGridSpec(
-            num_scalar_prefetch=1,
-            grid=(1,),
-            in_specs=[piece, fixed((PAIR, 2 * HD)), piece, piece],
-            out_specs=[fixed((TILE, KVH * HD))] * 2,
-        ),
+        in_specs=[SCALARS] + [HERE] * 4,
+        out_specs=[HERE] * 2,
         out_shape=[jax.ShapeDtypeStruct((TILE, KVH * HD), jnp.bfloat16)] * 2,
+        compiler_params=SMALL_PARAMS,
         name="place_keys",
-    )(me, own, side, peer, far)
+    )(me, *pieces)
 
 
 def per_device(steps, queries, keys, values, outputs, out_grad, ancestors):
@@ -530,21 +552,24 @@
     q_set = (queries, q_peer, to_side(q_send))
     v_list = [v_level] + [up(v_level, shift) for shift in range(1, steps)]
     g_set = (out_grad, g_peer, to_side(g_send))
-    deltas = row_deltas(outputs, out_grad)
+    deltas = row_deltas(outputs, out_grad, kv_send)
     d_peer = to_peer(deltas)
     d_set = (deltas, d_peer, to_side(pack_deltas(me, deltas, d_peer)))
 
     lse = statistics(me, ancestors, q_set, k_list)
-    dq_far, *far = gradients(me, ancestors, q_set, g_set, d_set, lse, k_list[2:], v_list[2:])
+    common = (me, ancestors, q_set, g_set, d_set, lse)
+    dq_far, *far = gradients("far", *common, k_list[2:], v_list[2:])
     back = [down(far[shift - 2], shift) for shift in range(2, steps)]
-    dq_own, dq_peer, dq_side, total, near = gradients(
-        me, ancestors, q_set, g_set, d_set, lse, k_list[:2], v_list[:2], dq_far
+    dq_side, *accs = gradients("side", *common, k_list[:2], v_list[:2], dq_far)
+    dq_side = to_side(dq_side)
+    dq_own, dq_peer, total, near = gradients(
+        "own", *common, k_list[:2], v_list[:2], dq_far, *accs
     )
-    dq_side = to_side(dq_side)
-    back.append(down(near, 1))
+    total, near = add_far(total, back, near)
+    near = down(near, 1)
     dq_peer = to_peer(dq_peer)
 
-    sum_own, sum_peer, sum_side = add_sums(total, back, dq_side)
+    sum_own, sum_peer, sum_side = add_sums(total, near)
     dq_far = to_peer(dq_side[TILE:])
     sum_peer = to_peer(sum_peer)
     sum_side = to_side(sum_side)

time: 113 us -> 95.4 us (0.84)
  the two profiles are of different devices: /device:TPU:3 before, /device:TPU:0 now
where the time goes in v4:
time: 95.4 us; the launch traced here: 94.9 us
  waiting for transfers between devices  39.8 us (42%)
  starting transfers between devices  33.9 us (36%)
  Pallas kernels  14.6 us (15%)
  local copies, waits for them, and re-layouts  5.65 us (6%)
    ppermute x3, waiting for transfers between devices, down(): lax.ppermute(x, 'level', [(z + shift, z) for z in range(steps - shift)])  29.6 us
    ppermute x6, starting transfers between devices, up(): lax.ppermute(x, 'level', [(z, z + shift) for z in range(steps - shift)])  21.3 us
    pallas_call x3, Pallas kernels, gradients(): pl.pallas_call(functools.partial(grads_kernel, ancestors.shape[1], stage,...  8.9 us
    ppermute x6, starting transfers between devices, to_side(): return lax.ppermute(x, 'side', [(0, 1), (1, 0)])  6.88 us
    unnamed x16, local copies, waits for them, and re-layouts  5.6 us
    ppermute x9, waiting for transfers between devices, to_peer(): return lax.ppermute(x, 'core', [(0, 1), (1, 0)])  5.03 us
    ppermute x3, starting transfers between devices, down(): lax.ppermute(x, 'level', [(z + shift, z) for z in range(steps - shift)])  3.88 us
    ppermute x6, waiting for transfers between devices, to_side(): return lax.ppermute(x, 'side', [(0, 1), (1, 0)])  3.62 us
  transfers between devices with their start and end apart: 24, of which 8 were waited for; matrix products, arithmetic and copies ran while one was open for 0% of the time, Pallas kernels for 14%

profile of v4, /device:TPU:0, one launch (start us, length us, event | category | flops | bytes accessed | tf_op | source)
XLA Modules:
  0.0 94.9 jit_solution(5536368595771617296)
XLA Ops:
  0.6 0.5 collective-permute-start
  1.1 0.1 collective-permute-start.1
  1.2 0.4 collective-permute-start.4
  1.7 0.1 collective-permute-start.5
  1.7 3.6 %collective-permute-done.4.k_peer = bf16[128,512]{1,0:T(8,128)(2,1)S(1)} collective-permute-done((bf16[128,512]{1,0:T(8,128)(2,1)}, bf16[128,512]{1,0:T(8,128)(2,1)S(1)}, u32[]{:S(2)}, u32[]{:S(2)}) %collective-permute-start.4) | collective-permute-done | bytes 131104 | tf_op jit(solution)/shard_map/ppermute | solution.py:534
  5.3 0.2 collective-permute-done.5.v_peer
  5.5 0.9 copy-done.5
  6.4 0.9 copy-done.6
  7.4 3.0 %collective-permute-start.8 = (bf16[256,256]{1,0:T(8,128)(2,1)S(1)}, bf16[256,256]{1,0:T(8,128)(2,1)S(1)}, u32[]{:S(2)}, u32[]{:S(2)}) collective-permute-start(bf16[256,256]{1,0:T(8,128)(2,1)S(1)} %get-tuple-element.26.after_ref), channel_id=1, source_target_pairs={{0,2},{2,0},{1,3},{3,1},{4,6},{6,4},{5,7},{7,5},{8,10},{10,8},{9,1... | collective-permute-start | bytes 393224 | tf_op jit(solution)/shard_map/ppermute | solution.py:537
  10.3 0.0 collective-permute-done.q_peer
  10.3 0.0 collective-permute-done.1.g_peer
  10.3 1.2 %copy-done = bf16[128,4096]{1,0:T(8,128)(2,1)S(1)} copy-done((bf16[128,4096]{1,0:T(8,128)(2,1)S(1)}, bf16[128,4096]{1,0:T(8,128)(2,1)}, u32[]{:S(2)}) %copy-start) | copy-done | bytes 1048600
  11.6 1.2 %copy-done.2 = bf16[128,4096]{1,0:T(8,128)(2,1)S(1)} copy-done((bf16[128,4096]{1,0:T(8,128)(2,1)S(1)}, bf16[128,4096]{1,0:T(8,128)(2,1)}, u32[]{:S(2)}) %copy-start.2) | copy-done | bytes 1048600
  12.8 0.1 pack_queries.1
  12.9 0.0 copy-start.3
  12.9 0.0 copy-start.7
  12.9 0.1 collective-permute-start.2
  13.0 1.0 %copy-done.1 = bf16[128,4096]{1,0:T(8,128)(2,1)S(1)} copy-done((bf16[128,4096]{1,0:T(8,128)(2,1)S(1)}, bf16[128,4096]{1,0:T(8,128)(2,1)}, u32[]{:S(2)}) %copy-start.1) | copy-done | bytes 1048600
  14.0 0.3 copy-done.4
  14.3 0.6 row_deltas.1.d_own
  14.9 0.1 collective-permute-start.6
  15.0 0.8 collective-permute-start.3
  15.8 0.0 collective-permute-done.8
  15.8 5.5 %collective-permute-start.11 = (bf16[512,128]{1,0:T(8,128)(2,1)S(1)}, bf16[512,128]{1,0:T(8,128)(2,1)S(1)}, u32[]{:S(2)}, u32[]{:S(2)}) collective-permute-start(bf16[512,128]{1,0:T(8,128)(2,1)S(1)} %pad_maximum_fusion.rest_0_), channel_id=1, source_target_pairs={{0,12},{1,13},{2,14},{3,15},{16,28},{17,29},{18,30},{19,31}} | collective-permute-start | bytes 393224 | tf_op jit(solution)/shard_map/ppermute | solution.py:540
  21.3 1.3 %collective-permute-start.10 = (bf16[512,128]{1,0:T(8,128)(2,1)S(1)}, bf16[512,128]{1,0:T(8,128)(2,1)S(1)}, u32[]{:S(2)}, u32[]{:S(2)}) collective-permute-start(bf16[512,128]{1,0:T(8,128)(2,1)S(1)} %pad_maximum_fusion.rest_0_), channel_id=1, source_target_pairs={{0,8},{4,12},{1,9},{5,13},{2,10},{6,14},{3,11},{7,15},{16,24},{20,... | collective-permute-start | bytes 393224 | tf_op jit(solution)/shard_map/ppermute | solution.py:540
  22.6 0.0 collective-permute-done.6.d_peer
  22.6 2.5 %collective-permute-start.9 = (bf16[512,128]{1,0:T(8,128)(2,1)S(1)}, bf16[512,128]{1,0:T(8,128)(2,1)S(1)}, u32[]{:S(2)}, u32[]{:S(2)}) collective-permute-start(bf16[512,128]{1,0:T(8,128)(2,1)S(1)} %pad_maximum_fusion.rest_0_), channel_id=1, source_target_pairs={{0,4},{4,8},{8,12},{1,5},{5,9},{9,13},{2,6},{6,10},{10,14},{3,7},{... | collective-permute-start | bytes 393224 | tf_op jit(solution)/shard_map/ppermute | solution.py:540
  25.2 0.0 collective-permute-done.11.rest_3_.rest_1_
  25.2 1.4 %collective-permute-start.7 = (f32[16,128]{1,0:T(8,128)S(1)}, f32[16,128]{1,0:T(8,128)S(1)}, u32[]{:S(2)}, u32[]{:S(2)}) collective-permute-start(f32[16,128]{1,0:T(8,128)S(1)} %pack_deltas.1), channel_id=1, source_target_pairs={{0,2},{2,0},{1,3},{3,1},{4,6},{6,4},{5,7},{7,5},{8,10},{10,8},{9,1... | collective-permute-start | bytes 24584 | tf_op jit(solution)/shard_map/ppermute | solution.py:537
  26.6 1.4 %collective-permute-done.10.rest_2_.rest_0_ = bf16[512,128]{1,0:T(8,128)(2,1)S(1)} collective-permute-done((bf16[512,128]{1,0:T(8,128)(2,1)S(1)}, bf16[512,128]{1,0:T(8,128)(2,1)S(1)}, u32[]{:S(2)}, u32[]{:S(2)}) %collective-permute-start.10) | collective-permute-done | bytes 131104 | tf_op jit(solution)/shard_map/ppermute | solution.py:540
  28.0 8.2 %collective-permute-start.14 = (bf16[512,128]{1,0:T(8,128)(2,1)S(1)}, bf16[512,128]{1,0:T(8,128)(2,1)S(1)}, u32[]{:S(2)}, u32[]{:S(2)}) collective-permute-start(bf16[512,128]{1,0:T(8,128)(2,1)S(1)} %pad_maximum_fusion.1.rest_2_), channel_id=1, source_target_pairs={{0,12},{1,13},{2,14},{3,15},{16,28},{17,29},{18,30},{19,31}} | collective-permute-start | bytes 393224 | tf_op jit(solution)/shard_map/ppermute | solution.py:540
  36.3 0.0 collective-permute-done.9.rest_1_
  36.3 1.8 %collective-permute-start.13 = (bf16[512,128]{1,0:T(8,128)(2,1)S(1)}, bf16[512,128]{1,0:T(8,128)(2,1)S(1)}, u32[]{:S(2)}, u32[]{:S(2)}) collective-permute-start(bf16[512,128]{1,0:T(8,128)(2,1)S(1)} %pad_maximum_fusion.1.rest_2_), channel_id=1, source_target_pairs={{0,8},{4,12},{1,9},{5,13},{2,10},{6,14},{3,11},{7,15},{16,24},{20,... | collective-permute-start | bytes 393224 | tf_op jit(solution)/shard_map/ppermute | solution.py:540
  38.1 0.0 collective-permute-done.2.q_side
  38.1 1.9 %collective-permute-start.12 = (bf16[512,128]{1,0:T(8,128)(2,1)S(1)}, bf16[512,128]{1,0:T(8,128)(2,1)S(1)}, u32[]{:S(2)}, u32[]{:S(2)}) collective-permute-start(bf16[512,128]{1,0:T(8,128)(2,1)S(1)} %pad_maximum_fusion.1.rest_2_), channel_id=1, source_target_pairs={{0,4},{4,8},{8,12},{1,5},{5,9},{9,13},{2,6},{6,10},{10,14},{3,7},{... | collective-permute-start | bytes 393224 | tf_op jit(solution)/shard_map/ppermute | solution.py:540
  40.1 3.1 %statistics.1.lse_ref = f32[4,1,1024]{2,1,0:T(1,128)S(1)} custom-call(s32[1]{0:T(128)} %bitcast.me_ref, s32[16,10]{1,0:T(8,128)S(1)} %copy-done.7, bf16[128,4096]{1,0:T(8,128)(2,1)S(1)} %copy-done.3, bf16[128,4096]{1,0:T(8,128)(2,1)S(1)} %collective-permute-done.q_peer, bf16[256,1024]{1,0:T(8,128)(2,1)S(1)} %collective-permute-done.2.q_side, ...), custom_call_target="tpu_custom_call" | custom-call | flops 2952790016 | bytes 16777216 | tf_op jit(solution)/shard_map/statistics/pallas_call | solution.py:297
  43.2 0.0 collective-permute-done.7.d_side
  43.2 0.0 collective-permute-done.14.rest_3_
  43.2 0.0 collective-permute-done.13.rest_2_
  43.2 0.0 collective-permute-done.3.g_side
  43.2 1.2 %far_grads.1 = (f32[4,128,1024]{2,1,0:T(8,128)S(1)}, bf16[512,256]{1,0:T(8,128)(2,1)S(1)}, bf16[512,256]{1,0:T(8,128)(2,1)S(1)}) custom-call(s32[1]{0:T(128)} %bitcast.me_ref, s32[16,10]{1,0:T(8,128)S(1)} %copy-done.7, bf16[128,4096]{1,0:T(8,128)(2,1)S(1)} %copy-done.3, bf16[128,4096]{1,0:T(8,128)(2,1)S(1)} %collective-permute-done.q_peer, ...), custom_call_target="tpu_custom_call" | custom-call | flops 14763950080 | bytes 16777216 | tf_op jit(solution)/shard_map/far_grads/pallas_call | solution.py:348
  44.5 1.3 %collective-permute-start.18 = (bf16[512,256]{1,0:T(8,128)(2,1)S(1)}, bf16[512,256]{1,0:T(8,128)(2,1)S(1)}, u32[]{:S(2)}, u32[]{:S(2)}) collective-permute-start(bf16[512,256]{1,0:T(8,128)(2,1)S(1)} %get-tuple-element.35), channel_id=1, source_target_pairs={{8,0},{12,4},{9,1},{13,5},{10,2},{14,6},{11,3},{15,7},{24,16},{28,... | collective-permute-start | bytes 786440 | tf_op jit(solution)/shard_map/ppermute | solution.py:543
  45.8 1.3 %collective-permute-start.19 = (bf16[512,256]{1,0:T(8,128)(2,1)S(1)}, bf16[512,256]{1,0:T(8,128)(2,1)S(1)}, u32[]{:S(2)}, u32[]{:S(2)}) collective-permute-start(bf16[512,256]{1,0:T(8,128)(2,1)S(1)} %get-tuple-element.36), channel_id=1, source_target_pairs={{12,0},{13,1},{14,2},{15,3},{28,16},{29,17},{30,18},{31,19}} | collective-permute-start | bytes 786440 | tf_op jit(solution)/shard_map/ppermute | solution.py:543
  47.1 0.0 collective-permute-done.12.rest_3_
  47.1 4.4 %side_grads.1 = (bf16[256,1024]{1,0:T(8,128)(2,1)S(1)}, f32[1024,128]{1,0:T(8,128)S(1)}, f32[1024,128]{1,0:T(8,128)S(1)}) custom-call(s32[1]{0:T(128)} %bitcast.me_ref, s32[16,10]{1,0:T(8,128)S(1)} %copy-done.7, bf16[128,4096]{1,0:T(8,128)(2,1)S(1)} %copy-done.3, bf16[128,4096]{1,0:T(8,128)(2,1)S(1)} %collective-permute-done.q_peer, ...), custom_call_target="tpu_custom_call" | custom-call | flops 14763950080 | bytes 16777216 | tf_op jit(solution)/shard_map/side_grads/pallas_call | solution.py:348
  51.5 0.3 collective-permute-start.15
  51.8 3.3 %own_grads.1 = (bf16[128,1024]{1,0:T(8,128)(2,1)S(1)}, bf16[128,1024]{1,0:T(8,128)(2,1)S(1)}, f32[512,256]{1,0:T(8,128)S(1)}, bf16[512,256]{1,0:T(8,128)(2,1)S(1)}) custom-call(s32[1]{0:T(128)} %bitcast.me_ref, s32[16,10]{1,0:T(8,128)S(1)} %copy-done.7, bf16[128,4096]{1,0:T(8,128)(2,1)S(1)} %copy-done.3, bf16[128,4096]{1,0:T(8,128)(2,1)S(1)} %collective-permute-done.q_peer, ...), custom_call_target="tpu_custom_call" | custom-call | flops 14763950080 | bytes 16777216 | tf_op jit(solution)/shard_map/own_grads/pallas_call | solution.py:348
  55.1 9.5 %collective-permute-done.18.refs_0_ = bf16[512,256]{1,0:T(8,128)(2,1)S(1)} collective-permute-done((bf16[512,256]{1,0:T(8,128)(2,1)S(1)}, bf16[512,256]{1,0:T(8,128)(2,1)S(1)}, u32[]{:S(2)}, u32[]{:S(2)}) %collective-permute-start.18) | collective-permute-done | bytes 262176 | tf_op jit(solution)/shard_map/ppermute | solution.py:543
  64.6 12.6 %collective-permute-done.19.refs_1_ = bf16[512,256]{1,0:T(8,128)(2,1)S(1)} collective-permute-done((bf16[512,256]{1,0:T(8,128)(2,1)S(1)}, bf16[512,256]{1,0:T(8,128)(2,1)S(1)}, u32[]{:S(2)}, u32[]{:S(2)}) %collective-permute-start.19) | collective-permute-done | bytes 262176 | tf_op jit(solution)/shard_map/ppermute | solution.py:543
  77.2 0.1 add_far.1
  77.3 1.3 %collective-permute-start.20 = (bf16[512,256]{1,0:T(8,128)(2,1)S(1)}, bf16[512,256]{1,0:T(8,128)(2,1)S(1)}, u32[]{:S(2)}, u32[]{:S(2)}) collective-permute-start(bf16[512,256]{1,0:T(8,128)(2,1)S(1)} %get-tuple-element.39), channel_id=1, source_target_pairs={{4,0},{8,4},{12,8},{5,1},{9,5},{13,9},{6,2},{10,6},{14,10},{7,3},{... | collective-permute-start | bytes 786440 | tf_op jit(solution)/shard_map/ppermute | solution.py:543
  78.6 0.1 collective-permute-start.16
  78.7 0.6 collective-permute-start.17
  79.3 7.5 %collective-permute-done.20.near_ref = bf16[512,256]{1,0:T(8,128)(2,1)S(1)} collective-permute-done((bf16[512,256]{1,0:T(8,128)(2,1)S(1)}, bf16[512,256]{1,0:T(8,128)(2,1)S(1)}, u32[]{:S(2)}, u32[]{:S(2)}) %collective-permute-start.20) | collective-permute-done | bytes 262176 | tf_op jit(solution)/shard_map/ppermute | solution.py:543
  86.7 0.1 add_sums.1
  86.8 1.4 %collective-permute-start.21 = (bf16[256,256]{1,0:T(8,128)(2,1)S(1)}, bf16[256,256]{1,0:T(8,128)(2,1)S(1)}, u32[]{:S(2)}, u32[]{:S(2)}) collective-permute-start(bf16[256,256]{1,0:T(8,128)(2,1)S(1)} %get-tuple-element.41), channel_id=1, source_target_pairs={{0,2},{2,0},{1,3},{3,1},{4,6},{6,4},{5,7},{7,5},{8,10},{10,8},{9,1... | collective-permute-start | bytes 393224 | tf_op jit(solution)/shard_map/ppermute | solution.py:537
  88.2 0.0 collective-permute-start.22
  88.2 3.6 %collective-permute-done.21.side = bf16[256,256]{1,0:T(8,128)(2,1)S(1)} collective-permute-done((bf16[256,256]{1,0:T(8,128)(2,1)S(1)}, bf16[256,256]{1,0:T(8,128)(2,1)S(1)}, u32[]{:S(2)}, u32[]{:S(2)}) %collective-permute-start.21) | collective-permute-done | bytes 131104 | tf_op jit(solution)/shard_map/ppermute | solution.py:537
  91.8 0.0 collective-permute-done.22.peer
  91.8 1.2 %collective-permute-done.23.far = bf16[128,256]{1,0:T(8,128)(2,1)S(1)} collective-permute-done((bf16[128,256]{1,0:T(8,128)(2,1)S(1)}, bf16[128,256]{1,0:T(8,128)(2,1)S(1)}, u32[]{:S(2)}, u32[]{:S(2)}) %collective-permute-start.23) | collective-permute-done | bytes 65568 | tf_op jit(solution)/shard_map/ppermute | solution.py:534
  93.1 0.7 place_keys.1
  93.8 0.0 collective-permute-done.16.peer
  93.8 0.0 collective-permute-done.17.far
  93.8 1.0 %place_queries.1 = bf16[128,4096]{1,0:T(8,128)(2,1)} custom-call(s32[1]{0:T(128)} %bitcast.me_ref, bf16[128,1024]{1,0:T(8,128)(2,1)S(1)} %get-tuple-element.31.own, bf16[256,1024]{1,0:T(8,128)(2,1)S(1)} %collective-permute-done.15.side, bf16[128,1024]{1,0:T(8,128)(2,1)S(1)} %collective-permute-done.16.peer, bf16[128,1024]{1,0:T(8,128)(2,1)S(1)} %collective-permute-done.17.far), custom_call_target="tpu_custom_call" | custom-call | tf_op jit(solution)/shard_map/place_queries/pallas_call | solution.py:501
  (18 shorter events, 0.1 us)
Async XLA Ops:
  0.6 9.7 %collective-permute-start = (bf16[128,4096]{1,0:T(8,128)(2,1)}, bf16[128,4096]{1,0:T(8,128)(2,1)S(1)}, u32[]{:S(2)}, u32[]{:S(2)}) collective-permute-start(bf16[128,4096]{1,0:T(8,128)(2,1)} %q_own.9), channel_id=1, source_target_pairs={{0,1},{1,0},{2,3},{3,2},{4,5},{5,4},{6,7},{7,6},{8,9},{9,8},{10,11... | collective-permute-start | bytes 3145736 | tf_op jit(solution)/shard_map/ppermute | solution.py:534
  1.1 9.2 %collective-permute-start.1 = (bf16[128,4096]{1,0:T(8,128)(2,1)}, bf16[128,4096]{1,0:T(8,128)(2,1)S(1)}, u32[]{:S(2)}, u32[]{:S(2)}) collective-permute-start(bf16[128,4096]{1,0:T(8,128)(2,1)} %g_own.7), channel_id=1, source_target_pairs={{0,1},{1,0},{2,3},{3,2},{4,5},{5,4},{6,7},{7,6},{8,9},{9,8},{10,11... | collective-permute-start | bytes 3145736 | tf_op jit(solution)/shard_map/ppermute | solution.py:534
  1.2 4.1 %collective-permute-start.4 = (bf16[128,512]{1,0:T(8,128)(2,1)}, bf16[128,512]{1,0:T(8,128)(2,1)S(1)}, u32[]{:S(2)}, u32[]{:S(2)}) collective-permute-start(bf16[128,512]{1,0:T(8,128)(2,1)} %k_own.1), channel_id=1, source_target_pairs={{0,1},{1,0},{2,3},{3,2},{4,5},{5,4},{6,7},{7,6},{8,9},{9,8},{10,11... | collective-permute-start | bytes 393224 | tf_op jit(solution)/shard_map/ppermute | solution.py:534
  1.7 3.9 %collective-permute-start.5 = (bf16[128,512]{1,0:T(8,128)(2,1)}, bf16[128,512]{1,0:T(8,128)(2,1)S(1)}, u32[]{:S(2)}, u32[]{:S(2)}) collective-permute-start(bf16[128,512]{1,0:T(8,128)(2,1)} %v_own.1), channel_id=1, source_target_pairs={{0,1},{1,0},{2,3},{3,2},{4,5},{5,4},{6,7},{7,6},{8,9},{9,8},{10,11... | collective-permute-start | bytes 393224 | tf_op jit(solution)/shard_map/ppermute | solution.py:534
  5.5 0.9 copy-start.5
  6.4 0.9 copy-start.6
  7.4 8.4 %collective-permute-start.8 = (bf16[256,256]{1,0:T(8,128)(2,1)S(1)}, bf16[256,256]{1,0:T(8,128)(2,1)S(1)}, u32[]{:S(2)}, u32[]{:S(2)}) collective-permute-start(bf16[256,256]{1,0:T(8,128)(2,1)S(1)} %get-tuple-element.26.after_ref), channel_id=1, source_target_pairs={{0,2},{2,0},{1,3},{3,1},{4,6},{6,4},{5,7},{7,5},{8,10},{10,8},{9,1... | collective-permute-start | bytes 393224 | tf_op jit(solution)/shard_map/ppermute | solution.py:537
  10.3 1.2 %copy-start = (bf16[128,4096]{1,0:T(8,128)(2,1)S(1)}, bf16[128,4096]{1,0:T(8,128)(2,1)}, u32[]{:S(2)}) copy-start(bf16[128,4096]{1,0:T(8,128)(2,1)} %g_own.7) | copy-start | bytes 3145732
  11.6 1.2 %copy-start.2 = (bf16[128,4096]{1,0:T(8,128)(2,1)S(1)}, bf16[128,4096]{1,0:T(8,128)(2,1)}, u32[]{:S(2)}) copy-start(bf16[128,4096]{1,0:T(8,128)(2,1)} %q_own.9) | copy-start | bytes 3145732
  12.8 1.2 %copy-start.1 = (bf16[128,4096]{1,0:T(8,128)(2,1)S(1)}, bf16[128,4096]{1,0:T(8,128)(2,1)}, u32[]{:S(2)}) copy-start(bf16[128,4096]{1,0:T(8,128)(2,1)} %g_own.7) | copy-start | bytes 3145732
  12.8 1.5 %copy-start.4 = (bf16[128,4096]{1,0:T(8,128)(2,1)S(1)}, bf16[128,4096]{1,0:T(8,128)(2,1)}, u32[]{:S(2)}) copy-start(bf16[128,4096]{1,0:T(8,128)(2,1)} %out_ref.1) | copy-start | bytes 3145732
  12.9 27.2 %copy-start.3 = (bf16[128,4096]{1,0:T(8,128)(2,1)S(1)}, bf16[128,4096]{1,0:T(8,128)(2,1)}, u32[]{:S(2)}) copy-start(bf16[128,4096]{1,0:T(8,128)(2,1)} %q_own.9) | copy-start | bytes 3145732
  12.9 27.2 %copy-start.7 = (s32[16,10]{1,0:T(8,128)S(1)}, s32[16,10]{1,0:T(8,128)}, u32[]{:S(2)}) copy-start(s32[16,10]{1,0:T(8,128)} %anc_ref.7) | copy-start | bytes 1924
  12.9 25.2 %collective-permute-start.2 = (bf16[256,1024]{1,0:T(8,128)(2,1)S(1)}, bf16[256,1024]{1,0:T(8,128)(2,1)S(1)}, u32[]{:S(2)}, u32[]{:S(2)}) collective-permute-start(bf16[256,1024]{1,0:T(8,128)(2,1)S(1)} %get-tuple-element.24), channel_id=1, source_target_pairs={{0,2},{2,0},{1,3},{3,1},{4,6},{6,4},{5,7},{7,5},{8,10},{10,8},{9,1... | collective-permute-start | bytes 1572872 | tf_op jit(solution)/shard_map/ppermute | solution.py:537
  14.9 7.7 %collective-permute-start.6 = (f32[32,128]{1,0:T(8,128)S(1)}, f32[32,128]{1,0:T(8,128)S(1)}, u32[]{:S(2)}, u32[]{:S(2)}) collective-permute-start(f32[32,128]{1,0:T(8,128)S(1)} %row_deltas.1.d_own), channel_id=1, source_target_pairs={{0,1},{1,0},{2,3},{3,2},{4,5},{5,4},{6,7},{7,6},{8,9},{9,8},{10,11... | collective-permute-start | bytes 49160 | tf_op jit(solution)/shard_map/ppermute | solution.py:534
  15.0 28.2 %collective-permute-start.3 = (bf16[256,1024]{1,0:T(8,128)(2,1)S(1)}, bf16[256,1024]{1,0:T(8,128)(2,1)S(1)}, u32[]{:S(2)}, u32[]{:S(2)}) collective-permute-start(bf16[256,1024]{1,0:T(8,128)(2,1)S(1)} %get-tuple-element.25), channel_id=1, source_target_pairs={{0,2},{2,0},{1,3},{3,1},{4,6},{6,4},{5,7},{7,5},{8,10},{10,8},{9,1... | collective-permute-start | bytes 1572872 | tf_op jit(solution)/shard_map/ppermute | solution.py:537
  15.8 9.4 %collective-permute-start.11 = (bf16[512,128]{1,0:T(8,128)(2,1)S(1)}, bf16[512,128]{1,0:T(8,128)(2,1)S(1)}, u32[]{:S(2)}, u32[]{:S(2)}) collective-permute-start(bf16[512,128]{1,0:T(8,128)(2,1)S(1)} %pad_maximum_fusion.rest_0_), channel_id=1, source_target_pairs={{0,12},{1,13},{2,14},{3,15},{16,28},{17,29},{18,30},{19,31}} | collective-permute-start | bytes 393224 | tf_op jit(solution)/shard_map/ppermute | solution.py:540
  21.3 6.7 %collective-permute-start.10 = (bf16[512,128]{1,0:T(8,128)(2,1)S(1)}, bf16[512,128]{1,0:T(8,128)(2,1)S(1)}, u32[]{:S(2)}, u32[]{:S(2)}) collective-permute-start(bf16[512,128]{1,0:T(8,128)(2,1)S(1)} %pad_maximum_fusion.rest_0_), channel_id=1, source_target_pairs={{0,8},{4,12},{1,9},{5,13},{2,10},{6,14},{3,11},{7,15},{16,24},{20,... | collective-permute-start | bytes 393224 | tf_op jit(solution)/shard_map/ppermute | solution.py:540
  22.6 13.6 %collective-permute-start.9 = (bf16[512,128]{1,0:T(8,128)(2,1)S(1)}, bf16[512,128]{1,0:T(8,128)(2,1)S(1)}, u32[]{:S(2)}, u32[]{:S(2)}) collective-permute-start(bf16[512,128]{1,0:T(8,128)(2,1)S(1)} %pad_maximum_fusion.rest_0_), channel_id=1, source_target_pairs={{0,4},{4,8},{8,12},{1,5},{5,9},{9,13},{2,6},{6,10},{10,14},{3,7},{... | collective-permute-start | bytes 393224 | tf_op jit(solution)/shard_map/ppermute | solution.py:540
  25.2 18.0 %collective-permute-start.7 = (f32[16,128]{1,0:T(8,128)S(1)}, f32[16,128]{1,0:T(8,128)S(1)}, u32[]{:S(2)}, u32[]{:S(2)}) collective-permute-start(f32[16,128]{1,0:T(8,128)S(1)} %pack_deltas.1), channel_id=1, source_target_pairs={{0,2},{2,0},{1,3},{3,1},{4,6},{6,4},{5,7},{7,5},{8,10},{10,8},{9,1... | collective-permute-start | bytes 24584 | tf_op jit(solution)/shard_map/ppermute | solution.py:537
  28.0 15.2 %collective-permute-start.14 = (bf16[512,128]{1,0:T(8,128)(2,1)S(1)}, bf16[512,128]{1,0:T(8,128)(2,1)S(1)}, u32[]{:S(2)}, u32[]{:S(2)}) collective-permute-start(bf16[512,128]{1,0:T(8,128)(2,1)S(1)} %pad_maximum_fusion.1.rest_2_), channel_id=1, source_target_pairs={{0,12},{1,13},{2,14},{3,15},{16,28},{17,29},{18,30},{19,31}} | collective-permute-start | bytes 393224 | tf_op jit(solution)/shard_map/ppermute | solution.py:540
  36.3 6.9 %collective-permute-start.13 = (bf16[512,128]{1,0:T(8,128)(2,1)S(1)}, bf16[512,128]{1,0:T(8,128)(2,1)S(1)}, u32[]{:S(2)}, u32[]{:S(2)}) collective-permute-start(bf16[512,128]{1,0:T(8,128)(2,1)S(1)} %pad_maximum_fusion.1.rest_2_), channel_id=1, source_target_pairs={{0,8},{4,12},{1,9},{5,13},{2,10},{6,14},{3,11},{7,15},{16,24},{20,... | collective-permute-start | bytes 393224 | tf_op jit(solution)/shard_map/ppermute | solution.py:540
  38.1 9.0 %collective-permute-start.12 = (bf16[512,128]{1,0:T(8,128)(2,1)S(1)}, bf16[512,128]{1,0:T(8,128)(2,1)S(1)}, u32[]{:S(2)}, u32[]{:S(2)}) collective-permute-start(bf16[512,128]{1,0:T(8,128)(2,1)S(1)} %pad_maximum_fusion.1.rest_2_), channel_id=1, source_target_pairs={{0,4},{4,8},{8,12},{1,5},{5,9},{9,13},{2,6},{6,10},{10,14},{3,7},{... | collective-permute-start | bytes 393224 | tf_op jit(solution)/shard_map/ppermute | solution.py:540
  44.5 20.1 %collective-permute-start.18 = (bf16[512,256]{1,0:T(8,128)(2,1)S(1)}, bf16[512,256]{1,0:T(8,128)(2,1)S(1)}, u32[]{:S(2)}, u32[]{:S(2)}) collective-permute-start(bf16[512,256]{1,0:T(8,128)(2,1)S(1)} %get-tuple-element.35), channel_id=1, source_target_pairs={{8,0},{12,4},{9,1},{13,5},{10,2},{14,6},{11,3},{15,7},{24,16},{28,... | collective-permute-start | bytes 786440 | tf_op jit(solution)/shard_map/ppermute | solution.py:543
  45.8 31.4 %collective-permute-start.19 = (bf16[512,256]{1,0:T(8,128)(2,1)S(1)}, bf16[512,256]{1,0:T(8,128)(2,1)S(1)}, u32[]{:S(2)}, u32[]{:S(2)}) collective-permute-start(bf16[512,256]{1,0:T(8,128)(2,1)S(1)} %get-tuple-element.36), channel_id=1, source_target_pairs={{12,0},{13,1},{14,2},{15,3},{28,16},{29,17},{30,18},{31,19}} | collective-permute-start | bytes 786440 | tf_op jit(solution)/shard_map/ppermute | solution.py:543
  51.5 27.2 %collective-permute-start.15 = (bf16[256,1024]{1,0:T(8,128)(2,1)S(1)}, bf16[256,1024]{1,0:T(8,128)(2,1)S(1)}, u32[]{:S(2)}, u32[]{:S(2)}) collective-permute-start(bf16[256,1024]{1,0:T(8,128)(2,1)S(1)} %get-tuple-element.32), channel_id=1, source_target_pairs={{0,2},{2,0},{1,3},{3,1},{4,6},{6,4},{5,7},{7,5},{8,10},{10,8},{9,1... | collective-permute-start | bytes 1572872 | tf_op jit(solution)/shard_map/ppermute | solution.py:537
  77.3 9.4 %collective-permute-start.20 = (bf16[512,256]{1,0:T(8,128)(2,1)S(1)}, bf16[512,256]{1,0:T(8,128)(2,1)S(1)}, u32[]{:S(2)}, u32[]{:S(2)}) collective-permute-start(bf16[512,256]{1,0:T(8,128)(2,1)S(1)} %get-tuple-element.39), channel_id=1, source_target_pairs={{4,0},{8,4},{12,8},{5,1},{9,5},{13,9},{6,2},{10,6},{14,10},{7,3},{... | collective-permute-start | bytes 786440 | tf_op jit(solution)/shard_map/ppermute | solution.py:543
  78.6 15.2 %collective-permute-start.16 = (bf16[128,1024]{1,0:T(8,128)(2,1)S(1)}, bf16[128,1024]{1,0:T(8,128)(2,1)S(1)}, u32[]{:S(2)}, u32[]{:S(2)}) collective-permute-start(bf16[128,1024]{1,0:T(8,128)(2,1)S(1)} %get-tuple-element.33), channel_id=1, source_target_pairs={{0,1},{1,0},{2,3},{3,2},{4,5},{5,4},{6,7},{7,6},{8,9},{9,8},{10,11... | collective-permute-start | bytes 786440 | tf_op jit(solution)/shard_map/ppermute | solution.py:534
  78.7 15.1 %collective-permute-start.17 = (bf16[128,1024]{1,0:T(8,128)(2,1)S(1)}, bf16[128,1024]{1,0:T(8,128)(2,1)S(1)}, u32[]{:S(2)}, u32[]{:S(2)}) collective-permute-start(bf16[128,1024]{1,0:T(8,128)(2,1)S(1)} %slice.26), channel_id=1, source_target_pairs={{0,1},{1,0},{2,3},{3,2},{4,5},{5,4},{6,7},{7,6},{8,9},{9,8},{10,11... | collective-permute-start | bytes 786440 | tf_op jit(solution)/shard_map/ppermute | solution.py:534
  86.8 5.0 %collective-permute-start.21 = (bf16[256,256]{1,0:T(8,128)(2,1)S(1)}, bf16[256,256]{1,0:T(8,128)(2,1)S(1)}, u32[]{:S(2)}, u32[]{:S(2)}) collective-permute-start(bf16[256,256]{1,0:T(8,128)(2,1)S(1)} %get-tuple-element.41), channel_id=1, source_target_pairs={{0,2},{2,0},{1,3},{3,1},{4,6},{6,4},{5,7},{7,5},{8,10},{10,8},{9,1... | collective-permute-start | bytes 393224 | tf_op jit(solution)/shard_map/ppermute | solution.py:537
  88.2 3.6 %collective-permute-start.22 = (bf16[128,256]{1,0:T(8,128)(2,1)S(1)}, bf16[128,256]{1,0:T(8,128)(2,1)S(1)}, u32[]{:S(2)}, u32[]{:S(2)}) collective-permute-start(bf16[128,256]{1,0:T(8,128)(2,1)S(1)} %get-tuple-element.42), channel_id=1, source_target_pairs={{0,1},{1,0},{2,3},{3,2},{4,5},{5,4},{6,7},{7,6},{8,9},{9,8},{10,11... | collective-permute-start | bytes 196616 | tf_op jit(solution)/shard_map/ppermute | solution.py:534
  91.8 1.3 %collective-permute-start.23 = (bf16[128,256]{1,0:T(8,128)(2,1)S(1)}, bf16[128,256]{1,0:T(8,128)(2,1)S(1)}, u32[]{:S(2)}, u32[]{:S(2)}) collective-permute-start(bf16[128,256]{1,0:T(8,128)(2,1)S(1)} %slice.27), channel_id=1, source_target_pairs={{0,1},{1,0},{2,3},{3,2},{4,5},{5,4},{6,7},{7,6},{8,9},{9,8},{10,11... | collective-permute-start | bytes 196616 | tf_op jit(solution)/shard_map/ppermute | solution.py:534

commit v5 on v4

--- a/solution.py
+++ b/solution.py
@@ -43,25 +43,48 @@
     )(outputs, out_grad, after)
 
 
-def live_counts(anc_ref, me, u, depth):
-    tile = me ^ u
+def list_items(items, anc_ref, me, tiles, depth, part):
+    tile_of, first_of, second_of, flags_of = items
     cut = ((me >> 2) - 1) * QUAD
-    near, live = jnp.int32(1), jnp.int32(1)
-    for slot in range(depth):
-        entry = anc_ref[tile, slot]
-        live += (entry >= 0).astype(jnp.int32)
-        near += ((entry >= 0) & (entry >= cut)).astype(jnp.int32)
-    return tile, near, live
-
-
-def chunk_slots(anc_ref, me, tile, depth, start, stop, lowest):
-    def slot_of(entry):
-        seen = jnp.where(entry == 0, tile, anc_ref[tile, jnp.clip(entry - 1, 0, depth - 1)])
-        return ((me >> 2) - (seen >> 2) - lowest) * QUAD + ((seen ^ me) & (QUAD - 1))
-
-    good = start + 1 < stop
-    first = slot_of(start)
-    return first, jnp.where(good, slot_of(start + 1), first), good
+    lowest = 2 if part == "far" else 0
+    count = jnp.int32(0)
+    for place, u in enumerate(tiles):
+        tile = me ^ u
+        near, live = jnp.int32(1), jnp.int32(1)
+        for slot in range(depth):
+            entry = anc_ref[tile, slot]
+            live += (entry >= 0).astype(jnp.int32)
+            near += ((entry >= 0) & (entry >= cut)).astype(jnp.int32)
+        start = near if part == "far" else jnp.int32(0)
+        stop = near if part == "near" else live
+        chunks = (stop - start + 1) // 2
+
+        def slot_of(entry, tile=tile):
+            seen = jnp.where(entry == 0, tile, anc_ref[tile, jnp.clip(entry - 1, 0, depth - 1)])
+            return ((me >> 2) - (seen >> 2) - lowest) * QUAD + ((seen ^ me) & (QUAD - 1))
+
+        def note(chunk, carry, place=place, start=start, stop=stop, count=count, slot_of=slot_of):
+            entry = start + 2 * chunk
+            good = entry + 1 < stop
+            first = slot_of(entry)
+            tile_of[count + chunk] = place
+            first_of[count + chunk] = first
+            second_of[count + chunk] = jnp.where(good, slot_of(entry + 1), first)
+            flags_of[count + chunk] = 1 + 2 * good.astype(jnp.int32) + 4 * (entry == 0).astype(jnp.int32)
+            return carry
+
+        lax.fori_loop(0, chunks, note, 0)
+        count += chunks
+    for extra in range(2):
+        tile_of[count + extra] = 0
+        first_of[count + extra] = 0
+        second_of[count + extra] = 0
+        flags_of[count + extra] = 0
+    return count
+
+
+def item_scratch(tiles, depth):
+    return [pltpu.SMEM((tiles * ((depth + 2) // 2) + 2,), jnp.int32)] * 4
 
 
 def slot_rows(slot):
@@ -72,16 +95,16 @@
     return jnp.concatenate([ref[slot_rows(first), :], ref[slot_rows(second), :]], axis=0)
 
 
-def two_heads(ref, u, pair):
-    left = ref[u, :, 2 * pair * HD : (2 * pair + 1) * HD]
-    right = ref[u, :, (2 * pair + 1) * HD : (2 * pair + 2) * HD]
-    return jnp.concatenate([left, right], axis=0)
-
-
-def causal_mask():
+def heads_below(ref, u, first, count):
+    return jnp.concatenate(
+        [ref[u, :, head * HD : (head + 1) * HD] for head in range(first, first + count)], axis=0
+    )
+
+
+def visible_mask(flags):
     key_pos = lax.broadcasted_iota(jnp.int32, (TILE, PAIR), 0)
     query_pos = lax.broadcasted_iota(jnp.int32, (TILE, PAIR), 1) & (TILE - 1)
-    return key_pos <= query_pos
+    return key_pos - query_pos <= jnp.where((flags & 4) != 0, 0, TILE)
 
 
 def gather_queries(scratch, own, peer, side):
@@ -93,56 +116,56 @@
 
 def stats_kernel(depth, steps, me_ref, anc_ref, q_own, q_peer, q_side, *rest):
     k_refs = rest[:steps]
-    lse_ref, q_all, k_all, top_max, total = rest[steps:]
+    lse_ref, q_all, k_all, item_max, item_sum, *items = rest[steps:]
     me = me_ref[0]
     gather_queries(q_all, q_own, q_peer, q_side)
     for shift, k_ref in enumerate(k_refs):
         k_all[shift * LEVEL : (shift + 1) * LEVEL, :] = k_ref[...]
-
-    def one_tile(u, carry):
-        tile, _, live = live_counts(anc_ref, me, u, depth)
-
-        def chunk_stats(index, is_first):
-            first, second, good = chunk_slots(anc_ref, me, tile, depth, 2 * index, live, 0)
-            key_block = two_tiles(k_all, first, second)
-            for pair in range(GROUP // 2):
-                rows = slice(pair * PAIR, (pair + 1) * PAIR)
-                raw = lax.dot_general(
-                    key_block,
-                    two_heads(q_all, u, pair),
-                    NT_DIMS,
-                    preferred_element_type=jnp.float32,
-                )
-                top, low = raw[:TILE], raw[TILE:]
-                if is_first:
-                    top = jnp.where(causal_mask(), top, MASKED)
-                low_max = jnp.max(low, axis=0, keepdims=True)
-                new_max = jnp.maximum(
-                    jnp.max(top, axis=0, keepdims=True), jnp.where(good, low_max, MASKED)
-                )
-                if not is_first:
-                    old_max = top_max[:, rows]
-                    new_max = jnp.maximum(old_max, new_max)
-                low_base = jnp.where(good, new_max, -MASKED)
-                new_sum = jnp.sum(
-                    jnp.exp2((top - new_max) * SCALE2), axis=0, keepdims=True
-                ) + jnp.sum(jnp.exp2((low - low_base) * SCALE2), axis=0, keepdims=True)
-                if not is_first:
-                    new_sum += total[:, rows] * jnp.exp2((old_max - new_max) * SCALE2)
-                top_max[:, rows] = new_max
-                total[:, rows] = new_sum
-
-        chunk_stats(0, True)
-
-        def step(index, carry):
-            chunk_stats(index, False)
-            return carry
-
-        lax.fori_loop(1, (live + 1) // 2, step, 0)
-        lse_ref[u] = top_max[...] * SCALE2 + jnp.log2(total[...])
+    count = list_items(items, anc_ref, me, range(QUAD), depth, "all")
+    tile_of, first_of, second_of, flags_of = items
+
+    def one_item(index):
+        u, flags = tile_of[index], flags_of[index]
+        good = (flags & 2) != 0
+        key_block = two_tiles(k_all, first_of[index], second_of[index])
+        mask = visible_mask(flags)
+        for pair in range(GROUP // 2):
+            rows = slice(pair * PAIR, (pair + 1) * PAIR)
+            raw = lax.dot_general(
+                key_block,
+                heads_below(q_all, u, 2 * pair, 2),
+                NT_DIMS,
+                preferred_element_type=jnp.float32,
+            )
+            top, low = jnp.where(mask, raw[:TILE], MASKED), raw[TILE:]
+            low_max = jnp.max(low, axis=0, keepdims=True)
+            new_max = jnp.maximum(
+                jnp.max(top, axis=0, keepdims=True), jnp.where(good, low_max, MASKED)
+            )
+            low_base = jnp.where(good, new_max, -MASKED)
+            item_max[index, :, rows] = new_max
+            item_sum[index, :, rows] = jnp.sum(
+                jnp.exp2((top - new_max) * SCALE2), axis=0, keepdims=True
+            ) + jnp.sum(jnp.exp2((low - low_base) * SCALE2), axis=0, keepdims=True)
+
+    def step(index, carry):
+        one_item(2 * index)
+        one_item(2 * index + 1)
         return carry
 
-    lax.fori_loop(0, QUAD, one_tile, 0)
+    lax.fori_loop(0, (count + 1) // 2, step, 0)
+
+    lse_ref[...] = jnp.full_like(lse_ref, MASKED)
+
+    def combine(index, carry):
+        u = tile_of[index]
+        old = lse_ref[u]
+        new = item_max[index] * SCALE2 + jnp.log2(item_sum[index])
+        top = jnp.maximum(old, new)
+        lse_ref[u] = top + jnp.log2(jnp.exp2(old - top) + jnp.exp2(new - top))
+        return carry
+
+    lax.fori_loop(0, count, combine, 0)
 
 
 def grads_kernel(depth, stage, steps, me_ref, anc_ref, q_own, q_peer, q_side, g_own, g_peer, g_side, d_own, d_peer, d_side, lse_ref, *rest):
@@ -152,14 +175,15 @@
     if stage == "own":
         dk_in, dv_in, rest = rest[0], rest[1], rest[2:]
     tiles = {"far": (0, 1, 2, 3), "side": (2, 3), "own": (0, 1)}[stage]
-    lowest = 2 if stage == "far" else 0
     if stage == "far":
         dq_acc, partial_refs, rest = rest[0], rest[1 : 1 + steps], rest[1 + steps :]
     elif stage == "side":
         dq_side, dk_acc, dv_acc, rest = rest[0], rest[1], rest[2], rest[3:]
     else:
         dq_own, dq_peer, partial_refs, rest = rest[0], rest[1], rest[2 : 2 + steps], rest[2 + steps :]
-    q_all, g_all, delta, k_all, v_all, rest = *rest[:5], rest[5:]
+    items, rest = rest[:4], rest[4:]
+    q_all, g_all, delta, k_all, v_all = rest[:5]
+    buffers, rest = ((rest[5], rest[6]), (rest[7], rest[8])), rest[9:]
     if stage != "side":
         dk_acc, dv_acc, rest = rest[0], rest[1], rest[2:]
     if stage != "far":
@@ -186,68 +210,70 @@
     else:
         dk_acc[...] = jnp.zeros_like(dk_acc)
         dv_acc[...] = jnp.zeros_like(dv_acc)
-
-    def one_tile(place, carry):
-        u = tiles[0] + place
-        tile, near, live = live_counts(anc_ref, me, u, depth)
-        start, stop = (near, live) if stage == "far" else (0, near)
-        if stage == "far":
-            dq_acc[place] = jnp.zeros((HD, ROWS), jnp.float32)
-        else:
-            dq_acc[place] = dq_in[place]
-
-        def chunk_grads(index, is_first):
-            first, second, good = chunk_slots(
-                anc_ref, me, tile, depth, start + 2 * index, stop, lowest
+    if stage == "far":
+        dq_acc[...] = jnp.zeros_like(dq_acc)
+    else:
+        dq_acc[...] = dq_in[...]
+    for buffer in buffers[1]:
+        buffer[...] = jnp.zeros_like(buffer)
+    count = list_items(items, anc_ref, me, tiles, depth, "far" if stage == "far" else "near")
+    tile_of, first_of, second_of, flags_of = items
+
+    def scores_part(index, low_ref, score_ref):
+        place, flags = tile_of[index], flags_of[index]
+        first, second = first_of[index], second_of[index]
+        key_block = two_tiles(k_all, first, second)
+        value_block = two_tiles(v_all, first, second)
+        for pair in range(GROUP // 2):
+            rows = slice(pair * PAIR, (pair + 1) * PAIR)
+            raw = lax.dot_general(
+                key_block,
+                heads_below(q_all, place, 2 * pair, 2),
+                NT_DIMS,
+                preferred_element_type=jnp.float32,
             )
-            key_block = two_tiles(k_all, first, second)
-            value_block = two_tiles(v_all, first, second)
-            key_turned = key_block.T
-            dk = jnp.zeros((PAIR, HD), jnp.float32)
-            dv = jnp.zeros((PAIR, HD), jnp.float32)
-            for pair in range(GROUP // 2):
-                rows = slice(pair * PAIR, (pair + 1) * PAIR)
-                query_block = two_heads(q_all, place, pair)
-                grad_block = two_heads(g_all, place, pair)
-                raw = lax.dot_general(
-                    key_block, query_block, NT_DIMS, preferred_element_type=jnp.float32
-                )
-                grad_probs = lax.dot_general(
-                    value_block, grad_block, NT_DIMS, preferred_element_type=jnp.float32
-                )
-                lse = lse_ref[u, :, rows]
-                away = delta[place, :, rows]
-                lows, scores = [], []
-                for part in range(2):
-                    half = slice(part * TILE, (part + 1) * TILE)
-                    base = lse if part == 0 else jnp.where(good, lse, -MASKED)
-                    attn = jnp.exp2(raw[half] * SCALE2 - base)
-                    if is_first and part == 0:
-                        attn = jnp.where(causal_mask(), attn, 0.0)
-                    lows.append(attn.astype(jnp.bfloat16))
-                    scores.append((attn * (grad_probs[half] - away)).astype(jnp.bfloat16))
-                attn_low = jnp.concatenate(lows, axis=0)
-                grad_scores = jnp.concatenate(scores, axis=0)
-                dv += jnp.dot(attn_low, grad_block, preferred_element_type=jnp.float32)
-                dk += jnp.dot(grad_scores, query_block, preferred_element_type=jnp.float32)
-                dq_acc[place, :, rows] += jnp.dot(
-                    key_turned, grad_scores, preferred_element_type=jnp.float32
-                )
-            dk_acc[slot_rows(first), :] += dk[:TILE]
-            dk_acc[slot_rows(second), :] += dk[TILE:]
-            dv_acc[slot_rows(first), :] += dv[:TILE]
-            dv_acc[slot_rows(second), :] += dv[TILE:]
-
-        def step(index, carry):
-            chunk_grads(index, False)
-            return carry
-
-        if stage != "far":
-            chunk_grads(0, True)
-        lax.fori_loop(0 if stage == "far" else 1, (stop - start + 1) // 2, step, 0)
+            grad_probs = lax.dot_general(
+                value_block,
+                heads_below(g_all, place, 2 * pair, 2),
+                NT_DIMS,
+                preferred_element_type=jnp.float32,
+            )
+            lse = lse_ref[tiles[0] + place, :, rows]
+            away = delta[place, :, rows]
+            for part in range(2):
+                half = slice(part * TILE, (part + 1) * TILE)
+                base = jnp.where((flags & (1 + part)) != 0, lse, -MASKED)
+                attn = jnp.exp2(raw[half] * SCALE2 - base)
+                if stage != "far" and part == 0:
+                    attn = jnp.where(visible_mask(flags), attn, 0.0)
+                low_ref[half, rows] = attn.astype(jnp.bfloat16)
+                score_ref[half, rows] = (attn * (grad_probs[half] - away)).astype(jnp.bfloat16)
+
+    def grads_part(index, low_ref, score_ref):
+        index = jnp.maximum(index, 0)
+        place, first, second = tile_of[index], first_of[index], second_of[index]
+        dv = jnp.dot(
+            low_ref[...], heads_below(g_all, place, 0, GROUP), preferred_element_type=jnp.float32
+        )
+        dk = jnp.dot(
+            score_ref[...], heads_below(q_all, place, 0, GROUP), preferred_element_type=jnp.float32
+        )
+        dq_acc[place] += jnp.dot(
+            two_tiles(k_all, first, second).T, score_ref[...], preferred_element_type=jnp.float32
+        )
+        dk_acc[slot_rows(first), :] += dk[:TILE]
+        dk_acc[slot_rows(second), :] += dk[TILE:]
+        dv_acc[slot_rows(first), :] += dv[:TILE]
+        dv_acc[slot_rows(second), :] += dv[TILE:]
+
+    def step(index, carry):
+        scores_part(2 * index, *buffers[0])
+        grads_part(2 * index - 1, *buffers[1])
+        scores_part(2 * index + 1, *buffers[1])
+        grads_part(2 * index, *buffers[0])
         return carry
 
-    lax.fori_loop(0, len(tiles), one_tile, 0)
+    lax.fori_loop(0, jnp.where(count > 0, (count + 2) // 2, 0), step, 0)
 
     if stage != "far":
         for place in range(2):
@@ -294,6 +320,8 @@
 
 def statistics(me, ancestors, q_set, k_list):
     steps = len(k_list)
+    items = item_scratch(QUAD, ancestors.shape[1])
+    count = items[0].shape[0]
     return pl.pallas_call(
         functools.partial(stats_kernel, ancestors.shape[1], steps),
         grid_spec=pltpu.PrefetchScalarGridSpec(
@@ -304,8 +332,9 @@
             scratch_shapes=[
                 pltpu.VMEM((QUAD, TILE, ROWS), jnp.bfloat16),
                 pltpu.VMEM((steps * LEVEL, HD), jnp.bfloat16),
-                pltpu.VMEM((1, ROWS), jnp.float32),
-                pltpu.VMEM((1, ROWS), jnp.float32),
+                pltpu.VMEM((count, 1, ROWS), jnp.float32),
+                pltpu.VMEM((count, 1, ROWS), jnp.float32),
+                *items,
             ],
         ),
         out_shape=jax.ShapeDtypeStruct((QUAD, 1, ROWS), jnp.float32),
@@ -334,13 +363,14 @@
         sums[0] = jax.ShapeDtypeStruct((LEVEL, 2 * HD), jnp.float32)
         out_specs = [WIDE_OUT, WIDE_OUT] + [SUMS] * steps
         out_shape = [wide, wide] + sums
-    scratch = [
+    scratch = item_scratch(tiles, ancestors.shape[1]) + [
         pltpu.VMEM((tiles, TILE, ROWS), jnp.bfloat16),
         pltpu.VMEM((tiles, TILE, ROWS), jnp.bfloat16),
         pltpu.VMEM((tiles, 1, ROWS), jnp.float32),
         pltpu.VMEM(acc, jnp.bfloat16),
         pltpu.VMEM(acc, jnp.bfloat16),
     ]
+    scratch += [pltpu.VMEM((PAIR, ROWS), jnp.bfloat16)] * 4
     if stage != "side":
         scratch += [pltpu.VMEM(acc, jnp.float32)] * 2
     if stage != "far":
@@ -539,6 +569,13 @@
     def up(x, shift):
         return lax.ppermute(x, "level", [(z, z + shift) for z in range(steps - shift)])
 
+    def up_all(x):
+        arrivals = [x] + [up(x, shift) for shift in range(1, min(steps, 3))]
+        for shift in range(3, steps):
+            pairs = [(z, z + 1) for z in range(shift - 1, steps - 1)]
+            arrivals.append(lax.ppermute(arrivals[-1], "level", pairs))
+        return arrivals
+
     def down(x, shift):
         return lax.ppermute(x, "level", [(z + shift, z) for z in range(steps - shift)])
 
@@ -546,11 +583,11 @@
     kv_side = to_side(kv_send)
     k_level = jnp.concatenate([kv_chip[:, :HD], kv_side[:, :HD]], axis=0)
     v_level = jnp.concatenate([kv_chip[:, HD:], kv_side[:, HD:]], axis=0)
-    k_list = [k_level] + [up(k_level, shift) for shift in range(1, steps)]
+    k_list = up_all(k_level)
     q_peer, g_peer = to_peer(queries), to_peer(out_grad)
     q_send, g_send = pack_queries(me, queries, q_peer, out_grad, g_peer)
     q_set = (queries, q_peer, to_side(q_send))
-    v_list = [v_level] + [up(v_level, shift) for shift in range(1, steps)]
+    v_list = up_all(v_level)
     g_set = (out_grad, g_peer, to_side(g_send))
     deltas = row_deltas(outputs, out_grad, kv_send)
     d_peer = to_peer(deltas)

time: 95.4 us -> 93.4 us (0.979)
  starting transfers between devices: 33.9 us -> 27.2 us
  waiting for transfers between devices: 39.8 us -> 43 us
  Pallas kernels: 14.6 us -> 17.1 us
  local copies, waits for them, and re-layouts: 5.65 us -> 4.32 us
    ppermute x6 -> x4, starting transfers between devices: 21.3 us -> 14.5 us  [up(): lax.ppermute(x, 'level', [(z, z + shift) for z in range(steps - shift)])]
    pallas_call x3, Pallas kernels: 8.9 us -> 11.2 us  [gradients(): pl.pallas_call(functools.partial(grads_kernel, ancestors.shape[1], stage,...]
    ppermute x6 -> x4, waiting for transfers between devices: 1.5 us -> 3.69 us  [up(): lax.ppermute(x, 'level', [(z, z + shift) for z in range(steps - shift)])]
    ppermute x6, waiting for transfers between devices: 3.62 us -> 5.67 us  [to_side(): return lax.ppermute(x, 'side', [(0, 1), (1, 0)])]
    ppermute x0 -> x2, starting transfers between devices: none -> 1.34 us  [up_all(): arrivals.append(lax.ppermute(arrivals[-1], 'level', pairs))]
    unnamed x16, local copies, waits for them, and re-layouts: 5.6 us -> 4.27 us
    ppermute x6, starting transfers between devices: 6.88 us -> 5.69 us  [to_side(): return lax.ppermute(x, 'side', [(0, 1), (1, 0)])]
    ppermute x3, waiting for transfers between devices: 29.6 us -> 28.6 us  [down(): lax.ppermute(x, 'level', [(z + shift, z) for z in range(steps - shift)])]
  transfers between devices with their start and end apart: 24 -> 24, of which waited for: 8 -> 9; matrix products, arithmetic and copies ran while one was open for 0% -> 0% of each run, Pallas kernels for 14% -> 17%
where the time goes in v5:
time: 93.4 us; the launch traced here: 92.7 us
  waiting for transfers between devices  43 us (46%)
  starting transfers between devices  27.2 us (29%)
  Pallas kernels  17.1 us (18%)
  local copies, waits for them, and re-layouts  4.32 us (5%)
  between operations  0.97 us (1%)
    ppermute x3, waiting for transfers between devices, down(): lax.ppermute(x, 'level', [(z + shift, z) for z in range(steps - shift)])  28.6 us
    ppermute x4, starting transfers between devices, up(): lax.ppermute(x, 'level', [(z, z + shift) for z in range(steps - shift)])  14.5 us
    pallas_call x3, Pallas kernels, gradients(): pl.pallas_call(functools.partial(grads_kernel, ancestors.shape[1], stage,...  11.2 us
    ppermute x6, starting transfers between devices, to_side(): return lax.ppermute(x, 'side', [(0, 1), (1, 0)])  5.69 us
    ppermute x6, waiting for transfers between devices, to_side(): return lax.ppermute(x, 'side', [(0, 1), (1, 0)])  5.67 us
    ppermute x9, waiting for transfers between devices, to_peer(): return lax.ppermute(x, 'core', [(0, 1), (1, 0)])  5.03 us
    unnamed x16, local copies, waits for them, and re-layouts  4.27 us
    ppermute x3, starting transfers between devices, down(): lax.ppermute(x, 'level', [(z + shift, z) for z in range(steps - shift)])  3.88 us
  transfers between devices with their start and end apart: 24, of which 9 were waited for; matrix products, arithmetic and copies ran while one was open for 0% of the time, Pallas kernels for 17%

profile of v5, /device:TPU:0, one launch (start us, length us, event | category | flops | bytes accessed | tf_op | source)
XLA Modules:
  0.0 92.7 jit_solution(7517609131777687429)
XLA Ops:
  0.6 0.5 collective-permute-start
  1.1 0.1 collective-permute-start.1
  1.2 0.4 collective-permute-start.4
  1.7 0.1 collective-permute-start.5
  1.7 3.6 %collective-permute-done.4.k_peer = bf16[128,512]{1,0:T(8,128)(2,1)S(1)} collective-permute-done((bf16[128,512]{1,0:T(8,128)(2,1)}, bf16[128,512]{1,0:T(8,128)(2,1)S(1)}, u32[]{:S(2)}, u32[]{:S(2)}) %collective-permute-start.4) | collective-permute-done | bytes 131104 | tf_op jit(solution)/shard_map/ppermute | solution.py:564
  5.3 0.2 collective-permute-done.5.v_peer
  5.5 0.9 copy-done.5
  6.4 0.9 copy-done.6
  7.4 3.0 %collective-permute-start.8 = (bf16[256,256]{1,0:T(8,128)(2,1)S(1)}, bf16[256,256]{1,0:T(8,128)(2,1)S(1)}, u32[]{:S(2)}, u32[]{:S(2)}) collective-permute-start(bf16[256,256]{1,0:T(8,128)(2,1)S(1)} %get-tuple-element.26.after_ref), channel_id=1, source_target_pairs={{0,2},{2,0},{1,3},{3,1},{4,6},{6,4},{5,7},{7,5},{8,10},{10,8},{9,1... | collective-permute-start | bytes 393224 | tf_op jit(solution)/shard_map/ppermute | solution.py:567
  10.3 0.0 collective-permute-done.q_peer
  10.4 0.0 collective-permute-done.1.g_peer
  10.4 0.0 copy-start
  10.4 1.2 %copy-done = bf16[128,4096]{1,0:T(8,128)(2,1)S(1)} copy-done((bf16[128,4096]{1,0:T(8,128)(2,1)S(1)}, bf16[128,4096]{1,0:T(8,128)(2,1)}, u32[]{:S(2)}) %copy-start) | copy-done | bytes 1048600
  11.6 1.2 %copy-done.2 = bf16[128,4096]{1,0:T(8,128)(2,1)S(1)} copy-done((bf16[128,4096]{1,0:T(8,128)(2,1)S(1)}, bf16[128,4096]{1,0:T(8,128)(2,1)}, u32[]{:S(2)}) %copy-start.2) | copy-done | bytes 1048600
  12.8 0.1 pack_queries.1
  12.9 0.0 copy-start.3
  12.9 0.0 copy-start.7
  12.9 0.1 collective-permute-start.2
  13.0 1.1 %collective-permute-done.8 = bf16[256,256]{1,0:T(8,128)(2,1)S(1)} collective-permute-done((bf16[256,256]{1,0:T(8,128)(2,1)S(1)}, bf16[256,256]{1,0:T(8,128)(2,1)S(1)}, u32[]{:S(2)}, u32[]{:S(2)}) %collective-permute-start.8) | collective-permute-done | bytes 131104 | tf_op jit(solution)/shard_map/ppermute | solution.py:567
  14.2 4.7 %collective-permute-start.10 = (bf16[512,128]{1,0:T(8,128)(2,1)S(1)}, bf16[512,128]{1,0:T(8,128)(2,1)S(1)}, u32[]{:S(2)}, u32[]{:S(2)}) collective-permute-start(bf16[512,128]{1,0:T(8,128)(2,1)S(1)} %pad_maximum_fusion.rest_0_), channel_id=1, source_target_pairs={{0,8},{4,12},{1,9},{5,13},{2,10},{6,14},{3,11},{7,15},{16,24},{20,... | collective-permute-start | bytes 393224 | tf_op jit(solution)/shard_map/ppermute | solution.py:570
  18.9 1.6 %collective-permute-start.3 = (bf16[256,1024]{1,0:T(8,128)(2,1)S(1)}, bf16[256,1024]{1,0:T(8,128)(2,1)S(1)}, u32[]{:S(2)}, u32[]{:S(2)}) collective-permute-start(bf16[256,1024]{1,0:T(8,128)(2,1)S(1)} %get-tuple-element.25), channel_id=1, source_target_pairs={{0,2},{2,0},{1,3},{3,1},{4,6},{6,4},{5,7},{7,5},{8,10},{10,8},{9,1... | collective-permute-start | bytes 1572872 | tf_op jit(solution)/shard_map/ppermute | solution.py:567
  20.5 0.6 row_deltas.1.d_own
  21.1 0.1 collective-permute-start.6
  21.2 3.5 %collective-permute-start.9 = (bf16[512,128]{1,0:T(8,128)(2,1)S(1)}, bf16[512,128]{1,0:T(8,128)(2,1)S(1)}, u32[]{:S(2)}, u32[]{:S(2)}) collective-permute-start(bf16[512,128]{1,0:T(8,128)(2,1)S(1)} %pad_maximum_fusion.rest_0_), channel_id=1, source_target_pairs={{0,4},{4,8},{8,12},{1,5},{5,9},{9,13},{2,6},{6,10},{10,14},{3,7},{... | collective-permute-start | bytes 393224 | tf_op jit(solution)/shard_map/ppermute | solution.py:570
  24.7 0.0 collective-permute-done.6.d_peer
  24.7 1.3 %collective-permute-start.13 = (bf16[512,128]{1,0:T(8,128)(2,1)S(1)}, bf16[512,128]{1,0:T(8,128)(2,1)S(1)}, u32[]{:S(2)}, u32[]{:S(2)}) collective-permute-start(bf16[512,128]{1,0:T(8,128)(2,1)S(1)} %pad_maximum_fusion.1.rest_2_), channel_id=1, source_target_pairs={{0,8},{4,12},{1,9},{5,13},{2,10},{6,14},{3,11},{7,15},{16,24},{20,... | collective-permute-start | bytes 393224 | tf_op jit(solution)/shard_map/ppermute | solution.py:570
  26.0 0.0 collective-permute-done.10.rest_2_.rest_0_
  26.0 0.7 collective-permute-start.11
  26.7 1.7 %collective-permute-done.9.rest_1_ = bf16[512,128]{1,0:T(8,128)(2,1)S(1)} collective-permute-done((bf16[512,128]{1,0:T(8,128)(2,1)S(1)}, bf16[512,128]{1,0:T(8,128)(2,1)S(1)}, u32[]{:S(2)}, u32[]{:S(2)}) %collective-permute-start.9) | collective-permute-done | bytes 131104 | tf_op jit(solution)/shard_map/ppermute | solution.py:570
  28.5 0.5 collective-permute-start.7
  29.0 1.9 %collective-permute-done.13.rest_2_ = bf16[512,128]{1,0:T(8,128)(2,1)S(1)} collective-permute-done((bf16[512,128]{1,0:T(8,128)(2,1)S(1)}, bf16[512,128]{1,0:T(8,128)(2,1)S(1)}, u32[]{:S(2)}, u32[]{:S(2)}) %collective-permute-start.13) | collective-permute-done | bytes 131104 | tf_op jit(solution)/shard_map/ppermute | solution.py:570
  30.9 5.0 %collective-permute-start.12 = (bf16[512,128]{1,0:T(8,128)(2,1)S(1)}, bf16[512,128]{1,0:T(8,128)(2,1)S(1)}, u32[]{:S(2)}, u32[]{:S(2)}) collective-permute-start(bf16[512,128]{1,0:T(8,128)(2,1)S(1)} %pad_maximum_fusion.1.rest_2_), channel_id=1, source_target_pairs={{0,4},{4,8},{8,12},{1,5},{5,9},{9,13},{2,6},{6,10},{10,14},{3,7},{... | collective-permute-start | bytes 393224 | tf_op jit(solution)/shard_map/ppermute | solution.py:570
  35.9 0.0 collective-permute-done.11.rest_3_.rest_1_
  35.9 0.7 collective-permute-start.14
  36.6 0.0 collective-permute-done.2.q_side
  36.6 3.3 %statistics.1.lse_ref = f32[4,1,1024]{2,1,0:T(1,128)S(1)} custom-call(s32[1]{0:T(128)} %bitcast.me_ref, s32[16,10]{1,0:T(8,128)S(1)} %copy-done.7, bf16[128,4096]{1,0:T(8,128)(2,1)S(1)} %copy-done.3, bf16[128,4096]{1,0:T(8,128)(2,1)S(1)} %collective-permute-done.q_peer, bf16[256,1024]{1,0:T(8,128)(2,1)S(1)} %collective-permute-done.2.q_side, ...), custom_call_target="tpu_custom_call" | custom-call | flops 2952790016 | bytes 16777216 | tf_op jit(solution)/shard_map/statistics/pallas_call | solution.py:325
  39.9 0.0 collective-permute-done.7.d_side
  39.9 0.0 collective-permute-done.14.rest_3_
  40.0 0.0 collective-permute-done.3.g_side
  40.0 1.4 %far_grads.1 = (f32[4,128,1024]{2,1,0:T(8,128)S(1)}, bf16[512,256]{1,0:T(8,128)(2,1)S(1)}, bf16[512,256]{1,0:T(8,128)(2,1)S(1)}) custom-call(s32[1]{0:T(128)} %bitcast.me_ref, s32[16,10]{1,0:T(8,128)S(1)} %copy-done.7, bf16[128,4096]{1,0:T(8,128)(2,1)S(1)} %copy-done.3, bf16[128,4096]{1,0:T(8,128)(2,1)S(1)} %collective-permute-done.q_peer, ...), custom_call_target="tpu_custom_call" | custom-call | flops 14763950080 | bytes 16777216 | tf_op jit(solution)/shard_map/far_grads/pallas_call | solution.py:378
  41.3 1.3 %collective-permute-start.18 = (bf16[512,256]{1,0:T(8,128)(2,1)S(1)}, bf16[512,256]{1,0:T(8,128)(2,1)S(1)}, u32[]{:S(2)}, u32[]{:S(2)}) collective-permute-start(bf16[512,256]{1,0:T(8,128)(2,1)S(1)} %get-tuple-element.35), channel_id=1, source_target_pairs={{8,0},{12,4},{9,1},{13,5},{10,2},{14,6},{11,3},{15,7},{24,16},{28,... | collective-permute-start | bytes 786440 | tf_op jit(solution)/shard_map/ppermute | solution.py:580
  42.6 1.3 %collective-permute-start.19 = (bf16[512,256]{1,0:T(8,128)(2,1)S(1)}, bf16[512,256]{1,0:T(8,128)(2,1)S(1)}, u32[]{:S(2)}, u32[]{:S(2)}) collective-permute-start(bf16[512,256]{1,0:T(8,128)(2,1)S(1)} %get-tuple-element.36), channel_id=1, source_target_pairs={{12,0},{13,1},{14,2},{15,3},{28,16},{29,17},{30,18},{31,19}} | collective-permute-start | bytes 786440 | tf_op jit(solution)/shard_map/ppermute | solution.py:580
  43.9 0.0 collective-permute-done.12.rest_3_
  43.9 5.6 %side_grads.1 = (bf16[256,1024]{1,0:T(8,128)(2,1)S(1)}, f32[1024,128]{1,0:T(8,128)S(1)}, f32[1024,128]{1,0:T(8,128)S(1)}) custom-call(s32[1]{0:T(128)} %bitcast.me_ref, s32[16,10]{1,0:T(8,128)S(1)} %copy-done.7, bf16[128,4096]{1,0:T(8,128)(2,1)S(1)} %copy-done.3, bf16[128,4096]{1,0:T(8,128)(2,1)S(1)} %collective-permute-done.q_peer, ...), custom_call_target="tpu_custom_call" | custom-call | flops 14763950080 | bytes 16777216 | tf_op jit(solution)/shard_map/side_grads/pallas_call | solution.py:378
  49.6 0.1 collective-permute-start.15
  49.7 4.2 %own_grads.1 = (bf16[128,1024]{1,0:T(8,128)(2,1)S(1)}, bf16[128,1024]{1,0:T(8,128)(2,1)S(1)}, f32[512,256]{1,0:T(8,128)S(1)}, bf16[512,256]{1,0:T(8,128)(2,1)S(1)}) custom-call(s32[1]{0:T(128)} %bitcast.me_ref, s32[16,10]{1,0:T(8,128)S(1)} %copy-done.7, bf16[128,4096]{1,0:T(8,128)(2,1)S(1)} %copy-done.3, bf16[128,4096]{1,0:T(8,128)(2,1)S(1)} %collective-permute-done.q_peer, ...), custom_call_target="tpu_custom_call" | custom-call | flops 14763950080 | bytes 16777216 | tf_op jit(solution)/shard_map/own_grads/pallas_call | solution.py:378
  53.9 22.3 %collective-permute-done.18.refs_0_ = bf16[512,256]{1,0:T(8,128)(2,1)S(1)} collective-permute-done((bf16[512,256]{1,0:T(8,128)(2,1)S(1)}, bf16[512,256]{1,0:T(8,128)(2,1)S(1)}, u32[]{:S(2)}, u32[]{:S(2)}) %collective-permute-start.18) | collective-permute-done | bytes 262176 | tf_op jit(solution)/shard_map/ppermute | solution.py:580
  76.2 0.0 collective-permute-done.19.refs_1_
  76.2 0.1 add_far.1
  76.2 1.3 %collective-permute-start.20 = (bf16[512,256]{1,0:T(8,128)(2,1)S(1)}, bf16[512,256]{1,0:T(8,128)(2,1)S(1)}, u32[]{:S(2)}, u32[]{:S(2)}) collective-permute-start(bf16[512,256]{1,0:T(8,128)(2,1)S(1)} %get-tuple-element.39), channel_id=1, source_target_pairs={{4,0},{8,4},{12,8},{5,1},{9,5},{13,9},{6,2},{10,6},{14,10},{7,3},{... | collective-permute-start | bytes 786440 | tf_op jit(solution)/shard_map/ppermute | solution.py:580
  77.5 0.1 collective-permute-start.16
  77.7 0.6 collective-permute-start.17
  78.2 6.3 %collective-permute-done.20.near_ref = bf16[512,256]{1,0:T(8,128)(2,1)S(1)} collective-permute-done((bf16[512,256]{1,0:T(8,128)(2,1)S(1)}, bf16[512,256]{1,0:T(8,128)(2,1)S(1)}, u32[]{:S(2)}, u32[]{:S(2)}) %collective-permute-start.20) | collective-permute-done | bytes 262176 | tf_op jit(solution)/shard_map/ppermute | solution.py:580
  84.5 0.1 add_sums.1
  84.6 0.5 collective-permute-start.21
  85.1 0.0 collective-permute-start.22
  85.1 4.5 %collective-permute-done.21.side = bf16[256,256]{1,0:T(8,128)(2,1)S(1)} collective-permute-done((bf16[256,256]{1,0:T(8,128)(2,1)S(1)}, bf16[256,256]{1,0:T(8,128)(2,1)S(1)}, u32[]{:S(2)}, u32[]{:S(2)}) %collective-permute-start.21) | collective-permute-done | bytes 131104 | tf_op jit(solution)/shard_map/ppermute | solution.py:567
  89.6 0.0 collective-permute-start.23
  89.6 0.0 collective-permute-done.22.peer
  89.6 1.2 %collective-permute-done.23.far = bf16[128,256]{1,0:T(8,128)(2,1)S(1)} collective-permute-done((bf16[128,256]{1,0:T(8,128)(2,1)S(1)}, bf16[128,256]{1,0:T(8,128)(2,1)S(1)}, u32[]{:S(2)}, u32[]{:S(2)}) %collective-permute-start.23) | collective-permute-done | bytes 65568 | tf_op jit(solution)/shard_map/ppermute | solution.py:564
  90.9 0.7 place_keys.1
  91.6 0.0 collective-permute-done.16.peer
  91.6 0.0 collective-permute-done.17.far
  91.6 1.0 %place_queries.1 = bf16[128,4096]{1,0:T(8,128)(2,1)} custom-call(s32[1]{0:T(128)} %bitcast.me_ref, bf16[128,1024]{1,0:T(8,128)(2,1)S(1)} %get-tuple-element.31.own, bf16[256,1024]{1,0:T(8,128)(2,1)S(1)} %collective-permute-done.15.side, bf16[128,1024]{1,0:T(8,128)(2,1)S(1)} %collective-permute-done.16.peer, bf16[128,1024]{1,0:T(8,128)(2,1)S(1)} %collective-permute-done.17.far), custom_call_target="tpu_custom_call" | custom-call | tf_op jit(solution)/shard_map/place_queries/pallas_call | solution.py:531
  (18 shorter events, 0.1 us)
Async XLA Ops:
  0.6 9.7 %collective-permute-start = (bf16[128,4096]{1,0:T(8,128)(2,1)}, bf16[128,4096]{1,0:T(8,128)(2,1)S(1)}, u32[]{:S(2)}, u32[]{:S(2)}) collective-permute-start(bf16[128,4096]{1,0:T(8,128)(2,1)} %q_own.9), channel_id=1, source_target_pairs={{0,1},{1,0},{2,3},{3,2},{4,5},{5,4},{6,7},{7,6},{8,9},{9,8},{10,11... | collective-permute-start | bytes 3145736 | tf_op jit(solution)/shard_map/ppermute | solution.py:564
  1.1 9.2 %collective-permute-start.1 = (bf16[128,4096]{1,0:T(8,128)(2,1)}, bf16[128,4096]{1,0:T(8,128)(2,1)S(1)}, u32[]{:S(2)}, u32[]{:S(2)}) collective-permute-start(bf16[128,4096]{1,0:T(8,128)(2,1)} %g_own.7), channel_id=1, source_target_pairs={{0,1},{1,0},{2,3},{3,2},{4,5},{5,4},{6,7},{7,6},{8,9},{9,8},{10,11... | collective-permute-start | bytes 3145736 | tf_op jit(solution)/shard_map/ppermute | solution.py:564
  1.2 4.1 %collective-permute-start.4 = (bf16[128,512]{1,0:T(8,128)(2,1)}, bf16[128,512]{1,0:T(8,128)(2,1)S(1)}, u32[]{:S(2)}, u32[]{:S(2)}) collective-permute-start(bf16[128,512]{1,0:T(8,128)(2,1)} %k_own.1), channel_id=1, source_target_pairs={{0,1},{1,0},{2,3},{3,2},{4,5},{5,4},{6,7},{7,6},{8,9},{9,8},{10,11... | collective-permute-start | bytes 393224 | tf_op jit(solution)/shard_map/ppermute | solution.py:564
  1.7 3.9 %collective-permute-start.5 = (bf16[128,512]{1,0:T(8,128)(2,1)}, bf16[128,512]{1,0:T(8,128)(2,1)S(1)}, u32[]{:S(2)}, u32[]{:S(2)}) collective-permute-start(bf16[128,512]{1,0:T(8,128)(2,1)} %v_own.1), channel_id=1, source_target_pairs={{0,1},{1,0},{2,3},{3,2},{4,5},{5,4},{6,7},{7,6},{8,9},{9,8},{10,11... | collective-permute-start | bytes 393224 | tf_op jit(solution)/shard_map/ppermute | solution.py:564
  5.5 0.9 copy-start.5
  6.4 0.9 copy-start.6
  7.4 6.8 %collective-permute-start.8 = (bf16[256,256]{1,0:T(8,128)(2,1)S(1)}, bf16[256,256]{1,0:T(8,128)(2,1)S(1)}, u32[]{:S(2)}, u32[]{:S(2)}) collective-permute-start(bf16[256,256]{1,0:T(8,128)(2,1)S(1)} %get-tuple-element.26.after_ref), channel_id=1, source_target_pairs={{0,2},{2,0},{1,3},{3,1},{4,6},{6,4},{5,7},{7,5},{8,10},{10,8},{9,1... | collective-permute-start | bytes 393224 | tf_op jit(solution)/shard_map/ppermute | solution.py:567
  10.4 1.2 %copy-start = (bf16[128,4096]{1,0:T(8,128)(2,1)S(1)}, bf16[128,4096]{1,0:T(8,128)(2,1)}, u32[]{:S(2)}) copy-start(bf16[128,4096]{1,0:T(8,128)(2,1)} %g_own.7) | copy-start | bytes 3145732
  11.6 1.2 %copy-start.2 = (bf16[128,4096]{1,0:T(8,128)(2,1)S(1)}, bf16[128,4096]{1,0:T(8,128)(2,1)}, u32[]{:S(2)}) copy-start(bf16[128,4096]{1,0:T(8,128)(2,1)} %q_own.9) | copy-start | bytes 3145732
  12.8 7.7 %copy-start.1 = (bf16[128,4096]{1,0:T(8,128)(2,1)S(1)}, bf16[128,4096]{1,0:T(8,128)(2,1)}, u32[]{:S(2)}) copy-start(bf16[128,4096]{1,0:T(8,128)(2,1)} %g_own.7) | copy-start | bytes 3145732
  12.8 7.7 %copy-start.4 = (bf16[128,4096]{1,0:T(8,128)(2,1)S(1)}, bf16[128,4096]{1,0:T(8,128)(2,1)}, u32[]{:S(2)}) copy-start(bf16[128,4096]{1,0:T(8,128)(2,1)} %out_ref.1) | copy-start | bytes 3145732
  12.9 23.7 %copy-start.3 = (bf16[128,4096]{1,0:T(8,128)(2,1)S(1)}, bf16[128,4096]{1,0:T(8,128)(2,1)}, u32[]{:S(2)}) copy-start(bf16[128,4096]{1,0:T(8,128)(2,1)} %q_own.9) | copy-start | bytes 3145732
  12.9 23.7 %copy-start.7 = (s32[16,10]{1,0:T(8,128)S(1)}, s32[16,10]{1,0:T(8,128)}, u32[]{:S(2)}) copy-start(s32[16,10]{1,0:T(8,128)} %anc_ref.7) | copy-start | bytes 1924
  12.9 23.7 %collective-permute-start.2 = (bf16[256,1024]{1,0:T(8,128)(2,1)S(1)}, bf16[256,1024]{1,0:T(8,128)(2,1)S(1)}, u32[]{:S(2)}, u32[]{:S(2)}) collective-permute-start(bf16[256,1024]{1,0:T(8,128)(2,1)S(1)} %get-tuple-element.24), channel_id=1, source_target_pairs={{0,2},{2,0},{1,3},{3,1},{4,6},{6,4},{5,7},{7,5},{8,10},{10,8},{9,1... | collective-permute-start | bytes 1572872 | tf_op jit(solution)/shard_map/ppermute | solution.py:567
  14.2 11.8 %collective-permute-start.10 = (bf16[512,128]{1,0:T(8,128)(2,1)S(1)}, bf16[512,128]{1,0:T(8,128)(2,1)S(1)}, u32[]{:S(2)}, u32[]{:S(2)}) collective-permute-start(bf16[512,128]{1,0:T(8,128)(2,1)S(1)} %pad_maximum_fusion.rest_0_), channel_id=1, source_target_pairs={{0,8},{4,12},{1,9},{5,13},{2,10},{6,14},{3,11},{7,15},{16,24},{20,... | collective-permute-start | bytes 393224 | tf_op jit(solution)/shard_map/ppermute | solution.py:570
  18.9 21.1 %collective-permute-start.3 = (bf16[256,1024]{1,0:T(8,128)(2,1)S(1)}, bf16[256,1024]{1,0:T(8,128)(2,1)S(1)}, u32[]{:S(2)}, u32[]{:S(2)}) collective-permute-start(bf16[256,1024]{1,0:T(8,128)(2,1)S(1)} %get-tuple-element.25), channel_id=1, source_target_pairs={{0,2},{2,0},{1,3},{3,1},{4,6},{6,4},{5,7},{7,5},{8,10},{10,8},{9,1... | collective-permute-start | bytes 1572872 | tf_op jit(solution)/shard_map/ppermute | solution.py:567
  21.1 3.6 %collective-permute-start.6 = (f32[32,128]{1,0:T(8,128)S(1)}, f32[32,128]{1,0:T(8,128)S(1)}, u32[]{:S(2)}, u32[]{:S(2)}) collective-permute-start(f32[32,128]{1,0:T(8,128)S(1)} %row_deltas.1.d_own), channel_id=1, source_target_pairs={{0,1},{1,0},{2,3},{3,2},{4,5},{5,4},{6,7},{7,6},{8,9},{9,8},{10,11... | collective-permute-start | bytes 49160 | tf_op jit(solution)/shard_map/ppermute | solution.py:564
  21.2 7.3 %collective-permute-start.9 = (bf16[512,128]{1,0:T(8,128)(2,1)S(1)}, bf16[512,128]{1,0:T(8,128)(2,1)S(1)}, u32[]{:S(2)}, u32[]{:S(2)}) collective-permute-start(bf16[512,128]{1,0:T(8,128)(2,1)S(1)} %pad_maximum_fusion.rest_0_), channel_id=1, source_target_pairs={{0,4},{4,8},{8,12},{1,5},{5,9},{9,13},{2,6},{6,10},{10,14},{3,7},{... | collective-permute-start | bytes 393224 | tf_op jit(solution)/shard_map/ppermute | solution.py:570
  24.7 6.2 %collective-permute-start.13 = (bf16[512,128]{1,0:T(8,128)(2,1)S(1)}, bf16[512,128]{1,0:T(8,128)(2,1)S(1)}, u32[]{:S(2)}, u32[]{:S(2)}) collective-permute-start(bf16[512,128]{1,0:T(8,128)(2,1)S(1)} %pad_maximum_fusion.1.rest_2_), channel_id=1, source_target_pairs={{0,8},{4,12},{1,9},{5,13},{2,10},{6,14},{3,11},{7,15},{16,24},{20,... | collective-permute-start | bytes 393224 | tf_op jit(solution)/shard_map/ppermute | solution.py:570
  26.0 9.9 %collective-permute-start.11 = (bf16[512,128]{1,0:T(8,128)(2,1)S(1)}, bf16[512,128]{1,0:T(8,128)(2,1)S(1)}, u32[]{:S(2)}, u32[]{:S(2)}) collective-permute-start(bf16[512,128]{1,0:T(8,128)(2,1)S(1)} %collective-permute-done.10.rest_2_.rest_0_), channel_id=1, source_target_pairs={{8,12},{9,13},{10,14},{11,15},{24,28},{25,29},{26,30},{27,31}} | collective-permute-start | bytes 393224 | tf_op jit(solution)/shard_map/ppermute | solution.py:576
  28.5 11.5 %collective-permute-start.7 = (f32[16,128]{1,0:T(8,128)S(1)}, f32[16,128]{1,0:T(8,128)S(1)}, u32[]{:S(2)}, u32[]{:S(2)}) collective-permute-start(f32[16,128]{1,0:T(8,128)S(1)} %pack_deltas.1), channel_id=1, source_target_pairs={{0,2},{2,0},{1,3},{3,1},{4,6},{6,4},{5,7},{7,5},{8,10},{10,8},{9,1... | collective-permute-start | bytes 24584 | tf_op jit(solution)/shard_map/ppermute | solution.py:567
  30.9 13.0 %collective-permute-start.12 = (bf16[512,128]{1,0:T(8,128)(2,1)S(1)}, bf16[512,128]{1,0:T(8,128)(2,1)S(1)}, u32[]{:S(2)}, u32[]{:S(2)}) collective-permute-start(bf16[512,128]{1,0:T(8,128)(2,1)S(1)} %pad_maximum_fusion.1.rest_2_), channel_id=1, source_target_pairs={{0,4},{4,8},{8,12},{1,5},{5,9},{9,13},{2,6},{6,10},{10,14},{3,7},{... | collective-permute-start | bytes 393224 | tf_op jit(solution)/shard_map/ppermute | solution.py:570
  35.9 4.0 %collective-permute-start.14 = (bf16[512,128]{1,0:T(8,128)(2,1)S(1)}, bf16[512,128]{1,0:T(8,128)(2,1)S(1)}, u32[]{:S(2)}, u32[]{:S(2)}) collective-permute-start(bf16[512,128]{1,0:T(8,128)(2,1)S(1)} %collective-permute-done.13.rest_2_), channel_id=1, source_target_pairs={{8,12},{9,13},{10,14},{11,15},{24,28},{25,29},{26,30},{27,31}} | collective-permute-start | bytes 393224 | tf_op jit(solution)/shard_map/ppermute | solution.py:576
  41.3 34.8 %collective-permute-start.18 = (bf16[512,256]{1,0:T(8,128)(2,1)S(1)}, bf16[512,256]{1,0:T(8,128)(2,1)S(1)}, u32[]{:S(2)}, u32[]{:S(2)}) collective-permute-start(bf16[512,256]{1,0:T(8,128)(2,1)S(1)} %get-tuple-element.35), channel_id=1, source_target_pairs={{8,0},{12,4},{9,1},{13,5},{10,2},{14,6},{11,3},{15,7},{24,16},{28,... | collective-permute-start | bytes 786440 | tf_op jit(solution)/shard_map/ppermute | solution.py:580
  42.6 33.5 %collective-permute-start.19 = (bf16[512,256]{1,0:T(8,128)(2,1)S(1)}, bf16[512,256]{1,0:T(8,128)(2,1)S(1)}, u32[]{:S(2)}, u32[]{:S(2)}) collective-permute-start(bf16[512,256]{1,0:T(8,128)(2,1)S(1)} %get-tuple-element.36), channel_id=1, source_target_pairs={{12,0},{13,1},{14,2},{15,3},{28,16},{29,17},{30,18},{31,19}} | collective-permute-start | bytes 786440 | tf_op jit(solution)/shard_map/ppermute | solution.py:580
  49.6 28.0 %collective-permute-start.15 = (bf16[256,1024]{1,0:T(8,128)(2,1)S(1)}, bf16[256,1024]{1,0:T(8,128)(2,1)S(1)}, u32[]{:S(2)}, u32[]{:S(2)}) collective-permute-start(bf16[256,1024]{1,0:T(8,128)(2,1)S(1)} %get-tuple-element.32), channel_id=1, source_target_pairs={{0,2},{2,0},{1,3},{3,1},{4,6},{6,4},{5,7},{7,5},{8,10},{10,8},{9,1... | collective-permute-start | bytes 1572872 | tf_op jit(solution)/shard_map/ppermute | solution.py:567
  76.2 8.3 %collective-permute-start.20 = (bf16[512,256]{1,0:T(8,128)(2,1)S(1)}, bf16[512,256]{1,0:T(8,128)(2,1)S(1)}, u32[]{:S(2)}, u32[]{:S(2)}) collective-permute-start(bf16[512,256]{1,0:T(8,128)(2,1)S(1)} %get-tuple-element.39), channel_id=1, source_target_pairs={{4,0},{8,4},{12,8},{5,1},{9,5},{13,9},{6,2},{10,6},{14,10},{7,3},{... | collective-permute-start | bytes 786440 | tf_op jit(solution)/shard_map/ppermute | solution.py:580
  77.5 14.1 %collective-permute-start.16 = (bf16[128,1024]{1,0:T(8,128)(2,1)S(1)}, bf16[128,1024]{1,0:T(8,128)(2,1)S(1)}, u32[]{:S(2)}, u32[]{:S(2)}) collective-permute-start(bf16[128,1024]{1,0:T(8,128)(2,1)S(1)} %get-tuple-element.33), channel_id=1, source_target_pairs={{0,1},{1,0},{2,3},{3,2},{4,5},{5,4},{6,7},{7,6},{8,9},{9,8},{10,11... | collective-permute-start | bytes 786440 | tf_op jit(solution)/shard_map/ppermute | solution.py:564
  77.7 13.9 %collective-permute-start.17 = (bf16[128,1024]{1,0:T(8,128)(2,1)S(1)}, bf16[128,1024]{1,0:T(8,128)(2,1)S(1)}, u32[]{:S(2)}, u32[]{:S(2)}) collective-permute-start(bf16[128,1024]{1,0:T(8,128)(2,1)S(1)} %slice.26), channel_id=1, source_target_pairs={{0,1},{1,0},{2,3},{3,2},{4,5},{5,4},{6,7},{7,6},{8,9},{9,8},{10,11... | collective-permute-start | bytes 786440 | tf_op jit(solution)/shard_map/ppermute | solution.py:564
  84.6 5.0 %collective-permute-start.21 = (bf16[256,256]{1,0:T(8,128)(2,1)S(1)}, bf16[256,256]{1,0:T(8,128)(2,1)S(1)}, u32[]{:S(2)}, u32[]{:S(2)}) collective-permute-start(bf16[256,256]{1,0:T(8,128)(2,1)S(1)} %get-tuple-element.41), channel_id=1, source_target_pairs={{0,2},{2,0},{1,3},{3,1},{4,6},{6,4},{5,7},{7,5},{8,10},{10,8},{9,1... | collective-permute-start | bytes 393224 | tf_op jit(solution)/shard_map/ppermute | solution.py:567
  85.1 4.6 %collective-permute-start.22 = (bf16[128,256]{1,0:T(8,128)(2,1)S(1)}, bf16[128,256]{1,0:T(8,128)(2,1)S(1)}, u32[]{:S(2)}, u32[]{:S(2)}) collective-permute-start(bf16[128,256]{1,0:T(8,128)(2,1)S(1)} %get-tuple-element.42), channel_id=1, source_target_pairs={{0,1},{1,0},{2,3},{3,2},{4,5},{5,4},{6,7},{7,6},{8,9},{9,8},{10,11... | collective-permute-start | bytes 196616 | tf_op jit(solution)/shard_map/ppermute | solution.py:564
  89.6 1.3 %collective-permute-start.23 = (bf16[128,256]{1,0:T(8,128)(2,1)S(1)}, bf16[128,256]{1,0:T(8,128)(2,1)S(1)}, u32[]{:S(2)}, u32[]{:S(2)}) collective-permute-start(bf16[128,256]{1,0:T(8,128)(2,1)S(1)} %slice.27), channel_id=1, source_target_pairs={{0,1},{1,0},{2,3},{3,2},{4,5},{5,4},{6,7},{7,6},{8,9},{9,8},{10,11... | collective-permute-start | bytes 196616 | tf_op jit(solution)/shard_map/ppermute | solution.py:564

commit v6 on v5

--- a/solution.py
+++ b/solution.py
@@ -107,21 +107,23 @@
     return key_pos - query_pos <= jnp.where((flags & 4) != 0, 0, TILE)
 
 
-def gather_queries(scratch, own, peer, side):
-    scratch[0] = own[...]
-    scratch[1] = peer[...]
-    scratch[2] = side[:TILE, :]
-    scratch[3] = side[TILE:, :]
-
-
-def stats_kernel(depth, steps, me_ref, anc_ref, q_own, q_peer, q_side, *rest):
+def stats_kernel(depth, tiles, steps, me_ref, anc_ref, *rest):
+    if tiles[0] == 0:
+        (q_own, q_peer), rest = rest[:2], rest[2:]
+    else:
+        q_side, rest = rest[0], rest[1:]
     k_refs = rest[:steps]
     lse_ref, q_all, k_all, item_max, item_sum, *items = rest[steps:]
     me = me_ref[0]
-    gather_queries(q_all, q_own, q_peer, q_side)
+    if tiles[0] == 0:
+        q_all[0] = q_own[...]
+        q_all[1] = q_peer[...]
+    else:
+        q_all[0] = q_side[:TILE, :]
+        q_all[1] = q_side[TILE:, :]
     for shift, k_ref in enumerate(k_refs):
         k_all[shift * LEVEL : (shift + 1) * LEVEL, :] = k_ref[...]
-    count = list_items(items, anc_ref, me, range(QUAD), depth, "all")
+    count = list_items(items, anc_ref, me, tiles, depth, "all")
     tile_of, first_of, second_of, flags_of = items
 
     def one_item(index):
@@ -168,7 +170,7 @@
     lax.fori_loop(0, count, combine, 0)
 
 
-def grads_kernel(depth, stage, steps, me_ref, anc_ref, q_own, q_peer, q_side, g_own, g_peer, g_side, d_own, d_peer, d_side, lse_ref, *rest):
+def grads_kernel(depth, stage, steps, me_ref, anc_ref, q_own, q_peer, q_side, g_own, g_peer, g_side, d_own, d_peer, d_side, lse_own, lse_side, *rest):
     kv_refs, rest = rest[: 2 * steps], rest[2 * steps :]
     if stage != "far":
         dq_in, rest = rest[0], rest[1:]
@@ -182,8 +184,8 @@
     else:
         dq_own, dq_peer, partial_refs, rest = rest[0], rest[1], rest[2 : 2 + steps], rest[2 + steps :]
     items, rest = rest[:4], rest[4:]
-    q_all, g_all, delta, k_all, v_all = rest[:5]
-    buffers, rest = ((rest[5], rest[6]), (rest[7], rest[8])), rest[9:]
+    q_all, g_all, delta, lse_all, k_all, v_all = rest[:6]
+    buffers, rest = ((rest[6], rest[7]), (rest[8], rest[9])), rest[10:]
     if stage != "side":
         dk_acc, dv_acc, rest = rest[0], rest[1], rest[2:]
     if stage != "far":
@@ -201,6 +203,7 @@
             cols = slice(head * TILE, (head + 1) * TILE)
             d_ref, row = ((d_own, 0), (d_peer, 0), (d_side, 0), (d_side, GROUP))[u]
             delta[place, :, cols] = d_ref[row + head : row + head + 1, :]
+        lse_all[place] = (lse_own, lse_side)[u // 2][u % 2]
     for shift in range(steps):
         k_all[shift * LEVEL : (shift + 1) * LEVEL, :] = kv_refs[shift][...]
         v_all[shift * LEVEL : (shift + 1) * LEVEL, :] = kv_refs[steps + shift][...]
@@ -238,7 +241,7 @@
                 NT_DIMS,
                 preferred_element_type=jnp.float32,
             )
-            lse = lse_ref[tiles[0] + place, :, rows]
+            lse = lse_all[place, :, rows]
             away = delta[place, :, rows]
             for part in range(2):
                 half = slice(part * TILE, (part + 1) * TILE)
@@ -311,37 +314,37 @@
 WIDE = pl.BlockSpec((TILE, ROWS), lambda i, me_ref, anc_ref: (0, own_head(me_ref)))
 SMALL = pl.BlockSpec((GROUP, TILE), lambda i, me_ref, anc_ref: (own_head(me_ref), 0))
 SIDE = fixed((PAIR, ROWS))
-LSE = fixed((QUAD, 1, ROWS))
+LSE = fixed((2, 1, ROWS))
 KEYS = fixed((LEVEL, HD))
 SUMS = fixed((LEVEL, 2 * HD))
 DQ = fixed((QUAD, HD, ROWS))
 WIDE_OUT = fixed((TILE, ROWS))
 
 
-def statistics(me, ancestors, q_set, k_list):
+def statistics(tiles, me, ancestors, queries, k_list):
     steps = len(k_list)
-    items = item_scratch(QUAD, ancestors.shape[1])
+    items = item_scratch(2, ancestors.shape[1])
     count = items[0].shape[0]
     return pl.pallas_call(
-        functools.partial(stats_kernel, ancestors.shape[1], steps),
+        functools.partial(stats_kernel, ancestors.shape[1], tiles, steps),
         grid_spec=pltpu.PrefetchScalarGridSpec(
             num_scalar_prefetch=2,
             grid=(1,),
-            in_specs=[WIDE, WIDE, SIDE] + [KEYS] * steps,
+            in_specs=([WIDE, WIDE] if tiles[0] == 0 else [SIDE]) + [KEYS] * steps,
             out_specs=LSE,
             scratch_shapes=[
-                pltpu.VMEM((QUAD, TILE, ROWS), jnp.bfloat16),
+                pltpu.VMEM((2, TILE, ROWS), jnp.bfloat16),
                 pltpu.VMEM((steps * LEVEL, HD), jnp.bfloat16),
                 pltpu.VMEM((count, 1, ROWS), jnp.float32),
                 pltpu.VMEM((count, 1, ROWS), jnp.float32),
                 *items,
             ],
         ),
-        out_shape=jax.ShapeDtypeStruct((QUAD, 1, ROWS), jnp.float32),
+        out_shape=jax.ShapeDtypeStruct((2, 1, ROWS), jnp.float32),
         compiler_params=PARAMS,
         cost_estimate=work(ancestors, 1),
-        name="statistics",
-    )(me, ancestors, *q_set, *k_list)
+        name="own_stats" if tiles[0] == 0 else "side_stats",
+    )(me, ancestors, *queries, *k_list)
 
 
 def gradients(stage, me, ancestors, q_set, g_set, d_set, lse, k_list, v_list, *carried):
@@ -367,6 +370,7 @@
         pltpu.VMEM((tiles, TILE, ROWS), jnp.bfloat16),
         pltpu.VMEM((tiles, TILE, ROWS), jnp.bfloat16),
         pltpu.VMEM((tiles, 1, ROWS), jnp.float32),
+        pltpu.VMEM((tiles, 1, ROWS), jnp.float32),
         pltpu.VMEM(acc, jnp.bfloat16),
         pltpu.VMEM(acc, jnp.bfloat16),
     ]
@@ -380,7 +384,7 @@
         grid_spec=pltpu.PrefetchScalarGridSpec(
             num_scalar_prefetch=2,
             grid=(1,),
-            in_specs=[WIDE, WIDE, SIDE, WIDE, WIDE, SIDE, SMALL, SMALL, fixed((2 * GROUP, TILE)), LSE]
+            in_specs=[WIDE, WIDE, SIDE, WIDE, WIDE, SIDE, SMALL, SMALL, fixed((2 * GROUP, TILE)), LSE, LSE]
             + [KEYS] * (2 * steps)
             + extra_specs,
             out_specs=out_specs,
@@ -390,7 +394,7 @@
         compiler_params=PARAMS,
         cost_estimate=work(ancestors, 5),
         name=stage + "_grads",
-    )(me, ancestors, *q_set, *g_set, *d_set, lse, *k_list, *v_list, *carried)
+    )(me, ancestors, *q_set, *g_set, *d_set, *lse, *k_list, *v_list, *carried)
 
 
 def side_head(me_ref):
@@ -401,47 +405,72 @@
     return pl.ds(pl.multiple_of(head * width, width), width)
 
 
-def pack_keys_kernel(me_ref, k_own, v_own, k_peer, v_peer, mine_ref, send_ref):
+SCALARS = pl.BlockSpec(memory_space=pltpu.SMEM)
+HERE = pl.BlockSpec(memory_space=pltpu.VMEM)
+
+
+def pack_own_kernel(me_ref, k_own, v_own, mine_ref, send_ref):
     for head, out_ref in ((own_head(me_ref), mine_ref), (side_head(me_ref), send_ref)):
         at = head_columns(head, HD)
         out_ref[:TILE, :HD] = k_own[:, at]
         out_ref[:TILE, HD:] = v_own[:, at]
+
+
+def pack_peer_kernel(me_ref, k_peer, v_peer, mine_in, send_in, mine_ref, send_ref):
+    for head, in_ref, out_ref in (
+        (own_head(me_ref), mine_in, mine_ref),
+        (side_head(me_ref), send_in, send_ref),
+    ):
+        at = head_columns(head, HD)
+        out_ref[:TILE, :] = in_ref[:TILE, :]
         out_ref[TILE:, :HD] = k_peer[:, at]
         out_ref[TILE:, HD:] = v_peer[:, at]
 
 
-SCALARS = pl.BlockSpec(memory_space=pltpu.SMEM)
-HERE = pl.BlockSpec(memory_space=pltpu.VMEM)
-
-
-def pack_keys(me, *arrays):
-    return pl.pallas_call(
-        pack_keys_kernel,
-        in_specs=[SCALARS] + [HERE] * 4,
+def pack_keys(name, kernel, *arrays):
+    return pl.pallas_call(
+        kernel,
+        in_specs=[SCALARS] + [HERE] * (len(arrays) - 1),
         out_specs=[HERE] * 2,
         out_shape=[jax.ShapeDtypeStruct((PAIR, 2 * HD), jnp.bfloat16)] * 2,
         compiler_params=SMALL_PARAMS,
-        name="pack_keys",
-    )(me, *arrays)
-
-
-def pack_queries_kernel(me_ref, q_own, q_peer, g_own, g_peer, q_ref, g_ref):
+        name=name,
+    )(*arrays)
+
+
+def pack_queries_kernel(me_ref, own, peer, send_ref):
     at = head_columns(side_head(me_ref), ROWS)
-    q_ref[:TILE, :] = q_own[:, at]
-    q_ref[TILE:, :] = q_peer[:, at]
-    g_ref[:TILE, :] = g_own[:, at]
-    g_ref[TILE:, :] = g_peer[:, at]
-
-
-def pack_queries(me, *arrays):
+    send_ref[:TILE, :] = own[:, at]
+    send_ref[TILE:, :] = peer[:, at]
+
+
+def pack_queries(me, own, peer):
     return pl.pallas_call(
         pack_queries_kernel,
-        in_specs=[SCALARS] + [HERE] * 4,
+        in_specs=[SCALARS, HERE, HERE],
+        out_specs=HERE,
+        out_shape=jax.ShapeDtypeStruct((PAIR, ROWS), jnp.bfloat16),
+        compiler_params=SMALL_PARAMS,
+        name="pack_queries",
+    )(me, own, peer)
+
+
+def join_keys_kernel(chip_ref, side_ref, k_ref, v_ref):
+    for place, ref in enumerate((chip_ref, side_ref)):
+        rows = slice(place * PAIR, (place + 1) * PAIR)
+        k_ref[rows, :] = ref[:, :HD]
+        v_ref[rows, :] = ref[:, HD:]
+
+
+def join_keys(chip, side):
+    return pl.pallas_call(
+        join_keys_kernel,
+        in_specs=[HERE] * 2,
         out_specs=[HERE] * 2,
-        out_shape=[jax.ShapeDtypeStruct((PAIR, ROWS), jnp.bfloat16)] * 2,
-        compiler_params=SMALL_PARAMS,
-        name="pack_queries",
-    )(me, *arrays)
+        out_shape=[jax.ShapeDtypeStruct((LEVEL, HD), jnp.bfloat16)] * 2,
+        compiler_params=SMALL_PARAMS,
+        name="join_keys",
+    )(chip, side)
 
 
 def pack_deltas_kernel(me_ref, d_own, d_peer, send_ref):
@@ -566,12 +595,15 @@
     def to_side(x):
         return lax.ppermute(x, "side", [(0, 1), (1, 0)])
 
+    def after(x, done):
+        return lax.optimization_barrier((x, done))[0]
+
     def up(x, shift):
         return lax.ppermute(x, "level", [(z, z + shift) for z in range(steps - shift)])
 
-    def up_all(x):
-        arrivals = [x] + [up(x, shift) for shift in range(1, min(steps, 3))]
-        for shift in range(3, steps):
+    def up_chain(x):
+        arrivals = [x]
+        for shift in range(1, steps):
             pairs = [(z, z + 1) for z in range(shift - 1, steps - 1)]
             arrivals.append(lax.ppermute(arrivals[-1], "level", pairs))
         return arrivals
@@ -579,21 +611,25 @@
     def down(x, shift):
         return lax.ppermute(x, "level", [(z + shift, z) for z in range(steps - shift)])
 
-    kv_chip, kv_send = pack_keys(me, keys, values, to_peer(keys), to_peer(values))
+    k_peer, v_peer = to_peer(keys), to_peer(values)
+    own_parts = pack_keys("pack_own", pack_own_kernel, me, keys, values)
+    kv_chip, kv_send = pack_keys("pack_peer", pack_peer_kernel, me, k_peer, v_peer, *own_parts)
     kv_side = to_side(kv_send)
-    k_level = jnp.concatenate([kv_chip[:, :HD], kv_side[:, :HD]], axis=0)
-    v_level = jnp.concatenate([kv_chip[:, HD:], kv_side[:, HD:]], axis=0)
-    k_list = up_all(k_level)
-    q_peer, g_peer = to_peer(queries), to_peer(out_grad)
-    q_send, g_send = pack_queries(me, queries, q_peer, out_grad, g_peer)
+    q_peer = to_peer(after(queries, own_parts))
+    q_send = pack_queries(me, queries, q_peer)
     q_set = (queries, q_peer, to_side(q_send))
-    v_list = up_all(v_level)
-    g_set = (out_grad, g_peer, to_side(g_send))
-    deltas = row_deltas(outputs, out_grad, kv_send)
+    k_level, v_level = join_keys(kv_chip, after(kv_side, q_send))
+    k_list = up_chain(k_level)
+    g_peer = to_peer(after(out_grad, k_list[1]))
+    v_level = after(v_level, k_list[2])
+    v_list = [v_level] + [up(v_level, shift) for shift in range(1, steps)]
+    g_set = (out_grad, g_peer, to_side(after(pack_queries(me, out_grad, g_peer), k_list[1])))
+    deltas = row_deltas(outputs, out_grad, k_list[2])
     d_peer = to_peer(deltas)
     d_set = (deltas, d_peer, to_side(pack_deltas(me, deltas, d_peer)))
 
-    lse = statistics(me, ancestors, q_set, k_list)
+    lse = [statistics((0, 1), me, ancestors, q_set[:2], k_list)]
+    lse.append(statistics((2, 3), me, ancestors, q_set[2:], after(k_list, lse[0])))
     common = (me, ancestors, q_set, g_set, d_set, lse)
     dq_far, *far = gradients("far", *common, k_list[2:], v_list[2:])
     back = [down(far[shift - 2], shift) for shift in range(2, steps)]
@@ -604,13 +640,14 @@
     )
     total, near = add_far(total, back, near)
     near = down(near, 1)
-    dq_peer = to_peer(dq_peer)
 
     sum_own, sum_peer, sum_side = add_sums(total, near)
-    dq_far = to_peer(dq_side[TILE:])
+    dq_peer = to_peer(after(dq_peer, total))
     sum_peer = to_peer(sum_peer)
     sum_side = to_side(sum_side)
     sum_far = to_peer(sum_side[TILE:])
+    dq_side = after(dq_side, sum_side)
+    dq_far = to_peer(dq_side[TILE:])
     return (
         place_queries(me, dq_own, dq_side, dq_peer, dq_far),
         *place_keys(me, sum_own, sum_side, sum_peer, sum_far),

time: 93.4 us -> 98.3 us (1.052)
  starting transfers between devices: 27.2 us -> 37.7 us
  waiting for transfers between devices: 43 us -> 40.2 us
  local copies, waits for them, and re-layouts: 4.32 us -> 2.31 us
    ppermute x3, waiting for transfers between devices: 28.6 us -> 21 us  [down(): lax.ppermute(x, 'level', [(z + shift, z) for z in range(steps - shift)])]
    ppermute x6, waiting for transfers between devices: 5.67 us -> 13.1 us  [to_side(): return lax.ppermute(x, 'side', [(0, 1), (1, 0)])]
    ppermute x6, starting transfers between devices: 5.69 us -> 10.6 us  [to_side(): return lax.ppermute(x, 'side', [(0, 1), (1, 0)])]
    ppermute x2 -> x3, starting transfers between devices: 1.34 us -> 5.16 us  [up_chain(): arrivals.append(lax.ppermute(arrivals[-1], 'level', pairs))]
    ppermute x4 -> x3, waiting for transfers between devices: 3.69 us -> 0.01 us  [up(): lax.ppermute(x, 'level', [(z, z + shift) for z in range(steps - shift)])]
    ppermute x2 -> x3, waiting for transfers between devices: 0.01 us -> 2.5 us  [up_chain(): arrivals.append(lax.ppermute(arrivals[-1], 'level', pairs))]
    unnamed x16 -> x12, local copies, waits for them, and re-layouts: 4.27 us -> 2.29 us
    pallas_call x3 -> x7, Pallas kernels: 3.41 us -> 5.01 us  [the longest x2 3.93 us: statistics(): pl.pallas_call(functools.partial(stats_kernel, ancestors.shape[1], tiles,...]
  transfers between devices with their start and end apart: 24 -> 24, of which waited for: 9 -> 10; matrix products, arithmetic and copies ran while one was open for 0% -> 0% of each run, Pallas kernels for 17% -> 15%
where the time goes in v6:
time: 98.3 us
  waiting for transfers between devices  40.2 us (41%)
  starting transfers between devices  37.7 us (38%)
  Pallas kernels  17.2 us (17%)
  local copies, waits for them, and re-layouts  2.31 us (2%)
    ppermute x3, waiting for transfers between devices, down(): lax.ppermute(x, 'level', [(z + shift, z) for z in range(steps - shift)])  21 us
    ppermute x3, starting transfers between devices, up(): lax.ppermute(x, 'level', [(z, z + shift) for z in range(steps - shift)])  16.1 us
    ppermute x6, waiting for transfers between devices, to_side(): return lax.ppermute(x, 'side', [(0, 1), (1, 0)])  13.1 us
    ppermute x6, starting transfers between devices, to_side(): return lax.ppermute(x, 'side', [(0, 1), (1, 0)])  10.6 us
    pallas_call x3, Pallas kernels, gradients(): pl.pallas_call(functools.partial(grads_kernel, ancestors.shape[1], stage,...  9.65 us
    ppermute x3, starting transfers between devices, up_chain(): arrivals.append(lax.ppermute(arrivals[-1], 'level', pairs))  5.16 us
    pallas_call x2, Pallas kernels, statistics(): pl.pallas_call(functools.partial(stats_kernel, ancestors.shape[1], tiles,...  3.93 us
    ppermute x3, starting transfers between devices, down(): lax.ppermute(x, 'level', [(z + shift, z) for z in range(steps - shift)])  3.88 us
  transfers between devices with their start and end apart: 24, of which 10 were waited for; matrix products, arithmetic and copies ran while one was open for 0% of the time, Pallas kernels for 15%

profile of v6, /device:TPU:0, one launch (start us, length us, event | category | flops | bytes accessed | tf_op | source)
XLA Modules:
  0.0 98.3 jit_solution(4683822088472283200)
XLA Ops:
  0.7 0.0 copy-start.4
  0.7 1.0 %copy-done.4 = bf16[128,512]{1,0:T(8,128)(2,1)S(1)} copy-done((bf16[128,512]{1,0:T(8,128)(2,1)S(1)}, bf16[128,512]{1,0:T(8,128)(2,1)}, u32[]{:S(2)}) %copy-start.4) | copy-done | bytes 131096
  1.7 0.9 pack_own.1
  2.6 0.5 collective-permute-start
  3.2 0.1 collective-permute-start.2
  3.2 0.4 collective-permute-start.3
  3.7 2.2 %collective-permute-done.2.k_peer = bf16[128,512]{1,0:T(8,128)(2,1)S(1)} collective-permute-done((bf16[128,512]{1,0:T(8,128)(2,1)}, bf16[128,512]{1,0:T(8,128)(2,1)S(1)}, u32[]{:S(2)}, u32[]{:S(2)}) %collective-permute-start.2) | collective-permute-done | bytes 131104 | tf_op jit(solution)/shard_map/ppermute | solution.py:593
  5.8 0.2 collective-permute-done.3.v_peer
  6.1 3.0 %collective-permute-start.4 = (bf16[256,256]{1,0:T(8,128)(2,1)S(1)}, bf16[256,256]{1,0:T(8,128)(2,1)S(1)}, u32[]{:S(2)}, u32[]{:S(2)}) collective-permute-start(bf16[256,256]{1,0:T(8,128)(2,1)S(1)} %get-tuple-element.41), channel_id=1, source_target_pairs={{0,2},{2,0},{1,3},{3,1},{4,6},{6,4},{5,7},{7,5},{8,10},{10,8},{9,1... | collective-permute-start | bytes 393224 | tf_op jit(solution)/shard_map/ppermute | solution.py:596
  9.0 0.0 collective-permute-done.peer.rest_1_.q_peer
  9.0 1.2 %copy-done.2 = bf16[128,4096]{1,0:T(8,128)(2,1)S(1)} copy-done((bf16[128,4096]{1,0:T(8,128)(2,1)S(1)}, bf16[128,4096]{1,0:T(8,128)(2,1)}, u32[]{:S(2)}) %copy-start.2) | copy-done | bytes 1048600
  10.3 2.5 %collective-permute-done.4.side_ref = bf16[256,256]{1,0:T(8,128)(2,1)S(1)} collective-permute-done((bf16[256,256]{1,0:T(8,128)(2,1)S(1)}, bf16[256,256]{1,0:T(8,128)(2,1)S(1)}, u32[]{:S(2)}, u32[]{:S(2)}) %collective-permute-start.4) | collective-permute-done | bytes 131104 | tf_op jit(solution)/shard_map/ppermute | solution.py:596
  12.9 0.0 copy-start.3
  12.9 0.0 copy-start.5
  12.9 3.8 %collective-permute-start.5 = (bf16[512,128]{1,0:T(8,128)(2,1)S(1)}, bf16[512,128]{1,0:T(8,128)(2,1)S(1)}, u32[]{:S(2)}, u32[]{:S(2)}) collective-permute-start(bf16[512,128]{1,0:T(8,128)(2,1)S(1)} %get-tuple-element.46.rest_2_.rest_1_.rest_0_), channel_id=1, source_target_pairs={{0,4},{4,8},{8,12},{1,5},{5,9},{9,13},{2,6},{6,10},{10,14},{3,7},{... | collective-permute-start | bytes 393224 | tf_op jit(solution)/shard_map/ppermute | solution.py:608
  16.7 2.5 %collective-permute-done.5.rest_3_.rest_2_.rest_1_ = bf16[512,128]{1,0:T(8,128)(2,1)S(1)} collective-permute-done((bf16[512,128]{1,0:T(8,128)(2,1)S(1)}, bf16[512,128]{1,0:T(8,128)(2,1)S(1)}, u32[]{:S(2)}, u32[]{:S(2)}) %collective-permute-start.5) | collective-permute-done | bytes 131104 | tf_op jit(solution)/shard_map/ppermute | solution.py:608
  19.2 0.0 collective-permute-start.6
  19.2 0.7 collective-permute-start.8
  19.9 1.6 %collective-permute-start.1 = (bf16[256,1024]{1,0:T(8,128)(2,1)S(1)}, bf16[256,1024]{1,0:T(8,128)(2,1)S(1)}, u32[]{:S(2)}, u32[]{:S(2)}) collective-permute-start(bf16[256,1024]{1,0:T(8,128)(2,1)S(1)} %pack_queries.2), channel_id=1, source_target_pairs={{0,2},{2,0},{1,3},{3,1},{4,6},{6,4},{5,7},{7,5},{8,10},{10,8},{9,1... | collective-permute-start | bytes 1572872 | tf_op jit(solution)/shard_map/ppermute | solution.py:596
  21.5 0.0 collective-permute-done.8.after_ref.rest_4_.rest_3_.rest_0_
  21.5 0.7 collective-permute-start.11
  22.2 0.6 row_deltas.1.d_own
  22.8 0.3 collective-permute-start.9
  23.1 12.3 %collective-permute-start.14 = (bf16[512,128]{1,0:T(8,128)(2,1)S(1)}, bf16[512,128]{1,0:T(8,128)(2,1)S(1)}, u32[]{:S(2)}, u32[]{:S(2)}) collective-permute-start(bf16[512,128]{1,0:T(8,128)(2,1)S(1)} %get-tuple-element.51.rest_2_), channel_id=1, source_target_pairs={{0,12},{1,13},{2,14},{3,15},{16,28},{17,29},{18,30},{19,31}} | collective-permute-start | bytes 393224 | tf_op jit(solution)/shard_map/ppermute | solution.py:602
  35.4 0.0 collective-permute-done.9.d_peer
  35.4 2.3 %collective-permute-start.13 = (bf16[512,128]{1,0:T(8,128)(2,1)S(1)}, bf16[512,128]{1,0:T(8,128)(2,1)S(1)}, u32[]{:S(2)}, u32[]{:S(2)}) collective-permute-start(bf16[512,128]{1,0:T(8,128)(2,1)S(1)} %get-tuple-element.51.rest_2_), channel_id=1, source_target_pairs={{0,8},{4,12},{1,9},{5,13},{2,10},{6,14},{3,11},{7,15},{16,24},{20,... | collective-permute-start | bytes 393224 | tf_op jit(solution)/shard_map/ppermute | solution.py:602
  37.8 0.0 collective-permute-done.6.peer.g_peer
  37.8 1.4 %collective-permute-start.12 = (bf16[512,128]{1,0:T(8,128)(2,1)S(1)}, bf16[512,128]{1,0:T(8,128)(2,1)S(1)}, u32[]{:S(2)}, u32[]{:S(2)}) collective-permute-start(bf16[512,128]{1,0:T(8,128)(2,1)S(1)} %get-tuple-element.51.rest_2_), channel_id=1, source_target_pairs={{0,4},{4,8},{8,12},{1,5},{5,9},{9,13},{2,6},{6,10},{10,14},{3,7},{... | collective-permute-start | bytes 393224 | tf_op jit(solution)/shard_map/ppermute | solution.py:602
  39.3 0.0 collective-permute-done.11.rest_5_.rest_4_.rest_1_
  39.3 1.6 %collective-permute-start.7 = (bf16[256,1024]{1,0:T(8,128)(2,1)S(1)}, bf16[256,1024]{1,0:T(8,128)(2,1)S(1)}, u32[]{:S(2)}, u32[]{:S(2)}) collective-permute-start(bf16[256,1024]{1,0:T(8,128)(2,1)S(1)} %pack_queries.3), channel_id=1, source_target_pairs={{0,2},{2,0},{1,3},{3,1},{4,6},{6,4},{5,7},{7,5},{8,10},{10,8},{9,1... | collective-permute-start | bytes 1572872 | tf_op jit(solution)/shard_map/ppermute | solution.py:596
  40.9 1.6 %own_stats.1.lse_own = f32[2,1,1024]{2,1,0:T(1,128)S(1)} custom-call(s32[1]{0:T(128)} %bitcast.me_ref, s32[16,10]{1,0:T(8,128)S(1)} %copy-done.5, bf16[128,4096]{1,0:T(8,128)(2,1)S(1)} %copy-done.3, bf16[128,4096]{1,0:T(8,128)(2,1)S(1)} %collective-permute-done.peer.rest_1_.q_peer, bf16[512,128]{1,0:T(8,128)(2,1)S(1)} %get-tuple-element.46.rest_2_.rest_1_.rest_0_, ...), custom_call_target="tpu_custom_call" | custom-call | flops 2952790016 | bytes 16777216 | tf_op jit(solution)/shard_map/own_stats/pallas_call | solution.py:328
  42.5 0.0 collective-permute-done.1.rest_0_.q_side
  42.5 1.3 %collective-permute-start.10 = (f32[16,128]{1,0:T(8,128)S(1)}, f32[16,128]{1,0:T(8,128)S(1)}, u32[]{:S(2)}, u32[]{:S(2)}) collective-permute-start(f32[16,128]{1,0:T(8,128)S(1)} %pack_deltas.1), channel_id=1, source_target_pairs={{0,2},{2,0},{1,3},{3,1},{4,6},{6,4},{5,7},{7,5},{8,10},{10,8},{9,1... | collective-permute-start | bytes 24584 | tf_op jit(solution)/shard_map/ppermute | solution.py:596
  43.8 2.4 %side_stats.1.lse_side = f32[2,1,1024]{2,1,0:T(1,128)S(1)} custom-call(s32[1]{0:T(128)} %bitcast.me_ref, s32[16,10]{1,0:T(8,128)S(1)} %copy-done.5, bf16[256,1024]{1,0:T(8,128)(2,1)S(1)} %collective-permute-done.1.rest_0_.q_side, bf16[512,128]{1,0:T(8,128)(2,1)S(1)} %get-tuple-element.46.rest_2_.rest_1_.rest_0_, ...), custom_call_target="tpu_custom_call" | custom-call | flops 2952790016 | bytes 16777216 | tf_op jit(solution)/shard_map/side_stats/pallas_call | solution.py:328
  46.2 7.1 %collective-permute-done.10.d_side = f32[16,128]{1,0:T(8,128)S(1)} collective-permute-done((f32[16,128]{1,0:T(8,128)S(1)}, f32[16,128]{1,0:T(8,128)S(1)}, u32[]{:S(2)}, u32[]{:S(2)}) %collective-permute-start.10) | collective-permute-done | bytes 8224 | tf_op jit(solution)/shard_map/ppermute | solution.py:596
  53.3 0.0 collective-permute-done.14.rest_3_
  53.3 0.0 collective-permute-done.13.rest_2_
  53.3 0.0 collective-permute-done.7.g_side
  53.3 1.4 %far_grads.1 = (f32[4,128,1024]{2,1,0:T(8,128)S(1)}, bf16[512,256]{1,0:T(8,128)(2,1)S(1)}, bf16[512,256]{1,0:T(8,128)(2,1)S(1)}) custom-call(s32[1]{0:T(128)} %bitcast.me_ref, s32[16,10]{1,0:T(8,128)S(1)} %copy-done.5, bf16[128,4096]{1,0:T(8,128)(2,1)S(1)} %copy-done.3, bf16[128,4096]{1,0:T(8,128)(2,1)S(1)} %collective-permute-done.peer.rest_1_.q_peer, ...), custom_call_target="tpu_custom_call" | custom-call | flops 14763950080 | bytes 16777216 | tf_op jit(solution)/shard_map/far_grads/pallas_call | solution.py:382
  54.7 1.3 %collective-permute-start.16 = (bf16[512,256]{1,0:T(8,128)(2,1)S(1)}, bf16[512,256]{1,0:T(8,128)(2,1)S(1)}, u32[]{:S(2)}, u32[]{:S(2)}) collective-permute-start(bf16[512,256]{1,0:T(8,128)(2,1)S(1)} %get-tuple-element.58), channel_id=1, source_target_pairs={{8,0},{12,4},{9,1},{13,5},{10,2},{14,6},{11,3},{15,7},{24,16},{28,... | collective-permute-start | bytes 786440 | tf_op jit(solution)/shard_map/ppermute | solution.py:612
  56.0 1.3 %collective-permute-start.17 = (bf16[512,256]{1,0:T(8,128)(2,1)S(1)}, bf16[512,256]{1,0:T(8,128)(2,1)S(1)}, u32[]{:S(2)}, u32[]{:S(2)}) collective-permute-start(bf16[512,256]{1,0:T(8,128)(2,1)S(1)} %get-tuple-element.59), channel_id=1, source_target_pairs={{12,0},{13,1},{14,2},{15,3},{28,16},{29,17},{30,18},{31,19}} | collective-permute-start | bytes 786440 | tf_op jit(solution)/shard_map/ppermute | solution.py:612
  57.3 0.0 collective-permute-done.12.rest_3_
  57.3 4.2 %side_grads.1 = (bf16[256,1024]{1,0:T(8,128)(2,1)S(1)}, f32[1024,128]{1,0:T(8,128)S(1)}, f32[1024,128]{1,0:T(8,128)S(1)}) custom-call(s32[1]{0:T(128)} %bitcast.me_ref, s32[16,10]{1,0:T(8,128)S(1)} %copy-done.5, bf16[128,4096]{1,0:T(8,128)(2,1)S(1)} %copy-done.3, bf16[128,4096]{1,0:T(8,128)(2,1)S(1)} %collective-permute-done.peer.rest_1_.q_peer, ...), custom_call_target="tpu_custom_call" | custom-call | flops 14763950080 | bytes 16777216 | tf_op jit(solution)/shard_map/side_grads/pallas_call | solution.py:382
  61.4 1.6 %collective-permute-start.15 = (bf16[256,1024]{1,0:T(8,128)(2,1)S(1)}, bf16[256,1024]{1,0:T(8,128)(2,1)S(1)}, u32[]{:S(2)}, u32[]{:S(2)}) collective-permute-start(bf16[256,1024]{1,0:T(8,128)(2,1)S(1)} %get-tuple-element.56), channel_id=1, source_target_pairs={{0,2},{2,0},{1,3},{3,1},{4,6},{6,4},{5,7},{7,5},{8,10},{10,8},{9,1... | collective-permute-start | bytes 1572872 | tf_op jit(solution)/shard_map/ppermute | solution.py:596
  63.0 4.1 %own_grads.1 = (bf16[128,1024]{1,0:T(8,128)(2,1)S(1)}, bf16[128,1024]{1,0:T(8,128)(2,1)S(1)}, f32[512,256]{1,0:T(8,128)S(1)}, bf16[512,256]{1,0:T(8,128)(2,1)S(1)}) custom-call(s32[1]{0:T(128)} %bitcast.me_ref, s32[16,10]{1,0:T(8,128)S(1)} %copy-done.5, bf16[128,4096]{1,0:T(8,128)(2,1)S(1)} %copy-done.3, ...), custom_call_target="tpu_custom_call" | custom-call | flops 14763950080 | bytes 16777216 | tf_op jit(solution)/shard_map/own_grads/pallas_call | solution.py:382
  67.2 13.1 %collective-permute-done.16.refs_0_ = bf16[512,256]{1,0:T(8,128)(2,1)S(1)} collective-permute-done((bf16[512,256]{1,0:T(8,128)(2,1)S(1)}, bf16[512,256]{1,0:T(8,128)(2,1)S(1)}, u32[]{:S(2)}, u32[]{:S(2)}) %collective-permute-start.16) | collective-permute-done | bytes 262176 | tf_op jit(solution)/shard_map/ppermute | solution.py:612
  80.3 0.0 collective-permute-done.17.refs_1_
  80.3 0.1 add_far.1
  80.4 1.3 %collective-permute-start.18 = (bf16[512,256]{1,0:T(8,128)(2,1)S(1)}, bf16[512,256]{1,0:T(8,128)(2,1)S(1)}, u32[]{:S(2)}, u32[]{:S(2)}) collective-permute-start(bf16[512,256]{1,0:T(8,128)(2,1)S(1)} %get-tuple-element.62), channel_id=1, source_target_pairs={{4,0},{8,4},{12,8},{5,1},{9,5},{13,9},{6,2},{10,6},{14,10},{7,3},{... | collective-permute-start | bytes 786440 | tf_op jit(solution)/shard_map/ppermute | solution.py:612
  81.7 7.9 %collective-permute-done.18.near_ref = bf16[512,256]{1,0:T(8,128)(2,1)S(1)} collective-permute-done((bf16[512,256]{1,0:T(8,128)(2,1)S(1)}, bf16[512,256]{1,0:T(8,128)(2,1)S(1)}, u32[]{:S(2)}, u32[]{:S(2)}) %collective-permute-start.18) | collective-permute-done | bytes 262176 | tf_op jit(solution)/shard_map/ppermute | solution.py:612
  89.6 0.1 add_sums.1
  89.6 1.6 %collective-permute-start.19 = (bf16[256,256]{1,0:T(8,128)(2,1)S(1)}, bf16[256,256]{1,0:T(8,128)(2,1)S(1)}, u32[]{:S(2)}, u32[]{:S(2)}) collective-permute-start(bf16[256,256]{1,0:T(8,128)(2,1)S(1)} %get-tuple-element.63), channel_id=1, source_target_pairs={{0,2},{2,0},{1,3},{3,1},{4,6},{6,4},{5,7},{7,5},{8,10},{10,8},{9,1... | collective-permute-start | bytes 393224 | tf_op jit(solution)/shard_map/ppermute | solution.py:596
  91.2 0.0 collective-permute-start.20
  91.2 0.0 collective-permute-done.15.side
  91.2 3.4 %collective-permute-done.19.side = bf16[256,256]{1,0:T(8,128)(2,1)S(1)} collective-permute-done((bf16[256,256]{1,0:T(8,128)(2,1)S(1)}, bf16[256,256]{1,0:T(8,128)(2,1)S(1)}, u32[]{:S(2)}, u32[]{:S(2)}) %collective-permute-start.19) | collective-permute-done | bytes 131104 | tf_op jit(solution)/shard_map/ppermute | solution.py:596
  94.7 0.1 collective-permute-start.21
  94.8 0.5 collective-permute-start.22
  95.3 0.1 collective-permute-start.23
  95.4 1.0 %collective-permute-done.22.peer = bf16[128,256]{1,0:T(8,128)(2,1)S(1)} collective-permute-done((bf16[128,256]{1,0:T(8,128)(2,1)S(1)}, bf16[128,256]{1,0:T(8,128)(2,1)S(1)}, u32[]{:S(2)}, u32[]{:S(2)}) %collective-permute-start.22) | collective-permute-done | bytes 65568 | tf_op jit(solution)/shard_map/ppermute | solution.py:593
  96.4 0.1 collective-permute-done.23.far
  96.5 0.7 place_keys.1
  97.3 0.0 collective-permute-done.20.peer
  97.3 0.0 collective-permute-done.21.far
  97.3 1.0 %place_queries.1 = bf16[128,4096]{1,0:T(8,128)(2,1)} custom-call(s32[1]{0:T(128)} %bitcast.me_ref, bf16[128,1024]{1,0:T(8,128)(2,1)S(1)} %get-tuple-element.55.own, bf16[256,1024]{1,0:T(8,128)(2,1)S(1)} %collective-permute-done.15.side, bf16[128,1024]{1,0:T(8,128)(2,1)S(1)} %collective-permute-done.20.peer, bf16[128,1024]{1,0:T(8,128)(2,1)S(1)} %collective-permute-done.21.far), custom_call_target="tpu_custom_call" | custom-call | tf_op jit(solution)/shard_map/place_queries/pallas_call | solution.py:560
  (14 shorter events, 0.2 us)
Async XLA Ops:
  0.6 18.6 %copy-start = (bf16[128,4096]{1,0:T(8,128)(2,1)S(1)}, bf16[128,4096]{1,0:T(8,128)(2,1)}, u32[]{:S(2)}) copy-start(bf16[128,4096]{1,0:T(8,128)(2,1)} %g_own.5) | copy-start | bytes 3145732
  0.6 21.5 %copy-start.1 = (bf16[128,4096]{1,0:T(8,128)(2,1)S(1)}, bf16[128,4096]{1,0:T(8,128)(2,1)}, u32[]{:S(2)}) copy-start(bf16[128,4096]{1,0:T(8,128)(2,1)} %out_ref.1) | copy-start | bytes 3145732
  0.7 1.1 %copy-start.4 = (bf16[128,512]{1,0:T(8,128)(2,1)S(1)}, bf16[128,512]{1,0:T(8,128)(2,1)}, u32[]{:S(2)}) copy-start(bf16[128,512]{1,0:T(8,128)(2,1)} %v_own.1) | copy-start | bytes 393220
  2.6 6.4 %collective-permute-start = (bf16[128,4096]{1,0:T(8,128)(2,1)}, bf16[128,4096]{1,0:T(8,128)(2,1)S(1)}, u32[]{:S(2)}, u32[]{:S(2)}) collective-permute-start(bf16[128,4096]{1,0:T(8,128)(2,1)} %q_own.5), channel_id=1, source_target_pairs={{0,1},{1,0},{2,3},{3,2},{4,5},{5,4},{6,7},{7,6},{8,9},{9,8},{10,11... | collective-permute-start | bytes 3145736 | tf_op jit(solution)/shard_map/ppermute | solution.py:593
  3.2 2.7 %collective-permute-start.2 = (bf16[128,512]{1,0:T(8,128)(2,1)}, bf16[128,512]{1,0:T(8,128)(2,1)S(1)}, u32[]{:S(2)}, u32[]{:S(2)}) collective-permute-start(bf16[128,512]{1,0:T(8,128)(2,1)} %k_own.1), channel_id=1, source_target_pairs={{0,1},{1,0},{2,3},{3,2},{4,5},{5,4},{6,7},{7,6},{8,9},{9,8},{10,11... | collective-permute-start | bytes 393224 | tf_op jit(solution)/shard_map/ppermute | solution.py:593
  3.2 2.8 %collective-permute-start.3 = (bf16[128,512]{1,0:T(8,128)(2,1)}, bf16[128,512]{1,0:T(8,128)(2,1)S(1)}, u32[]{:S(2)}, u32[]{:S(2)}) collective-permute-start(bf16[128,512]{1,0:T(8,128)(2,1)} %v_own.1), channel_id=1, source_target_pairs={{0,1},{1,0},{2,3},{3,2},{4,5},{5,4},{6,7},{7,6},{8,9},{9,8},{10,11... | collective-permute-start | bytes 393224 | tf_op jit(solution)/shard_map/ppermute | solution.py:593
  6.1 6.8 %collective-permute-start.4 = (bf16[256,256]{1,0:T(8,128)(2,1)S(1)}, bf16[256,256]{1,0:T(8,128)(2,1)S(1)}, u32[]{:S(2)}, u32[]{:S(2)}) collective-permute-start(bf16[256,256]{1,0:T(8,128)(2,1)S(1)} %get-tuple-element.41), channel_id=1, source_target_pairs={{0,2},{2,0},{1,3},{3,1},{4,6},{6,4},{5,7},{7,5},{8,10},{10,8},{9,1... | collective-permute-start | bytes 393224 | tf_op jit(solution)/shard_map/ppermute | solution.py:596
  9.0 1.2 %copy-start.2 = (bf16[128,4096]{1,0:T(8,128)(2,1)S(1)}, bf16[128,4096]{1,0:T(8,128)(2,1)}, u32[]{:S(2)}) copy-start(bf16[128,4096]{1,0:T(8,128)(2,1)} %q_own.5) | copy-start | bytes 3145732
  12.9 28.0 %copy-start.3 = (bf16[128,4096]{1,0:T(8,128)(2,1)S(1)}, bf16[128,4096]{1,0:T(8,128)(2,1)}, u32[]{:S(2)}) copy-start(bf16[128,4096]{1,0:T(8,128)(2,1)} %q_own.5) | copy-start | bytes 3145732
  12.9 28.0 %copy-start.5 = (s32[16,10]{1,0:T(8,128)S(1)}, s32[16,10]{1,0:T(8,128)}, u32[]{:S(2)}) copy-start(s32[16,10]{1,0:T(8,128)} %anc_ref.9) | copy-start | bytes 1924
  12.9 6.3 %collective-permute-start.5 = (bf16[512,128]{1,0:T(8,128)(2,1)S(1)}, bf16[512,128]{1,0:T(8,128)(2,1)S(1)}, u32[]{:S(2)}, u32[]{:S(2)}) collective-permute-start(bf16[512,128]{1,0:T(8,128)(2,1)S(1)} %get-tuple-element.46.rest_2_.rest_1_.rest_0_), channel_id=1, source_target_pairs={{0,4},{4,8},{8,12},{1,5},{5,9},{9,13},{2,6},{6,10},{10,14},{3,7},{... | collective-permute-start | bytes 393224 | tf_op jit(solution)/shard_map/ppermute | solution.py:608
  19.2 18.5 %collective-permute-start.6 = (bf16[128,4096]{1,0:T(8,128)(2,1)S(1)}, bf16[128,4096]{1,0:T(8,128)(2,1)S(1)}, u32[]{:S(2)}, u32[]{:S(2)}) collective-permute-start(bf16[128,4096]{1,0:T(8,128)(2,1)S(1)} %copy-done), channel_id=1, source_target_pairs={{0,1},{1,0},{2,3},{3,2},{4,5},{5,4},{6,7},{7,6},{8,9},{9,8},{10,11... | collective-permute-start | bytes 3145736 | tf_op jit(solution)/shard_map/ppermute | solution.py:593
  19.2 2.3 %collective-permute-start.8 = (bf16[512,128]{1,0:T(8,128)(2,1)S(1)}, bf16[512,128]{1,0:T(8,128)(2,1)S(1)}, u32[]{:S(2)}, u32[]{:S(2)}) collective-permute-start(bf16[512,128]{1,0:T(8,128)(2,1)S(1)} %collective-permute-done.5.rest_3_.rest_2_.rest_1_), channel_id=1, source_target_pairs={{4,8},{8,12},{5,9},{9,13},{6,10},{10,14},{7,11},{11,15},{20,24},{2... | collective-permute-start | bytes 393224 | tf_op jit(solution)/shard_map/ppermute | solution.py:608
  19.9 22.6 %collective-permute-start.1 = (bf16[256,1024]{1,0:T(8,128)(2,1)S(1)}, bf16[256,1024]{1,0:T(8,128)(2,1)S(1)}, u32[]{:S(2)}, u32[]{:S(2)}) collective-permute-start(bf16[256,1024]{1,0:T(8,128)(2,1)S(1)} %pack_queries.2), channel_id=1, source_target_pairs={{0,2},{2,0},{1,3},{3,1},{4,6},{6,4},{5,7},{7,5},{8,10},{10,8},{9,1... | collective-permute-start | bytes 1572872 | tf_op jit(solution)/shard_map/ppermute | solution.py:596
  21.5 17.8 %collective-permute-start.11 = (bf16[512,128]{1,0:T(8,128)(2,1)S(1)}, bf16[512,128]{1,0:T(8,128)(2,1)S(1)}, u32[]{:S(2)}, u32[]{:S(2)}) collective-permute-start(bf16[512,128]{1,0:T(8,128)(2,1)S(1)} %collective-permute-done.8.after_ref.rest_4_.rest_3_.rest_0_), channel_id=1, source_target_pairs={{8,12},{9,13},{10,14},{11,15},{24,28},{25,29},{26,30},{27,31}} | collective-permute-start | bytes 393224 | tf_op jit(solution)/shard_map/ppermute | solution.py:608
  22.8 12.6 %collective-permute-start.9 = (f32[32,128]{1,0:T(8,128)S(1)}, f32[32,128]{1,0:T(8,128)S(1)}, u32[]{:S(2)}, u32[]{:S(2)}) collective-permute-start(f32[32,128]{1,0:T(8,128)S(1)} %row_deltas.1.d_own), channel_id=1, source_target_pairs={{0,1},{1,0},{2,3},{3,2},{4,5},{5,4},{6,7},{7,6},{8,9},{9,8},{10,11... | collective-permute-start | bytes 49160 | tf_op jit(solution)/shard_map/ppermute | solution.py:593
  23.1 30.2 %collective-permute-start.14 = (bf16[512,128]{1,0:T(8,128)(2,1)S(1)}, bf16[512,128]{1,0:T(8,128)(2,1)S(1)}, u32[]{:S(2)}, u32[]{:S(2)}) collective-permute-start(bf16[512,128]{1,0:T(8,128)(2,1)S(1)} %get-tuple-element.51.rest_2_), channel_id=1, source_target_pairs={{0,12},{1,13},{2,14},{3,15},{16,28},{17,29},{18,30},{19,31}} | collective-permute-start | bytes 393224 | tf_op jit(solution)/shard_map/ppermute | solution.py:602
  35.4 17.9 %collective-permute-start.13 = (bf16[512,128]{1,0:T(8,128)(2,1)S(1)}, bf16[512,128]{1,0:T(8,128)(2,1)S(1)}, u32[]{:S(2)}, u32[]{:S(2)}) collective-permute-start(bf16[512,128]{1,0:T(8,128)(2,1)S(1)} %get-tuple-element.51.rest_2_), channel_id=1, source_target_pairs={{0,8},{4,12},{1,9},{5,13},{2,10},{6,14},{3,11},{7,15},{16,24},{20,... | collective-permute-start | bytes 393224 | tf_op jit(solution)/shard_map/ppermute | solution.py:602
  37.8 19.5 %collective-permute-start.12 = (bf16[512,128]{1,0:T(8,128)(2,1)S(1)}, bf16[512,128]{1,0:T(8,128)(2,1)S(1)}, u32[]{:S(2)}, u32[]{:S(2)}) collective-permute-start(bf16[512,128]{1,0:T(8,128)(2,1)S(1)} %get-tuple-element.51.rest_2_), channel_id=1, source_target_pairs={{0,4},{4,8},{8,12},{1,5},{5,9},{9,13},{2,6},{6,10},{10,14},{3,7},{... | collective-permute-start | bytes 393224 | tf_op jit(solution)/shard_map/ppermute | solution.py:602
  39.3 14.0 %collective-permute-start.7 = (bf16[256,1024]{1,0:T(8,128)(2,1)S(1)}, bf16[256,1024]{1,0:T(8,128)(2,1)S(1)}, u32[]{:S(2)}, u32[]{:S(2)}) collective-permute-start(bf16[256,1024]{1,0:T(8,128)(2,1)S(1)} %pack_queries.3), channel_id=1, source_target_pairs={{0,2},{2,0},{1,3},{3,1},{4,6},{6,4},{5,7},{7,5},{8,10},{10,8},{9,1... | collective-permute-start | bytes 1572872 | tf_op jit(solution)/shard_map/ppermute | solution.py:596
  42.5 10.8 %collective-permute-start.10 = (f32[16,128]{1,0:T(8,128)S(1)}, f32[16,128]{1,0:T(8,128)S(1)}, u32[]{:S(2)}, u32[]{:S(2)}) collective-permute-start(f32[16,128]{1,0:T(8,128)S(1)} %pack_deltas.1), channel_id=1, source_target_pairs={{0,2},{2,0},{1,3},{3,1},{4,6},{6,4},{5,7},{7,5},{8,10},{10,8},{9,1... | collective-permute-start | bytes 24584 | tf_op jit(solution)/shard_map/ppermute | solution.py:596
  54.7 25.6 %collective-permute-start.16 = (bf16[512,256]{1,0:T(8,128)(2,1)S(1)}, bf16[512,256]{1,0:T(8,128)(2,1)S(1)}, u32[]{:S(2)}, u32[]{:S(2)}) collective-permute-start(bf16[512,256]{1,0:T(8,128)(2,1)S(1)} %get-tuple-element.58), channel_id=1, source_target_pairs={{8,0},{12,4},{9,1},{13,5},{10,2},{14,6},{11,3},{15,7},{24,16},{28,... | collective-permute-start | bytes 786440 | tf_op jit(solution)/shard_map/ppermute | solution.py:612
  56.0 24.3 %collective-permute-start.17 = (bf16[512,256]{1,0:T(8,128)(2,1)S(1)}, bf16[512,256]{1,0:T(8,128)(2,1)S(1)}, u32[]{:S(2)}, u32[]{:S(2)}) collective-permute-start(bf16[512,256]{1,0:T(8,128)(2,1)S(1)} %get-tuple-element.59), channel_id=1, source_target_pairs={{12,0},{13,1},{14,2},{15,3},{28,16},{29,17},{30,18},{31,19}} | collective-permute-start | bytes 786440 | tf_op jit(solution)/shard_map/ppermute | solution.py:612
  61.4 29.8 %collective-permute-start.15 = (bf16[256,1024]{1,0:T(8,128)(2,1)S(1)}, bf16[256,1024]{1,0:T(8,128)(2,1)S(1)}, u32[]{:S(2)}, u32[]{:S(2)}) collective-permute-start(bf16[256,1024]{1,0:T(8,128)(2,1)S(1)} %get-tuple-element.56), channel_id=1, source_target_pairs={{0,2},{2,0},{1,3},{3,1},{4,6},{6,4},{5,7},{7,5},{8,10},{10,8},{9,1... | collective-permute-start | bytes 1572872 | tf_op jit(solution)/shard_map/ppermute | solution.py:596
  80.4 9.2 %collective-permute-start.18 = (bf16[512,256]{1,0:T(8,128)(2,1)S(1)}, bf16[512,256]{1,0:T(8,128)(2,1)S(1)}, u32[]{:S(2)}, u32[]{:S(2)}) collective-permute-start(bf16[512,256]{1,0:T(8,128)(2,1)S(1)} %get-tuple-element.62), channel_id=1, source_target_pairs={{4,0},{8,4},{12,8},{5,1},{9,5},{13,9},{6,2},{10,6},{14,10},{7,3},{... | collective-permute-start | bytes 786440 | tf_op jit(solution)/shard_map/ppermute | solution.py:612
  89.6 5.0 %collective-permute-start.19 = (bf16[256,256]{1,0:T(8,128)(2,1)S(1)}, bf16[256,256]{1,0:T(8,128)(2,1)S(1)}, u32[]{:S(2)}, u32[]{:S(2)}) collective-permute-start(bf16[256,256]{1,0:T(8,128)(2,1)S(1)} %get-tuple-element.63), channel_id=1, source_target_pairs={{0,2},{2,0},{1,3},{3,1},{4,6},{6,4},{5,7},{7,5},{8,10},{10,8},{9,1... | collective-permute-start | bytes 393224 | tf_op jit(solution)/shard_map/ppermute | solution.py:596
  91.2 6.1 %collective-permute-start.20 = (bf16[128,1024]{1,0:T(8,128)(2,1)S(1)}, bf16[128,1024]{1,0:T(8,128)(2,1)S(1)}, u32[]{:S(2)}, u32[]{:S(2)}) collective-permute-start(bf16[128,1024]{1,0:T(8,128)(2,1)S(1)} %get-tuple-element.66), channel_id=1, source_target_pairs={{0,1},{1,0},{2,3},{3,2},{4,5},{5,4},{6,7},{7,6},{8,9},{9,8},{10,11... | collective-permute-start | bytes 786440 | tf_op jit(solution)/shard_map/ppermute | solution.py:593
  94.7 2.6 %collective-permute-start.21 = (bf16[128,1024]{1,0:T(8,128)(2,1)S(1)}, bf16[128,1024]{1,0:T(8,128)(2,1)S(1)}, u32[]{:S(2)}, u32[]{:S(2)}) collective-permute-start(bf16[128,1024]{1,0:T(8,128)(2,1)S(1)} %slice.6), channel_id=1, source_target_pairs={{0,1},{1,0},{2,3},{3,2},{4,5},{5,4},{6,7},{7,6},{8,9},{9,8},{10,11... | collective-permute-start | bytes 786440 | tf_op jit(solution)/shard_map/ppermute | solution.py:593
  94.8 1.6 %collective-permute-start.22 = (bf16[128,256]{1,0:T(8,128)(2,1)S(1)}, bf16[128,256]{1,0:T(8,128)(2,1)S(1)}, u32[]{:S(2)}, u32[]{:S(2)}) collective-permute-start(bf16[128,256]{1,0:T(8,128)(2,1)S(1)} %get-tuple-element.68), channel_id=1, source_target_pairs={{0,1},{1,0},{2,3},{3,2},{4,5},{5,4},{6,7},{7,6},{8,9},{9,8},{10,11... | collective-permute-start | bytes 196616 | tf_op jit(solution)/shard_map/ppermute | solution.py:593
  95.3 1.3 %collective-permute-start.23 = (bf16[128,256]{1,0:T(8,128)(2,1)S(1)}, bf16[128,256]{1,0:T(8,128)(2,1)S(1)}, u32[]{:S(2)}, u32[]{:S(2)}) collective-permute-start(bf16[128,256]{1,0:T(8,128)(2,1)S(1)} %slice.8), channel_id=1, source_target_pairs={{0,1},{1,0},{2,3},{3,2},{4,5},{5,4},{6,7},{7,6},{8,9},{9,8},{10,11... | collective-permute-start | bytes 196616 | tf_op jit(solution)/shard_map/ppermute | solution.py:593

commit v7 on v5

--- a/solution.py
+++ b/solution.py
@@ -21,26 +21,31 @@
 SCALE = HD ** (-0.5)
 SCALE2 = SCALE / math.log(2.0)
 MASKED = -1e30
+SCALARS = pl.BlockSpec(memory_space=pltpu.SMEM)
+HERE = pl.BlockSpec(memory_space=pltpu.VMEM)
 NT_DIMS = (((1,), (1,)), ((), ()))
 PARAMS = pltpu.CompilerParams(vmem_limit_bytes=28 * 1024 * 1024)
 SMALL_PARAMS = pltpu.CompilerParams(vmem_limit_bytes=16 * 1024 * 1024)
 
 
-def delta_kernel(out_ref, grad_ref, after_ref, delta_ref):
-    for head in range(QH):
-        cols = slice(head * HD, (head + 1) * HD)
-        product = out_ref[:, cols].astype(jnp.float32) * grad_ref[:, cols].astype(jnp.float32)
-        delta_ref[head : head + 1, :] = jnp.sum(product.T, axis=0, keepdims=True)
-
-
-def row_deltas(outputs, out_grad, after):
+def delta_kernel(me_ref, out_ref, grad_ref, after_ref, *delta_refs):
+    for flip, delta_ref in enumerate(delta_refs):
+        base = (own_head(me_ref) ^ flip) * ROWS
+        for head in range(GROUP):
+            cols = pl.ds(pl.multiple_of(base + head * HD, HD), HD)
+            product = out_ref[:, cols].astype(jnp.float32) * grad_ref[:, cols].astype(jnp.float32)
+            delta_ref[head : head + 1, :] = jnp.sum(product.T, axis=0, keepdims=True)
+
+
+def row_deltas(me, outputs, out_grad, after):
     return pl.pallas_call(
         delta_kernel,
-        in_specs=[pl.BlockSpec(memory_space=pltpu.VMEM)] * 2 + [pl.BlockSpec(memory_space=pl.ANY)],
-        out_shape=jax.ShapeDtypeStruct((QH, TILE), jnp.float32),
+        in_specs=[SCALARS, HERE, HERE, pl.BlockSpec(memory_space=pl.ANY)],
+        out_specs=[HERE] * QUAD,
+        out_shape=[jax.ShapeDtypeStruct((GROUP, TILE), jnp.float32)] * QUAD,
         compiler_params=SMALL_PARAMS,
         name="row_deltas",
-    )(outputs, out_grad, after)
+    )(me, outputs, out_grad, after)
 
 
 def list_items(items, anc_ref, me, tiles, depth, part):
@@ -107,18 +112,13 @@
     return key_pos - query_pos <= jnp.where((flags & 4) != 0, 0, TILE)
 
 
-def gather_queries(scratch, own, peer, side):
-    scratch[0] = own[...]
-    scratch[1] = peer[...]
-    scratch[2] = side[:TILE, :]
-    scratch[3] = side[TILE:, :]
-
-
-def stats_kernel(depth, steps, me_ref, anc_ref, q_own, q_peer, q_side, *rest):
+def stats_kernel(depth, steps, me_ref, anc_ref, *rest):
+    q_refs, rest = rest[:QUAD], rest[QUAD:]
     k_refs = rest[:steps]
     lse_ref, q_all, k_all, item_max, item_sum, *items = rest[steps:]
     me = me_ref[0]
-    gather_queries(q_all, q_own, q_peer, q_side)
+    for u, q_ref in enumerate(q_refs):
+        q_all[u] = q_ref[...]
     for shift, k_ref in enumerate(k_refs):
         k_all[shift * LEVEL : (shift + 1) * LEVEL, :] = k_ref[...]
     count = list_items(items, anc_ref, me, range(QUAD), depth, "all")
@@ -168,7 +168,9 @@
     lax.fori_loop(0, count, combine, 0)
 
 
-def grads_kernel(depth, stage, steps, me_ref, anc_ref, q_own, q_peer, q_side, g_own, g_peer, g_side, d_own, d_peer, d_side, lse_ref, *rest):
+def grads_kernel(depth, stage, steps, me_ref, anc_ref, *rest):
+    q_refs, g_refs, d_refs, rest = rest[:4], rest[4:8], rest[8:12], rest[12:]
+    lse_ref, rest = rest[0], rest[1:]
     kv_refs, rest = rest[: 2 * steps], rest[2 * steps :]
     if stage != "far":
         dq_in, rest = rest[0], rest[1:]
@@ -178,9 +180,10 @@
     if stage == "far":
         dq_acc, partial_refs, rest = rest[0], rest[1 : 1 + steps], rest[1 + steps :]
     elif stage == "side":
-        dq_side, dk_acc, dv_acc, rest = rest[0], rest[1], rest[2], rest[3:]
+        dq_refs = (rest[0].at[:TILE, :], rest[0].at[TILE:, :])
+        dk_acc, dv_acc, rest = rest[1], rest[2], rest[3:]
     else:
-        dq_own, dq_peer, partial_refs, rest = rest[0], rest[1], rest[2 : 2 + steps], rest[2 + steps :]
+        dq_refs, partial_refs, rest = rest[:2], rest[2 : 2 + steps], rest[2 + steps :]
     items, rest = rest[:4], rest[4:]
     q_all, g_all, delta, k_all, v_all = rest[:5]
     buffers, rest = ((rest[5], rest[6]), (rest[7], rest[8])), rest[9:]
@@ -190,17 +193,11 @@
         dq_acc = rest[0]
     me = me_ref[0]
     for place, u in enumerate(tiles):
-        if u < 2:
-            q_all[place] = (q_own, q_peer)[u][...]
-            g_all[place] = (g_own, g_peer)[u][...]
-        else:
-            rows = slice((u - 2) * TILE, (u - 1) * TILE)
-            q_all[place] = q_side[rows, :]
-            g_all[place] = g_side[rows, :]
+        q_all[place] = q_refs[u][...]
+        g_all[place] = g_refs[u][...]
         for head in range(GROUP):
             cols = slice(head * TILE, (head + 1) * TILE)
-            d_ref, row = ((d_own, 0), (d_peer, 0), (d_side, 0), (d_side, GROUP))[u]
-            delta[place, :, cols] = d_ref[row + head : row + head + 1, :]
+            delta[place, :, cols] = d_refs[u][head : head + 1, :]
     for shift in range(steps):
         k_all[shift * LEVEL : (shift + 1) * LEVEL, :] = kv_refs[shift][...]
         v_all[shift * LEVEL : (shift + 1) * LEVEL, :] = kv_refs[steps + shift][...]
@@ -279,11 +276,7 @@
         for place in range(2):
             for head in range(GROUP):
                 cols = slice(head * HD, (head + 1) * HD)
-                turned = (dq_acc[place, :, cols] * SCALE).T.astype(jnp.bfloat16)
-                if stage == "side":
-                    dq_side[place * TILE : (place + 1) * TILE, cols] = turned
-                else:
-                    (dq_own, dq_peer)[place][:, cols] = turned
+                dq_refs[place][:, cols] = (dq_acc[place, :, cols] * SCALE).T.astype(jnp.bfloat16)
     if stage != "side":
         for shift, out_ref in enumerate(partial_refs):
             rows = slice(shift * LEVEL, (shift + 1) * LEVEL)
@@ -309,13 +302,12 @@
 
 
 WIDE = pl.BlockSpec((TILE, ROWS), lambda i, me_ref, anc_ref: (0, own_head(me_ref)))
-SMALL = pl.BlockSpec((GROUP, TILE), lambda i, me_ref, anc_ref: (own_head(me_ref), 0))
-SIDE = fixed((PAIR, ROWS))
 LSE = fixed((QUAD, 1, ROWS))
 KEYS = fixed((LEVEL, HD))
 SUMS = fixed((LEVEL, 2 * HD))
 DQ = fixed((QUAD, HD, ROWS))
-WIDE_OUT = fixed((TILE, ROWS))
+PIECE = fixed((TILE, ROWS))
+SIDE = fixed((PAIR, ROWS))
 
 
 def statistics(me, ancestors, q_set, k_list):
@@ -327,7 +319,7 @@
         grid_spec=pltpu.PrefetchScalarGridSpec(
             num_scalar_prefetch=2,
             grid=(1,),
-            in_specs=[WIDE, WIDE, SIDE] + [KEYS] * steps,
+            in_specs=[WIDE] + [PIECE] * 3 + [KEYS] * steps,
             out_specs=LSE,
             scratch_shapes=[
                 pltpu.VMEM((QUAD, TILE, ROWS), jnp.bfloat16),
@@ -361,7 +353,7 @@
         out_shape = [jax.ShapeDtypeStruct((PAIR, ROWS), jnp.bfloat16)] + accs
     else:
         sums[0] = jax.ShapeDtypeStruct((LEVEL, 2 * HD), jnp.float32)
-        out_specs = [WIDE_OUT, WIDE_OUT] + [SUMS] * steps
+        out_specs = [PIECE, PIECE] + [SUMS] * steps
         out_shape = [wide, wide] + sums
     scratch = item_scratch(tiles, ancestors.shape[1]) + [
         pltpu.VMEM((tiles, TILE, ROWS), jnp.bfloat16),
@@ -380,7 +372,7 @@
         grid_spec=pltpu.PrefetchScalarGridSpec(
             num_scalar_prefetch=2,
             grid=(1,),
-            in_specs=[WIDE, WIDE, SIDE, WIDE, WIDE, SIDE, SMALL, SMALL, fixed((2 * GROUP, TILE)), LSE]
+            in_specs=([WIDE] + [PIECE] * 3) * 2 + [fixed((GROUP, TILE))] * 4 + [LSE]
             + [KEYS] * (2 * steps)
             + extra_specs,
             out_specs=out_specs,
@@ -393,76 +385,61 @@
     )(me, ancestors, *q_set, *g_set, *d_set, lse, *k_list, *v_list, *carried)
 
 
-def side_head(me_ref):
-    return own_head(me_ref) ^ 1
-
-
 def head_columns(head, width):
     return pl.ds(pl.multiple_of(head * width, width), width)
 
 
-def pack_keys_kernel(me_ref, k_own, v_own, k_peer, v_peer, mine_ref, send_ref):
-    for head, out_ref in ((own_head(me_ref), mine_ref), (side_head(me_ref), send_ref)):
-        at = head_columns(head, HD)
-        out_ref[:TILE, :HD] = k_own[:, at]
-        out_ref[:TILE, HD:] = v_own[:, at]
-        out_ref[TILE:, :HD] = k_peer[:, at]
-        out_ref[TILE:, HD:] = v_peer[:, at]
-
-
-SCALARS = pl.BlockSpec(memory_space=pltpu.SMEM)
-HERE = pl.BlockSpec(memory_space=pltpu.VMEM)
-
-
-def pack_keys(me, *arrays):
+def pack_keys_kernel(me_ref, keys, values, *out_refs):
+    for flip, out_ref in enumerate(out_refs):
+        at = head_columns(own_head(me_ref) ^ flip, HD)
+        out_ref[:, :HD] = keys[:, at]
+        out_ref[:, HD:] = values[:, at]
+
+
+def pack_keys(me, keys, values):
     return pl.pallas_call(
         pack_keys_kernel,
-        in_specs=[SCALARS] + [HERE] * 4,
+        in_specs=[SCALARS, HERE, HERE],
+        out_specs=[HERE] * QUAD,
+        out_shape=[jax.ShapeDtypeStruct((TILE, 2 * HD), jnp.bfloat16)] * QUAD,
+        compiler_params=SMALL_PARAMS,
+        name="pack_keys",
+    )(me, keys, values)
+
+
+def join_keys_kernel(*refs):
+    k_ref, v_ref = refs[-2:]
+    for place, ref in enumerate(refs[:-2]):
+        rows = slice(place * TILE, (place + 1) * TILE)
+        k_ref[rows, :] = ref[:, :HD]
+        v_ref[rows, :] = ref[:, HD:]
+
+
+def join_keys(*pieces):
+    return pl.pallas_call(
+        join_keys_kernel,
+        in_specs=[HERE] * QUAD,
         out_specs=[HERE] * 2,
-        out_shape=[jax.ShapeDtypeStruct((PAIR, 2 * HD), jnp.bfloat16)] * 2,
-        compiler_params=SMALL_PARAMS,
-        name="pack_keys",
-    )(me, *arrays)
-
-
-def pack_queries_kernel(me_ref, q_own, q_peer, g_own, g_peer, q_ref, g_ref):
-    at = head_columns(side_head(me_ref), ROWS)
-    q_ref[:TILE, :] = q_own[:, at]
-    q_ref[TILE:, :] = q_peer[:, at]
-    g_ref[:TILE, :] = g_own[:, at]
-    g_ref[TILE:, :] = g_peer[:, at]
-
-
-def pack_queries(me, *arrays):
+        out_shape=[jax.ShapeDtypeStruct((LEVEL, HD), jnp.bfloat16)] * 2,
+        compiler_params=SMALL_PARAMS,
+        name="join_keys",
+    )(*pieces)
+
+
+def pack_queries_kernel(me_ref, whole, *out_refs):
+    for flip, out_ref in enumerate(out_refs):
+        out_ref[...] = whole[:, head_columns(own_head(me_ref) ^ (flip + 1), ROWS)]
+
+
+def pack_queries(me, whole):
     return pl.pallas_call(
         pack_queries_kernel,
-        in_specs=[SCALARS] + [HERE] * 4,
-        out_specs=[HERE] * 2,
-        out_shape=[jax.ShapeDtypeStruct((PAIR, ROWS), jnp.bfloat16)] * 2,
+        in_specs=[SCALARS, HERE],
+        out_specs=[HERE] * 3,
+        out_shape=[jax.ShapeDtypeStruct((TILE, ROWS), jnp.bfloat16)] * 3,
         compiler_params=SMALL_PARAMS,
         name="pack_queries",
-    )(me, *arrays)
-
-
-def pack_deltas_kernel(me_ref, d_own, d_peer, send_ref):
-    send_ref[:GROUP, :] = d_own[...]
-    send_ref[GROUP:, :] = d_peer[...]
-
-
-def pack_deltas(me, deltas, d_peer):
-    away = pl.BlockSpec((GROUP, TILE), lambda i, me_ref: (side_head(me_ref), 0))
-    return pl.pallas_call(
-        pack_deltas_kernel,
-        grid_spec=pltpu.PrefetchScalarGridSpec(
-            num_scalar_prefetch=1,
-            grid=(1,),
-            in_specs=[away] * 2,
-            out_specs=fixed((2 * GROUP, TILE)),
-        ),
-        out_shape=jax.ShapeDtypeStruct((2 * GROUP, TILE), jnp.float32),
-        compiler_params=SMALL_PARAMS,
-        name="pack_deltas",
-    )(me, deltas, d_peer)
+    )(me, whole)
 
 
 def add_far_kernel(total_ref, *refs):
@@ -490,41 +467,30 @@
     )(acc, *parts, passing)
 
 
-def add_sums_kernel(total_ref, near_ref, own_ref, peer_ref, send_ref):
+def add_sums_kernel(total_ref, near_ref, *out_refs):
     total = total_ref[...] + near_ref[...].astype(jnp.float32)
     scaled = jnp.concatenate([total[:, :HD] * SCALE, total[:, HD:]], axis=1).astype(jnp.bfloat16)
-    own_ref[...] = scaled[:TILE]
-    peer_ref[...] = scaled[TILE:PAIR]
-    send_ref[...] = scaled[PAIR:]
+    for place, out_ref in enumerate(out_refs):
+        out_ref[...] = scaled[place * TILE : (place + 1) * TILE]
 
 
 def add_sums(total, near):
-    here = pl.BlockSpec(memory_space=pltpu.VMEM)
     return pl.pallas_call(
         add_sums_kernel,
-        in_specs=[here] * 2,
-        out_specs=[here] * 3,
-        out_shape=[
-            jax.ShapeDtypeStruct((TILE, 2 * HD), jnp.bfloat16),
-            jax.ShapeDtypeStruct((TILE, 2 * HD), jnp.bfloat16),
-            jax.ShapeDtypeStruct((PAIR, 2 * HD), jnp.bfloat16),
-        ],
+        in_specs=[HERE] * 2,
+        out_specs=[HERE] * QUAD,
+        out_shape=[jax.ShapeDtypeStruct((TILE, 2 * HD), jnp.bfloat16)] * QUAD,
         compiler_params=SMALL_PARAMS,
         name="add_sums",
     )(total, near)
 
 
-def placed(me_ref, width):
-    head = own_head(me_ref)
-    return [head_columns(head ^ flip, width) for flip in range(4)]
-
-
-def place_queries_kernel(me_ref, own, side, peer, far, dq_ref):
-    at = placed(me_ref, ROWS)
-    dq_ref[:, at[0]] = own[...]
-    dq_ref[:, at[1]] = side[:TILE, :]
-    dq_ref[:, at[2]] = peer[...]
-    dq_ref[:, at[3]] = far[...]
+FLIPS = (0, 2, 1, 3)
+
+
+def place_queries_kernel(me_ref, *refs):
+    for flip, piece in zip(FLIPS, refs[:-1]):
+        refs[-1][:, head_columns(own_head(me_ref) ^ flip, ROWS)] = piece[:TILE, :]
 
 
 def place_queries(me, *pieces):
@@ -538,11 +504,12 @@
     )(me, *pieces)
 
 
-def place_keys_kernel(me_ref, own, side, peer, far, dk_ref, dv_ref):
-    at = placed(me_ref, HD)
-    for spot, part in zip(at, (own[...], side[:TILE, :], peer[...], far[...])):
-        dk_ref[:, spot] = part[:, :HD]
-        dv_ref[:, spot] = part[:, HD:]
+def place_keys_kernel(me_ref, *refs):
+    dk_ref, dv_ref = refs[-2:]
+    for flip, piece in zip(FLIPS, refs[:-2]):
+        at = head_columns(own_head(me_ref) ^ flip, HD)
+        dk_ref[:, at] = piece[:, :HD]
+        dv_ref[:, at] = piece[:, HD:]
 
 
 def place_keys(me, *pieces):
@@ -560,60 +527,54 @@
     level, side, core = (lax.axis_index(name) for name in ("level", "side", "core"))
     me = (QUAD * level + 2 * side + core).reshape(1).astype(jnp.int32)
 
-    def to_peer(x):
-        return lax.ppermute(x, "core", [(0, 1), (1, 0)])
-
-    def to_side(x):
-        return lax.ppermute(x, "side", [(0, 1), (1, 0)])
+    def to_partner(x, flip):
+        return lax.ppermute(x, ("side", "core"), [(t, t ^ flip) for t in range(QUAD)])
+
+    def after(x, done):
+        return lax.optimization_barrier((x, done))[0]
 
     def up(x, shift):
         return lax.ppermute(x, "level", [(z, z + shift) for z in range(steps - shift)])
 
     def up_all(x):
-        arrivals = [x] + [up(x, shift) for shift in range(1, min(steps, 3))]
-        for shift in range(3, steps):
-            pairs = [(z, z + 1) for z in range(shift - 1, steps - 1)]
-            arrivals.append(lax.ppermute(arrivals[-1], "level", pairs))
-        return arrivals
+        return [x] + [up(x, shift) for shift in range(1, steps)]
 
     def down(x, shift):
         return lax.ppermute(x, "level", [(z + shift, z) for z in range(steps - shift)])
 
-    kv_chip, kv_send = pack_keys(me, keys, values, to_peer(keys), to_peer(values))
-    kv_side = to_side(kv_send)
-    k_level = jnp.concatenate([kv_chip[:, :HD], kv_side[:, :HD]], axis=0)
-    v_level = jnp.concatenate([kv_chip[:, HD:], kv_side[:, HD:]], axis=0)
+    def exchange(by_head):
+        mine, beside, across, corner = by_head
+        return [mine, to_partner(across, 1), to_partner(beside, 2), to_partner(corner, 3)]
+
+    kv_quad = exchange(pack_keys(me, keys, values))
+    q_sent = pack_queries(me, after(queries, kv_quad[1]))
+    q_set = exchange([queries, *q_sent])
+    k_level, v_level = join_keys(*after(kv_quad, q_sent))
     k_list = up_all(k_level)
-    q_peer, g_peer = to_peer(queries), to_peer(out_grad)
-    q_send, g_send = pack_queries(me, queries, q_peer, out_grad, g_peer)
-    q_set = (queries, q_peer, to_side(q_send))
-    v_list = up_all(v_level)
-    g_set = (out_grad, g_peer, to_side(g_send))
-    deltas = row_deltas(outputs, out_grad, kv_send)
-    d_peer = to_peer(deltas)
-    d_set = (deltas, d_peer, to_side(pack_deltas(me, deltas, d_peer)))
+    v_list = up_all(after(v_level, k_list))
+    g_set = exchange([out_grad, *pack_queries(me, after(out_grad, q_set[2]))])
+    d_set = exchange(row_deltas(me, outputs, out_grad, after(k_list[1], k_list)))
 
     lse = statistics(me, ancestors, q_set, k_list)
     common = (me, ancestors, q_set, g_set, d_set, lse)
     dq_far, *far = gradients("far", *common, k_list[2:], v_list[2:])
     back = [down(far[shift - 2], shift) for shift in range(2, steps)]
     dq_side, *accs = gradients("side", *common, k_list[:2], v_list[:2], dq_far)
-    dq_side = to_side(dq_side)
-    dq_own, dq_peer, total, near = gradients(
+    dq_side = to_partner(dq_side, 2)
+    dq_own, dq_core, total, near = gradients(
         "own", *common, k_list[:2], v_list[:2], dq_far, *accs
     )
     total, near = add_far(total, back, near)
     near = down(near, 1)
-    dq_peer = to_peer(dq_peer)
-
-    sum_own, sum_peer, sum_side = add_sums(total, near)
-    dq_far = to_peer(dq_side[TILE:])
-    sum_peer = to_peer(sum_peer)
-    sum_side = to_side(sum_side)
-    sum_far = to_peer(sum_side[TILE:])
+    dq_core = to_partner(dq_core, 1)
+
+    sums = add_sums(total, near)
+    sums = [sums[0]] + [to_partner(sums[flip], flip) for flip in range(1, QUAD)]
+    dq_side = after(dq_side, sums)
+    dq_corner = to_partner(dq_side[TILE:], 1)
     return (
-        place_queries(me, dq_own, dq_side, dq_peer, dq_far),
-        *place_keys(me, sum_own, sum_side, sum_peer, sum_far),
+        place_queries(me, dq_own, dq_core, dq_side, dq_corner),
+        *place_keys(me, *sums),
     )
 
 

time: 93.4 us -> 96.3 us (1.031); the launches traced: 92.7 us -> 97.6 us
  starting transfers between devices: 27.2 us -> 40.2 us
  waiting for transfers between devices: 43 us -> 36.4 us
  Pallas kernels: 17.1 us -> 15.7 us
    ppermute x4 -> x6, starting transfers between devices: 14.5 us -> 23 us  [up(): lax.ppermute(x, 'level', [(z, z + shift) for z in range(steps - shift)])]
    ppermute x3, waiting for transfers between devices: 28.6 us -> 22 us  [down(): lax.ppermute(x, 'level', [(z + shift, z) for z in range(steps - shift)])]
    ppermute x17 -> x18, starting transfers between devices: 8.83 us -> 13.3 us  [to_partner(): lax.ppermute(x, ('side', 'core'), [(t, t ^ flip) for t in range(QUAD)])]
    pallas_call x3, Pallas kernels: 11.2 us -> 9.71 us  [gradients(): pl.pallas_call(functools.partial(grads_kernel, ancestors.shape[1], stage,...]
    ppermute x17 -> x18, waiting for transfers between devices: 10.7 us -> 10.9 us  [to_partner(): lax.ppermute(x, ('side', 'core'), [(t, t ^ flip) for t in range(QUAD)])]
    ppermute x4 -> x6, waiting for transfers between devices: 3.69 us -> 3.56 us  [up(): lax.ppermute(x, 'level', [(z, z + shift) for z in range(steps - shift)])]
    unnamed x16 -> x14, local copies, waits for them, and re-layouts: 4.27 us -> 4.35 us
  transfers between devices with their start and end apart: 24 -> 27, of which waited for: 9 -> 10; matrix products, arithmetic and copies ran while one was open for 0% -> 0% of each run, Pallas kernels for 17% -> 15%
where the time goes in v7:
time: 96.3 us; the launch traced here: 97.6 us
  starting transfers between devices  40.2 us (42%)
  waiting for transfers between devices  36.4 us (38%)
  Pallas kernels  15.7 us (16%)
  local copies, waits for them, and re-layouts  4.37 us (5%)
    ppermute x6, starting transfers between devices, up(): lax.ppermute(x, 'level', [(z, z + shift) for z in range(steps - shift)])  23 us
    ppermute x3, waiting for transfers between devices, down(): lax.ppermute(x, 'level', [(z + shift, z) for z in range(steps - shift)])  22 us
    ppermute x18, starting transfers between devices, to_partner(): lax.ppermute(x, ('side', 'core'), [(t, t ^ flip) for t in range(QUAD)])  13.3 us
    ppermute x18, waiting for transfers between devices, to_partner(): lax.ppermute(x, ('side', 'core'), [(t, t ^ flip) for t in range(QUAD)])  10.9 us
    pallas_call x3, Pallas kernels, gradients(): pl.pallas_call(functools.partial(grads_kernel, ancestors.shape[1], stage,...  9.71 us
    unnamed x14, local copies, waits for them, and re-layouts  4.35 us
    ppermute x3, starting transfers between devices, down(): lax.ppermute(x, 'level', [(z + shift, z) for z in range(steps - shift)])  3.88 us
    ppermute x6, waiting for transfers between devices, up(): lax.ppermute(x, 'level', [(z, z + shift) for z in range(steps - shift)])  3.56 us
  transfers between devices with their start and end apart: 27, of which 10 were waited for; matrix products, arithmetic and copies ran while one was open for 0% of the time, Pallas kernels for 15%

profile of v7, /device:TPU:0, one launch (start us, length us, event | category | flops | bytes accessed | tf_op | source)
XLA Modules:
  0.0 97.6 jit_solution(16216292697986457273)
XLA Ops:
  0.7 1.0 %copy-done.4 = bf16[128,512]{1,0:T(8,128)(2,1)S(1)} copy-done((bf16[128,512]{1,0:T(8,128)(2,1)S(1)}, bf16[128,512]{1,0:T(8,128)(2,1)}, u32[]{:S(2)}) %copy-start.4) | copy-done | bytes 131096
  1.6 0.9 copy-done.5
  2.6 0.5 collective-permute-start
  3.1 2.6 %collective-permute-start.7 = (bf16[128,256]{1,0:T(8,128)(2,1)S(1)}, bf16[128,256]{1,0:T(8,128)(2,1)S(1)}, u32[]{:S(2)}, u32[]{:S(2)}) collective-permute-start(bf16[128,256]{1,0:T(8,128)(2,1)S(1)} %get-tuple-element.56), channel_id=1, source_target_pairs={{0,2},{1,3},{2,0},{3,1},{4,6},{5,7},{6,4},{7,5},{8,10},{9,11},{10,... | collective-permute-start | bytes 196616 | tf_op jit(solution)/shard_map/ppermute | solution.py:531
  5.7 0.1 collective-permute-start.8
  5.8 0.0 collective-permute-done.refs_1_
  5.8 1.2 %copy-done.2 = bf16[128,4096]{1,0:T(8,128)(2,1)S(1)} copy-done((bf16[128,4096]{1,0:T(8,128)(2,1)S(1)}, bf16[128,4096]{1,0:T(8,128)(2,1)}, u32[]{:S(2)}) %copy-start.2) | copy-done | bytes 1048600
  7.0 0.1 pack_queries.2
  7.1 1.3 %collective-permute-done.7.refs_2_ = bf16[128,256]{1,0:T(8,128)(2,1)S(1)} collective-permute-done((bf16[128,256]{1,0:T(8,128)(2,1)S(1)}, bf16[128,256]{1,0:T(8,128)(2,1)S(1)}, u32[]{:S(2)}, u32[]{:S(2)}) %collective-permute-start.7) | collective-permute-done | bytes 65568 | tf_op jit(solution)/shard_map/ppermute | solution.py:531
  8.4 1.4 %collective-permute-done.8.refs_3_ = bf16[128,256]{1,0:T(8,128)(2,1)S(1)} collective-permute-done((bf16[128,256]{1,0:T(8,128)(2,1)S(1)}, bf16[128,256]{1,0:T(8,128)(2,1)S(1)}, u32[]{:S(2)}, u32[]{:S(2)}) %collective-permute-start.8) | collective-permute-done | bytes 65568 | tf_op jit(solution)/shard_map/ppermute | solution.py:531
  9.8 5.5 %collective-permute-start.11 = (bf16[512,128]{1,0:T(8,128)(2,1)S(1)}, bf16[512,128]{1,0:T(8,128)(2,1)S(1)}, u32[]{:S(2)}, u32[]{:S(2)}) collective-permute-start(bf16[512,128]{1,0:T(8,128)(2,1)S(1)} %get-tuple-element.62.rest_4_.rest_13_), channel_id=1, source_target_pairs={{0,12},{1,13},{2,14},{3,15},{16,28},{17,29},{18,30},{19,31}} | collective-permute-start | bytes 393224 | tf_op jit(solution)/shard_map/ppermute | solution.py:537
  15.3 1.4 %collective-permute-start.2 = (bf16[128,1024]{1,0:T(8,128)(2,1)S(1)}, bf16[128,1024]{1,0:T(8,128)(2,1)S(1)}, u32[]{:S(2)}, u32[]{:S(2)}) collective-permute-start(bf16[128,1024]{1,0:T(8,128)(2,1)S(1)} %get-tuple-element.49), channel_id=1, source_target_pairs={{0,2},{1,3},{2,0},{3,1},{4,6},{5,7},{6,4},{7,5},{8,10},{9,11},{10,... | collective-permute-start | bytes 786440 | tf_op jit(solution)/shard_map/ppermute | solution.py:531
  16.7 0.0 collective-permute-start.1
  16.7 0.8 collective-permute-start.3
  17.5 1.3 %collective-permute-start.10 = (bf16[512,128]{1,0:T(8,128)(2,1)S(1)}, bf16[512,128]{1,0:T(8,128)(2,1)S(1)}, u32[]{:S(2)}, u32[]{:S(2)}) collective-permute-start(bf16[512,128]{1,0:T(8,128)(2,1)S(1)} %get-tuple-element.62.rest_4_.rest_13_), channel_id=1, source_target_pairs={{0,8},{4,12},{1,9},{5,13},{2,10},{6,14},{3,11},{7,15},{16,24},{20,... | collective-permute-start | bytes 393224 | tf_op jit(solution)/shard_map/ppermute | solution.py:537
  18.8 0.0 collective-permute-done.11.rest_7_.rest_14_
  18.8 2.5 %collective-permute-start.9 = (bf16[512,128]{1,0:T(8,128)(2,1)S(1)}, bf16[512,128]{1,0:T(8,128)(2,1)S(1)}, u32[]{:S(2)}, u32[]{:S(2)}) collective-permute-start(bf16[512,128]{1,0:T(8,128)(2,1)S(1)} %get-tuple-element.62.rest_4_.rest_13_), channel_id=1, source_target_pairs={{0,4},{4,8},{8,12},{1,5},{5,9},{9,13},{2,6},{6,10},{10,14},{3,7},{... | collective-permute-start | bytes 393224 | tf_op jit(solution)/shard_map/ppermute | solution.py:537
  21.3 1.4 %collective-permute-done.10.rest_6_.rest_13_ = bf16[512,128]{1,0:T(8,128)(2,1)S(1)} collective-permute-done((bf16[512,128]{1,0:T(8,128)(2,1)S(1)}, bf16[512,128]{1,0:T(8,128)(2,1)S(1)}, u32[]{:S(2)}, u32[]{:S(2)}) %collective-permute-start.10) | collective-permute-done | bytes 131104 | tf_op jit(solution)/shard_map/ppermute | solution.py:537
  22.7 2.2 %collective-permute-done.9.after_ref.rest_5_.rest_14_ = bf16[512,128]{1,0:T(8,128)(2,1)S(1)} collective-permute-done((bf16[512,128]{1,0:T(8,128)(2,1)S(1)}, bf16[512,128]{1,0:T(8,128)(2,1)S(1)}, u32[]{:S(2)}, u32[]{:S(2)}) %collective-permute-start.9) | collective-permute-done | bytes 131104 | tf_op jit(solution)/shard_map/ppermute | solution.py:537
  24.9 1.2 %copy-done.1 = bf16[128,4096]{1,0:T(8,128)(2,1)S(1)} copy-done((bf16[128,4096]{1,0:T(8,128)(2,1)S(1)}, bf16[128,4096]{1,0:T(8,128)(2,1)}, u32[]{:S(2)}) %copy-start.1) | copy-done | bytes 1048600
  26.1 0.6 row_deltas.1
  26.7 0.1 collective-permute-start.12
  26.8 1.4 %collective-permute-start.13 = (f32[8,128]{1,0:T(8,128)S(1)}, f32[8,128]{1,0:T(8,128)S(1)}, u32[]{:S(2)}, u32[]{:S(2)}) collective-permute-start(f32[8,128]{1,0:T(8,128)S(1)} %get-tuple-element.66), channel_id=1, source_target_pairs={{0,2},{1,3},{2,0},{3,1},{4,6},{5,7},{6,4},{7,5},{8,10},{9,11},{10,... | collective-permute-start | bytes 12296 | tf_op jit(solution)/shard_map/ppermute | solution.py:531
  28.2 0.0 collective-permute-done.2.rest_2_
  28.2 0.5 collective-permute-start.14
  28.7 0.1 pack_queries.3
  28.7 0.0 collective-permute-done.12.rest_9_
  28.7 7.9 %collective-permute-start.17 = (bf16[512,128]{1,0:T(8,128)(2,1)S(1)}, bf16[512,128]{1,0:T(8,128)(2,1)S(1)}, u32[]{:S(2)}, u32[]{:S(2)}) collective-permute-start(bf16[512,128]{1,0:T(8,128)(2,1)S(1)} %get-tuple-element.69.rest_15_), channel_id=1, source_target_pairs={{0,12},{1,13},{2,14},{3,15},{16,28},{17,29},{18,30},{19,31}} | collective-permute-start | bytes 393224 | tf_op jit(solution)/shard_map/ppermute | solution.py:537
  36.6 0.0 collective-permute-done.13.rest_10_
  36.6 1.3 %collective-permute-start.16 = (bf16[512,128]{1,0:T(8,128)(2,1)S(1)}, bf16[512,128]{1,0:T(8,128)(2,1)S(1)}, u32[]{:S(2)}, u32[]{:S(2)}) collective-permute-start(bf16[512,128]{1,0:T(8,128)(2,1)S(1)} %get-tuple-element.69.rest_15_), channel_id=1, source_target_pairs={{0,8},{4,12},{1,9},{5,13},{2,10},{6,14},{3,11},{7,15},{16,24},{20,... | collective-permute-start | bytes 393224 | tf_op jit(solution)/shard_map/ppermute | solution.py:537
  37.9 0.0 collective-permute-done.14.rest_11_
  38.0 0.1 collective-permute-start.4
  38.1 0.0 collective-permute-done.1.rest_1_
  38.1 1.6 %collective-permute-start.5 = (bf16[128,1024]{1,0:T(8,128)(2,1)S(1)}, bf16[128,1024]{1,0:T(8,128)(2,1)S(1)}, u32[]{:S(2)}, u32[]{:S(2)}) collective-permute-start(bf16[128,1024]{1,0:T(8,128)(2,1)S(1)} %get-tuple-element.53), channel_id=1, source_target_pairs={{0,2},{1,3},{2,0},{3,1},{4,6},{5,7},{6,4},{7,5},{8,10},{9,11},{10,... | collective-permute-start | bytes 786440 | tf_op jit(solution)/shard_map/ppermute | solution.py:531
  39.7 0.0 collective-permute-done.3.rest_3_
  39.7 0.2 collective-permute-start.6
  39.9 3.3 %statistics.1.rest_12_ = f32[4,1,1024]{2,1,0:T(1,128)S(1)} custom-call(s32[1]{0:T(128)} %bitcast.me_ref, s32[16,10]{1,0:T(8,128)S(1)} %copy-done.6, bf16[128,4096]{1,0:T(8,128)(2,1)S(1)} %copy-done.3, bf16[128,1024]{1,0:T(8,128)(2,1)S(1)} %collective-permute-done.1.rest_1_, bf16[128,1024]{1,0:T(8,128)(2,1)S(1)} %collective-permute-done.2.rest_2_, ...), custom_call_target="tpu_custom_call" | custom-call | flops 2952790016 | bytes 16777216 | tf_op jit(solution)/shard_map/statistics/pallas_call | solution.py:317
  43.2 0.0 collective-permute-done.17.rest_16_
  43.2 4.5 %collective-permute-start.15 = (bf16[512,128]{1,0:T(8,128)(2,1)S(1)}, bf16[512,128]{1,0:T(8,128)(2,1)S(1)}, u32[]{:S(2)}, u32[]{:S(2)}) collective-permute-start(bf16[512,128]{1,0:T(8,128)(2,1)S(1)} %get-tuple-element.69.rest_15_), channel_id=1, source_target_pairs={{0,4},{4,8},{8,12},{1,5},{5,9},{9,13},{2,6},{6,10},{10,14},{3,7},{... | collective-permute-start | bytes 393224 | tf_op jit(solution)/shard_map/ppermute | solution.py:537
  47.7 0.0 collective-permute-done.4.rest_5_
  47.7 4.2 %collective-permute-done.6.rest_7_ = bf16[128,1024]{1,0:T(8,128)(2,1)S(1)} collective-permute-done((bf16[128,1024]{1,0:T(8,128)(2,1)S(1)}, bf16[128,1024]{1,0:T(8,128)(2,1)S(1)}, u32[]{:S(2)}, u32[]{:S(2)}) %collective-permute-start.6) | collective-permute-done | bytes 262176 | tf_op jit(solution)/shard_map/ppermute | solution.py:531
  51.9 1.3 %far_grads.1 = (f32[4,128,1024]{2,1,0:T(8,128)S(1)}, bf16[512,256]{1,0:T(8,128)(2,1)S(1)}, bf16[512,256]{1,0:T(8,128)(2,1)S(1)}) custom-call(s32[1]{0:T(128)} %bitcast.me_ref, s32[16,10]{1,0:T(8,128)S(1)} %copy-done.6, bf16[128,4096]{1,0:T(8,128)(2,1)S(1)} %copy-done.3, bf16[128,1024]{1,0:T(8,128)(2,1)S(1)} %collective-permute-done.1.rest_1_, ...), custom_call_target="tpu_custom_call" | custom-call | flops 14763950080 | bytes 16777216 | tf_op jit(solution)/shard_map/far_grads/pallas_call | solution.py:370
  53.3 1.3 %collective-permute-start.20 = (bf16[512,256]{1,0:T(8,128)(2,1)S(1)}, bf16[512,256]{1,0:T(8,128)(2,1)S(1)}, u32[]{:S(2)}, u32[]{:S(2)}) collective-permute-start(bf16[512,256]{1,0:T(8,128)(2,1)S(1)} %get-tuple-element.77), channel_id=1, source_target_pairs={{8,0},{12,4},{9,1},{13,5},{10,2},{14,6},{11,3},{15,7},{24,16},{28,... | collective-permute-start | bytes 786440 | tf_op jit(solution)/shard_map/ppermute | solution.py:543
  54.6 1.3 %collective-permute-start.21 = (bf16[512,256]{1,0:T(8,128)(2,1)S(1)}, bf16[512,256]{1,0:T(8,128)(2,1)S(1)}, u32[]{:S(2)}, u32[]{:S(2)}) collective-permute-start(bf16[512,256]{1,0:T(8,128)(2,1)S(1)} %get-tuple-element.78), channel_id=1, source_target_pairs={{12,0},{13,1},{14,2},{15,3},{28,16},{29,17},{30,18},{31,19}} | collective-permute-start | bytes 786440 | tf_op jit(solution)/shard_map/ppermute | solution.py:543
  55.9 0.0 collective-permute-done.15.rest_16_
  55.9 4.2 %side_grads.1 = (bf16[256,1024]{1,0:T(8,128)(2,1)S(1)}, f32[1024,128]{1,0:T(8,128)S(1)}, f32[1024,128]{1,0:T(8,128)S(1)}) custom-call(s32[1]{0:T(128)} %bitcast.me_ref, s32[16,10]{1,0:T(8,128)S(1)} %copy-done.6, bf16[128,4096]{1,0:T(8,128)(2,1)S(1)} %copy-done.3, bf16[128,1024]{1,0:T(8,128)(2,1)S(1)} %collective-permute-done.1.rest_1_, ...), custom_call_target="tpu_custom_call" | custom-call | flops 14763950080 | bytes 16777216 | tf_op jit(solution)/shard_map/side_grads/pallas_call | solution.py:370
  60.1 1.6 %collective-permute-start.19 = (bf16[256,1024]{1,0:T(8,128)(2,1)S(1)}, bf16[256,1024]{1,0:T(8,128)(2,1)S(1)}, u32[]{:S(2)}, u32[]{:S(2)}) collective-permute-start(bf16[256,1024]{1,0:T(8,128)(2,1)S(1)} %get-tuple-element.75), channel_id=1, source_target_pairs={{0,2},{1,3},{2,0},{3,1},{4,6},{5,7},{6,4},{7,5},{8,10},{9,11},{10,... | collective-permute-start | bytes 1572872 | tf_op jit(solution)/shard_map/ppermute | solution.py:531
  61.7 4.2 %own_grads.1 = (bf16[128,1024]{1,0:T(8,128)(2,1)S(1)}, bf16[128,1024]{1,0:T(8,128)(2,1)S(1)}, f32[512,256]{1,0:T(8,128)S(1)}, bf16[512,256]{1,0:T(8,128)(2,1)S(1)}) custom-call(s32[1]{0:T(128)} %bitcast.me_ref, s32[16,10]{1,0:T(8,128)S(1)} %copy-done.6, bf16[128,4096]{1,0:T(8,128)(2,1)S(1)} %copy-done.3, ...), custom_call_target="tpu_custom_call" | custom-call | flops 14763950080 | bytes 16777216 | tf_op jit(solution)/shard_map/own_grads/pallas_call | solution.py:370
  65.9 13.3 %collective-permute-done.20.refs_0_ = bf16[512,256]{1,0:T(8,128)(2,1)S(1)} collective-permute-done((bf16[512,256]{1,0:T(8,128)(2,1)S(1)}, bf16[512,256]{1,0:T(8,128)(2,1)S(1)}, u32[]{:S(2)}, u32[]{:S(2)}) %collective-permute-start.20) | collective-permute-done | bytes 262176 | tf_op jit(solution)/shard_map/ppermute | solution.py:543
  79.2 0.1 add_far.1
  79.3 1.3 %collective-permute-start.22 = (bf16[512,256]{1,0:T(8,128)(2,1)S(1)}, bf16[512,256]{1,0:T(8,128)(2,1)S(1)}, u32[]{:S(2)}, u32[]{:S(2)}) collective-permute-start(bf16[512,256]{1,0:T(8,128)(2,1)S(1)} %get-tuple-element.81), channel_id=1, source_target_pairs={{4,0},{8,4},{12,8},{5,1},{9,5},{13,9},{6,2},{10,6},{14,10},{7,3},{... | collective-permute-start | bytes 786440 | tf_op jit(solution)/shard_map/ppermute | solution.py:543
  80.6 8.7 %collective-permute-done.22.near_ref = bf16[512,256]{1,0:T(8,128)(2,1)S(1)} collective-permute-done((bf16[512,256]{1,0:T(8,128)(2,1)S(1)}, bf16[512,256]{1,0:T(8,128)(2,1)S(1)}, u32[]{:S(2)}, u32[]{:S(2)}) %collective-permute-start.22) | collective-permute-done | bytes 262176 | tf_op jit(solution)/shard_map/ppermute | solution.py:543
  89.2 0.1 add_sums.1
  89.3 0.1 collective-permute-start.23
  89.4 1.5 %collective-permute-start.24 = (bf16[128,256]{1,0:T(8,128)(2,1)S(1)}, bf16[128,256]{1,0:T(8,128)(2,1)S(1)}, u32[]{:S(2)}, u32[]{:S(2)}) collective-permute-start(bf16[128,256]{1,0:T(8,128)(2,1)S(1)} %get-tuple-element.84), channel_id=1, source_target_pairs={{0,2},{1,3},{2,0},{3,1},{4,6},{5,7},{6,4},{7,5},{8,10},{9,11},{10,... | collective-permute-start | bytes 196616 | tf_op jit(solution)/shard_map/ppermute | solution.py:531
  90.8 0.4 collective-permute-start.25
  91.2 0.3 collective-permute-start.18
  91.6 0.0 collective-permute-done.19.refs_2_
  91.6 2.4 %collective-permute-done.24.refs_2_ = bf16[128,256]{1,0:T(8,128)(2,1)S(1)} collective-permute-done((bf16[128,256]{1,0:T(8,128)(2,1)S(1)}, bf16[128,256]{1,0:T(8,128)(2,1)S(1)}, u32[]{:S(2)}, u32[]{:S(2)}) %collective-permute-start.24) | collective-permute-done | bytes 65568 | tf_op jit(solution)/shard_map/ppermute | solution.py:531
  93.9 1.0 %collective-permute-done.25.refs_3_ = bf16[128,256]{1,0:T(8,128)(2,1)S(1)} collective-permute-done((bf16[128,256]{1,0:T(8,128)(2,1)S(1)}, bf16[128,256]{1,0:T(8,128)(2,1)S(1)}, u32[]{:S(2)}, u32[]{:S(2)}) %collective-permute-start.25) | collective-permute-done | bytes 65568 | tf_op jit(solution)/shard_map/ppermute | solution.py:531
  95.0 0.2 collective-permute-start.26
  95.2 0.7 place_keys.1
  95.9 0.7 collective-permute-done.26.refs_3_
  96.6 1.0 %place_queries.1 = bf16[128,4096]{1,0:T(8,128)(2,1)} custom-call(s32[1]{0:T(128)} %bitcast.me_ref, bf16[128,1024]{1,0:T(8,128)(2,1)S(1)} %get-tuple-element.73.refs_0_, bf16[128,1024]{1,0:T(8,128)(2,1)S(1)} %collective-permute-done.18.refs_1_, bf16[256,1024]{1,0:T(8,128)(2,1)S(1)} %collective-permute-done.19.refs_2_, ...), custom_call_target="tpu_custom_call" | custom-call | tf_op jit(solution)/shard_map/place_queries/pallas_call | solution.py:497
  (18 shorter events, 0.1 us)
Async XLA Ops:
  0.6 24.2 %copy-start = (bf16[128,4096]{1,0:T(8,128)(2,1)S(1)}, bf16[128,4096]{1,0:T(8,128)(2,1)}, u32[]{:S(2)}) copy-start(bf16[128,4096]{1,0:T(8,128)(2,1)} %rest_4_.5) | copy-start | bytes 3145732
  0.6 1.0 %copy-start.4 = (bf16[128,512]{1,0:T(8,128)(2,1)S(1)}, bf16[128,512]{1,0:T(8,128)(2,1)}, u32[]{:S(2)}) copy-start(bf16[128,512]{1,0:T(8,128)(2,1)} %keys.1) | copy-start | bytes 393220
  1.6 0.9 copy-start.5
  2.6 3.2 %collective-permute-start = (bf16[128,256]{1,0:T(8,128)(2,1)S(1)}, bf16[128,256]{1,0:T(8,128)(2,1)S(1)}, u32[]{:S(2)}, u32[]{:S(2)}) collective-permute-start(bf16[128,256]{1,0:T(8,128)(2,1)S(1)} %get-tuple-element.46), channel_id=1, source_target_pairs={{0,1},{1,0},{2,3},{3,2},{4,5},{5,4},{6,7},{7,6},{8,9},{9,8},{10,11... | collective-permute-start | bytes 196616 | tf_op jit(solution)/shard_map/ppermute | solution.py:531
  3.1 5.3 %collective-permute-start.7 = (bf16[128,256]{1,0:T(8,128)(2,1)S(1)}, bf16[128,256]{1,0:T(8,128)(2,1)S(1)}, u32[]{:S(2)}, u32[]{:S(2)}) collective-permute-start(bf16[128,256]{1,0:T(8,128)(2,1)S(1)} %get-tuple-element.56), channel_id=1, source_target_pairs={{0,2},{1,3},{2,0},{3,1},{4,6},{5,7},{6,4},{7,5},{8,10},{9,11},{10,... | collective-permute-start | bytes 196616 | tf_op jit(solution)/shard_map/ppermute | solution.py:531
  5.7 4.0 %collective-permute-start.8 = (bf16[128,256]{1,0:T(8,128)(2,1)S(1)}, bf16[128,256]{1,0:T(8,128)(2,1)S(1)}, u32[]{:S(2)}, u32[]{:S(2)}) collective-permute-start(bf16[128,256]{1,0:T(8,128)(2,1)S(1)} %get-tuple-element.57), channel_id=1, source_target_pairs={{0,3},{1,2},{2,1},{3,0},{4,7},{5,6},{6,5},{7,4},{8,11},{9,10},{10,... | collective-permute-start | bytes 196616 | tf_op jit(solution)/shard_map/ppermute | solution.py:531
  5.8 1.2 %copy-start.2 = (bf16[128,4096]{1,0:T(8,128)(2,1)S(1)}, bf16[128,4096]{1,0:T(8,128)(2,1)}, u32[]{:S(2)}) copy-start(bf16[128,4096]{1,0:T(8,128)(2,1)} %rest_0_.7) | copy-start | bytes 3145732
  7.0 32.9 %copy-start.6 = (s32[16,10]{1,0:T(8,128)S(1)}, s32[16,10]{1,0:T(8,128)}, u32[]{:S(2)}) copy-start(s32[16,10]{1,0:T(8,128)} %anc_ref.7) | copy-start | bytes 1924
  9.8 9.0 %collective-permute-start.11 = (bf16[512,128]{1,0:T(8,128)(2,1)S(1)}, bf16[512,128]{1,0:T(8,128)(2,1)S(1)}, u32[]{:S(2)}, u32[]{:S(2)}) collective-permute-start(bf16[512,128]{1,0:T(8,128)(2,1)S(1)} %get-tuple-element.62.rest_4_.rest_13_), channel_id=1, source_target_pairs={{0,12},{1,13},{2,14},{3,15},{16,28},{17,29},{18,30},{19,31}} | collective-permute-start | bytes 393224 | tf_op jit(solution)/shard_map/ppermute | solution.py:537
  15.3 12.9 %collective-permute-start.2 = (bf16[128,1024]{1,0:T(8,128)(2,1)S(1)}, bf16[128,1024]{1,0:T(8,128)(2,1)S(1)}, u32[]{:S(2)}, u32[]{:S(2)}) collective-permute-start(bf16[128,1024]{1,0:T(8,128)(2,1)S(1)} %get-tuple-element.49), channel_id=1, source_target_pairs={{0,2},{1,3},{2,0},{3,1},{4,6},{5,7},{6,4},{7,5},{8,10},{9,11},{10,... | collective-permute-start | bytes 786440 | tf_op jit(solution)/shard_map/ppermute | solution.py:531
  16.7 21.4 %collective-permute-start.1 = (bf16[128,1024]{1,0:T(8,128)(2,1)S(1)}, bf16[128,1024]{1,0:T(8,128)(2,1)S(1)}, u32[]{:S(2)}, u32[]{:S(2)}) collective-permute-start(bf16[128,1024]{1,0:T(8,128)(2,1)S(1)} %get-tuple-element.48), channel_id=1, source_target_pairs={{0,1},{1,0},{2,3},{3,2},{4,5},{5,4},{6,7},{7,6},{8,9},{9,8},{10,11... | collective-permute-start | bytes 786440 | tf_op jit(solution)/shard_map/ppermute | solution.py:531
  16.7 22.9 %collective-permute-start.3 = (bf16[128,1024]{1,0:T(8,128)(2,1)S(1)}, bf16[128,1024]{1,0:T(8,128)(2,1)S(1)}, u32[]{:S(2)}, u32[]{:S(2)}) collective-permute-start(bf16[128,1024]{1,0:T(8,128)(2,1)S(1)} %get-tuple-element.50), channel_id=1, source_target_pairs={{0,3},{1,2},{2,1},{3,0},{4,7},{5,6},{6,5},{7,4},{8,11},{9,10},{10,... | collective-permute-start | bytes 786440 | tf_op jit(solution)/shard_map/ppermute | solution.py:531
  17.5 5.2 %collective-permute-start.10 = (bf16[512,128]{1,0:T(8,128)(2,1)S(1)}, bf16[512,128]{1,0:T(8,128)(2,1)S(1)}, u32[]{:S(2)}, u32[]{:S(2)}) collective-permute-start(bf16[512,128]{1,0:T(8,128)(2,1)S(1)} %get-tuple-element.62.rest_4_.rest_13_), channel_id=1, source_target_pairs={{0,8},{4,12},{1,9},{5,13},{2,10},{6,14},{3,11},{7,15},{16,24},{20,... | collective-permute-start | bytes 393224 | tf_op jit(solution)/shard_map/ppermute | solution.py:537
  18.8 6.0 %collective-permute-start.9 = (bf16[512,128]{1,0:T(8,128)(2,1)S(1)}, bf16[512,128]{1,0:T(8,128)(2,1)S(1)}, u32[]{:S(2)}, u32[]{:S(2)}) collective-permute-start(bf16[512,128]{1,0:T(8,128)(2,1)S(1)} %get-tuple-element.62.rest_4_.rest_13_), channel_id=1, source_target_pairs={{0,4},{4,8},{8,12},{1,5},{5,9},{9,13},{2,6},{6,10},{10,14},{3,7},{... | collective-permute-start | bytes 393224 | tf_op jit(solution)/shard_map/ppermute | solution.py:537
  24.9 1.2 %copy-start.1 = (bf16[128,4096]{1,0:T(8,128)(2,1)S(1)}, bf16[128,4096]{1,0:T(8,128)(2,1)}, u32[]{:S(2)}) copy-start(bf16[128,4096]{1,0:T(8,128)(2,1)} %out_ref.1) | copy-start | bytes 3145732
  26.1 13.8 %copy-start.3 = (bf16[128,4096]{1,0:T(8,128)(2,1)S(1)}, bf16[128,4096]{1,0:T(8,128)(2,1)}, u32[]{:S(2)}) copy-start(bf16[128,4096]{1,0:T(8,128)(2,1)} %rest_0_.7) | copy-start | bytes 3145732
  26.7 2.0 %collective-permute-start.12 = (f32[8,128]{1,0:T(8,128)S(1)}, f32[8,128]{1,0:T(8,128)S(1)}, u32[]{:S(2)}, u32[]{:S(2)}) collective-permute-start(f32[8,128]{1,0:T(8,128)S(1)} %get-tuple-element.65), channel_id=1, source_target_pairs={{0,1},{1,0},{2,3},{3,2},{4,5},{5,4},{6,7},{7,6},{8,9},{9,8},{10,11... | collective-permute-start | bytes 12296 | tf_op jit(solution)/shard_map/ppermute | solution.py:531
  26.8 9.8 %collective-permute-start.13 = (f32[8,128]{1,0:T(8,128)S(1)}, f32[8,128]{1,0:T(8,128)S(1)}, u32[]{:S(2)}, u32[]{:S(2)}) collective-permute-start(f32[8,128]{1,0:T(8,128)S(1)} %get-tuple-element.66), channel_id=1, source_target_pairs={{0,2},{1,3},{2,0},{3,1},{4,6},{5,7},{6,4},{7,5},{8,10},{9,11},{10,... | collective-permute-start | bytes 12296 | tf_op jit(solution)/shard_map/ppermute | solution.py:531
  28.2 9.7 %collective-permute-start.14 = (f32[8,128]{1,0:T(8,128)S(1)}, f32[8,128]{1,0:T(8,128)S(1)}, u32[]{:S(2)}, u32[]{:S(2)}) collective-permute-start(f32[8,128]{1,0:T(8,128)S(1)} %get-tuple-element.67), channel_id=1, source_target_pairs={{0,3},{1,2},{2,1},{3,0},{4,7},{5,6},{6,5},{7,4},{8,11},{9,10},{10,... | collective-permute-start | bytes 12296 | tf_op jit(solution)/shard_map/ppermute | solution.py:531
  28.7 14.4 %collective-permute-start.17 = (bf16[512,128]{1,0:T(8,128)(2,1)S(1)}, bf16[512,128]{1,0:T(8,128)(2,1)S(1)}, u32[]{:S(2)}, u32[]{:S(2)}) collective-permute-start(bf16[512,128]{1,0:T(8,128)(2,1)S(1)} %get-tuple-element.69.rest_15_), channel_id=1, source_target_pairs={{0,12},{1,13},{2,14},{3,15},{16,28},{17,29},{18,30},{19,31}} | collective-permute-start | bytes 393224 | tf_op jit(solution)/shard_map/ppermute | solution.py:537
  36.6 11.1 %collective-permute-start.16 = (bf16[512,128]{1,0:T(8,128)(2,1)S(1)}, bf16[512,128]{1,0:T(8,128)(2,1)S(1)}, u32[]{:S(2)}, u32[]{:S(2)}) collective-permute-start(bf16[512,128]{1,0:T(8,128)(2,1)S(1)} %get-tuple-element.69.rest_15_), channel_id=1, source_target_pairs={{0,8},{4,12},{1,9},{5,13},{2,10},{6,14},{3,11},{7,15},{16,24},{20,... | collective-permute-start | bytes 393224 | tf_op jit(solution)/shard_map/ppermute | solution.py:537
  38.0 9.8 %collective-permute-start.4 = (bf16[128,1024]{1,0:T(8,128)(2,1)S(1)}, bf16[128,1024]{1,0:T(8,128)(2,1)S(1)}, u32[]{:S(2)}, u32[]{:S(2)}) collective-permute-start(bf16[128,1024]{1,0:T(8,128)(2,1)S(1)} %get-tuple-element.52), channel_id=1, source_target_pairs={{0,1},{1,0},{2,3},{3,2},{4,5},{5,4},{6,7},{7,6},{8,9},{9,8},{10,11... | collective-permute-start | bytes 786440 | tf_op jit(solution)/shard_map/ppermute | solution.py:531
  38.1 9.7 %collective-permute-start.5 = (bf16[128,1024]{1,0:T(8,128)(2,1)S(1)}, bf16[128,1024]{1,0:T(8,128)(2,1)S(1)}, u32[]{:S(2)}, u32[]{:S(2)}) collective-permute-start(bf16[128,1024]{1,0:T(8,128)(2,1)S(1)} %get-tuple-element.53), channel_id=1, source_target_pairs={{0,2},{1,3},{2,0},{3,1},{4,6},{5,7},{6,4},{7,5},{8,10},{9,11},{10,... | collective-permute-start | bytes 786440 | tf_op jit(solution)/shard_map/ppermute | solution.py:531
  39.7 12.2 %collective-permute-start.6 = (bf16[128,1024]{1,0:T(8,128)(2,1)S(1)}, bf16[128,1024]{1,0:T(8,128)(2,1)S(1)}, u32[]{:S(2)}, u32[]{:S(2)}) collective-permute-start(bf16[128,1024]{1,0:T(8,128)(2,1)S(1)} %get-tuple-element.54), channel_id=1, source_target_pairs={{0,3},{1,2},{2,1},{3,0},{4,7},{5,6},{6,5},{7,4},{8,11},{9,10},{10,... | collective-permute-start | bytes 786440 | tf_op jit(solution)/shard_map/ppermute | solution.py:531
  43.2 12.7 %collective-permute-start.15 = (bf16[512,128]{1,0:T(8,128)(2,1)S(1)}, bf16[512,128]{1,0:T(8,128)(2,1)S(1)}, u32[]{:S(2)}, u32[]{:S(2)}) collective-permute-start(bf16[512,128]{1,0:T(8,128)(2,1)S(1)} %get-tuple-element.69.rest_15_), channel_id=1, source_target_pairs={{0,4},{4,8},{8,12},{1,5},{5,9},{9,13},{2,6},{6,10},{10,14},{3,7},{... | collective-permute-start | bytes 393224 | tf_op jit(solution)/shard_map/ppermute | solution.py:537
  53.3 25.9 %collective-permute-start.20 = (bf16[512,256]{1,0:T(8,128)(2,1)S(1)}, bf16[512,256]{1,0:T(8,128)(2,1)S(1)}, u32[]{:S(2)}, u32[]{:S(2)}) collective-permute-start(bf16[512,256]{1,0:T(8,128)(2,1)S(1)} %get-tuple-element.77), channel_id=1, source_target_pairs={{8,0},{12,4},{9,1},{13,5},{10,2},{14,6},{11,3},{15,7},{24,16},{28,... | collective-permute-start | bytes 786440 | tf_op jit(solution)/shard_map/ppermute | solution.py:543
  54.6 24.6 %collective-permute-start.21 = (bf16[512,256]{1,0:T(8,128)(2,1)S(1)}, bf16[512,256]{1,0:T(8,128)(2,1)S(1)}, u32[]{:S(2)}, u32[]{:S(2)}) collective-permute-start(bf16[512,256]{1,0:T(8,128)(2,1)S(1)} %get-tuple-element.78), channel_id=1, source_target_pairs={{12,0},{13,1},{14,2},{15,3},{28,16},{29,17},{30,18},{31,19}} | collective-permute-start | bytes 786440 | tf_op jit(solution)/shard_map/ppermute | solution.py:543
  60.1 31.5 %collective-permute-start.19 = (bf16[256,1024]{1,0:T(8,128)(2,1)S(1)}, bf16[256,1024]{1,0:T(8,128)(2,1)S(1)}, u32[]{:S(2)}, u32[]{:S(2)}) collective-permute-start(bf16[256,1024]{1,0:T(8,128)(2,1)S(1)} %get-tuple-element.75), channel_id=1, source_target_pairs={{0,2},{1,3},{2,0},{3,1},{4,6},{5,7},{6,4},{7,5},{8,10},{9,11},{10,... | collective-permute-start | bytes 1572872 | tf_op jit(solution)/shard_map/ppermute | solution.py:531
  79.3 10.0 %collective-permute-start.22 = (bf16[512,256]{1,0:T(8,128)(2,1)S(1)}, bf16[512,256]{1,0:T(8,128)(2,1)S(1)}, u32[]{:S(2)}, u32[]{:S(2)}) collective-permute-start(bf16[512,256]{1,0:T(8,128)(2,1)S(1)} %get-tuple-element.81), channel_id=1, source_target_pairs={{4,0},{8,4},{12,8},{5,1},{9,5},{13,9},{6,2},{10,6},{14,10},{7,3},{... | collective-permute-start | bytes 786440 | tf_op jit(solution)/shard_map/ppermute | solution.py:543
  89.3 2.3 %collective-permute-start.23 = (bf16[128,256]{1,0:T(8,128)(2,1)S(1)}, bf16[128,256]{1,0:T(8,128)(2,1)S(1)}, u32[]{:S(2)}, u32[]{:S(2)}) collective-permute-start(bf16[128,256]{1,0:T(8,128)(2,1)S(1)} %get-tuple-element.83), channel_id=1, source_target_pairs={{0,1},{1,0},{2,3},{3,2},{4,5},{5,4},{6,7},{7,6},{8,9},{9,8},{10,11... | collective-permute-start | bytes 196616 | tf_op jit(solution)/shard_map/ppermute | solution.py:531
  89.4 4.6 %collective-permute-start.24 = (bf16[128,256]{1,0:T(8,128)(2,1)S(1)}, bf16[128,256]{1,0:T(8,128)(2,1)S(1)}, u32[]{:S(2)}, u32[]{:S(2)}) collective-permute-start(bf16[128,256]{1,0:T(8,128)(2,1)S(1)} %get-tuple-element.84), channel_id=1, source_target_pairs={{0,2},{1,3},{2,0},{3,1},{4,6},{5,7},{6,4},{7,5},{8,10},{9,11},{10,... | collective-permute-start | bytes 196616 | tf_op jit(solution)/shard_map/ppermute | solution.py:531
  90.8 4.1 %collective-permute-start.25 = (bf16[128,256]{1,0:T(8,128)(2,1)S(1)}, bf16[128,256]{1,0:T(8,128)(2,1)S(1)}, u32[]{:S(2)}, u32[]{:S(2)}) collective-permute-start(bf16[128,256]{1,0:T(8,128)(2,1)S(1)} %get-tuple-element.85), channel_id=1, source_target_pairs={{0,3},{1,2},{2,1},{3,0},{4,7},{5,6},{6,5},{7,4},{8,11},{9,10},{10,... | collective-permute-start | bytes 196616 | tf_op jit(solution)/shard_map/ppermute | solution.py:531
  91.2 4.7 %collective-permute-start.18 = (bf16[128,1024]{1,0:T(8,128)(2,1)S(1)}, bf16[128,1024]{1,0:T(8,128)(2,1)S(1)}, u32[]{:S(2)}, u32[]{:S(2)}) collective-permute-start(bf16[128,1024]{1,0:T(8,128)(2,1)S(1)} %get-tuple-element.74), channel_id=1, source_target_pairs={{0,1},{1,0},{2,3},{3,2},{4,5},{5,4},{6,7},{7,6},{8,9},{9,8},{10,11... | collective-permute-start | bytes 786440 | tf_op jit(solution)/shard_map/ppermute | solution.py:531
  95.0 1.6 %collective-permute-start.26 = (bf16[128,1024]{1,0:T(8,128)(2,1)S(1)}, bf16[128,1024]{1,0:T(8,128)(2,1)S(1)}, u32[]{:S(2)}, u32[]{:S(2)}) collective-permute-start(bf16[128,1024]{1,0:T(8,128)(2,1)S(1)} %slice.3), channel_id=1, source_target_pairs={{0,1},{1,0},{2,3},{3,2},{4,5},{5,4},{6,7},{7,6},{8,9},{9,8},{10,11... | collective-permute-start | bytes 786440 | tf_op jit(solution)/shard_map/ppermute | solution.py:531

commit v8 on v7

--- a/solution.py
+++ b/solution.py
@@ -28,21 +28,24 @@
 SMALL_PARAMS = pltpu.CompilerParams(vmem_limit_bytes=16 * 1024 * 1024)
 
 
-def delta_kernel(me_ref, out_ref, grad_ref, after_ref, *delta_refs):
-    for flip, delta_ref in enumerate(delta_refs):
+def delta_kernel(me_ref, out_ref, grad_ref, after_ref, mine_ref, beside_ref, pair_ref):
+    for flip in range(QUAD):
         base = (own_head(me_ref) ^ flip) * ROWS
+        delta_ref, row = ((mine_ref, 0), (beside_ref, 0), (pair_ref, 0), (pair_ref, GROUP))[flip]
         for head in range(GROUP):
             cols = pl.ds(pl.multiple_of(base + head * HD, HD), HD)
             product = out_ref[:, cols].astype(jnp.float32) * grad_ref[:, cols].astype(jnp.float32)
-            delta_ref[head : head + 1, :] = jnp.sum(product.T, axis=0, keepdims=True)
+            delta_ref[row + head : row + head + 1, :] = jnp.sum(product.T, axis=0, keepdims=True)
 
 
 def row_deltas(me, outputs, out_grad, after):
     return pl.pallas_call(
         delta_kernel,
         in_specs=[SCALARS, HERE, HERE, pl.BlockSpec(memory_space=pl.ANY)],
-        out_specs=[HERE] * QUAD,
-        out_shape=[jax.ShapeDtypeStruct((GROUP, TILE), jnp.float32)] * QUAD,
+        out_specs=[HERE] * 3,
+        out_shape=[
+            jax.ShapeDtypeStruct((count * GROUP, TILE), jnp.float32) for count in (1, 1, 2)
+        ],
         compiler_params=SMALL_PARAMS,
         name="row_deltas",
     )(me, outputs, out_grad, after)
@@ -112,8 +115,12 @@
     return key_pos - query_pos <= jnp.where((flags & 4) != 0, 0, TILE)
 
 
+def four_tiles(own, peer, side, rows):
+    return own, peer, side.at[:rows, :], side.at[rows:, :]
+
+
 def stats_kernel(depth, steps, me_ref, anc_ref, *rest):
-    q_refs, rest = rest[:QUAD], rest[QUAD:]
+    q_refs, rest = four_tiles(*rest[:3], TILE), rest[3:]
     k_refs = rest[:steps]
     lse_ref, q_all, k_all, item_max, item_sum, *items = rest[steps:]
     me = me_ref[0]
@@ -169,7 +176,8 @@
 
 
 def grads_kernel(depth, stage, steps, me_ref, anc_ref, *rest):
-    q_refs, g_refs, d_refs, rest = rest[:4], rest[4:8], rest[8:12], rest[12:]
+    q_refs, g_refs = four_tiles(*rest[:3], TILE), four_tiles(*rest[3:6], TILE)
+    d_refs, rest = four_tiles(*rest[6:9], GROUP), rest[9:]
     lse_ref, rest = rest[0], rest[1:]
     kv_refs, rest = rest[: 2 * steps], rest[2 * steps :]
     if stage != "far":
@@ -308,6 +316,8 @@
 DQ = fixed((QUAD, HD, ROWS))
 PIECE = fixed((TILE, ROWS))
 SIDE = fixed((PAIR, ROWS))
+DELTA = fixed((GROUP, TILE))
+PAIR_DELTA = fixed((2 * GROUP, TILE))
 
 
 def statistics(me, ancestors, q_set, k_list):
@@ -319,7 +329,7 @@
         grid_spec=pltpu.PrefetchScalarGridSpec(
             num_scalar_prefetch=2,
             grid=(1,),
-            in_specs=[WIDE] + [PIECE] * 3 + [KEYS] * steps,
+            in_specs=[WIDE, WIDE, SIDE] + [KEYS] * steps,
             out_specs=LSE,
             scratch_shapes=[
                 pltpu.VMEM((QUAD, TILE, ROWS), jnp.bfloat16),
@@ -372,7 +382,7 @@
         grid_spec=pltpu.PrefetchScalarGridSpec(
             num_scalar_prefetch=2,
             grid=(1,),
-            in_specs=([WIDE] + [PIECE] * 3) * 2 + [fixed((GROUP, TILE))] * 4 + [LSE]
+            in_specs=[WIDE, WIDE, SIDE] * 2 + [DELTA, PAIR_DELTA, PAIR_DELTA, LSE]
             + [KEYS] * (2 * steps)
             + extra_specs,
             out_specs=out_specs,
@@ -426,20 +436,37 @@
     )(*pieces)
 
 
-def pack_queries_kernel(me_ref, whole, *out_refs):
-    for flip, out_ref in enumerate(out_refs):
-        out_ref[...] = whole[:, head_columns(own_head(me_ref) ^ (flip + 1), ROWS)]
-
-
-def pack_queries(me, whole):
+def pack_queries_kernel(me_ref, own, peer, send_ref):
+    at = head_columns(own_head(me_ref) ^ 1, ROWS)
+    send_ref[:TILE, :] = own[:, at]
+    send_ref[TILE:, :] = peer[:, at]
+
+
+def pack_queries(me, own, peer):
     return pl.pallas_call(
         pack_queries_kernel,
-        in_specs=[SCALARS, HERE],
-        out_specs=[HERE] * 3,
-        out_shape=[jax.ShapeDtypeStruct((TILE, ROWS), jnp.bfloat16)] * 3,
+        in_specs=[SCALARS, HERE, HERE],
+        out_specs=HERE,
+        out_shape=jax.ShapeDtypeStruct((PAIR, ROWS), jnp.bfloat16),
         compiler_params=SMALL_PARAMS,
         name="pack_queries",
-    )(me, whole)
+    )(me, own, peer)
+
+
+def pack_deltas_kernel(own, pair, send_ref):
+    send_ref[:GROUP, :] = own[...]
+    send_ref[GROUP:, :] = pair[GROUP:, :]
+
+
+def pack_deltas(own, pair):
+    return pl.pallas_call(
+        pack_deltas_kernel,
+        in_specs=[HERE] * 2,
+        out_specs=HERE,
+        out_shape=jax.ShapeDtypeStruct((2 * GROUP, TILE), jnp.float32),
+        compiler_params=SMALL_PARAMS,
+        name="pack_deltas",
+    )(own, pair)
 
 
 def add_far_kernel(total_ref, *refs):
@@ -547,13 +574,16 @@
         return [mine, to_partner(across, 1), to_partner(beside, 2), to_partner(corner, 3)]
 
     kv_quad = exchange(pack_keys(me, keys, values))
-    q_sent = pack_queries(me, after(queries, kv_quad[1]))
-    q_set = exchange([queries, *q_sent])
-    k_level, v_level = join_keys(*after(kv_quad, q_sent))
+    k_level, v_level = join_keys(*kv_quad)
     k_list = up_all(k_level)
+    q_peer = to_partner(queries, 1)
+    q_set = [queries, q_peer, to_partner(pack_queries(me, queries, after(q_peer, k_level)), 2)]
+    g_peer = to_partner(out_grad, 1)
+    g_set = [out_grad, g_peer, to_partner(pack_queries(me, out_grad, after(g_peer, k_list)), 2)]
     v_list = up_all(after(v_level, k_list))
-    g_set = exchange([out_grad, *pack_queries(me, after(out_grad, q_set[2]))])
-    d_set = exchange(row_deltas(me, outputs, out_grad, after(k_list[1], k_list)))
+    d_own, d_beside, d_pair = row_deltas(me, outputs, out_grad, after(k_level, k_list))
+    d_pair = to_partner(d_pair, 1)
+    d_set = [d_own, d_pair, to_partner(pack_deltas(d_beside, d_pair), 2)]
 
     lse = statistics(me, ancestors, q_set, k_list)
     common = (me, ancestors, q_set, g_set, d_set, lse)
@@ -564,9 +594,10 @@
     dq_own, dq_core, total, near = gradients(
         "own", *common, k_list[:2], v_list[:2], dq_far, *accs
     )
-    total, near = add_far(total, back, near)
     near = down(near, 1)
+    total, dq_core = add_far(total, back, dq_core)
     dq_core = to_partner(dq_core, 1)
+    total = after(total, dq_core)
 
     sums = add_sums(total, near)
     sums = [sums[0]] + [to_partner(sums[flip], flip) for flip in range(1, QUAD)]

time: 96.3 us -> 92.8 us (0.964)
  starting transfers between devices: 40.2 us -> 32.8 us
  waiting for transfers between devices: 36.4 us -> 39.7 us
  Pallas kernels: 15.7 us -> 17.2 us
  local copies, waits for them, and re-layouts: 4.37 us -> 3.07 us
    ppermute x3, waiting for transfers between devices: 22 us -> 26.2 us  [down(): lax.ppermute(x, 'level', [(z + shift, z) for z in range(steps - shift)])]
    ppermute x18 -> x15, starting transfers between devices: 13.3 us -> 9.65 us  [to_partner(): lax.ppermute(x, ('side', 'core'), [(t, t ^ flip) for t in range(QUAD)])]
    ppermute x6, starting transfers between devices: 23 us -> 19.3 us  [up(): lax.ppermute(x, 'level', [(z, z + shift) for z in range(steps - shift)])]
    ppermute x18 -> x15, waiting for transfers between devices: 10.9 us -> 8.73 us  [to_partner(): lax.ppermute(x, ('side', 'core'), [(t, t ^ flip) for t in range(QUAD)])]
    pallas_call x3, Pallas kernels: 9.71 us -> 11.2 us  [gradients(): pl.pallas_call(functools.partial(grads_kernel, ancestors.shape[1], stage,...]
    unnamed x14, local copies, waits for them, and re-layouts: 4.35 us -> 3.05 us
    ppermute x6, waiting for transfers between devices: 3.56 us -> 4.78 us  [up(): lax.ppermute(x, 'level', [(z, z + shift) for z in range(steps - shift)])]
  transfers between devices with their start and end apart: 27 -> 24, of which waited for: 10 -> 12; matrix products, arithmetic and copies ran while one was open for 0% -> 0% of each run, Pallas kernels for 15% -> 17%
where the time goes in v8:
time: 92.8 us; the launch traced here: 93.7 us
  waiting for transfers between devices  39.7 us (43%)
  starting transfers between devices  32.8 us (35%)
  Pallas kernels  17.2 us (19%)
  local copies, waits for them, and re-layouts  3.07 us (3%)
    ppermute x3, waiting for transfers between devices, down(): lax.ppermute(x, 'level', [(z + shift, z) for z in range(steps - shift)])  26.2 us
    ppermute x6, starting transfers between devices, up(): lax.ppermute(x, 'level', [(z, z + shift) for z in range(steps - shift)])  19.3 us
    pallas_call x3, Pallas kernels, gradients(): pl.pallas_call(functools.partial(grads_kernel, ancestors.shape[1], stage,...  11.2 us
    ppermute x15, starting transfers between devices, to_partner(): lax.ppermute(x, ('side', 'core'), [(t, t ^ flip) for t in range(QUAD)])  9.65 us
    ppermute x15, waiting for transfers between devices, to_partner(): lax.ppermute(x, ('side', 'core'), [(t, t ^ flip) for t in range(QUAD)])  8.73 us
    ppermute x6, waiting for transfers between devices, up(): lax.ppermute(x, 'level', [(z, z + shift) for z in range(steps - shift)])  4.78 us
    ppermute x3, starting transfers between devices, down(): lax.ppermute(x, 'level', [(z + shift, z) for z in range(steps - shift)])  3.88 us
    pallas_call x1, Pallas kernels, statistics(): pl.pallas_call(functools.partial(stats_kernel, ancestors.shape[1], steps)...  3.3 us
  transfers between devices with their start and end apart: 24, of which 12 were waited for; matrix products, arithmetic and copies ran while one was open for 0% of the time, Pallas kernels for 17%

profile of v8, /device:TPU:0, one launch (start us, length us, event | category | flops | bytes accessed | tf_op | source)
XLA Modules:
  0.0 93.7 jit_solution(787982643046266477)
XLA Ops:
  0.6 0.0 copy-start
  0.6 0.5 collective-permute-start
  1.2 0.1 collective-permute-start.5
  1.2 0.9 copy-done.4
  2.1 0.9 copy-done.5
  3.1 0.5 collective-permute-start.1
  3.6 2.6 %collective-permute-start.2 = (bf16[128,256]{1,0:T(8,128)(2,1)S(1)}, bf16[128,256]{1,0:T(8,128)(2,1)S(1)}, u32[]{:S(2)}, u32[]{:S(2)}) collective-permute-start(bf16[128,256]{1,0:T(8,128)(2,1)S(1)} %get-tuple-element.38), channel_id=1, source_target_pairs={{0,2},{1,3},{2,0},{3,1},{4,6},{5,7},{6,4},{7,5},{8,10},{9,11},{10,... | collective-permute-start | bytes 196616 | tf_op jit(solution)/shard_map/ppermute | solution.py:558
  6.2 0.1 collective-permute-start.3
  6.3 0.0 collective-permute-done.1.refs_1_
  6.3 2.6 %collective-permute-done.2.refs_2_ = bf16[128,256]{1,0:T(8,128)(2,1)S(1)} collective-permute-done((bf16[128,256]{1,0:T(8,128)(2,1)S(1)}, bf16[128,256]{1,0:T(8,128)(2,1)S(1)}, u32[]{:S(2)}, u32[]{:S(2)}) %collective-permute-start.2) | collective-permute-done | bytes 65568 | tf_op jit(solution)/shard_map/ppermute | solution.py:558
  8.9 1.4 %collective-permute-done.3.refs_3_ = bf16[128,256]{1,0:T(8,128)(2,1)S(1)} collective-permute-done((bf16[128,256]{1,0:T(8,128)(2,1)S(1)}, bf16[128,256]{1,0:T(8,128)(2,1)S(1)}, u32[]{:S(2)}, u32[]{:S(2)}) %collective-permute-start.3) | collective-permute-done | bytes 65568 | tf_op jit(solution)/shard_map/ppermute | solution.py:558
  10.3 0.0 collective-permute-done.peer.rest_1_
  10.3 0.0 copy-start.2
  10.3 1.2 %copy-done.2 = bf16[128,4096]{1,0:T(8,128)(2,1)S(1)} copy-done((bf16[128,4096]{1,0:T(8,128)(2,1)S(1)}, bf16[128,4096]{1,0:T(8,128)(2,1)}, u32[]{:S(2)}) %copy-start.2) | copy-done | bytes 1048600
  11.6 0.0 copy-start.3
  11.6 0.0 copy-start.6
  11.6 1.4 %collective-permute-start.4 = (bf16[256,1024]{1,0:T(8,128)(2,1)S(1)}, bf16[256,1024]{1,0:T(8,128)(2,1)S(1)}, u32[]{:S(2)}, u32[]{:S(2)}) collective-permute-start(bf16[256,1024]{1,0:T(8,128)(2,1)S(1)} %pack_queries.2), channel_id=1, source_target_pairs={{0,2},{1,3},{2,0},{3,1},{4,6},{5,7},{6,4},{7,5},{8,10},{9,11},{10,... | collective-permute-start | bytes 1572872 | tf_op jit(solution)/shard_map/ppermute | solution.py:558
  13.0 5.5 %collective-permute-start.8 = (bf16[512,128]{1,0:T(8,128)(2,1)S(1)}, bf16[512,128]{1,0:T(8,128)(2,1)S(1)}, u32[]{:S(2)}, u32[]{:S(2)}) collective-permute-start(bf16[512,128]{1,0:T(8,128)(2,1)S(1)} %get-tuple-element.43.after_ref.rest_3_.rest_10_), channel_id=1, source_target_pairs={{0,12},{1,13},{2,14},{3,15},{16,28},{17,29},{18,30},{19,31}} | collective-permute-start | bytes 393224 | tf_op jit(solution)/shard_map/ppermute | solution.py:564
  18.5 1.3 %collective-permute-start.7 = (bf16[512,128]{1,0:T(8,128)(2,1)S(1)}, bf16[512,128]{1,0:T(8,128)(2,1)S(1)}, u32[]{:S(2)}, u32[]{:S(2)}) collective-permute-start(bf16[512,128]{1,0:T(8,128)(2,1)S(1)} %get-tuple-element.43.after_ref.rest_3_.rest_10_), channel_id=1, source_target_pairs={{0,8},{4,12},{1,9},{5,13},{2,10},{6,14},{3,11},{7,15},{16,24},{20,... | collective-permute-start | bytes 393224 | tf_op jit(solution)/shard_map/ppermute | solution.py:564
  19.8 2.5 %collective-permute-start.6 = (bf16[512,128]{1,0:T(8,128)(2,1)S(1)}, bf16[512,128]{1,0:T(8,128)(2,1)S(1)}, u32[]{:S(2)}, u32[]{:S(2)}) collective-permute-start(bf16[512,128]{1,0:T(8,128)(2,1)S(1)} %get-tuple-element.43.after_ref.rest_3_.rest_10_), channel_id=1, source_target_pairs={{0,4},{4,8},{8,12},{1,5},{5,9},{9,13},{2,6},{6,10},{10,14},{3,7},{... | collective-permute-start | bytes 393224 | tf_op jit(solution)/shard_map/ppermute | solution.py:564
  22.3 0.1 collective-permute-done.8.rest_6_.rest_11_
  22.4 2.8 %collective-permute-done.7.rest_5_.rest_10_ = bf16[512,128]{1,0:T(8,128)(2,1)S(1)} collective-permute-done((bf16[512,128]{1,0:T(8,128)(2,1)S(1)}, bf16[512,128]{1,0:T(8,128)(2,1)S(1)}, u32[]{:S(2)}, u32[]{:S(2)}) %collective-permute-start.7) | collective-permute-done | bytes 131104 | tf_op jit(solution)/shard_map/ppermute | solution.py:564
  25.2 1.8 %collective-permute-done.6.rest_4_.rest_11_ = bf16[512,128]{1,0:T(8,128)(2,1)S(1)} collective-permute-done((bf16[512,128]{1,0:T(8,128)(2,1)S(1)}, bf16[512,128]{1,0:T(8,128)(2,1)S(1)}, u32[]{:S(2)}, u32[]{:S(2)}) %collective-permute-start.6) | collective-permute-done | bytes 131104 | tf_op jit(solution)/shard_map/ppermute | solution.py:564
  27.1 0.0 collective-permute-done.5.peer.rest_4_
  27.1 0.8 collective-permute-start.9
  27.9 0.6 row_deltas.1
  28.5 0.1 collective-permute-start.10
  28.6 6.3 %collective-permute-start.14 = (bf16[512,128]{1,0:T(8,128)(2,1)S(1)}, bf16[512,128]{1,0:T(8,128)(2,1)S(1)}, u32[]{:S(2)}, u32[]{:S(2)}) collective-permute-start(bf16[512,128]{1,0:T(8,128)(2,1)S(1)} %get-tuple-element.48.rest_12_), channel_id=1, source_target_pairs={{0,12},{1,13},{2,14},{3,15},{16,28},{17,29},{18,30},{19,31}} | collective-permute-start | bytes 393224 | tf_op jit(solution)/shard_map/ppermute | solution.py:564
  34.8 2.5 %collective-permute-start.13 = (bf16[512,128]{1,0:T(8,128)(2,1)S(1)}, bf16[512,128]{1,0:T(8,128)(2,1)S(1)}, u32[]{:S(2)}, u32[]{:S(2)}) collective-permute-start(bf16[512,128]{1,0:T(8,128)(2,1)S(1)} %get-tuple-element.48.rest_12_), channel_id=1, source_target_pairs={{0,8},{4,12},{1,9},{5,13},{2,10},{6,14},{3,11},{7,15},{16,24},{20,... | collective-permute-start | bytes 393224 | tf_op jit(solution)/shard_map/ppermute | solution.py:564
  37.3 0.0 collective-permute-done.10.pair.rest_7_
  37.3 1.3 %collective-permute-start.12 = (bf16[512,128]{1,0:T(8,128)(2,1)S(1)}, bf16[512,128]{1,0:T(8,128)(2,1)S(1)}, u32[]{:S(2)}, u32[]{:S(2)}) collective-permute-start(bf16[512,128]{1,0:T(8,128)(2,1)S(1)} %get-tuple-element.48.rest_12_), channel_id=1, source_target_pairs={{0,4},{4,8},{8,12},{1,5},{5,9},{9,13},{2,6},{6,10},{10,14},{3,7},{... | collective-permute-start | bytes 393224 | tf_op jit(solution)/shard_map/ppermute | solution.py:564
  38.6 0.0 collective-permute-done.4.rest_2_
  38.7 1.4 %collective-permute-start.11 = (f32[16,128]{1,0:T(8,128)S(1)}, f32[16,128]{1,0:T(8,128)S(1)}, u32[]{:S(2)}, u32[]{:S(2)}) collective-permute-start(f32[16,128]{1,0:T(8,128)S(1)} %pack_deltas.1), channel_id=1, source_target_pairs={{0,2},{1,3},{2,0},{3,1},{4,6},{5,7},{6,4},{7,5},{8,10},{9,11},{10,... | collective-permute-start | bytes 24584 | tf_op jit(solution)/shard_map/ppermute | solution.py:558
  40.1 3.3 %statistics.1.rest_9_ = f32[4,1,1024]{2,1,0:T(1,128)S(1)} custom-call(s32[1]{0:T(128)} %bitcast.me_ref, s32[16,10]{1,0:T(8,128)S(1)} %copy-done.6, bf16[128,4096]{1,0:T(8,128)(2,1)S(1)} %copy-done.3, bf16[128,4096]{1,0:T(8,128)(2,1)S(1)} %collective-permute-done.peer.rest_1_, bf16[256,1024]{1,0:T(8,128)(2,1)S(1)} %collective-permute-done.4.rest_2_, ...), custom_call_target="tpu_custom_call" | custom-call | flops 2952790016 | bytes 16777216 | tf_op jit(solution)/shard_map/statistics/pallas_call | solution.py:327
  43.4 0.0 collective-permute-done.11.rest_8_
  43.4 0.0 collective-permute-done.14.rest_13_
  43.4 0.0 collective-permute-done.13.rest_12_
  43.4 0.0 collective-permute-done.9.rest_5_
  43.4 1.4 %far_grads.1 = (f32[4,128,1024]{2,1,0:T(8,128)S(1)}, bf16[512,256]{1,0:T(8,128)(2,1)S(1)}, bf16[512,256]{1,0:T(8,128)(2,1)S(1)}) custom-call(s32[1]{0:T(128)} %bitcast.me_ref, s32[16,10]{1,0:T(8,128)S(1)} %copy-done.6, bf16[128,4096]{1,0:T(8,128)(2,1)S(1)} %copy-done.3, bf16[128,4096]{1,0:T(8,128)(2,1)S(1)} %collective-permute-done.peer.rest_1_, ...), custom_call_target="tpu_custom_call" | custom-call | flops 14763950080 | bytes 16777216 | tf_op jit(solution)/shard_map/far_grads/pallas_call | solution.py:380
  44.8 1.3 %collective-permute-start.15 = (bf16[512,256]{1,0:T(8,128)(2,1)S(1)}, bf16[512,256]{1,0:T(8,128)(2,1)S(1)}, u32[]{:S(2)}, u32[]{:S(2)}) collective-permute-start(bf16[512,256]{1,0:T(8,128)(2,1)S(1)} %get-tuple-element.54), channel_id=1, source_target_pairs={{8,0},{12,4},{9,1},{13,5},{10,2},{14,6},{11,3},{15,7},{24,16},{28,... | collective-permute-start | bytes 786440 | tf_op jit(solution)/shard_map/ppermute | solution.py:570
  46.1 1.3 %collective-permute-start.16 = (bf16[512,256]{1,0:T(8,128)(2,1)S(1)}, bf16[512,256]{1,0:T(8,128)(2,1)S(1)}, u32[]{:S(2)}, u32[]{:S(2)}) collective-permute-start(bf16[512,256]{1,0:T(8,128)(2,1)S(1)} %get-tuple-element.55), channel_id=1, source_target_pairs={{12,0},{13,1},{14,2},{15,3},{28,16},{29,17},{30,18},{31,19}} | collective-permute-start | bytes 786440 | tf_op jit(solution)/shard_map/ppermute | solution.py:570
  47.4 0.0 collective-permute-done.12.rest_13_
  47.4 5.6 %side_grads.1 = (bf16[256,1024]{1,0:T(8,128)(2,1)S(1)}, f32[1024,128]{1,0:T(8,128)S(1)}, f32[1024,128]{1,0:T(8,128)S(1)}) custom-call(s32[1]{0:T(128)} %bitcast.me_ref, s32[16,10]{1,0:T(8,128)S(1)} %copy-done.6, bf16[128,4096]{1,0:T(8,128)(2,1)S(1)} %copy-done.3, bf16[128,4096]{1,0:T(8,128)(2,1)S(1)} %collective-permute-done.peer.rest_1_, ...), custom_call_target="tpu_custom_call" | custom-call | flops 14763950080 | bytes 16777216 | tf_op jit(solution)/shard_map/side_grads/pallas_call | solution.py:380
  53.0 0.1 collective-permute-start.18
  53.1 4.2 %own_grads.1 = (bf16[128,1024]{1,0:T(8,128)(2,1)S(1)}, bf16[128,1024]{1,0:T(8,128)(2,1)S(1)}, f32[512,256]{1,0:T(8,128)S(1)}, bf16[512,256]{1,0:T(8,128)(2,1)S(1)}) custom-call(s32[1]{0:T(128)} %bitcast.me_ref, s32[16,10]{1,0:T(8,128)S(1)} %copy-done.6, bf16[128,4096]{1,0:T(8,128)(2,1)S(1)} %copy-done.3, ...), custom_call_target="tpu_custom_call" | custom-call | flops 14763950080 | bytes 16777216 | tf_op jit(solution)/shard_map/own_grads/pallas_call | solution.py:380
  57.3 4.1 %collective-permute-done.15.refs_0_ = bf16[512,256]{1,0:T(8,128)(2,1)S(1)} collective-permute-done((bf16[512,256]{1,0:T(8,128)(2,1)S(1)}, bf16[512,256]{1,0:T(8,128)(2,1)S(1)}, u32[]{:S(2)}, u32[]{:S(2)}) %collective-permute-start.15) | collective-permute-done | bytes 262176 | tf_op jit(solution)/shard_map/ppermute | solution.py:570
  61.4 13.1 %collective-permute-done.16.refs_1_ = bf16[512,256]{1,0:T(8,128)(2,1)S(1)} collective-permute-done((bf16[512,256]{1,0:T(8,128)(2,1)S(1)}, bf16[512,256]{1,0:T(8,128)(2,1)S(1)}, u32[]{:S(2)}, u32[]{:S(2)}) %collective-permute-start.16) | collective-permute-done | bytes 262176 | tf_op jit(solution)/shard_map/ppermute | solution.py:570
  74.4 0.1 add_far.1
  74.5 0.1 collective-permute-start.17
  74.6 1.3 %collective-permute-start.19 = (bf16[512,256]{1,0:T(8,128)(2,1)S(1)}, bf16[512,256]{1,0:T(8,128)(2,1)S(1)}, u32[]{:S(2)}, u32[]{:S(2)}) collective-permute-start(bf16[512,256]{1,0:T(8,128)(2,1)S(1)} %get-tuple-element.61), channel_id=1, source_target_pairs={{4,0},{8,4},{12,8},{5,1},{9,5},{13,9},{6,2},{10,6},{14,10},{7,3},{... | collective-permute-start | bytes 786440 | tf_op jit(solution)/shard_map/ppermute | solution.py:570
  75.9 0.2 collective-permute-done.17.refs_1_
  76.1 9.1 %collective-permute-done.19.near_ref = bf16[512,256]{1,0:T(8,128)(2,1)S(1)} collective-permute-done((bf16[512,256]{1,0:T(8,128)(2,1)S(1)}, bf16[512,256]{1,0:T(8,128)(2,1)S(1)}, u32[]{:S(2)}, u32[]{:S(2)}) %collective-permute-start.19) | collective-permute-done | bytes 262176 | tf_op jit(solution)/shard_map/ppermute | solution.py:570
  85.2 0.1 add_sums.1
  85.3 0.1 collective-permute-start.20
  85.3 1.4 %collective-permute-start.21 = (bf16[128,256]{1,0:T(8,128)(2,1)S(1)}, bf16[128,256]{1,0:T(8,128)(2,1)S(1)}, u32[]{:S(2)}, u32[]{:S(2)}) collective-permute-start(bf16[128,256]{1,0:T(8,128)(2,1)S(1)} %get-tuple-element.64), channel_id=1, source_target_pairs={{0,2},{1,3},{2,0},{3,1},{4,6},{5,7},{6,4},{7,5},{8,10},{9,11},{10,... | collective-permute-start | bytes 196616 | tf_op jit(solution)/shard_map/ppermute | solution.py:558
  86.7 0.5 collective-permute-start.22
  87.2 0.0 collective-permute-done.18.refs_2_
  87.2 0.0 collective-permute-done.20.refs_1_
  87.2 2.8 %collective-permute-done.21.refs_2_ = bf16[128,256]{1,0:T(8,128)(2,1)S(1)} collective-permute-done((bf16[128,256]{1,0:T(8,128)(2,1)S(1)}, bf16[128,256]{1,0:T(8,128)(2,1)S(1)}, u32[]{:S(2)}, u32[]{:S(2)}) %collective-permute-start.21) | collective-permute-done | bytes 65568 | tf_op jit(solution)/shard_map/ppermute | solution.py:558
  90.0 1.0 %collective-permute-done.22.refs_3_ = bf16[128,256]{1,0:T(8,128)(2,1)S(1)} collective-permute-done((bf16[128,256]{1,0:T(8,128)(2,1)S(1)}, bf16[128,256]{1,0:T(8,128)(2,1)S(1)}, u32[]{:S(2)}, u32[]{:S(2)}) %collective-permute-start.22) | collective-permute-done | bytes 65568 | tf_op jit(solution)/shard_map/ppermute | solution.py:558
  91.1 0.2 collective-permute-start.23
  91.2 0.7 place_keys.1
  92.0 0.7 collective-permute-done.23.refs_3_
  92.7 1.0 %place_queries.1 = bf16[128,4096]{1,0:T(8,128)(2,1)} custom-call(s32[1]{0:T(128)} %bitcast.me_ref, bf16[128,1024]{1,0:T(8,128)(2,1)S(1)} %get-tuple-element.52.refs_0_, bf16[128,1024]{1,0:T(8,128)(2,1)S(1)} %collective-permute-done.17.refs_1_, bf16[256,1024]{1,0:T(8,128)(2,1)S(1)} %collective-permute-done.18.refs_2_, ...), custom_call_target="tpu_custom_call" | custom-call | tf_op jit(solution)/shard_map/place_queries/pallas_call | solution.py:524
  (13 shorter events, 0.2 us)
Async XLA Ops:
  0.6 26.4 %copy-start = (bf16[128,4096]{1,0:T(8,128)(2,1)S(1)}, bf16[128,4096]{1,0:T(8,128)(2,1)}, u32[]{:S(2)}) copy-start(bf16[128,4096]{1,0:T(8,128)(2,1)} %rest_3_.5) | copy-start | bytes 3145732
  0.6 9.7 %collective-permute-start = (bf16[128,4096]{1,0:T(8,128)(2,1)}, bf16[128,4096]{1,0:T(8,128)(2,1)S(1)}, u32[]{:S(2)}, u32[]{:S(2)}) collective-permute-start(bf16[128,4096]{1,0:T(8,128)(2,1)} %rest_0_.7), channel_id=1, source_target_pairs={{0,1},{1,0},{2,3},{3,2},{4,5},{5,4},{6,7},{7,6},{8,9},{9,8},{10,11... | collective-permute-start | bytes 3145736 | tf_op jit(solution)/shard_map/ppermute | solution.py:558
  1.2 25.9 %collective-permute-start.5 = (bf16[128,4096]{1,0:T(8,128)(2,1)}, bf16[128,4096]{1,0:T(8,128)(2,1)S(1)}, u32[]{:S(2)}, u32[]{:S(2)}) collective-permute-start(bf16[128,4096]{1,0:T(8,128)(2,1)} %rest_3_.5), channel_id=1, source_target_pairs={{0,1},{1,0},{2,3},{3,2},{4,5},{5,4},{6,7},{7,6},{8,9},{9,8},{10,11... | collective-permute-start | bytes 3145736 | tf_op jit(solution)/shard_map/ppermute | solution.py:558
  1.2 0.9 copy-start.4
  2.1 0.9 copy-start.5
  3.1 3.2 %collective-permute-start.1 = (bf16[128,256]{1,0:T(8,128)(2,1)S(1)}, bf16[128,256]{1,0:T(8,128)(2,1)S(1)}, u32[]{:S(2)}, u32[]{:S(2)}) collective-permute-start(bf16[128,256]{1,0:T(8,128)(2,1)S(1)} %get-tuple-element.37), channel_id=1, source_target_pairs={{0,1},{1,0},{2,3},{3,2},{4,5},{5,4},{6,7},{7,6},{8,9},{9,8},{10,11... | collective-permute-start | bytes 196616 | tf_op jit(solution)/shard_map/ppermute | solution.py:558
  3.6 5.3 %collective-permute-start.2 = (bf16[128,256]{1,0:T(8,128)(2,1)S(1)}, bf16[128,256]{1,0:T(8,128)(2,1)S(1)}, u32[]{:S(2)}, u32[]{:S(2)}) collective-permute-start(bf16[128,256]{1,0:T(8,128)(2,1)S(1)} %get-tuple-element.38), channel_id=1, source_target_pairs={{0,2},{1,3},{2,0},{3,1},{4,6},{5,7},{6,4},{7,5},{8,10},{9,11},{10,... | collective-permute-start | bytes 196616 | tf_op jit(solution)/shard_map/ppermute | solution.py:558
  6.2 4.0 %collective-permute-start.3 = (bf16[128,256]{1,0:T(8,128)(2,1)S(1)}, bf16[128,256]{1,0:T(8,128)(2,1)S(1)}, u32[]{:S(2)}, u32[]{:S(2)}) collective-permute-start(bf16[128,256]{1,0:T(8,128)(2,1)S(1)} %get-tuple-element.39), channel_id=1, source_target_pairs={{0,3},{1,2},{2,1},{3,0},{4,7},{5,6},{6,5},{7,4},{8,11},{9,10},{10,... | collective-permute-start | bytes 196616 | tf_op jit(solution)/shard_map/ppermute | solution.py:558
  10.3 1.2 %copy-start.2 = (bf16[128,4096]{1,0:T(8,128)(2,1)S(1)}, bf16[128,4096]{1,0:T(8,128)(2,1)}, u32[]{:S(2)}) copy-start(bf16[128,4096]{1,0:T(8,128)(2,1)} %rest_0_.7) | copy-start | bytes 3145732
  11.5 16.4 %copy-start.1 = (bf16[128,4096]{1,0:T(8,128)(2,1)S(1)}, bf16[128,4096]{1,0:T(8,128)(2,1)}, u32[]{:S(2)}) copy-start(bf16[128,4096]{1,0:T(8,128)(2,1)} %out_ref.1) | copy-start | bytes 3145732
  11.6 28.5 %copy-start.3 = (bf16[128,4096]{1,0:T(8,128)(2,1)S(1)}, bf16[128,4096]{1,0:T(8,128)(2,1)}, u32[]{:S(2)}) copy-start(bf16[128,4096]{1,0:T(8,128)(2,1)} %rest_0_.7) | copy-start | bytes 3145732
  11.6 28.5 %copy-start.6 = (s32[16,10]{1,0:T(8,128)S(1)}, s32[16,10]{1,0:T(8,128)}, u32[]{:S(2)}) copy-start(s32[16,10]{1,0:T(8,128)} %anc_ref.7) | copy-start | bytes 1924
  11.6 27.1 %collective-permute-start.4 = (bf16[256,1024]{1,0:T(8,128)(2,1)S(1)}, bf16[256,1024]{1,0:T(8,128)(2,1)S(1)}, u32[]{:S(2)}, u32[]{:S(2)}) collective-permute-start(bf16[256,1024]{1,0:T(8,128)(2,1)S(1)} %pack_queries.2), channel_id=1, source_target_pairs={{0,2},{1,3},{2,0},{3,1},{4,6},{5,7},{6,4},{7,5},{8,10},{9,11},{10,... | collective-permute-start | bytes 1572872 | tf_op jit(solution)/shard_map/ppermute | solution.py:558
  13.0 9.4 %collective-permute-start.8 = (bf16[512,128]{1,0:T(8,128)(2,1)S(1)}, bf16[512,128]{1,0:T(8,128)(2,1)S(1)}, u32[]{:S(2)}, u32[]{:S(2)}) collective-permute-start(bf16[512,128]{1,0:T(8,128)(2,1)S(1)} %get-tuple-element.43.after_ref.rest_3_.rest_10_), channel_id=1, source_target_pairs={{0,12},{1,13},{2,14},{3,15},{16,28},{17,29},{18,30},{19,31}} | collective-permute-start | bytes 393224 | tf_op jit(solution)/shard_map/ppermute | solution.py:564
  18.5 6.7 %collective-permute-start.7 = (bf16[512,128]{1,0:T(8,128)(2,1)S(1)}, bf16[512,128]{1,0:T(8,128)(2,1)S(1)}, u32[]{:S(2)}, u32[]{:S(2)}) collective-permute-start(bf16[512,128]{1,0:T(8,128)(2,1)S(1)} %get-tuple-element.43.after_ref.rest_3_.rest_10_), channel_id=1, source_target_pairs={{0,8},{4,12},{1,9},{5,13},{2,10},{6,14},{3,11},{7,15},{16,24},{20,... | collective-permute-start | bytes 393224 | tf_op jit(solution)/shard_map/ppermute | solution.py:564
  19.8 7.2 %collective-permute-start.6 = (bf16[512,128]{1,0:T(8,128)(2,1)S(1)}, bf16[512,128]{1,0:T(8,128)(2,1)S(1)}, u32[]{:S(2)}, u32[]{:S(2)}) collective-permute-start(bf16[512,128]{1,0:T(8,128)(2,1)S(1)} %get-tuple-element.43.after_ref.rest_3_.rest_10_), channel_id=1, source_target_pairs={{0,4},{4,8},{8,12},{1,5},{5,9},{9,13},{2,6},{6,10},{10,14},{3,7},{... | collective-permute-start | bytes 393224 | tf_op jit(solution)/shard_map/ppermute | solution.py:564
  27.1 16.3 %collective-permute-start.9 = (bf16[256,1024]{1,0:T(8,128)(2,1)S(1)}, bf16[256,1024]{1,0:T(8,128)(2,1)S(1)}, u32[]{:S(2)}, u32[]{:S(2)}) collective-permute-start(bf16[256,1024]{1,0:T(8,128)(2,1)S(1)} %pack_queries.3), channel_id=1, source_target_pairs={{0,2},{1,3},{2,0},{3,1},{4,6},{5,7},{6,4},{7,5},{8,10},{9,11},{10,... | collective-permute-start | bytes 1572872 | tf_op jit(solution)/shard_map/ppermute | solution.py:558
  28.5 8.8 %collective-permute-start.10 = (f32[16,128]{1,0:T(8,128)S(1)}, f32[16,128]{1,0:T(8,128)S(1)}, u32[]{:S(2)}, u32[]{:S(2)}) collective-permute-start(f32[16,128]{1,0:T(8,128)S(1)} %get-tuple-element.45), channel_id=1, source_target_pairs={{0,1},{1,0},{2,3},{3,2},{4,5},{5,4},{6,7},{7,6},{8,9},{9,8},{10,11... | collective-permute-start | bytes 24584 | tf_op jit(solution)/shard_map/ppermute | solution.py:558
  28.6 14.8 %collective-permute-start.14 = (bf16[512,128]{1,0:T(8,128)(2,1)S(1)}, bf16[512,128]{1,0:T(8,128)(2,1)S(1)}, u32[]{:S(2)}, u32[]{:S(2)}) collective-permute-start(bf16[512,128]{1,0:T(8,128)(2,1)S(1)} %get-tuple-element.48.rest_12_), channel_id=1, source_target_pairs={{0,12},{1,13},{2,14},{3,15},{16,28},{17,29},{18,30},{19,31}} | collective-permute-start | bytes 393224 | tf_op jit(solution)/shard_map/ppermute | solution.py:564
  34.8 8.5 %collective-permute-start.13 = (bf16[512,128]{1,0:T(8,128)(2,1)S(1)}, bf16[512,128]{1,0:T(8,128)(2,1)S(1)}, u32[]{:S(2)}, u32[]{:S(2)}) collective-permute-start(bf16[512,128]{1,0:T(8,128)(2,1)S(1)} %get-tuple-element.48.rest_12_), channel_id=1, source_target_pairs={{0,8},{4,12},{1,9},{5,13},{2,10},{6,14},{3,11},{7,15},{16,24},{20,... | collective-permute-start | bytes 393224 | tf_op jit(solution)/shard_map/ppermute | solution.py:564
  37.3 10.0 %collective-permute-start.12 = (bf16[512,128]{1,0:T(8,128)(2,1)S(1)}, bf16[512,128]{1,0:T(8,128)(2,1)S(1)}, u32[]{:S(2)}, u32[]{:S(2)}) collective-permute-start(bf16[512,128]{1,0:T(8,128)(2,1)S(1)} %get-tuple-element.48.rest_12_), channel_id=1, source_target_pairs={{0,4},{4,8},{8,12},{1,5},{5,9},{9,13},{2,6},{6,10},{10,14},{3,7},{... | collective-permute-start | bytes 393224 | tf_op jit(solution)/shard_map/ppermute | solution.py:564
  38.7 4.7 %collective-permute-start.11 = (f32[16,128]{1,0:T(8,128)S(1)}, f32[16,128]{1,0:T(8,128)S(1)}, u32[]{:S(2)}, u32[]{:S(2)}) collective-permute-start(f32[16,128]{1,0:T(8,128)S(1)} %pack_deltas.1), channel_id=1, source_target_pairs={{0,2},{1,3},{2,0},{3,1},{4,6},{5,7},{6,4},{7,5},{8,10},{9,11},{10,... | collective-permute-start | bytes 24584 | tf_op jit(solution)/shard_map/ppermute | solution.py:558
  44.8 16.6 %collective-permute-start.15 = (bf16[512,256]{1,0:T(8,128)(2,1)S(1)}, bf16[512,256]{1,0:T(8,128)(2,1)S(1)}, u32[]{:S(2)}, u32[]{:S(2)}) collective-permute-start(bf16[512,256]{1,0:T(8,128)(2,1)S(1)} %get-tuple-element.54), channel_id=1, source_target_pairs={{8,0},{12,4},{9,1},{13,5},{10,2},{14,6},{11,3},{15,7},{24,16},{28,... | collective-permute-start | bytes 786440 | tf_op jit(solution)/shard_map/ppermute | solution.py:570
  46.1 28.4 %collective-permute-start.16 = (bf16[512,256]{1,0:T(8,128)(2,1)S(1)}, bf16[512,256]{1,0:T(8,128)(2,1)S(1)}, u32[]{:S(2)}, u32[]{:S(2)}) collective-permute-start(bf16[512,256]{1,0:T(8,128)(2,1)S(1)} %get-tuple-element.55), channel_id=1, source_target_pairs={{12,0},{13,1},{14,2},{15,3},{28,16},{29,17},{30,18},{31,19}} | collective-permute-start | bytes 786440 | tf_op jit(solution)/shard_map/ppermute | solution.py:570
  53.0 34.2 %collective-permute-start.18 = (bf16[256,1024]{1,0:T(8,128)(2,1)S(1)}, bf16[256,1024]{1,0:T(8,128)(2,1)S(1)}, u32[]{:S(2)}, u32[]{:S(2)}) collective-permute-start(bf16[256,1024]{1,0:T(8,128)(2,1)S(1)} %get-tuple-element.58), channel_id=1, source_target_pairs={{0,2},{1,3},{2,0},{3,1},{4,6},{5,7},{6,4},{7,5},{8,10},{9,11},{10,... | collective-permute-start | bytes 1572872 | tf_op jit(solution)/shard_map/ppermute | solution.py:558
  74.5 1.6 %collective-permute-start.17 = (bf16[128,1024]{1,0:T(8,128)(2,1)S(1)}, bf16[128,1024]{1,0:T(8,128)(2,1)S(1)}, u32[]{:S(2)}, u32[]{:S(2)}) collective-permute-start(bf16[128,1024]{1,0:T(8,128)(2,1)S(1)} %get-tuple-element.57), channel_id=1, source_target_pairs={{0,1},{1,0},{2,3},{3,2},{4,5},{5,4},{6,7},{7,6},{8,9},{9,8},{10,11... | collective-permute-start | bytes 786440 | tf_op jit(solution)/shard_map/ppermute | solution.py:558
  74.6 10.6 %collective-permute-start.19 = (bf16[512,256]{1,0:T(8,128)(2,1)S(1)}, bf16[512,256]{1,0:T(8,128)(2,1)S(1)}, u32[]{:S(2)}, u32[]{:S(2)}) collective-permute-start(bf16[512,256]{1,0:T(8,128)(2,1)S(1)} %get-tuple-element.61), channel_id=1, source_target_pairs={{4,0},{8,4},{12,8},{5,1},{9,5},{13,9},{6,2},{10,6},{14,10},{7,3},{... | collective-permute-start | bytes 786440 | tf_op jit(solution)/shard_map/ppermute | solution.py:570
  85.3 1.9 %collective-permute-start.20 = (bf16[128,256]{1,0:T(8,128)(2,1)S(1)}, bf16[128,256]{1,0:T(8,128)(2,1)S(1)}, u32[]{:S(2)}, u32[]{:S(2)}) collective-permute-start(bf16[128,256]{1,0:T(8,128)(2,1)S(1)} %get-tuple-element.63), channel_id=1, source_target_pairs={{0,1},{1,0},{2,3},{3,2},{4,5},{5,4},{6,7},{7,6},{8,9},{9,8},{10,11... | collective-permute-start | bytes 196616 | tf_op jit(solution)/shard_map/ppermute | solution.py:558
  85.3 4.7 %collective-permute-start.21 = (bf16[128,256]{1,0:T(8,128)(2,1)S(1)}, bf16[128,256]{1,0:T(8,128)(2,1)S(1)}, u32[]{:S(2)}, u32[]{:S(2)}) collective-permute-start(bf16[128,256]{1,0:T(8,128)(2,1)S(1)} %get-tuple-element.64), channel_id=1, source_target_pairs={{0,2},{1,3},{2,0},{3,1},{4,6},{5,7},{6,4},{7,5},{8,10},{9,11},{10,... | collective-permute-start | bytes 196616 | tf_op jit(solution)/shard_map/ppermute | solution.py:558
  86.7 4.3 %collective-permute-start.22 = (bf16[128,256]{1,0:T(8,128)(2,1)S(1)}, bf16[128,256]{1,0:T(8,128)(2,1)S(1)}, u32[]{:S(2)}, u32[]{:S(2)}) collective-permute-start(bf16[128,256]{1,0:T(8,128)(2,1)S(1)} %get-tuple-element.65), channel_id=1, source_target_pairs={{0,3},{1,2},{2,1},{3,0},{4,7},{5,6},{6,5},{7,4},{8,11},{9,10},{10,... | collective-permute-start | bytes 196616 | tf_op jit(solution)/shard_map/ppermute | solution.py:558
  91.1 1.6 %collective-permute-start.23 = (bf16[128,1024]{1,0:T(8,128)(2,1)S(1)}, bf16[128,1024]{1,0:T(8,128)(2,1)S(1)}, u32[]{:S(2)}, u32[]{:S(2)}) collective-permute-start(bf16[128,1024]{1,0:T(8,128)(2,1)S(1)} %slice.3), channel_id=1, source_target_pairs={{0,1},{1,0},{2,3},{3,2},{4,5},{5,4},{6,7},{7,6},{8,9},{9,8},{10,11... | collective-permute-start | bytes 786440 | tf_op jit(solution)/shard_map/ppermute | solution.py:558

commit v9 on v8

--- a/solution.py
+++ b/solution.py
@@ -115,12 +115,17 @@
     return key_pos - query_pos <= jnp.where((flags & 4) != 0, 0, TILE)
 
 
+def query_tiles(me_ref, own, peer, side):
+    at = head_columns(own_head(me_ref), ROWS)
+    return four_tiles(own.at[:, at], peer.at[:, at], side, TILE)
+
+
 def four_tiles(own, peer, side, rows):
     return own, peer, side.at[:rows, :], side.at[rows:, :]
 
 
 def stats_kernel(depth, steps, me_ref, anc_ref, *rest):
-    q_refs, rest = four_tiles(*rest[:3], TILE), rest[3:]
+    q_refs, rest = query_tiles(me_ref, *rest[:3]), rest[3:]
     k_refs = rest[:steps]
     lse_ref, q_all, k_all, item_max, item_sum, *items = rest[steps:]
     me = me_ref[0]
@@ -176,7 +181,7 @@
 
 
 def grads_kernel(depth, stage, steps, me_ref, anc_ref, *rest):
-    q_refs, g_refs = four_tiles(*rest[:3], TILE), four_tiles(*rest[3:6], TILE)
+    q_refs, g_refs = query_tiles(me_ref, *rest[:3]), query_tiles(me_ref, *rest[3:6])
     d_refs, rest = four_tiles(*rest[6:9], GROUP), rest[9:]
     lse_ref, rest = rest[0], rest[1:]
     kv_refs, rest = rest[: 2 * steps], rest[2 * steps :]
@@ -218,7 +223,7 @@
     if stage == "far":
         dq_acc[...] = jnp.zeros_like(dq_acc)
     else:
-        dq_acc[...] = dq_in[...]
+        dq_acc[...] = dq_in[tiles[0] : tiles[0] + 2]
     for buffer in buffers[1]:
         buffer[...] = jnp.zeros_like(buffer)
     count = list_items(items, anc_ref, me, tiles, depth, "far" if stage == "far" else "near")
@@ -301,23 +306,8 @@
     )
 
 
-def fixed(shape):
-    return pl.BlockSpec(shape, lambda i, *_: (0,) * len(shape))
-
-
 def own_head(me_ref):
     return ((me_ref[0] & 1) << 1) | ((me_ref[0] >> 1) & 1)
-
-
-WIDE = pl.BlockSpec((TILE, ROWS), lambda i, me_ref, anc_ref: (0, own_head(me_ref)))
-LSE = fixed((QUAD, 1, ROWS))
-KEYS = fixed((LEVEL, HD))
-SUMS = fixed((LEVEL, 2 * HD))
-DQ = fixed((QUAD, HD, ROWS))
-PIECE = fixed((TILE, ROWS))
-SIDE = fixed((PAIR, ROWS))
-DELTA = fixed((GROUP, TILE))
-PAIR_DELTA = fixed((2 * GROUP, TILE))
 
 
 def statistics(me, ancestors, q_set, k_list):
@@ -329,8 +319,8 @@
         grid_spec=pltpu.PrefetchScalarGridSpec(
             num_scalar_prefetch=2,
             grid=(1,),
-            in_specs=[WIDE, WIDE, SIDE] + [KEYS] * steps,
-            out_specs=LSE,
+            in_specs=[HERE] * (3 + steps),
+            out_specs=HERE,
             scratch_shapes=[
                 pltpu.VMEM((QUAD, TILE, ROWS), jnp.bfloat16),
                 pltpu.VMEM((steps * LEVEL, HD), jnp.bfloat16),
@@ -353,17 +343,12 @@
     wide = jax.ShapeDtypeStruct((TILE, ROWS), jnp.bfloat16)
     sums = [jax.ShapeDtypeStruct((LEVEL, 2 * HD), jnp.bfloat16)] * steps
     accs = [jax.ShapeDtypeStruct(acc, jnp.float32)] * 2
-    dq_half = pl.BlockSpec((2, HD, ROWS), lambda i, *_: (1 if stage == "side" else 0, 0, 0))
-    extra_specs = [dq_half, fixed(acc), fixed(acc)][: len(carried)]
     if stage == "far":
-        out_specs = [DQ] + [SUMS] * steps
         out_shape = [jax.ShapeDtypeStruct((QUAD, HD, ROWS), jnp.float32)] + sums
     elif stage == "side":
-        out_specs = [SIDE, fixed(acc), fixed(acc)]
         out_shape = [jax.ShapeDtypeStruct((PAIR, ROWS), jnp.bfloat16)] + accs
     else:
         sums[0] = jax.ShapeDtypeStruct((LEVEL, 2 * HD), jnp.float32)
-        out_specs = [PIECE, PIECE] + [SUMS] * steps
         out_shape = [wide, wide] + sums
     scratch = item_scratch(tiles, ancestors.shape[1]) + [
         pltpu.VMEM((tiles, TILE, ROWS), jnp.bfloat16),
@@ -382,10 +367,8 @@
         grid_spec=pltpu.PrefetchScalarGridSpec(
             num_scalar_prefetch=2,
             grid=(1,),
-            in_specs=[WIDE, WIDE, SIDE] * 2 + [DELTA, PAIR_DELTA, PAIR_DELTA, LSE]
-            + [KEYS] * (2 * steps)
-            + extra_specs,
-            out_specs=out_specs,
+            in_specs=[HERE] * (10 + 2 * steps + len(carried)),
+            out_specs=[HERE] * len(out_shape),
             scratch_shapes=scratch,
         ),
         out_shape=out_shape,
@@ -600,8 +583,8 @@
     total = after(total, dq_core)
 
     sums = add_sums(total, near)
+    dq_side = after(dq_side, sums)
     sums = [sums[0]] + [to_partner(sums[flip], flip) for flip in range(1, QUAD)]
-    dq_side = after(dq_side, sums)
     dq_corner = to_partner(dq_side[TILE:], 1)
     return (
         place_queries(me, dq_own, dq_core, dq_side, dq_corner),

time: 92.8 us -> 93.5 us (level); the launches traced: 93.7 us -> 91.9 us
  Pallas kernels: 17.2 us -> 15.7 us
    pallas_call x3, Pallas kernels: 11.2 us -> 9.72 us  [gradients(): pl.pallas_call(functools.partial(grads_kernel, ancestors.shape[1], stage,...]
  transfers between devices with their start and end apart: 24 -> 24, of which waited for: 12 -> 11; matrix products, arithmetic and copies ran while one was open for 0% -> 0% of each run, Pallas kernels for 17% -> 16%
where the time goes in v9:
time: 93.5 us; the launch traced here: 91.9 us
  waiting for transfers between devices  38.8 us (41%)
  starting transfers between devices  33.4 us (36%)
  Pallas kernels  15.7 us (17%)
  local copies, waits for them, and re-layouts  3.07 us (3%)
    ppermute x3, waiting for transfers between devices, down(): lax.ppermute(x, 'level', [(z + shift, z) for z in range(steps - shift)])  25.6 us
    ppermute x6, starting transfers between devices, up(): lax.ppermute(x, 'level', [(z, z + shift) for z in range(steps - shift)])  19.3 us
    ppermute x15, starting transfers between devices, to_partner(): lax.ppermute(x, ('side', 'core'), [(t, t ^ flip) for t in range(QUAD)])  10.2 us
    pallas_call x3, Pallas kernels, gradients(): pl.pallas_call(functools.partial(grads_kernel, ancestors.shape[1], stage,...  9.72 us
    ppermute x15, waiting for transfers between devices, to_partner(): lax.ppermute(x, ('side', 'core'), [(t, t ^ flip) for t in range(QUAD)])  8.48 us
    ppermute x6, waiting for transfers between devices, up(): lax.ppermute(x, 'level', [(z, z + shift) for z in range(steps - shift)])  4.78 us
    ppermute x3, starting transfers between devices, down(): lax.ppermute(x, 'level', [(z + shift, z) for z in range(steps - shift)])  3.88 us
    pallas_call x1, Pallas kernels, statistics(): pl.pallas_call(functools.partial(stats_kernel, ancestors.shape[1], steps)...  3.25 us
  transfers between devices with their start and end apart: 24, of which 11 were waited for; matrix products, arithmetic and copies ran while one was open for 0% of the time, Pallas kernels for 16%

profile of v9, /device:TPU:0, one launch (start us, length us, event | category | flops | bytes accessed | tf_op | source)
XLA Modules:
  0.0 91.9 jit_solution(69163997502240441)
XLA Ops:
  0.6 0.5 collective-permute-start
  1.2 0.1 collective-permute-start.5
  1.2 0.9 copy-done.4
  2.1 0.9 copy-done.5
  3.1 0.5 collective-permute-start.1
  3.6 2.6 %collective-permute-start.2 = (bf16[128,256]{1,0:T(8,128)(2,1)S(1)}, bf16[128,256]{1,0:T(8,128)(2,1)S(1)}, u32[]{:S(2)}, u32[]{:S(2)}) collective-permute-start(bf16[128,256]{1,0:T(8,128)(2,1)S(1)} %get-tuple-element.38), channel_id=1, source_target_pairs={{0,2},{1,3},{2,0},{3,1},{4,6},{5,7},{6,4},{7,5},{8,10},{9,11},{10,... | collective-permute-start | bytes 196616 | tf_op jit(solution)/shard_map/ppermute | solution.py:541
  6.2 0.1 collective-permute-start.3
  6.3 0.0 collective-permute-done.1.refs_1_
  6.3 2.6 %collective-permute-done.2.refs_2_ = bf16[128,256]{1,0:T(8,128)(2,1)S(1)} collective-permute-done((bf16[128,256]{1,0:T(8,128)(2,1)S(1)}, bf16[128,256]{1,0:T(8,128)(2,1)S(1)}, u32[]{:S(2)}, u32[]{:S(2)}) %collective-permute-start.2) | collective-permute-done | bytes 65568 | tf_op jit(solution)/shard_map/ppermute | solution.py:541
  8.9 1.4 %collective-permute-done.3.refs_3_ = bf16[128,256]{1,0:T(8,128)(2,1)S(1)} collective-permute-done((bf16[128,256]{1,0:T(8,128)(2,1)S(1)}, bf16[128,256]{1,0:T(8,128)(2,1)S(1)}, u32[]{:S(2)}, u32[]{:S(2)}) %collective-permute-start.3) | collective-permute-done | bytes 65568 | tf_op jit(solution)/shard_map/ppermute | solution.py:541
  10.3 0.0 collective-permute-done.peer.rest_1_
  10.3 0.0 copy-start.2
  10.3 1.2 %copy-done.2 = bf16[128,4096]{1,0:T(8,128)(2,1)S(1)} copy-done((bf16[128,4096]{1,0:T(8,128)(2,1)S(1)}, bf16[128,4096]{1,0:T(8,128)(2,1)}, u32[]{:S(2)}) %copy-start.2) | copy-done | bytes 1048600
  11.6 0.0 copy-start.3
  11.6 0.0 copy-start.6
  11.6 1.4 %collective-permute-start.4 = (bf16[256,1024]{1,0:T(8,128)(2,1)S(1)}, bf16[256,1024]{1,0:T(8,128)(2,1)S(1)}, u32[]{:S(2)}, u32[]{:S(2)}) collective-permute-start(bf16[256,1024]{1,0:T(8,128)(2,1)S(1)} %pack_queries.2), channel_id=1, source_target_pairs={{0,2},{1,3},{2,0},{3,1},{4,6},{5,7},{6,4},{7,5},{8,10},{9,11},{10,... | collective-permute-start | bytes 1572872 | tf_op jit(solution)/shard_map/ppermute | solution.py:541
  13.0 5.5 %collective-permute-start.8 = (bf16[512,128]{1,0:T(8,128)(2,1)S(1)}, bf16[512,128]{1,0:T(8,128)(2,1)S(1)}, u32[]{:S(2)}, u32[]{:S(2)}) collective-permute-start(bf16[512,128]{1,0:T(8,128)(2,1)S(1)} %get-tuple-element.43.after_ref.rest_3_.rest_10_), channel_id=1, source_target_pairs={{0,12},{1,13},{2,14},{3,15},{16,28},{17,29},{18,30},{19,31}} | collective-permute-start | bytes 393224 | tf_op jit(solution)/shard_map/ppermute | solution.py:547
  18.5 1.3 %collective-permute-start.7 = (bf16[512,128]{1,0:T(8,128)(2,1)S(1)}, bf16[512,128]{1,0:T(8,128)(2,1)S(1)}, u32[]{:S(2)}, u32[]{:S(2)}) collective-permute-start(bf16[512,128]{1,0:T(8,128)(2,1)S(1)} %get-tuple-element.43.after_ref.rest_3_.rest_10_), channel_id=1, source_target_pairs={{0,8},{4,12},{1,9},{5,13},{2,10},{6,14},{3,11},{7,15},{16,24},{20,... | collective-permute-start | bytes 393224 | tf_op jit(solution)/shard_map/ppermute | solution.py:547
  19.8 2.5 %collective-permute-start.6 = (bf16[512,128]{1,0:T(8,128)(2,1)S(1)}, bf16[512,128]{1,0:T(8,128)(2,1)S(1)}, u32[]{:S(2)}, u32[]{:S(2)}) collective-permute-start(bf16[512,128]{1,0:T(8,128)(2,1)S(1)} %get-tuple-element.43.after_ref.rest_3_.rest_10_), channel_id=1, source_target_pairs={{0,4},{4,8},{8,12},{1,5},{5,9},{9,13},{2,6},{6,10},{10,14},{3,7},{... | collective-permute-start | bytes 393224 | tf_op jit(solution)/shard_map/ppermute | solution.py:547
  22.3 0.1 collective-permute-done.8.rest_6_.rest_11_
  22.4 2.8 %collective-permute-done.7.rest_5_.rest_10_ = bf16[512,128]{1,0:T(8,128)(2,1)S(1)} collective-permute-done((bf16[512,128]{1,0:T(8,128)(2,1)S(1)}, bf16[512,128]{1,0:T(8,128)(2,1)S(1)}, u32[]{:S(2)}, u32[]{:S(2)}) %collective-permute-start.7) | collective-permute-done | bytes 131104 | tf_op jit(solution)/shard_map/ppermute | solution.py:547
  25.2 1.8 %collective-permute-done.6.rest_4_.rest_11_ = bf16[512,128]{1,0:T(8,128)(2,1)S(1)} collective-permute-done((bf16[512,128]{1,0:T(8,128)(2,1)S(1)}, bf16[512,128]{1,0:T(8,128)(2,1)S(1)}, u32[]{:S(2)}, u32[]{:S(2)}) %collective-permute-start.6) | collective-permute-done | bytes 131104 | tf_op jit(solution)/shard_map/ppermute | solution.py:547
  27.1 0.0 collective-permute-done.5.peer.rest_4_
  27.1 0.0 copy-done
  27.1 0.8 collective-permute-start.9
  27.9 0.6 row_deltas.1
  28.5 0.1 collective-permute-start.10
  28.6 6.3 %collective-permute-start.14 = (bf16[512,128]{1,0:T(8,128)(2,1)S(1)}, bf16[512,128]{1,0:T(8,128)(2,1)S(1)}, u32[]{:S(2)}, u32[]{:S(2)}) collective-permute-start(bf16[512,128]{1,0:T(8,128)(2,1)S(1)} %get-tuple-element.48.rest_12_), channel_id=1, source_target_pairs={{0,12},{1,13},{2,14},{3,15},{16,28},{17,29},{18,30},{19,31}} | collective-permute-start | bytes 393224 | tf_op jit(solution)/shard_map/ppermute | solution.py:547
  34.8 2.5 %collective-permute-start.13 = (bf16[512,128]{1,0:T(8,128)(2,1)S(1)}, bf16[512,128]{1,0:T(8,128)(2,1)S(1)}, u32[]{:S(2)}, u32[]{:S(2)}) collective-permute-start(bf16[512,128]{1,0:T(8,128)(2,1)S(1)} %get-tuple-element.48.rest_12_), channel_id=1, source_target_pairs={{0,8},{4,12},{1,9},{5,13},{2,10},{6,14},{3,11},{7,15},{16,24},{20,... | collective-permute-start | bytes 393224 | tf_op jit(solution)/shard_map/ppermute | solution.py:547
  37.3 0.0 collective-permute-done.10.pair.rest_7_
  37.3 1.3 %collective-permute-start.12 = (bf16[512,128]{1,0:T(8,128)(2,1)S(1)}, bf16[512,128]{1,0:T(8,128)(2,1)S(1)}, u32[]{:S(2)}, u32[]{:S(2)}) collective-permute-start(bf16[512,128]{1,0:T(8,128)(2,1)S(1)} %get-tuple-element.48.rest_12_), channel_id=1, source_target_pairs={{0,4},{4,8},{8,12},{1,5},{5,9},{9,13},{2,6},{6,10},{10,14},{3,7},{... | collective-permute-start | bytes 393224 | tf_op jit(solution)/shard_map/ppermute | solution.py:547
  38.6 0.0 collective-permute-done.4.rest_2_
  38.7 1.4 %collective-permute-start.11 = (f32[16,128]{1,0:T(8,128)S(1)}, f32[16,128]{1,0:T(8,128)S(1)}, u32[]{:S(2)}, u32[]{:S(2)}) collective-permute-start(f32[16,128]{1,0:T(8,128)S(1)} %pack_deltas.1), channel_id=1, source_target_pairs={{0,2},{1,3},{2,0},{3,1},{4,6},{5,7},{6,4},{7,5},{8,10},{9,11},{10,... | collective-permute-start | bytes 24584 | tf_op jit(solution)/shard_map/ppermute | solution.py:541
  40.1 3.3 %statistics.1.rest_9_ = f32[4,1,1024]{2,1,0:T(1,128)S(1)} custom-call(s32[1]{0:T(128)} %bitcast.me_ref, s32[16,10]{1,0:T(8,128)S(1)} %copy-done.6, bf16[128,4096]{1,0:T(8,128)(2,1)S(1)} %copy-done.3, bf16[128,4096]{1,0:T(8,128)(2,1)S(1)} %collective-permute-done.peer.rest_1_, bf16[256,1024]{1,0:T(8,128)(2,1)S(1)} %collective-permute-done.4.rest_2_, ...), custom_call_target="tpu_custom_call" | custom-call | flops 2952790016 | bytes 16777216 | tf_op jit(solution)/shard_map/statistics/pallas_call | solution.py:317
  43.3 0.0 collective-permute-done.11.rest_8_
  43.3 0.0 collective-permute-done.14.rest_13_
  43.3 0.0 collective-permute-done.13.rest_12_
  43.3 0.0 collective-permute-done.9.rest_5_
  43.4 1.4 %far_grads.1 = (f32[4,128,1024]{2,1,0:T(8,128)S(1)}, bf16[512,256]{1,0:T(8,128)(2,1)S(1)}, bf16[512,256]{1,0:T(8,128)(2,1)S(1)}) custom-call(s32[1]{0:T(128)} %bitcast.me_ref, s32[16,10]{1,0:T(8,128)S(1)} %copy-done.6, bf16[128,4096]{1,0:T(8,128)(2,1)S(1)} %copy-done.3, bf16[128,4096]{1,0:T(8,128)(2,1)S(1)} %collective-permute-done.peer.rest_1_, ...), custom_call_target="tpu_custom_call" | custom-call | flops 14763950080 | bytes 16777216 | tf_op jit(solution)/shard_map/far_grads/pallas_call | solution.py:365
  44.7 1.3 %collective-permute-start.15 = (bf16[512,256]{1,0:T(8,128)(2,1)S(1)}, bf16[512,256]{1,0:T(8,128)(2,1)S(1)}, u32[]{:S(2)}, u32[]{:S(2)}) collective-permute-start(bf16[512,256]{1,0:T(8,128)(2,1)S(1)} %get-tuple-element.54), channel_id=1, source_target_pairs={{8,0},{12,4},{9,1},{13,5},{10,2},{14,6},{11,3},{15,7},{24,16},{28,... | collective-permute-start | bytes 786440 | tf_op jit(solution)/shard_map/ppermute | solution.py:553
  46.0 1.3 %collective-permute-start.16 = (bf16[512,256]{1,0:T(8,128)(2,1)S(1)}, bf16[512,256]{1,0:T(8,128)(2,1)S(1)}, u32[]{:S(2)}, u32[]{:S(2)}) collective-permute-start(bf16[512,256]{1,0:T(8,128)(2,1)S(1)} %get-tuple-element.55), channel_id=1, source_target_pairs={{12,0},{13,1},{14,2},{15,3},{28,16},{29,17},{30,18},{31,19}} | collective-permute-start | bytes 786440 | tf_op jit(solution)/shard_map/ppermute | solution.py:553
  47.3 0.0 collective-permute-done.12.rest_13_
  47.3 4.2 %side_grads.1 = (bf16[256,1024]{1,0:T(8,128)(2,1)S(1)}, f32[1024,128]{1,0:T(8,128)S(1)}, f32[1024,128]{1,0:T(8,128)S(1)}) custom-call(s32[1]{0:T(128)} %bitcast.me_ref, s32[16,10]{1,0:T(8,128)S(1)} %copy-done.6, bf16[128,4096]{1,0:T(8,128)(2,1)S(1)} %copy-done.3, bf16[128,4096]{1,0:T(8,128)(2,1)S(1)} %collective-permute-done.peer.rest_1_, ...), custom_call_target="tpu_custom_call" | custom-call | flops 14763950080 | bytes 16777216 | tf_op jit(solution)/shard_map/side_grads/pallas_call | solution.py:365
  51.5 0.8 collective-permute-start.18
  52.3 4.2 %own_grads.1 = (bf16[128,1024]{1,0:T(8,128)(2,1)S(1)}, bf16[128,1024]{1,0:T(8,128)(2,1)S(1)}, f32[512,256]{1,0:T(8,128)S(1)}, bf16[512,256]{1,0:T(8,128)(2,1)S(1)}) custom-call(s32[1]{0:T(128)} %bitcast.me_ref, s32[16,10]{1,0:T(8,128)S(1)} %copy-done.6, bf16[128,4096]{1,0:T(8,128)(2,1)S(1)} %copy-done.3, ...), custom_call_target="tpu_custom_call" | custom-call | flops 14763950080 | bytes 16777216 | tf_op jit(solution)/shard_map/own_grads/pallas_call | solution.py:365
  56.5 4.6 %collective-permute-done.15.refs_0_ = bf16[512,256]{1,0:T(8,128)(2,1)S(1)} collective-permute-done((bf16[512,256]{1,0:T(8,128)(2,1)S(1)}, bf16[512,256]{1,0:T(8,128)(2,1)S(1)}, u32[]{:S(2)}, u32[]{:S(2)}) %collective-permute-start.15) | collective-permute-done | bytes 262176 | tf_op jit(solution)/shard_map/ppermute | solution.py:553
  61.1 11.9 %collective-permute-done.16.refs_1_ = bf16[512,256]{1,0:T(8,128)(2,1)S(1)} collective-permute-done((bf16[512,256]{1,0:T(8,128)(2,1)S(1)}, bf16[512,256]{1,0:T(8,128)(2,1)S(1)}, u32[]{:S(2)}, u32[]{:S(2)}) %collective-permute-start.16) | collective-permute-done | bytes 262176 | tf_op jit(solution)/shard_map/ppermute | solution.py:553
  73.0 0.1 add_far.1
  73.1 0.1 collective-permute-start.17
  73.1 1.3 %collective-permute-start.19 = (bf16[512,256]{1,0:T(8,128)(2,1)S(1)}, bf16[512,256]{1,0:T(8,128)(2,1)S(1)}, u32[]{:S(2)}, u32[]{:S(2)}) collective-permute-start(bf16[512,256]{1,0:T(8,128)(2,1)S(1)} %get-tuple-element.61), channel_id=1, source_target_pairs={{4,0},{8,4},{12,8},{5,1},{9,5},{13,9},{6,2},{10,6},{14,10},{7,3},{... | collective-permute-start | bytes 786440 | tf_op jit(solution)/shard_map/ppermute | solution.py:553
  74.4 0.2 collective-permute-done.17.refs_1_
  74.7 9.1 %collective-permute-done.19.near_ref = bf16[512,256]{1,0:T(8,128)(2,1)S(1)} collective-permute-done((bf16[512,256]{1,0:T(8,128)(2,1)S(1)}, bf16[512,256]{1,0:T(8,128)(2,1)S(1)}, u32[]{:S(2)}, u32[]{:S(2)}) %collective-permute-start.19) | collective-permute-done | bytes 262176 | tf_op jit(solution)/shard_map/ppermute | solution.py:553
  83.7 0.1 add_sums.1
  83.8 0.0 collective-permute-done.18.refs_2_
  83.8 0.1 collective-permute-start.20
  83.9 0.5 collective-permute-start.21
  84.4 1.3 %collective-permute-start.22 = (bf16[128,256]{1,0:T(8,128)(2,1)S(1)}, bf16[128,256]{1,0:T(8,128)(2,1)S(1)}, u32[]{:S(2)}, u32[]{:S(2)}) collective-permute-start(bf16[128,256]{1,0:T(8,128)(2,1)S(1)} %get-tuple-element.64), channel_id=1, source_target_pairs={{0,2},{1,3},{2,0},{3,1},{4,6},{5,7},{6,4},{7,5},{8,10},{9,11},{10,... | collective-permute-start | bytes 196616 | tf_op jit(solution)/shard_map/ppermute | solution.py:541
  85.7 0.1 collective-permute-start.23
  85.8 0.0 collective-permute-done.21.refs_1_
  85.8 2.8 %collective-permute-done.22.refs_2_ = bf16[128,256]{1,0:T(8,128)(2,1)S(1)} collective-permute-done((bf16[128,256]{1,0:T(8,128)(2,1)S(1)}, bf16[128,256]{1,0:T(8,128)(2,1)S(1)}, u32[]{:S(2)}, u32[]{:S(2)}) %collective-permute-start.22) | collective-permute-done | bytes 65568 | tf_op jit(solution)/shard_map/ppermute | solution.py:541
  88.7 1.4 %collective-permute-done.23.refs_3_ = bf16[128,256]{1,0:T(8,128)(2,1)S(1)} collective-permute-done((bf16[128,256]{1,0:T(8,128)(2,1)S(1)}, bf16[128,256]{1,0:T(8,128)(2,1)S(1)}, u32[]{:S(2)}, u32[]{:S(2)}) %collective-permute-start.23) | collective-permute-done | bytes 65568 | tf_op jit(solution)/shard_map/ppermute | solution.py:541
  90.1 0.7 place_keys.1
  90.8 0.0 collective-permute-done.20.refs_3_
  90.8 1.0 %place_queries.1 = bf16[128,4096]{1,0:T(8,128)(2,1)} custom-call(s32[1]{0:T(128)} %bitcast.me_ref, bf16[128,1024]{1,0:T(8,128)(2,1)S(1)} %get-tuple-element.52.refs_0_, bf16[128,1024]{1,0:T(8,128)(2,1)S(1)} %collective-permute-done.17.refs_1_, bf16[256,1024]{1,0:T(8,128)(2,1)S(1)} %collective-permute-done.18.refs_2_, ...), custom_call_target="tpu_custom_call" | custom-call | tf_op jit(solution)/shard_map/place_queries/pallas_call | solution.py:507
  (13 shorter events, 0.2 us)
Async XLA Ops:
  0.6 26.4 %copy-start = (bf16[128,4096]{1,0:T(8,128)(2,1)S(1)}, bf16[128,4096]{1,0:T(8,128)(2,1)}, u32[]{:S(2)}) copy-start(bf16[128,4096]{1,0:T(8,128)(2,1)} %rest_3_.5) | copy-start | bytes 3145732
  0.6 9.7 %collective-permute-start = (bf16[128,4096]{1,0:T(8,128)(2,1)}, bf16[128,4096]{1,0:T(8,128)(2,1)S(1)}, u32[]{:S(2)}, u32[]{:S(2)}) collective-permute-start(bf16[128,4096]{1,0:T(8,128)(2,1)} %rest_0_.7), channel_id=1, source_target_pairs={{0,1},{1,0},{2,3},{3,2},{4,5},{5,4},{6,7},{7,6},{8,9},{9,8},{10,11... | collective-permute-start | bytes 3145736 | tf_op jit(solution)/shard_map/ppermute | solution.py:541
  1.2 25.9 %collective-permute-start.5 = (bf16[128,4096]{1,0:T(8,128)(2,1)}, bf16[128,4096]{1,0:T(8,128)(2,1)S(1)}, u32[]{:S(2)}, u32[]{:S(2)}) collective-permute-start(bf16[128,4096]{1,0:T(8,128)(2,1)} %rest_3_.5), channel_id=1, source_target_pairs={{0,1},{1,0},{2,3},{3,2},{4,5},{5,4},{6,7},{7,6},{8,9},{9,8},{10,11... | collective-permute-start | bytes 3145736 | tf_op jit(solution)/shard_map/ppermute | solution.py:541
  1.2 0.9 copy-start.4
  2.1 0.9 copy-start.5
  3.1 3.2 %collective-permute-start.1 = (bf16[128,256]{1,0:T(8,128)(2,1)S(1)}, bf16[128,256]{1,0:T(8,128)(2,1)S(1)}, u32[]{:S(2)}, u32[]{:S(2)}) collective-permute-start(bf16[128,256]{1,0:T(8,128)(2,1)S(1)} %get-tuple-element.37), channel_id=1, source_target_pairs={{0,1},{1,0},{2,3},{3,2},{4,5},{5,4},{6,7},{7,6},{8,9},{9,8},{10,11... | collective-permute-start | bytes 196616 | tf_op jit(solution)/shard_map/ppermute | solution.py:541
  3.6 5.3 %collective-permute-start.2 = (bf16[128,256]{1,0:T(8,128)(2,1)S(1)}, bf16[128,256]{1,0:T(8,128)(2,1)S(1)}, u32[]{:S(2)}, u32[]{:S(2)}) collective-permute-start(bf16[128,256]{1,0:T(8,128)(2,1)S(1)} %get-tuple-element.38), channel_id=1, source_target_pairs={{0,2},{1,3},{2,0},{3,1},{4,6},{5,7},{6,4},{7,5},{8,10},{9,11},{10,... | collective-permute-start | bytes 196616 | tf_op jit(solution)/shard_map/ppermute | solution.py:541
  6.2 4.0 %collective-permute-start.3 = (bf16[128,256]{1,0:T(8,128)(2,1)S(1)}, bf16[128,256]{1,0:T(8,128)(2,1)S(1)}, u32[]{:S(2)}, u32[]{:S(2)}) collective-permute-start(bf16[128,256]{1,0:T(8,128)(2,1)S(1)} %get-tuple-element.39), channel_id=1, source_target_pairs={{0,3},{1,2},{2,1},{3,0},{4,7},{5,6},{6,5},{7,4},{8,11},{9,10},{10,... | collective-permute-start | bytes 196616 | tf_op jit(solution)/shard_map/ppermute | solution.py:541
  10.3 1.2 %copy-start.2 = (bf16[128,4096]{1,0:T(8,128)(2,1)S(1)}, bf16[128,4096]{1,0:T(8,128)(2,1)}, u32[]{:S(2)}) copy-start(bf16[128,4096]{1,0:T(8,128)(2,1)} %rest_0_.7) | copy-start | bytes 3145732
  11.5 16.4 %copy-start.1 = (bf16[128,4096]{1,0:T(8,128)(2,1)S(1)}, bf16[128,4096]{1,0:T(8,128)(2,1)}, u32[]{:S(2)}) copy-start(bf16[128,4096]{1,0:T(8,128)(2,1)} %out_ref.1) | copy-start | bytes 3145732
  11.6 28.5 %copy-start.3 = (bf16[128,4096]{1,0:T(8,128)(2,1)S(1)}, bf16[128,4096]{1,0:T(8,128)(2,1)}, u32[]{:S(2)}) copy-start(bf16[128,4096]{1,0:T(8,128)(2,1)} %rest_0_.7) | copy-start | bytes 3145732
  11.6 28.5 %copy-start.6 = (s32[16,10]{1,0:T(8,128)S(1)}, s32[16,10]{1,0:T(8,128)}, u32[]{:S(2)}) copy-start(s32[16,10]{1,0:T(8,128)} %anc_ref.7) | copy-start | bytes 1924
  11.6 27.1 %collective-permute-start.4 = (bf16[256,1024]{1,0:T(8,128)(2,1)S(1)}, bf16[256,1024]{1,0:T(8,128)(2,1)S(1)}, u32[]{:S(2)}, u32[]{:S(2)}) collective-permute-start(bf16[256,1024]{1,0:T(8,128)(2,1)S(1)} %pack_queries.2), channel_id=1, source_target_pairs={{0,2},{1,3},{2,0},{3,1},{4,6},{5,7},{6,4},{7,5},{8,10},{9,11},{10,... | collective-permute-start | bytes 1572872 | tf_op jit(solution)/shard_map/ppermute | solution.py:541
  13.0 9.4 %collective-permute-start.8 = (bf16[512,128]{1,0:T(8,128)(2,1)S(1)}, bf16[512,128]{1,0:T(8,128)(2,1)S(1)}, u32[]{:S(2)}, u32[]{:S(2)}) collective-permute-start(bf16[512,128]{1,0:T(8,128)(2,1)S(1)} %get-tuple-element.43.after_ref.rest_3_.rest_10_), channel_id=1, source_target_pairs={{0,12},{1,13},{2,14},{3,15},{16,28},{17,29},{18,30},{19,31}} | collective-permute-start | bytes 393224 | tf_op jit(solution)/shard_map/ppermute | solution.py:547
  18.5 6.7 %collective-permute-start.7 = (bf16[512,128]{1,0:T(8,128)(2,1)S(1)}, bf16[512,128]{1,0:T(8,128)(2,1)S(1)}, u32[]{:S(2)}, u32[]{:S(2)}) collective-permute-start(bf16[512,128]{1,0:T(8,128)(2,1)S(1)} %get-tuple-element.43.after_ref.rest_3_.rest_10_), channel_id=1, source_target_pairs={{0,8},{4,12},{1,9},{5,13},{2,10},{6,14},{3,11},{7,15},{16,24},{20,... | collective-permute-start | bytes 393224 | tf_op jit(solution)/shard_map/ppermute | solution.py:547
  19.8 7.2 %collective-permute-start.6 = (bf16[512,128]{1,0:T(8,128)(2,1)S(1)}, bf16[512,128]{1,0:T(8,128)(2,1)S(1)}, u32[]{:S(2)}, u32[]{:S(2)}) collective-permute-start(bf16[512,128]{1,0:T(8,128)(2,1)S(1)} %get-tuple-element.43.after_ref.rest_3_.rest_10_), channel_id=1, source_target_pairs={{0,4},{4,8},{8,12},{1,5},{5,9},{9,13},{2,6},{6,10},{10,14},{3,7},{... | collective-permute-start | bytes 393224 | tf_op jit(solution)/shard_map/ppermute | solution.py:547
  27.1 16.2 %collective-permute-start.9 = (bf16[256,1024]{1,0:T(8,128)(2,1)S(1)}, bf16[256,1024]{1,0:T(8,128)(2,1)S(1)}, u32[]{:S(2)}, u32[]{:S(2)}) collective-permute-start(bf16[256,1024]{1,0:T(8,128)(2,1)S(1)} %pack_queries.3), channel_id=1, source_target_pairs={{0,2},{1,3},{2,0},{3,1},{4,6},{5,7},{6,4},{7,5},{8,10},{9,11},{10,... | collective-permute-start | bytes 1572872 | tf_op jit(solution)/shard_map/ppermute | solution.py:541
  28.5 8.8 %collective-permute-start.10 = (f32[16,128]{1,0:T(8,128)S(1)}, f32[16,128]{1,0:T(8,128)S(1)}, u32[]{:S(2)}, u32[]{:S(2)}) collective-permute-start(f32[16,128]{1,0:T(8,128)S(1)} %get-tuple-element.45), channel_id=1, source_target_pairs={{0,1},{1,0},{2,3},{3,2},{4,5},{5,4},{6,7},{7,6},{8,9},{9,8},{10,11... | collective-permute-start | bytes 24584 | tf_op jit(solution)/shard_map/ppermute | solution.py:541
  28.6 14.7 %collective-permute-start.14 = (bf16[512,128]{1,0:T(8,128)(2,1)S(1)}, bf16[512,128]{1,0:T(8,128)(2,1)S(1)}, u32[]{:S(2)}, u32[]{:S(2)}) collective-permute-start(bf16[512,128]{1,0:T(8,128)(2,1)S(1)} %get-tuple-element.48.rest_12_), channel_id=1, source_target_pairs={{0,12},{1,13},{2,14},{3,15},{16,28},{17,29},{18,30},{19,31}} | collective-permute-start | bytes 393224 | tf_op jit(solution)/shard_map/ppermute | solution.py:547
  34.8 8.5 %collective-permute-start.13 = (bf16[512,128]{1,0:T(8,128)(2,1)S(1)}, bf16[512,128]{1,0:T(8,128)(2,1)S(1)}, u32[]{:S(2)}, u32[]{:S(2)}) collective-permute-start(bf16[512,128]{1,0:T(8,128)(2,1)S(1)} %get-tuple-element.48.rest_12_), channel_id=1, source_target_pairs={{0,8},{4,12},{1,9},{5,13},{2,10},{6,14},{3,11},{7,15},{16,24},{20,... | collective-permute-start | bytes 393224 | tf_op jit(solution)/shard_map/ppermute | solution.py:547
  37.3 10.0 %collective-permute-start.12 = (bf16[512,128]{1,0:T(8,128)(2,1)S(1)}, bf16[512,128]{1,0:T(8,128)(2,1)S(1)}, u32[]{:S(2)}, u32[]{:S(2)}) collective-permute-start(bf16[512,128]{1,0:T(8,128)(2,1)S(1)} %get-tuple-element.48.rest_12_), channel_id=1, source_target_pairs={{0,4},{4,8},{8,12},{1,5},{5,9},{9,13},{2,6},{6,10},{10,14},{3,7},{... | collective-permute-start | bytes 393224 | tf_op jit(solution)/shard_map/ppermute | solution.py:547
  38.7 4.7 %collective-permute-start.11 = (f32[16,128]{1,0:T(8,128)S(1)}, f32[16,128]{1,0:T(8,128)S(1)}, u32[]{:S(2)}, u32[]{:S(2)}) collective-permute-start(f32[16,128]{1,0:T(8,128)S(1)} %pack_deltas.1), channel_id=1, source_target_pairs={{0,2},{1,3},{2,0},{3,1},{4,6},{5,7},{6,4},{7,5},{8,10},{9,11},{10,... | collective-permute-start | bytes 24584 | tf_op jit(solution)/shard_map/ppermute | solution.py:541
  44.7 16.3 %collective-permute-start.15 = (bf16[512,256]{1,0:T(8,128)(2,1)S(1)}, bf16[512,256]{1,0:T(8,128)(2,1)S(1)}, u32[]{:S(2)}, u32[]{:S(2)}) collective-permute-start(bf16[512,256]{1,0:T(8,128)(2,1)S(1)} %get-tuple-element.54), channel_id=1, source_target_pairs={{8,0},{12,4},{9,1},{13,5},{10,2},{14,6},{11,3},{15,7},{24,16},{28,... | collective-permute-start | bytes 786440 | tf_op jit(solution)/shard_map/ppermute | solution.py:553
  46.0 27.0 %collective-permute-start.16 = (bf16[512,256]{1,0:T(8,128)(2,1)S(1)}, bf16[512,256]{1,0:T(8,128)(2,1)S(1)}, u32[]{:S(2)}, u32[]{:S(2)}) collective-permute-start(bf16[512,256]{1,0:T(8,128)(2,1)S(1)} %get-tuple-element.55), channel_id=1, source_target_pairs={{12,0},{13,1},{14,2},{15,3},{28,16},{29,17},{30,18},{31,19}} | collective-permute-start | bytes 786440 | tf_op jit(solution)/shard_map/ppermute | solution.py:553
  51.5 32.3 %collective-permute-start.18 = (bf16[256,1024]{1,0:T(8,128)(2,1)S(1)}, bf16[256,1024]{1,0:T(8,128)(2,1)S(1)}, u32[]{:S(2)}, u32[]{:S(2)}) collective-permute-start(bf16[256,1024]{1,0:T(8,128)(2,1)S(1)} %get-tuple-element.58), channel_id=1, source_target_pairs={{0,2},{1,3},{2,0},{3,1},{4,6},{5,7},{6,4},{7,5},{8,10},{9,11},{10,... | collective-permute-start | bytes 1572872 | tf_op jit(solution)/shard_map/ppermute | solution.py:541
  73.1 1.6 %collective-permute-start.17 = (bf16[128,1024]{1,0:T(8,128)(2,1)S(1)}, bf16[128,1024]{1,0:T(8,128)(2,1)S(1)}, u32[]{:S(2)}, u32[]{:S(2)}) collective-permute-start(bf16[128,1024]{1,0:T(8,128)(2,1)S(1)} %get-tuple-element.57), channel_id=1, source_target_pairs={{0,1},{1,0},{2,3},{3,2},{4,5},{5,4},{6,7},{7,6},{8,9},{9,8},{10,11... | collective-permute-start | bytes 786440 | tf_op jit(solution)/shard_map/ppermute | solution.py:541
  73.1 10.6 %collective-permute-start.19 = (bf16[512,256]{1,0:T(8,128)(2,1)S(1)}, bf16[512,256]{1,0:T(8,128)(2,1)S(1)}, u32[]{:S(2)}, u32[]{:S(2)}) collective-permute-start(bf16[512,256]{1,0:T(8,128)(2,1)S(1)} %get-tuple-element.61), channel_id=1, source_target_pairs={{4,0},{8,4},{12,8},{5,1},{9,5},{13,9},{6,2},{10,6},{14,10},{7,3},{... | collective-permute-start | bytes 786440 | tf_op jit(solution)/shard_map/ppermute | solution.py:553
  83.8 7.0 %collective-permute-start.20 = (bf16[128,1024]{1,0:T(8,128)(2,1)S(1)}, bf16[128,1024]{1,0:T(8,128)(2,1)S(1)}, u32[]{:S(2)}, u32[]{:S(2)}) collective-permute-start(bf16[128,1024]{1,0:T(8,128)(2,1)S(1)} %slice.3), channel_id=1, source_target_pairs={{0,1},{1,0},{2,3},{3,2},{4,5},{5,4},{6,7},{7,6},{8,9},{9,8},{10,11... | collective-permute-start | bytes 786440 | tf_op jit(solution)/shard_map/ppermute | solution.py:541
  83.9 1.9 %collective-permute-start.21 = (bf16[128,256]{1,0:T(8,128)(2,1)S(1)}, bf16[128,256]{1,0:T(8,128)(2,1)S(1)}, u32[]{:S(2)}, u32[]{:S(2)}) collective-permute-start(bf16[128,256]{1,0:T(8,128)(2,1)S(1)} %get-tuple-element.63), channel_id=1, source_target_pairs={{0,1},{1,0},{2,3},{3,2},{4,5},{5,4},{6,7},{7,6},{8,9},{9,8},{10,11... | collective-permute-start | bytes 196616 | tf_op jit(solution)/shard_map/ppermute | solution.py:541
  84.4 4.3 %collective-permute-start.22 = (bf16[128,256]{1,0:T(8,128)(2,1)S(1)}, bf16[128,256]{1,0:T(8,128)(2,1)S(1)}, u32[]{:S(2)}, u32[]{:S(2)}) collective-permute-start(bf16[128,256]{1,0:T(8,128)(2,1)S(1)} %get-tuple-element.64), channel_id=1, source_target_pairs={{0,2},{1,3},{2,0},{3,1},{4,6},{5,7},{6,4},{7,5},{8,10},{9,11},{10,... | collective-permute-start | bytes 196616 | tf_op jit(solution)/shard_map/ppermute | solution.py:541
  85.7 4.4 %collective-permute-start.23 = (bf16[128,256]{1,0:T(8,128)(2,1)S(1)}, bf16[128,256]{1,0:T(8,128)(2,1)S(1)}, u32[]{:S(2)}, u32[]{:S(2)}) collective-permute-start(bf16[128,256]{1,0:T(8,128)(2,1)S(1)} %get-tuple-element.65), channel_id=1, source_target_pairs={{0,3},{1,2},{2,1},{3,0},{4,7},{5,6},{6,5},{7,4},{8,11},{9,10},{10,... | collective-permute-start | bytes 196616 | tf_op jit(solution)/shard_map/ppermute | solution.py:541

commit v10 on v9

--- a/solution.py
+++ b/solution.py
@@ -283,7 +283,18 @@
         grads_part(2 * index, *buffers[0])
         return carry
 
-    lax.fori_loop(0, jnp.where(count > 0, (count + 2) // 2, 0), step, 0)
+    lax.fori_loop(0, count // 2, step, 0)
+
+    @pl.when((count & 1) == 1)
+    def _():
+        scores_part(count - 1, *buffers[0])
+        grads_part(count - 2, *buffers[1])
+        grads_part(count - 1, *buffers[0])
+
+    @pl.when(((count & 1) == 0) & (count > 0))
+    def _():
+        grads_part(count - 1, *buffers[1])
+
 
     if stage != "far":
         for place in range(2):

time: 93.5 us -> 92.5 us (0.989)
  no operation moved by 1% of the time
where the time goes in v10:
time: 92.5 us; the launch traced here: 91 us
  waiting for transfers between devices  38.8 us (42%)
  starting transfers between devices  32.7 us (35%)
  Pallas kernels  15.5 us (17%)
  local copies, waits for them, and re-layouts  3.07 us (3%)
  between operations  0.93 us (1%)
    ppermute x3, waiting for transfers between devices, down(): lax.ppermute(x, 'level', [(z + shift, z) for z in range(steps - shift)])  25.5 us
    ppermute x6, starting transfers between devices, up(): lax.ppermute(x, 'level', [(z, z + shift) for z in range(steps - shift)])  19.3 us
    ppermute x15, starting transfers between devices, to_partner(): lax.ppermute(x, ('side', 'core'), [(t, t ^ flip) for t in range(QUAD)])  9.53 us
    pallas_call x3, Pallas kernels, gradients(): pl.pallas_call(functools.partial(grads_kernel, ancestors.shape[1], stage,...  9.48 us
    ppermute x15, waiting for transfers between devices, to_partner(): lax.ppermute(x, ('side', 'core'), [(t, t ^ flip) for t in range(QUAD)])  8.48 us
    ppermute x6, waiting for transfers between devices, up(): lax.ppermute(x, 'level', [(z, z + shift) for z in range(steps - shift)])  4.78 us
    ppermute x3, starting transfers between devices, down(): lax.ppermute(x, 'level', [(z + shift, z) for z in range(steps - shift)])  3.88 us
    pallas_call x1, Pallas kernels, statistics(): pl.pallas_call(functools.partial(stats_kernel, ancestors.shape[1], steps)...  3.3 us
  transfers between devices with their start and end apart: 24, of which 11 were waited for; matrix products, arithmetic and copies ran while one was open for 0% of the time, Pallas kernels for 16%

profile of v10, /device:TPU:0, one launch (start us, length us, event | category | flops | bytes accessed | tf_op | source)
XLA Modules:
  0.0 91.0 jit_solution(14740439032659526391)
XLA Ops:
  0.6 0.0 copy-start
  0.6 0.5 collective-permute-start
  1.2 0.1 collective-permute-start.5
  1.2 0.9 copy-done.4
  2.1 0.9 copy-done.5
  3.1 0.5 collective-permute-start.1
  3.6 2.6 %collective-permute-start.2 = (bf16[128,256]{1,0:T(8,128)(2,1)S(1)}, bf16[128,256]{1,0:T(8,128)(2,1)S(1)}, u32[]{:S(2)}, u32[]{:S(2)}) collective-permute-start(bf16[128,256]{1,0:T(8,128)(2,1)S(1)} %get-tuple-element.38), channel_id=1, source_target_pairs={{0,2},{1,3},{2,0},{3,1},{4,6},{5,7},{6,4},{7,5},{8,10},{9,11},{10,... | collective-permute-start | bytes 196616 | tf_op jit(solution)/shard_map/ppermute | solution.py:552
  6.2 0.1 collective-permute-start.3
  6.3 0.0 collective-permute-done.1.refs_1_
  6.3 2.6 %collective-permute-done.2.refs_2_ = bf16[128,256]{1,0:T(8,128)(2,1)S(1)} collective-permute-done((bf16[128,256]{1,0:T(8,128)(2,1)S(1)}, bf16[128,256]{1,0:T(8,128)(2,1)S(1)}, u32[]{:S(2)}, u32[]{:S(2)}) %collective-permute-start.2) | collective-permute-done | bytes 65568 | tf_op jit(solution)/shard_map/ppermute | solution.py:552
  8.9 1.4 %collective-permute-done.3.refs_3_ = bf16[128,256]{1,0:T(8,128)(2,1)S(1)} collective-permute-done((bf16[128,256]{1,0:T(8,128)(2,1)S(1)}, bf16[128,256]{1,0:T(8,128)(2,1)S(1)}, u32[]{:S(2)}, u32[]{:S(2)}) %collective-permute-start.3) | collective-permute-done | bytes 65568 | tf_op jit(solution)/shard_map/ppermute | solution.py:552
  10.3 0.0 collective-permute-done.peer.rest_1_
  10.3 0.0 copy-start.2
  10.3 1.2 %copy-done.2 = bf16[128,4096]{1,0:T(8,128)(2,1)S(1)} copy-done((bf16[128,4096]{1,0:T(8,128)(2,1)S(1)}, bf16[128,4096]{1,0:T(8,128)(2,1)}, u32[]{:S(2)}) %copy-start.2) | copy-done | bytes 1048600
  11.6 0.0 copy-start.3
  11.6 0.0 copy-start.6
  11.6 1.4 %collective-permute-start.4 = (bf16[256,1024]{1,0:T(8,128)(2,1)S(1)}, bf16[256,1024]{1,0:T(8,128)(2,1)S(1)}, u32[]{:S(2)}, u32[]{:S(2)}) collective-permute-start(bf16[256,1024]{1,0:T(8,128)(2,1)S(1)} %pack_queries.2), channel_id=1, source_target_pairs={{0,2},{1,3},{2,0},{3,1},{4,6},{5,7},{6,4},{7,5},{8,10},{9,11},{10,... | collective-permute-start | bytes 1572872 | tf_op jit(solution)/shard_map/ppermute | solution.py:552
  13.0 5.5 %collective-permute-start.8 = (bf16[512,128]{1,0:T(8,128)(2,1)S(1)}, bf16[512,128]{1,0:T(8,128)(2,1)S(1)}, u32[]{:S(2)}, u32[]{:S(2)}) collective-permute-start(bf16[512,128]{1,0:T(8,128)(2,1)S(1)} %get-tuple-element.43.after_ref.rest_3_.rest_10_), channel_id=1, source_target_pairs={{0,12},{1,13},{2,14},{3,15},{16,28},{17,29},{18,30},{19,31}} | collective-permute-start | bytes 393224 | tf_op jit(solution)/shard_map/ppermute | solution.py:558
  18.5 1.3 %collective-permute-start.7 = (bf16[512,128]{1,0:T(8,128)(2,1)S(1)}, bf16[512,128]{1,0:T(8,128)(2,1)S(1)}, u32[]{:S(2)}, u32[]{:S(2)}) collective-permute-start(bf16[512,128]{1,0:T(8,128)(2,1)S(1)} %get-tuple-element.43.after_ref.rest_3_.rest_10_), channel_id=1, source_target_pairs={{0,8},{4,12},{1,9},{5,13},{2,10},{6,14},{3,11},{7,15},{16,24},{20,... | collective-permute-start | bytes 393224 | tf_op jit(solution)/shard_map/ppermute | solution.py:558
  19.8 2.5 %collective-permute-start.6 = (bf16[512,128]{1,0:T(8,128)(2,1)S(1)}, bf16[512,128]{1,0:T(8,128)(2,1)S(1)}, u32[]{:S(2)}, u32[]{:S(2)}) collective-permute-start(bf16[512,128]{1,0:T(8,128)(2,1)S(1)} %get-tuple-element.43.after_ref.rest_3_.rest_10_), channel_id=1, source_target_pairs={{0,4},{4,8},{8,12},{1,5},{5,9},{9,13},{2,6},{6,10},{10,14},{3,7},{... | collective-permute-start | bytes 393224 | tf_op jit(solution)/shard_map/ppermute | solution.py:558
  22.3 0.1 collective-permute-done.8.rest_6_.rest_11_
  22.4 2.8 %collective-permute-done.7.rest_5_.rest_10_ = bf16[512,128]{1,0:T(8,128)(2,1)S(1)} collective-permute-done((bf16[512,128]{1,0:T(8,128)(2,1)S(1)}, bf16[512,128]{1,0:T(8,128)(2,1)S(1)}, u32[]{:S(2)}, u32[]{:S(2)}) %collective-permute-start.7) | collective-permute-done | bytes 131104 | tf_op jit(solution)/shard_map/ppermute | solution.py:558
  25.2 1.8 %collective-permute-done.6.rest_4_.rest_11_ = bf16[512,128]{1,0:T(8,128)(2,1)S(1)} collective-permute-done((bf16[512,128]{1,0:T(8,128)(2,1)S(1)}, bf16[512,128]{1,0:T(8,128)(2,1)S(1)}, u32[]{:S(2)}, u32[]{:S(2)}) %collective-permute-start.6) | collective-permute-done | bytes 131104 | tf_op jit(solution)/shard_map/ppermute | solution.py:558
  27.1 0.0 collective-permute-done.5.peer.rest_4_
  27.1 0.8 collective-permute-start.9
  27.9 0.6 row_deltas.1
  28.5 0.1 collective-permute-start.10
  28.6 6.3 %collective-permute-start.14 = (bf16[512,128]{1,0:T(8,128)(2,1)S(1)}, bf16[512,128]{1,0:T(8,128)(2,1)S(1)}, u32[]{:S(2)}, u32[]{:S(2)}) collective-permute-start(bf16[512,128]{1,0:T(8,128)(2,1)S(1)} %get-tuple-element.48.rest_12_), channel_id=1, source_target_pairs={{0,12},{1,13},{2,14},{3,15},{16,28},{17,29},{18,30},{19,31}} | collective-permute-start | bytes 393224 | tf_op jit(solution)/shard_map/ppermute | solution.py:558
  34.8 2.5 %collective-permute-start.13 = (bf16[512,128]{1,0:T(8,128)(2,1)S(1)}, bf16[512,128]{1,0:T(8,128)(2,1)S(1)}, u32[]{:S(2)}, u32[]{:S(2)}) collective-permute-start(bf16[512,128]{1,0:T(8,128)(2,1)S(1)} %get-tuple-element.48.rest_12_), channel_id=1, source_target_pairs={{0,8},{4,12},{1,9},{5,13},{2,10},{6,14},{3,11},{7,15},{16,24},{20,... | collective-permute-start | bytes 393224 | tf_op jit(solution)/shard_map/ppermute | solution.py:558
  37.3 0.0 collective-permute-done.10.pair.rest_7_
  37.3 1.3 %collective-permute-start.12 = (bf16[512,128]{1,0:T(8,128)(2,1)S(1)}, bf16[512,128]{1,0:T(8,128)(2,1)S(1)}, u32[]{:S(2)}, u32[]{:S(2)}) collective-permute-start(bf16[512,128]{1,0:T(8,128)(2,1)S(1)} %get-tuple-element.48.rest_12_), channel_id=1, source_target_pairs={{0,4},{4,8},{8,12},{1,5},{5,9},{9,13},{2,6},{6,10},{10,14},{3,7},{... | collective-permute-start | bytes 393224 | tf_op jit(solution)/shard_map/ppermute | solution.py:558
  38.6 0.0 collective-permute-done.4.rest_2_
  38.7 1.4 %collective-permute-start.11 = (f32[16,128]{1,0:T(8,128)S(1)}, f32[16,128]{1,0:T(8,128)S(1)}, u32[]{:S(2)}, u32[]{:S(2)}) collective-permute-start(f32[16,128]{1,0:T(8,128)S(1)} %pack_deltas.1), channel_id=1, source_target_pairs={{0,2},{1,3},{2,0},{3,1},{4,6},{5,7},{6,4},{7,5},{8,10},{9,11},{10,... | collective-permute-start | bytes 24584 | tf_op jit(solution)/shard_map/ppermute | solution.py:552
  40.1 3.3 %statistics.1.rest_9_ = f32[4,1,1024]{2,1,0:T(1,128)S(1)} custom-call(s32[1]{0:T(128)} %bitcast.me_ref, s32[16,10]{1,0:T(8,128)S(1)} %copy-done.6, bf16[128,4096]{1,0:T(8,128)(2,1)S(1)} %copy-done.3, bf16[128,4096]{1,0:T(8,128)(2,1)S(1)} %collective-permute-done.peer.rest_1_, bf16[256,1024]{1,0:T(8,128)(2,1)S(1)} %collective-permute-done.4.rest_2_, ...), custom_call_target="tpu_custom_call" | custom-call | flops 2952790016 | bytes 16777216 | tf_op jit(solution)/shard_map/statistics/pallas_call | solution.py:328
  43.4 0.0 collective-permute-done.11.rest_8_
  43.4 0.0 collective-permute-done.14.rest_13_
  43.4 0.0 collective-permute-done.13.rest_12_
  43.4 0.0 collective-permute-done.9.rest_5_
  43.4 1.4 %far_grads.1 = (f32[4,128,1024]{2,1,0:T(8,128)S(1)}, bf16[512,256]{1,0:T(8,128)(2,1)S(1)}, bf16[512,256]{1,0:T(8,128)(2,1)S(1)}) custom-call(s32[1]{0:T(128)} %bitcast.me_ref, s32[16,10]{1,0:T(8,128)S(1)} %copy-done.6, bf16[128,4096]{1,0:T(8,128)(2,1)S(1)} %copy-done.3, bf16[128,4096]{1,0:T(8,128)(2,1)S(1)} %collective-permute-done.peer.rest_1_, ...), custom_call_target="tpu_custom_call" | custom-call | flops 14763950080 | bytes 16777216 | tf_op jit(solution)/shard_map/far_grads/pallas_call | solution.py:376
  44.8 1.3 %collective-permute-start.15 = (bf16[512,256]{1,0:T(8,128)(2,1)S(1)}, bf16[512,256]{1,0:T(8,128)(2,1)S(1)}, u32[]{:S(2)}, u32[]{:S(2)}) collective-permute-start(bf16[512,256]{1,0:T(8,128)(2,1)S(1)} %get-tuple-element.54), channel_id=1, source_target_pairs={{8,0},{12,4},{9,1},{13,5},{10,2},{14,6},{11,3},{15,7},{24,16},{28,... | collective-permute-start | bytes 786440 | tf_op jit(solution)/shard_map/ppermute | solution.py:564
  46.1 1.3 %collective-permute-start.16 = (bf16[512,256]{1,0:T(8,128)(2,1)S(1)}, bf16[512,256]{1,0:T(8,128)(2,1)S(1)}, u32[]{:S(2)}, u32[]{:S(2)}) collective-permute-start(bf16[512,256]{1,0:T(8,128)(2,1)S(1)} %get-tuple-element.55), channel_id=1, source_target_pairs={{12,0},{13,1},{14,2},{15,3},{28,16},{29,17},{30,18},{31,19}} | collective-permute-start | bytes 786440 | tf_op jit(solution)/shard_map/ppermute | solution.py:564
  47.4 0.0 collective-permute-done.12.rest_13_
  47.4 4.7 %side_grads.1 = (bf16[256,1024]{1,0:T(8,128)(2,1)S(1)}, f32[1024,128]{1,0:T(8,128)S(1)}, f32[1024,128]{1,0:T(8,128)S(1)}) custom-call(s32[1]{0:T(128)} %bitcast.me_ref, s32[16,10]{1,0:T(8,128)S(1)} %copy-done.6, bf16[128,4096]{1,0:T(8,128)(2,1)S(1)} %copy-done.3, bf16[128,4096]{1,0:T(8,128)(2,1)S(1)} %collective-permute-done.peer.rest_1_, ...), custom_call_target="tpu_custom_call" | custom-call | flops 14763950080 | bytes 16777216 | tf_op jit(solution)/shard_map/side_grads/pallas_call | solution.py:376
  52.1 0.1 collective-permute-start.18
  52.1 3.4 %own_grads.1 = (bf16[128,1024]{1,0:T(8,128)(2,1)S(1)}, bf16[128,1024]{1,0:T(8,128)(2,1)S(1)}, f32[512,256]{1,0:T(8,128)S(1)}, bf16[512,256]{1,0:T(8,128)(2,1)S(1)}) custom-call(s32[1]{0:T(128)} %bitcast.me_ref, s32[16,10]{1,0:T(8,128)S(1)} %copy-done.6, bf16[128,4096]{1,0:T(8,128)(2,1)S(1)} %copy-done.3, ...), custom_call_target="tpu_custom_call" | custom-call | flops 14763950080 | bytes 16777216 | tf_op jit(solution)/shard_map/own_grads/pallas_call | solution.py:376
  55.6 4.6 %collective-permute-done.15.refs_0_ = bf16[512,256]{1,0:T(8,128)(2,1)S(1)} collective-permute-done((bf16[512,256]{1,0:T(8,128)(2,1)S(1)}, bf16[512,256]{1,0:T(8,128)(2,1)S(1)}, u32[]{:S(2)}, u32[]{:S(2)}) %collective-permute-start.15) | collective-permute-done | bytes 262176 | tf_op jit(solution)/shard_map/ppermute | solution.py:564
  60.1 11.9 %collective-permute-done.16.refs_1_ = bf16[512,256]{1,0:T(8,128)(2,1)S(1)} collective-permute-done((bf16[512,256]{1,0:T(8,128)(2,1)S(1)}, bf16[512,256]{1,0:T(8,128)(2,1)S(1)}, u32[]{:S(2)}, u32[]{:S(2)}) %collective-permute-start.16) | collective-permute-done | bytes 262176 | tf_op jit(solution)/shard_map/ppermute | solution.py:564
  72.1 0.1 add_far.1
  72.1 0.1 collective-permute-start.17
  72.2 1.3 %collective-permute-start.19 = (bf16[512,256]{1,0:T(8,128)(2,1)S(1)}, bf16[512,256]{1,0:T(8,128)(2,1)S(1)}, u32[]{:S(2)}, u32[]{:S(2)}) collective-permute-start(bf16[512,256]{1,0:T(8,128)(2,1)S(1)} %get-tuple-element.61), channel_id=1, source_target_pairs={{4,0},{8,4},{12,8},{5,1},{9,5},{13,9},{6,2},{10,6},{14,10},{7,3},{... | collective-permute-start | bytes 786440 | tf_op jit(solution)/shard_map/ppermute | solution.py:564
  73.5 0.2 collective-permute-done.17.refs_1_
  73.7 9.1 %collective-permute-done.19.near_ref = bf16[512,256]{1,0:T(8,128)(2,1)S(1)} collective-permute-done((bf16[512,256]{1,0:T(8,128)(2,1)S(1)}, bf16[512,256]{1,0:T(8,128)(2,1)S(1)}, u32[]{:S(2)}, u32[]{:S(2)}) %collective-permute-start.19) | collective-permute-done | bytes 262176 | tf_op jit(solution)/shard_map/ppermute | solution.py:564
  82.8 0.1 add_sums.1
  82.9 0.0 collective-permute-done.18.refs_2_
  82.9 0.1 collective-permute-start.20
  83.0 0.5 collective-permute-start.21
  83.5 1.3 %collective-permute-start.22 = (bf16[128,256]{1,0:T(8,128)(2,1)S(1)}, bf16[128,256]{1,0:T(8,128)(2,1)S(1)}, u32[]{:S(2)}, u32[]{:S(2)}) collective-permute-start(bf16[128,256]{1,0:T(8,128)(2,1)S(1)} %get-tuple-element.64), channel_id=1, source_target_pairs={{0,2},{1,3},{2,0},{3,1},{4,6},{5,7},{6,4},{7,5},{8,10},{9,11},{10,... | collective-permute-start | bytes 196616 | tf_op jit(solution)/shard_map/ppermute | solution.py:552
  84.8 0.1 collective-permute-start.23
  84.9 0.0 collective-permute-done.21.refs_1_
  84.9 2.8 %collective-permute-done.22.refs_2_ = bf16[128,256]{1,0:T(8,128)(2,1)S(1)} collective-permute-done((bf16[128,256]{1,0:T(8,128)(2,1)S(1)}, bf16[128,256]{1,0:T(8,128)(2,1)S(1)}, u32[]{:S(2)}, u32[]{:S(2)}) %collective-permute-start.22) | collective-permute-done | bytes 65568 | tf_op jit(solution)/shard_map/ppermute | solution.py:552
  87.7 1.4 %collective-permute-done.23.refs_3_ = bf16[128,256]{1,0:T(8,128)(2,1)S(1)} collective-permute-done((bf16[128,256]{1,0:T(8,128)(2,1)S(1)}, bf16[128,256]{1,0:T(8,128)(2,1)S(1)}, u32[]{:S(2)}, u32[]{:S(2)}) %collective-permute-start.23) | collective-permute-done | bytes 65568 | tf_op jit(solution)/shard_map/ppermute | solution.py:552
  89.2 0.7 place_keys.1
  89.9 0.0 collective-permute-done.20.refs_3_
  89.9 1.0 %place_queries.1 = bf16[128,4096]{1,0:T(8,128)(2,1)} custom-call(s32[1]{0:T(128)} %bitcast.me_ref, bf16[128,1024]{1,0:T(8,128)(2,1)S(1)} %get-tuple-element.52.refs_0_, bf16[128,1024]{1,0:T(8,128)(2,1)S(1)} %collective-permute-done.17.refs_1_, bf16[256,1024]{1,0:T(8,128)(2,1)S(1)} %collective-permute-done.18.refs_2_, ...), custom_call_target="tpu_custom_call" | custom-call | tf_op jit(solution)/shard_map/place_queries/pallas_call | solution.py:518
  (13 shorter events, 0.2 us)
Async XLA Ops:
  0.6 26.4 %copy-start = (bf16[128,4096]{1,0:T(8,128)(2,1)S(1)}, bf16[128,4096]{1,0:T(8,128)(2,1)}, u32[]{:S(2)}) copy-start(bf16[128,4096]{1,0:T(8,128)(2,1)} %rest_3_.5) | copy-start | bytes 3145732
  0.6 9.7 %collective-permute-start = (bf16[128,4096]{1,0:T(8,128)(2,1)}, bf16[128,4096]{1,0:T(8,128)(2,1)S(1)}, u32[]{:S(2)}, u32[]{:S(2)}) collective-permute-start(bf16[128,4096]{1,0:T(8,128)(2,1)} %rest_0_.7), channel_id=1, source_target_pairs={{0,1},{1,0},{2,3},{3,2},{4,5},{5,4},{6,7},{7,6},{8,9},{9,8},{10,11... | collective-permute-start | bytes 3145736 | tf_op jit(solution)/shard_map/ppermute | solution.py:552
  1.2 25.9 %collective-permute-start.5 = (bf16[128,4096]{1,0:T(8,128)(2,1)}, bf16[128,4096]{1,0:T(8,128)(2,1)S(1)}, u32[]{:S(2)}, u32[]{:S(2)}) collective-permute-start(bf16[128,4096]{1,0:T(8,128)(2,1)} %rest_3_.5), channel_id=1, source_target_pairs={{0,1},{1,0},{2,3},{3,2},{4,5},{5,4},{6,7},{7,6},{8,9},{9,8},{10,11... | collective-permute-start | bytes 3145736 | tf_op jit(solution)/shard_map/ppermute | solution.py:552
  1.2 0.9 copy-start.4
  2.1 0.9 copy-start.5
  3.1 3.2 %collective-permute-start.1 = (bf16[128,256]{1,0:T(8,128)(2,1)S(1)}, bf16[128,256]{1,0:T(8,128)(2,1)S(1)}, u32[]{:S(2)}, u32[]{:S(2)}) collective-permute-start(bf16[128,256]{1,0:T(8,128)(2,1)S(1)} %get-tuple-element.37), channel_id=1, source_target_pairs={{0,1},{1,0},{2,3},{3,2},{4,5},{5,4},{6,7},{7,6},{8,9},{9,8},{10,11... | collective-permute-start | bytes 196616 | tf_op jit(solution)/shard_map/ppermute | solution.py:552
  3.6 5.3 %collective-permute-start.2 = (bf16[128,256]{1,0:T(8,128)(2,1)S(1)}, bf16[128,256]{1,0:T(8,128)(2,1)S(1)}, u32[]{:S(2)}, u32[]{:S(2)}) collective-permute-start(bf16[128,256]{1,0:T(8,128)(2,1)S(1)} %get-tuple-element.38), channel_id=1, source_target_pairs={{0,2},{1,3},{2,0},{3,1},{4,6},{5,7},{6,4},{7,5},{8,10},{9,11},{10,... | collective-permute-start | bytes 196616 | tf_op jit(solution)/shard_map/ppermute | solution.py:552
  6.2 4.0 %collective-permute-start.3 = (bf16[128,256]{1,0:T(8,128)(2,1)S(1)}, bf16[128,256]{1,0:T(8,128)(2,1)S(1)}, u32[]{:S(2)}, u32[]{:S(2)}) collective-permute-start(bf16[128,256]{1,0:T(8,128)(2,1)S(1)} %get-tuple-element.39), channel_id=1, source_target_pairs={{0,3},{1,2},{2,1},{3,0},{4,7},{5,6},{6,5},{7,4},{8,11},{9,10},{10,... | collective-permute-start | bytes 196616 | tf_op jit(solution)/shard_map/ppermute | solution.py:552
  10.3 1.2 %copy-start.2 = (bf16[128,4096]{1,0:T(8,128)(2,1)S(1)}, bf16[128,4096]{1,0:T(8,128)(2,1)}, u32[]{:S(2)}) copy-start(bf16[128,4096]{1,0:T(8,128)(2,1)} %rest_0_.7) | copy-start | bytes 3145732
  11.5 16.4 %copy-start.1 = (bf16[128,4096]{1,0:T(8,128)(2,1)S(1)}, bf16[128,4096]{1,0:T(8,128)(2,1)}, u32[]{:S(2)}) copy-start(bf16[128,4096]{1,0:T(8,128)(2,1)} %out_ref.1) | copy-start | bytes 3145732
  11.6 28.5 %copy-start.3 = (bf16[128,4096]{1,0:T(8,128)(2,1)S(1)}, bf16[128,4096]{1,0:T(8,128)(2,1)}, u32[]{:S(2)}) copy-start(bf16[128,4096]{1,0:T(8,128)(2,1)} %rest_0_.7) | copy-start | bytes 3145732
  11.6 28.5 %copy-start.6 = (s32[16,10]{1,0:T(8,128)S(1)}, s32[16,10]{1,0:T(8,128)}, u32[]{:S(2)}) copy-start(s32[16,10]{1,0:T(8,128)} %anc_ref.7) | copy-start | bytes 1924
  11.6 27.1 %collective-permute-start.4 = (bf16[256,1024]{1,0:T(8,128)(2,1)S(1)}, bf16[256,1024]{1,0:T(8,128)(2,1)S(1)}, u32[]{:S(2)}, u32[]{:S(2)}) collective-permute-start(bf16[256,1024]{1,0:T(8,128)(2,1)S(1)} %pack_queries.2), channel_id=1, source_target_pairs={{0,2},{1,3},{2,0},{3,1},{4,6},{5,7},{6,4},{7,5},{8,10},{9,11},{10,... | collective-permute-start | bytes 1572872 | tf_op jit(solution)/shard_map/ppermute | solution.py:552
  13.0 9.4 %collective-permute-start.8 = (bf16[512,128]{1,0:T(8,128)(2,1)S(1)}, bf16[512,128]{1,0:T(8,128)(2,1)S(1)}, u32[]{:S(2)}, u32[]{:S(2)}) collective-permute-start(bf16[512,128]{1,0:T(8,128)(2,1)S(1)} %get-tuple-element.43.after_ref.rest_3_.rest_10_), channel_id=1, source_target_pairs={{0,12},{1,13},{2,14},{3,15},{16,28},{17,29},{18,30},{19,31}} | collective-permute-start | bytes 393224 | tf_op jit(solution)/shard_map/ppermute | solution.py:558
  18.5 6.7 %collective-permute-start.7 = (bf16[512,128]{1,0:T(8,128)(2,1)S(1)}, bf16[512,128]{1,0:T(8,128)(2,1)S(1)}, u32[]{:S(2)}, u32[]{:S(2)}) collective-permute-start(bf16[512,128]{1,0:T(8,128)(2,1)S(1)} %get-tuple-element.43.after_ref.rest_3_.rest_10_), channel_id=1, source_target_pairs={{0,8},{4,12},{1,9},{5,13},{2,10},{6,14},{3,11},{7,15},{16,24},{20,... | collective-permute-start | bytes 393224 | tf_op jit(solution)/shard_map/ppermute | solution.py:558
  19.8 7.2 %collective-permute-start.6 = (bf16[512,128]{1,0:T(8,128)(2,1)S(1)}, bf16[512,128]{1,0:T(8,128)(2,1)S(1)}, u32[]{:S(2)}, u32[]{:S(2)}) collective-permute-start(bf16[512,128]{1,0:T(8,128)(2,1)S(1)} %get-tuple-element.43.after_ref.rest_3_.rest_10_), channel_id=1, source_target_pairs={{0,4},{4,8},{8,12},{1,5},{5,9},{9,13},{2,6},{6,10},{10,14},{3,7},{... | collective-permute-start | bytes 393224 | tf_op jit(solution)/shard_map/ppermute | solution.py:558
  27.1 16.3 %collective-permute-start.9 = (bf16[256,1024]{1,0:T(8,128)(2,1)S(1)}, bf16[256,1024]{1,0:T(8,128)(2,1)S(1)}, u32[]{:S(2)}, u32[]{:S(2)}) collective-permute-start(bf16[256,1024]{1,0:T(8,128)(2,1)S(1)} %pack_queries.3), channel_id=1, source_target_pairs={{0,2},{1,3},{2,0},{3,1},{4,6},{5,7},{6,4},{7,5},{8,10},{9,11},{10,... | collective-permute-start | bytes 1572872 | tf_op jit(solution)/shard_map/ppermute | solution.py:552
  28.5 8.8 %collective-permute-start.10 = (f32[16,128]{1,0:T(8,128)S(1)}, f32[16,128]{1,0:T(8,128)S(1)}, u32[]{:S(2)}, u32[]{:S(2)}) collective-permute-start(f32[16,128]{1,0:T(8,128)S(1)} %get-tuple-element.45), channel_id=1, source_target_pairs={{0,1},{1,0},{2,3},{3,2},{4,5},{5,4},{6,7},{7,6},{8,9},{9,8},{10,11... | collective-permute-start | bytes 24584 | tf_op jit(solution)/shard_map/ppermute | solution.py:552
  28.6 14.8 %collective-permute-start.14 = (bf16[512,128]{1,0:T(8,128)(2,1)S(1)}, bf16[512,128]{1,0:T(8,128)(2,1)S(1)}, u32[]{:S(2)}, u32[]{:S(2)}) collective-permute-start(bf16[512,128]{1,0:T(8,128)(2,1)S(1)} %get-tuple-element.48.rest_12_), channel_id=1, source_target_pairs={{0,12},{1,13},{2,14},{3,15},{16,28},{17,29},{18,30},{19,31}} | collective-permute-start | bytes 393224 | tf_op jit(solution)/shard_map/ppermute | solution.py:558
  34.8 8.5 %collective-permute-start.13 = (bf16[512,128]{1,0:T(8,128)(2,1)S(1)}, bf16[512,128]{1,0:T(8,128)(2,1)S(1)}, u32[]{:S(2)}, u32[]{:S(2)}) collective-permute-start(bf16[512,128]{1,0:T(8,128)(2,1)S(1)} %get-tuple-element.48.rest_12_), channel_id=1, source_target_pairs={{0,8},{4,12},{1,9},{5,13},{2,10},{6,14},{3,11},{7,15},{16,24},{20,... | collective-permute-start | bytes 393224 | tf_op jit(solution)/shard_map/ppermute | solution.py:558
  37.3 10.0 %collective-permute-start.12 = (bf16[512,128]{1,0:T(8,128)(2,1)S(1)}, bf16[512,128]{1,0:T(8,128)(2,1)S(1)}, u32[]{:S(2)}, u32[]{:S(2)}) collective-permute-start(bf16[512,128]{1,0:T(8,128)(2,1)S(1)} %get-tuple-element.48.rest_12_), channel_id=1, source_target_pairs={{0,4},{4,8},{8,12},{1,5},{5,9},{9,13},{2,6},{6,10},{10,14},{3,7},{... | collective-permute-start | bytes 393224 | tf_op jit(solution)/shard_map/ppermute | solution.py:558
  38.7 4.7 %collective-permute-start.11 = (f32[16,128]{1,0:T(8,128)S(1)}, f32[16,128]{1,0:T(8,128)S(1)}, u32[]{:S(2)}, u32[]{:S(2)}) collective-permute-start(f32[16,128]{1,0:T(8,128)S(1)} %pack_deltas.1), channel_id=1, source_target_pairs={{0,2},{1,3},{2,0},{3,1},{4,6},{5,7},{6,4},{7,5},{8,10},{9,11},{10,... | collective-permute-start | bytes 24584 | tf_op jit(solution)/shard_map/ppermute | solution.py:552
  44.8 15.4 %collective-permute-start.15 = (bf16[512,256]{1,0:T(8,128)(2,1)S(1)}, bf16[512,256]{1,0:T(8,128)(2,1)S(1)}, u32[]{:S(2)}, u32[]{:S(2)}) collective-permute-start(bf16[512,256]{1,0:T(8,128)(2,1)S(1)} %get-tuple-element.54), channel_id=1, source_target_pairs={{8,0},{12,4},{9,1},{13,5},{10,2},{14,6},{11,3},{15,7},{24,16},{28,... | collective-permute-start | bytes 786440 | tf_op jit(solution)/shard_map/ppermute | solution.py:564
  46.1 26.0 %collective-permute-start.16 = (bf16[512,256]{1,0:T(8,128)(2,1)S(1)}, bf16[512,256]{1,0:T(8,128)(2,1)S(1)}, u32[]{:S(2)}, u32[]{:S(2)}) collective-permute-start(bf16[512,256]{1,0:T(8,128)(2,1)S(1)} %get-tuple-element.55), channel_id=1, source_target_pairs={{12,0},{13,1},{14,2},{15,3},{28,16},{29,17},{30,18},{31,19}} | collective-permute-start | bytes 786440 | tf_op jit(solution)/shard_map/ppermute | solution.py:564
  52.1 30.8 %collective-permute-start.18 = (bf16[256,1024]{1,0:T(8,128)(2,1)S(1)}, bf16[256,1024]{1,0:T(8,128)(2,1)S(1)}, u32[]{:S(2)}, u32[]{:S(2)}) collective-permute-start(bf16[256,1024]{1,0:T(8,128)(2,1)S(1)} %get-tuple-element.58), channel_id=1, source_target_pairs={{0,2},{1,3},{2,0},{3,1},{4,6},{5,7},{6,4},{7,5},{8,10},{9,11},{10,... | collective-permute-start | bytes 1572872 | tf_op jit(solution)/shard_map/ppermute | solution.py:552
  72.1 1.6 %collective-permute-start.17 = (bf16[128,1024]{1,0:T(8,128)(2,1)S(1)}, bf16[128,1024]{1,0:T(8,128)(2,1)S(1)}, u32[]{:S(2)}, u32[]{:S(2)}) collective-permute-start(bf16[128,1024]{1,0:T(8,128)(2,1)S(1)} %get-tuple-element.57), channel_id=1, source_target_pairs={{0,1},{1,0},{2,3},{3,2},{4,5},{5,4},{6,7},{7,6},{8,9},{9,8},{10,11... | collective-permute-start | bytes 786440 | tf_op jit(solution)/shard_map/ppermute | solution.py:552
  72.2 10.6 %collective-permute-start.19 = (bf16[512,256]{1,0:T(8,128)(2,1)S(1)}, bf16[512,256]{1,0:T(8,128)(2,1)S(1)}, u32[]{:S(2)}, u32[]{:S(2)}) collective-permute-start(bf16[512,256]{1,0:T(8,128)(2,1)S(1)} %get-tuple-element.61), channel_id=1, source_target_pairs={{4,0},{8,4},{12,8},{5,1},{9,5},{13,9},{6,2},{10,6},{14,10},{7,3},{... | collective-permute-start | bytes 786440 | tf_op jit(solution)/shard_map/ppermute | solution.py:564
  82.9 7.0 %collective-permute-start.20 = (bf16[128,1024]{1,0:T(8,128)(2,1)S(1)}, bf16[128,1024]{1,0:T(8,128)(2,1)S(1)}, u32[]{:S(2)}, u32[]{:S(2)}) collective-permute-start(bf16[128,1024]{1,0:T(8,128)(2,1)S(1)} %slice.3), channel_id=1, source_target_pairs={{0,1},{1,0},{2,3},{3,2},{4,5},{5,4},{6,7},{7,6},{8,9},{9,8},{10,11... | collective-permute-start | bytes 786440 | tf_op jit(solution)/shard_map/ppermute | solution.py:552
  83.0 1.9 %collective-permute-start.21 = (bf16[128,256]{1,0:T(8,128)(2,1)S(1)}, bf16[128,256]{1,0:T(8,128)(2,1)S(1)}, u32[]{:S(2)}, u32[]{:S(2)}) collective-permute-start(bf16[128,256]{1,0:T(8,128)(2,1)S(1)} %get-tuple-element.63), channel_id=1, source_target_pairs={{0,1},{1,0},{2,3},{3,2},{4,5},{5,4},{6,7},{7,6},{8,9},{9,8},{10,11... | collective-permute-start | bytes 196616 | tf_op jit(solution)/shard_map/ppermute | solution.py:552
  83.5 4.3 %collective-permute-start.22 = (bf16[128,256]{1,0:T(8,128)(2,1)S(1)}, bf16[128,256]{1,0:T(8,128)(2,1)S(1)}, u32[]{:S(2)}, u32[]{:S(2)}) collective-permute-start(bf16[128,256]{1,0:T(8,128)(2,1)S(1)} %get-tuple-element.64), channel_id=1, source_target_pairs={{0,2},{1,3},{2,0},{3,1},{4,6},{5,7},{6,4},{7,5},{8,10},{9,11},{10,... | collective-permute-start | bytes 196616 | tf_op jit(solution)/shard_map/ppermute | solution.py:552
  84.8 4.4 %collective-permute-start.23 = (bf16[128,256]{1,0:T(8,128)(2,1)S(1)}, bf16[128,256]{1,0:T(8,128)(2,1)S(1)}, u32[]{:S(2)}, u32[]{:S(2)}) collective-permute-start(bf16[128,256]{1,0:T(8,128)(2,1)S(1)} %get-tuple-element.65), channel_id=1, source_target_pairs={{0,3},{1,2},{2,1},{3,0},{4,7},{5,6},{6,5},{7,4},{8,11},{9,10},{10,... | collective-permute-start | bytes 196616 | tf_op jit(solution)/shard_map/ppermute | solution.py:552

commit v11 on v10

--- a/solution.py
+++ b/solution.py
@@ -597,10 +597,8 @@
     dq_side = after(dq_side, sums)
     sums = [sums[0]] + [to_partner(sums[flip], flip) for flip in range(1, QUAD)]
     dq_corner = to_partner(dq_side[TILE:], 1)
-    return (
-        place_queries(me, dq_own, dq_core, dq_side, dq_corner),
-        *place_keys(me, *sums),
-    )
+    query_grad = place_queries(me, dq_own, dq_core, dq_side, dq_corner)
+    return (query_grad, *place_keys(me, *after(sums, query_grad)))
 
 
 def solution(mesh):

time: 92.5 us -> 92.3 us (level)
    ppermute x3, waiting for transfers between devices: 25.5 us -> 27.7 us  [down(): lax.ppermute(x, 'level', [(z + shift, z) for z in range(steps - shift)])]
    ppermute x15, waiting for transfers between devices: 8.48 us -> 6.84 us  [to_partner(): lax.ppermute(x, ('side', 'core'), [(t, t ^ flip) for t in range(QUAD)])]
  transfers between devices with their start and end apart: 24 -> 24, of which waited for: 11 -> 10; matrix products, arithmetic and copies ran while one was open for 0% -> 0% of each run, Pallas kernels for 16% -> 16%
where the time goes in v11:
time: 92.3 us; the launch traced here: 91.5 us
  waiting for transfers between devices  39.4 us (43%)
  starting transfers between devices  32.7 us (35%)
  Pallas kernels  15.5 us (17%)
  local copies, waits for them, and re-layouts  3.07 us (3%)
  between operations  0.93 us (1%)
    ppermute x3, waiting for transfers between devices, down(): lax.ppermute(x, 'level', [(z + shift, z) for z in range(steps - shift)])  27.7 us
    ppermute x6, starting transfers between devices, up(): lax.ppermute(x, 'level', [(z, z + shift) for z in range(steps - shift)])  19.3 us
    ppermute x15, starting transfers between devices, to_partner(): lax.ppermute(x, ('side', 'core'), [(t, t ^ flip) for t in range(QUAD)])  9.53 us
    pallas_call x3, Pallas kernels, gradients(): pl.pallas_call(functools.partial(grads_kernel, ancestors.shape[1], stage,...  9.48 us
    ppermute x15, waiting for transfers between devices, to_partner(): lax.ppermute(x, ('side', 'core'), [(t, t ^ flip) for t in range(QUAD)])  6.84 us
    ppermute x6, waiting for transfers between devices, up(): lax.ppermute(x, 'level', [(z, z + shift) for z in range(steps - shift)])  4.78 us
    ppermute x3, starting transfers between devices, down(): lax.ppermute(x, 'level', [(z + shift, z) for z in range(steps - shift)])  3.88 us
    pallas_call x1, Pallas kernels, statistics(): pl.pallas_call(functools.partial(stats_kernel, ancestors.shape[1], steps)...  3.3 us
  transfers between devices with their start and end apart: 24, of which 10 were waited for; matrix products, arithmetic and copies ran while one was open for 0% of the time, Pallas kernels for 16%

profile of v11, /device:TPU:0, one launch (start us, length us, event | category | flops | bytes accessed | tf_op | source)
XLA Modules:
  0.0 91.5 jit_solution(1784681106145511078)
XLA Ops:
  0.6 0.0 copy-start
  0.6 0.5 collective-permute-start
  1.2 0.1 collective-permute-start.5
  1.2 0.9 copy-done.4
  2.1 0.9 copy-done.5
  3.1 0.5 collective-permute-start.1
  3.6 2.6 %collective-permute-start.2 = (bf16[128,256]{1,0:T(8,128)(2,1)S(1)}, bf16[128,256]{1,0:T(8,128)(2,1)S(1)}, u32[]{:S(2)}, u32[]{:S(2)}) collective-permute-start(bf16[128,256]{1,0:T(8,128)(2,1)S(1)} %get-tuple-element.42), channel_id=1, source_target_pairs={{0,2},{1,3},{2,0},{3,1},{4,6},{5,7},{6,4},{7,5},{8,10},{9,11},{10,... | collective-permute-start | bytes 196616 | tf_op jit(solution)/shard_map/ppermute | solution.py:552
  6.2 0.1 collective-permute-start.3
  6.3 0.0 collective-permute-done.1.refs_1_
  6.3 2.6 %collective-permute-done.2.refs_2_ = bf16[128,256]{1,0:T(8,128)(2,1)S(1)} collective-permute-done((bf16[128,256]{1,0:T(8,128)(2,1)S(1)}, bf16[128,256]{1,0:T(8,128)(2,1)S(1)}, u32[]{:S(2)}, u32[]{:S(2)}) %collective-permute-start.2) | collective-permute-done | bytes 65568 | tf_op jit(solution)/shard_map/ppermute | solution.py:552
  8.9 1.4 %collective-permute-done.3.refs_3_ = bf16[128,256]{1,0:T(8,128)(2,1)S(1)} collective-permute-done((bf16[128,256]{1,0:T(8,128)(2,1)S(1)}, bf16[128,256]{1,0:T(8,128)(2,1)S(1)}, u32[]{:S(2)}, u32[]{:S(2)}) %collective-permute-start.3) | collective-permute-done | bytes 65568 | tf_op jit(solution)/shard_map/ppermute | solution.py:552
  10.3 0.0 collective-permute-done.peer.rest_1_
  10.3 0.0 copy-start.2
  10.3 1.2 %copy-done.2 = bf16[128,4096]{1,0:T(8,128)(2,1)S(1)} copy-done((bf16[128,4096]{1,0:T(8,128)(2,1)S(1)}, bf16[128,4096]{1,0:T(8,128)(2,1)}, u32[]{:S(2)}) %copy-start.2) | copy-done | bytes 1048600
  11.6 0.0 copy-start.3
  11.6 0.0 copy-start.6
  11.6 1.4 %collective-permute-start.4 = (bf16[256,1024]{1,0:T(8,128)(2,1)S(1)}, bf16[256,1024]{1,0:T(8,128)(2,1)S(1)}, u32[]{:S(2)}, u32[]{:S(2)}) collective-permute-start(bf16[256,1024]{1,0:T(8,128)(2,1)S(1)} %pack_queries.2), channel_id=1, source_target_pairs={{0,2},{1,3},{2,0},{3,1},{4,6},{5,7},{6,4},{7,5},{8,10},{9,11},{10,... | collective-permute-start | bytes 1572872 | tf_op jit(solution)/shard_map/ppermute | solution.py:552
  13.0 5.5 %collective-permute-start.8 = (bf16[512,128]{1,0:T(8,128)(2,1)S(1)}, bf16[512,128]{1,0:T(8,128)(2,1)S(1)}, u32[]{:S(2)}, u32[]{:S(2)}) collective-permute-start(bf16[512,128]{1,0:T(8,128)(2,1)S(1)} %get-tuple-element.47.after_ref.rest_3_.rest_10_), channel_id=1, source_target_pairs={{0,12},{1,13},{2,14},{3,15},{16,28},{17,29},{18,30},{19,31}} | collective-permute-start | bytes 393224 | tf_op jit(solution)/shard_map/ppermute | solution.py:558
  18.5 1.3 %collective-permute-start.7 = (bf16[512,128]{1,0:T(8,128)(2,1)S(1)}, bf16[512,128]{1,0:T(8,128)(2,1)S(1)}, u32[]{:S(2)}, u32[]{:S(2)}) collective-permute-start(bf16[512,128]{1,0:T(8,128)(2,1)S(1)} %get-tuple-element.47.after_ref.rest_3_.rest_10_), channel_id=1, source_target_pairs={{0,8},{4,12},{1,9},{5,13},{2,10},{6,14},{3,11},{7,15},{16,24},{20,... | collective-permute-start | bytes 393224 | tf_op jit(solution)/shard_map/ppermute | solution.py:558
  19.8 2.5 %collective-permute-start.6 = (bf16[512,128]{1,0:T(8,128)(2,1)S(1)}, bf16[512,128]{1,0:T(8,128)(2,1)S(1)}, u32[]{:S(2)}, u32[]{:S(2)}) collective-permute-start(bf16[512,128]{1,0:T(8,128)(2,1)S(1)} %get-tuple-element.47.after_ref.rest_3_.rest_10_), channel_id=1, source_target_pairs={{0,4},{4,8},{8,12},{1,5},{5,9},{9,13},{2,6},{6,10},{10,14},{3,7},{... | collective-permute-start | bytes 393224 | tf_op jit(solution)/shard_map/ppermute | solution.py:558
  22.3 0.1 collective-permute-done.8.rest_6_.rest_11_
  22.4 2.8 %collective-permute-done.7.rest_5_.rest_10_ = bf16[512,128]{1,0:T(8,128)(2,1)S(1)} collective-permute-done((bf16[512,128]{1,0:T(8,128)(2,1)S(1)}, bf16[512,128]{1,0:T(8,128)(2,1)S(1)}, u32[]{:S(2)}, u32[]{:S(2)}) %collective-permute-start.7) | collective-permute-done | bytes 131104 | tf_op jit(solution)/shard_map/ppermute | solution.py:558
  25.2 1.8 %collective-permute-done.6.rest_4_.rest_11_ = bf16[512,128]{1,0:T(8,128)(2,1)S(1)} collective-permute-done((bf16[512,128]{1,0:T(8,128)(2,1)S(1)}, bf16[512,128]{1,0:T(8,128)(2,1)S(1)}, u32[]{:S(2)}, u32[]{:S(2)}) %collective-permute-start.6) | collective-permute-done | bytes 131104 | tf_op jit(solution)/shard_map/ppermute | solution.py:558
  27.1 0.0 collective-permute-done.5.peer.rest_4_
  27.1 0.8 collective-permute-start.9
  27.9 0.6 row_deltas.1
  28.5 0.1 collective-permute-start.10
  28.6 6.3 %collective-permute-start.14 = (bf16[512,128]{1,0:T(8,128)(2,1)S(1)}, bf16[512,128]{1,0:T(8,128)(2,1)S(1)}, u32[]{:S(2)}, u32[]{:S(2)}) collective-permute-start(bf16[512,128]{1,0:T(8,128)(2,1)S(1)} %get-tuple-element.52.rest_12_), channel_id=1, source_target_pairs={{0,12},{1,13},{2,14},{3,15},{16,28},{17,29},{18,30},{19,31}} | collective-permute-start | bytes 393224 | tf_op jit(solution)/shard_map/ppermute | solution.py:558
  34.8 2.5 %collective-permute-start.13 = (bf16[512,128]{1,0:T(8,128)(2,1)S(1)}, bf16[512,128]{1,0:T(8,128)(2,1)S(1)}, u32[]{:S(2)}, u32[]{:S(2)}) collective-permute-start(bf16[512,128]{1,0:T(8,128)(2,1)S(1)} %get-tuple-element.52.rest_12_), channel_id=1, source_target_pairs={{0,8},{4,12},{1,9},{5,13},{2,10},{6,14},{3,11},{7,15},{16,24},{20,... | collective-permute-start | bytes 393224 | tf_op jit(solution)/shard_map/ppermute | solution.py:558
  37.3 0.0 collective-permute-done.10.pair.rest_7_
  37.3 1.3 %collective-permute-start.12 = (bf16[512,128]{1,0:T(8,128)(2,1)S(1)}, bf16[512,128]{1,0:T(8,128)(2,1)S(1)}, u32[]{:S(2)}, u32[]{:S(2)}) collective-permute-start(bf16[512,128]{1,0:T(8,128)(2,1)S(1)} %get-tuple-element.52.rest_12_), channel_id=1, source_target_pairs={{0,4},{4,8},{8,12},{1,5},{5,9},{9,13},{2,6},{6,10},{10,14},{3,7},{... | collective-permute-start | bytes 393224 | tf_op jit(solution)/shard_map/ppermute | solution.py:558
  38.6 0.0 collective-permute-done.4.rest_2_
  38.7 1.4 %collective-permute-start.11 = (f32[16,128]{1,0:T(8,128)S(1)}, f32[16,128]{1,0:T(8,128)S(1)}, u32[]{:S(2)}, u32[]{:S(2)}) collective-permute-start(f32[16,128]{1,0:T(8,128)S(1)} %pack_deltas.1), channel_id=1, source_target_pairs={{0,2},{1,3},{2,0},{3,1},{4,6},{5,7},{6,4},{7,5},{8,10},{9,11},{10,... | collective-permute-start | bytes 24584 | tf_op jit(solution)/shard_map/ppermute | solution.py:552
  40.1 3.3 %statistics.1.rest_9_ = f32[4,1,1024]{2,1,0:T(1,128)S(1)} custom-call(s32[1]{0:T(128)} %bitcast.me_ref, s32[16,10]{1,0:T(8,128)S(1)} %copy-done.6, bf16[128,4096]{1,0:T(8,128)(2,1)S(1)} %copy-done.3, bf16[128,4096]{1,0:T(8,128)(2,1)S(1)} %collective-permute-done.peer.rest_1_, bf16[256,1024]{1,0:T(8,128)(2,1)S(1)} %collective-permute-done.4.rest_2_, ...), custom_call_target="tpu_custom_call" | custom-call | flops 2952790016 | bytes 16777216 | tf_op jit(solution)/shard_map/statistics/pallas_call | solution.py:328
  43.4 0.0 collective-permute-done.11.rest_8_
  43.4 0.0 collective-permute-done.14.rest_13_
  43.4 0.0 collective-permute-done.13.rest_12_
  43.4 0.0 collective-permute-done.9.rest_5_
  43.4 1.4 %far_grads.1 = (f32[4,128,1024]{2,1,0:T(8,128)S(1)}, bf16[512,256]{1,0:T(8,128)(2,1)S(1)}, bf16[512,256]{1,0:T(8,128)(2,1)S(1)}) custom-call(s32[1]{0:T(128)} %bitcast.me_ref, s32[16,10]{1,0:T(8,128)S(1)} %copy-done.6, bf16[128,4096]{1,0:T(8,128)(2,1)S(1)} %copy-done.3, bf16[128,4096]{1,0:T(8,128)(2,1)S(1)} %collective-permute-done.peer.rest_1_, ...), custom_call_target="tpu_custom_call" | custom-call | flops 14763950080 | bytes 16777216 | tf_op jit(solution)/shard_map/far_grads/pallas_call | solution.py:376
  44.8 1.3 %collective-permute-start.15 = (bf16[512,256]{1,0:T(8,128)(2,1)S(1)}, bf16[512,256]{1,0:T(8,128)(2,1)S(1)}, u32[]{:S(2)}, u32[]{:S(2)}) collective-permute-start(bf16[512,256]{1,0:T(8,128)(2,1)S(1)} %get-tuple-element.58), channel_id=1, source_target_pairs={{8,0},{12,4},{9,1},{13,5},{10,2},{14,6},{11,3},{15,7},{24,16},{28,... | collective-permute-start | bytes 786440 | tf_op jit(solution)/shard_map/ppermute | solution.py:564
  46.1 1.3 %collective-permute-start.16 = (bf16[512,256]{1,0:T(8,128)(2,1)S(1)}, bf16[512,256]{1,0:T(8,128)(2,1)S(1)}, u32[]{:S(2)}, u32[]{:S(2)}) collective-permute-start(bf16[512,256]{1,0:T(8,128)(2,1)S(1)} %get-tuple-element.59), channel_id=1, source_target_pairs={{12,0},{13,1},{14,2},{15,3},{28,16},{29,17},{30,18},{31,19}} | collective-permute-start | bytes 786440 | tf_op jit(solution)/shard_map/ppermute | solution.py:564
  47.4 0.0 collective-permute-done.12.rest_13_
  47.4 4.7 %side_grads.1 = (bf16[256,1024]{1,0:T(8,128)(2,1)S(1)}, f32[1024,128]{1,0:T(8,128)S(1)}, f32[1024,128]{1,0:T(8,128)S(1)}) custom-call(s32[1]{0:T(128)} %bitcast.me_ref, s32[16,10]{1,0:T(8,128)S(1)} %copy-done.6, bf16[128,4096]{1,0:T(8,128)(2,1)S(1)} %copy-done.3, bf16[128,4096]{1,0:T(8,128)(2,1)S(1)} %collective-permute-done.peer.rest_1_, ...), custom_call_target="tpu_custom_call" | custom-call | flops 14763950080 | bytes 16777216 | tf_op jit(solution)/shard_map/side_grads/pallas_call | solution.py:376
  52.1 0.1 collective-permute-start.18
  52.1 3.4 %own_grads.1 = (bf16[128,1024]{1,0:T(8,128)(2,1)S(1)}, bf16[128,1024]{1,0:T(8,128)(2,1)S(1)}, f32[512,256]{1,0:T(8,128)S(1)}, bf16[512,256]{1,0:T(8,128)(2,1)S(1)}) custom-call(s32[1]{0:T(128)} %bitcast.me_ref, s32[16,10]{1,0:T(8,128)S(1)} %copy-done.6, bf16[128,4096]{1,0:T(8,128)(2,1)S(1)} %copy-done.3, ...), custom_call_target="tpu_custom_call" | custom-call | flops 14763950080 | bytes 16777216 | tf_op jit(solution)/shard_map/own_grads/pallas_call | solution.py:376
  55.6 18.7 %collective-permute-done.15.refs_0_ = bf16[512,256]{1,0:T(8,128)(2,1)S(1)} collective-permute-done((bf16[512,256]{1,0:T(8,128)(2,1)S(1)}, bf16[512,256]{1,0:T(8,128)(2,1)S(1)}, u32[]{:S(2)}, u32[]{:S(2)}) %collective-permute-start.15) | collective-permute-done | bytes 262176 | tf_op jit(solution)/shard_map/ppermute | solution.py:564
  74.3 0.0 collective-permute-done.16.refs_1_
  74.3 0.1 add_far.1
  74.4 0.1 collective-permute-start.17
  74.4 1.3 %collective-permute-start.19 = (bf16[512,256]{1,0:T(8,128)(2,1)S(1)}, bf16[512,256]{1,0:T(8,128)(2,1)S(1)}, u32[]{:S(2)}, u32[]{:S(2)}) collective-permute-start(bf16[512,256]{1,0:T(8,128)(2,1)S(1)} %get-tuple-element.65), channel_id=1, source_target_pairs={{4,0},{8,4},{12,8},{5,1},{9,5},{13,9},{6,2},{10,6},{14,10},{7,3},{... | collective-permute-start | bytes 786440 | tf_op jit(solution)/shard_map/ppermute | solution.py:564
  75.7 0.2 collective-permute-done.17.refs_1_
  76.0 9.1 %collective-permute-done.19.near_ref = bf16[512,256]{1,0:T(8,128)(2,1)S(1)} collective-permute-done((bf16[512,256]{1,0:T(8,128)(2,1)S(1)}, bf16[512,256]{1,0:T(8,128)(2,1)S(1)}, u32[]{:S(2)}, u32[]{:S(2)}) %collective-permute-start.19) | collective-permute-done | bytes 262176 | tf_op jit(solution)/shard_map/ppermute | solution.py:564
  85.0 0.1 add_sums.1
  85.1 0.0 collective-permute-done.18.refs_2_
  85.1 0.1 collective-permute-start.20
  85.2 0.5 collective-permute-start.21
  85.7 0.7 collective-permute-start.22
  86.4 0.7 collective-permute-start.23
  87.1 0.0 collective-permute-done.20.refs_3_
  87.1 1.0 %place_queries.1 = bf16[128,4096]{1,0:T(8,128)(2,1)} custom-call(s32[1]{0:T(128)} %bitcast.me_ref, bf16[128,1024]{1,0:T(8,128)(2,1)S(1)} %get-tuple-element.56.refs_0_, bf16[128,1024]{1,0:T(8,128)(2,1)S(1)} %collective-permute-done.17.refs_1_, bf16[256,1024]{1,0:T(8,128)(2,1)S(1)} %collective-permute-done.18.refs_2_, ...), custom_call_target="tpu_custom_call" | custom-call | tf_op jit(solution)/shard_map/place_queries/pallas_call | solution.py:518
  88.2 0.0 collective-permute-done.21.refs_1_
  88.2 2.4 %collective-permute-done.22.refs_2_ = bf16[128,256]{1,0:T(8,128)(2,1)S(1)} collective-permute-done((bf16[128,256]{1,0:T(8,128)(2,1)S(1)}, bf16[128,256]{1,0:T(8,128)(2,1)S(1)}, u32[]{:S(2)}, u32[]{:S(2)}) %collective-permute-start.22) | collective-permute-done | bytes 65568 | tf_op jit(solution)/shard_map/ppermute | solution.py:552
  90.5 0.3 collective-permute-done.23.refs_3_
  90.8 0.7 place_keys.1
  (13 shorter events, 0.2 us)
Async XLA Ops:
  0.6 26.4 %copy-start = (bf16[128,4096]{1,0:T(8,128)(2,1)S(1)}, bf16[128,4096]{1,0:T(8,128)(2,1)}, u32[]{:S(2)}) copy-start(bf16[128,4096]{1,0:T(8,128)(2,1)} %rest_3_.5) | copy-start | bytes 3145732
  0.6 9.7 %collective-permute-start = (bf16[128,4096]{1,0:T(8,128)(2,1)}, bf16[128,4096]{1,0:T(8,128)(2,1)S(1)}, u32[]{:S(2)}, u32[]{:S(2)}) collective-permute-start(bf16[128,4096]{1,0:T(8,128)(2,1)} %rest_0_.7), channel_id=1, source_target_pairs={{0,1},{1,0},{2,3},{3,2},{4,5},{5,4},{6,7},{7,6},{8,9},{9,8},{10,11... | collective-permute-start | bytes 3145736 | tf_op jit(solution)/shard_map/ppermute | solution.py:552
  1.2 25.9 %collective-permute-start.5 = (bf16[128,4096]{1,0:T(8,128)(2,1)}, bf16[128,4096]{1,0:T(8,128)(2,1)S(1)}, u32[]{:S(2)}, u32[]{:S(2)}) collective-permute-start(bf16[128,4096]{1,0:T(8,128)(2,1)} %rest_3_.5), channel_id=1, source_target_pairs={{0,1},{1,0},{2,3},{3,2},{4,5},{5,4},{6,7},{7,6},{8,9},{9,8},{10,11... | collective-permute-start | bytes 3145736 | tf_op jit(solution)/shard_map/ppermute | solution.py:552
  1.2 0.9 copy-start.4
  2.1 0.9 copy-start.5
  3.1 3.2 %collective-permute-start.1 = (bf16[128,256]{1,0:T(8,128)(2,1)S(1)}, bf16[128,256]{1,0:T(8,128)(2,1)S(1)}, u32[]{:S(2)}, u32[]{:S(2)}) collective-permute-start(bf16[128,256]{1,0:T(8,128)(2,1)S(1)} %get-tuple-element.41), channel_id=1, source_target_pairs={{0,1},{1,0},{2,3},{3,2},{4,5},{5,4},{6,7},{7,6},{8,9},{9,8},{10,11... | collective-permute-start | bytes 196616 | tf_op jit(solution)/shard_map/ppermute | solution.py:552
  3.6 5.3 %collective-permute-start.2 = (bf16[128,256]{1,0:T(8,128)(2,1)S(1)}, bf16[128,256]{1,0:T(8,128)(2,1)S(1)}, u32[]{:S(2)}, u32[]{:S(2)}) collective-permute-start(bf16[128,256]{1,0:T(8,128)(2,1)S(1)} %get-tuple-element.42), channel_id=1, source_target_pairs={{0,2},{1,3},{2,0},{3,1},{4,6},{5,7},{6,4},{7,5},{8,10},{9,11},{10,... | collective-permute-start | bytes 196616 | tf_op jit(solution)/shard_map/ppermute | solution.py:552
  6.2 4.0 %collective-permute-start.3 = (bf16[128,256]{1,0:T(8,128)(2,1)S(1)}, bf16[128,256]{1,0:T(8,128)(2,1)S(1)}, u32[]{:S(2)}, u32[]{:S(2)}) collective-permute-start(bf16[128,256]{1,0:T(8,128)(2,1)S(1)} %get-tuple-element.43), channel_id=1, source_target_pairs={{0,3},{1,2},{2,1},{3,0},{4,7},{5,6},{6,5},{7,4},{8,11},{9,10},{10,... | collective-permute-start | bytes 196616 | tf_op jit(solution)/shard_map/ppermute | solution.py:552
  10.3 1.2 %copy-start.2 = (bf16[128,4096]{1,0:T(8,128)(2,1)S(1)}, bf16[128,4096]{1,0:T(8,128)(2,1)}, u32[]{:S(2)}) copy-start(bf16[128,4096]{1,0:T(8,128)(2,1)} %rest_0_.7) | copy-start | bytes 3145732
  11.5 16.4 %copy-start.1 = (bf16[128,4096]{1,0:T(8,128)(2,1)S(1)}, bf16[128,4096]{1,0:T(8,128)(2,1)}, u32[]{:S(2)}) copy-start(bf16[128,4096]{1,0:T(8,128)(2,1)} %out_ref.1) | copy-start | bytes 3145732
  11.6 28.5 %copy-start.3 = (bf16[128,4096]{1,0:T(8,128)(2,1)S(1)}, bf16[128,4096]{1,0:T(8,128)(2,1)}, u32[]{:S(2)}) copy-start(bf16[128,4096]{1,0:T(8,128)(2,1)} %rest_0_.7) | copy-start | bytes 3145732
  11.6 28.5 %copy-start.6 = (s32[16,10]{1,0:T(8,128)S(1)}, s32[16,10]{1,0:T(8,128)}, u32[]{:S(2)}) copy-start(s32[16,10]{1,0:T(8,128)} %anc_ref.7) | copy-start | bytes 1924
  11.6 27.1 %collective-permute-start.4 = (bf16[256,1024]{1,0:T(8,128)(2,1)S(1)}, bf16[256,1024]{1,0:T(8,128)(2,1)S(1)}, u32[]{:S(2)}, u32[]{:S(2)}) collective-permute-start(bf16[256,1024]{1,0:T(8,128)(2,1)S(1)} %pack_queries.2), channel_id=1, source_target_pairs={{0,2},{1,3},{2,0},{3,1},{4,6},{5,7},{6,4},{7,5},{8,10},{9,11},{10,... | collective-permute-start | bytes 1572872 | tf_op jit(solution)/shard_map/ppermute | solution.py:552
  13.0 9.4 %collective-permute-start.8 = (bf16[512,128]{1,0:T(8,128)(2,1)S(1)}, bf16[512,128]{1,0:T(8,128)(2,1)S(1)}, u32[]{:S(2)}, u32[]{:S(2)}) collective-permute-start(bf16[512,128]{1,0:T(8,128)(2,1)S(1)} %get-tuple-element.47.after_ref.rest_3_.rest_10_), channel_id=1, source_target_pairs={{0,12},{1,13},{2,14},{3,15},{16,28},{17,29},{18,30},{19,31}} | collective-permute-start | bytes 393224 | tf_op jit(solution)/shard_map/ppermute | solution.py:558
  18.5 6.7 %collective-permute-start.7 = (bf16[512,128]{1,0:T(8,128)(2,1)S(1)}, bf16[512,128]{1,0:T(8,128)(2,1)S(1)}, u32[]{:S(2)}, u32[]{:S(2)}) collective-permute-start(bf16[512,128]{1,0:T(8,128)(2,1)S(1)} %get-tuple-element.47.after_ref.rest_3_.rest_10_), channel_id=1, source_target_pairs={{0,8},{4,12},{1,9},{5,13},{2,10},{6,14},{3,11},{7,15},{16,24},{20,... | collective-permute-start | bytes 393224 | tf_op jit(solution)/shard_map/ppermute | solution.py:558
  19.8 7.2 %collective-permute-start.6 = (bf16[512,128]{1,0:T(8,128)(2,1)S(1)}, bf16[512,128]{1,0:T(8,128)(2,1)S(1)}, u32[]{:S(2)}, u32[]{:S(2)}) collective-permute-start(bf16[512,128]{1,0:T(8,128)(2,1)S(1)} %get-tuple-element.47.after_ref.rest_3_.rest_10_), channel_id=1, source_target_pairs={{0,4},{4,8},{8,12},{1,5},{5,9},{9,13},{2,6},{6,10},{10,14},{3,7},{... | collective-permute-start | bytes 393224 | tf_op jit(solution)/shard_map/ppermute | solution.py:558
  27.1 16.3 %collective-permute-start.9 = (bf16[256,1024]{1,0:T(8,128)(2,1)S(1)}, bf16[256,1024]{1,0:T(8,128)(2,1)S(1)}, u32[]{:S(2)}, u32[]{:S(2)}) collective-permute-start(bf16[256,1024]{1,0:T(8,128)(2,1)S(1)} %pack_queries.3), channel_id=1, source_target_pairs={{0,2},{1,3},{2,0},{3,1},{4,6},{5,7},{6,4},{7,5},{8,10},{9,11},{10,... | collective-permute-start | bytes 1572872 | tf_op jit(solution)/shard_map/ppermute | solution.py:552
  28.5 8.8 %collective-permute-start.10 = (f32[16,128]{1,0:T(8,128)S(1)}, f32[16,128]{1,0:T(8,128)S(1)}, u32[]{:S(2)}, u32[]{:S(2)}) collective-permute-start(f32[16,128]{1,0:T(8,128)S(1)} %get-tuple-element.49), channel_id=1, source_target_pairs={{0,1},{1,0},{2,3},{3,2},{4,5},{5,4},{6,7},{7,6},{8,9},{9,8},{10,11... | collective-permute-start | bytes 24584 | tf_op jit(solution)/shard_map/ppermute | solution.py:552
  28.6 14.8 %collective-permute-start.14 = (bf16[512,128]{1,0:T(8,128)(2,1)S(1)}, bf16[512,128]{1,0:T(8,128)(2,1)S(1)}, u32[]{:S(2)}, u32[]{:S(2)}) collective-permute-start(bf16[512,128]{1,0:T(8,128)(2,1)S(1)} %get-tuple-element.52.rest_12_), channel_id=1, source_target_pairs={{0,12},{1,13},{2,14},{3,15},{16,28},{17,29},{18,30},{19,31}} | collective-permute-start | bytes 393224 | tf_op jit(solution)/shard_map/ppermute | solution.py:558
  34.8 8.5 %collective-permute-start.13 = (bf16[512,128]{1,0:T(8,128)(2,1)S(1)}, bf16[512,128]{1,0:T(8,128)(2,1)S(1)}, u32[]{:S(2)}, u32[]{:S(2)}) collective-permute-start(bf16[512,128]{1,0:T(8,128)(2,1)S(1)} %get-tuple-element.52.rest_12_), channel_id=1, source_target_pairs={{0,8},{4,12},{1,9},{5,13},{2,10},{6,14},{3,11},{7,15},{16,24},{20,... | collective-permute-start | bytes 393224 | tf_op jit(solution)/shard_map/ppermute | solution.py:558
  37.3 10.0 %collective-permute-start.12 = (bf16[512,128]{1,0:T(8,128)(2,1)S(1)}, bf16[512,128]{1,0:T(8,128)(2,1)S(1)}, u32[]{:S(2)}, u32[]{:S(2)}) collective-permute-start(bf16[512,128]{1,0:T(8,128)(2,1)S(1)} %get-tuple-element.52.rest_12_), channel_id=1, source_target_pairs={{0,4},{4,8},{8,12},{1,5},{5,9},{9,13},{2,6},{6,10},{10,14},{3,7},{... | collective-permute-start | bytes 393224 | tf_op jit(solution)/shard_map/ppermute | solution.py:558
  38.7 4.7 %collective-permute-start.11 = (f32[16,128]{1,0:T(8,128)S(1)}, f32[16,128]{1,0:T(8,128)S(1)}, u32[]{:S(2)}, u32[]{:S(2)}) collective-permute-start(f32[16,128]{1,0:T(8,128)S(1)} %pack_deltas.1), channel_id=1, source_target_pairs={{0,2},{1,3},{2,0},{3,1},{4,6},{5,7},{6,4},{7,5},{8,10},{9,11},{10,... | collective-permute-start | bytes 24584 | tf_op jit(solution)/shard_map/ppermute | solution.py:552
  44.8 29.5 %collective-permute-start.15 = (bf16[512,256]{1,0:T(8,128)(2,1)S(1)}, bf16[512,256]{1,0:T(8,128)(2,1)S(1)}, u32[]{:S(2)}, u32[]{:S(2)}) collective-permute-start(bf16[512,256]{1,0:T(8,128)(2,1)S(1)} %get-tuple-element.58), channel_id=1, source_target_pairs={{8,0},{12,4},{9,1},{13,5},{10,2},{14,6},{11,3},{15,7},{24,16},{28,... | collective-permute-start | bytes 786440 | tf_op jit(solution)/shard_map/ppermute | solution.py:564
  46.1 28.2 %collective-permute-start.16 = (bf16[512,256]{1,0:T(8,128)(2,1)S(1)}, bf16[512,256]{1,0:T(8,128)(2,1)S(1)}, u32[]{:S(2)}, u32[]{:S(2)}) collective-permute-start(bf16[512,256]{1,0:T(8,128)(2,1)S(1)} %get-tuple-element.59), channel_id=1, source_target_pairs={{12,0},{13,1},{14,2},{15,3},{28,16},{29,17},{30,18},{31,19}} | collective-permute-start | bytes 786440 | tf_op jit(solution)/shard_map/ppermute | solution.py:564
  52.1 33.0 %collective-permute-start.18 = (bf16[256,1024]{1,0:T(8,128)(2,1)S(1)}, bf16[256,1024]{1,0:T(8,128)(2,1)S(1)}, u32[]{:S(2)}, u32[]{:S(2)}) collective-permute-start(bf16[256,1024]{1,0:T(8,128)(2,1)S(1)} %get-tuple-element.62), channel_id=1, source_target_pairs={{0,2},{1,3},{2,0},{3,1},{4,6},{5,7},{6,4},{7,5},{8,10},{9,11},{10,... | collective-permute-start | bytes 1572872 | tf_op jit(solution)/shard_map/ppermute | solution.py:552
  74.4 1.6 %collective-permute-start.17 = (bf16[128,1024]{1,0:T(8,128)(2,1)S(1)}, bf16[128,1024]{1,0:T(8,128)(2,1)S(1)}, u32[]{:S(2)}, u32[]{:S(2)}) collective-permute-start(bf16[128,1024]{1,0:T(8,128)(2,1)S(1)} %get-tuple-element.61), channel_id=1, source_target_pairs={{0,1},{1,0},{2,3},{3,2},{4,5},{5,4},{6,7},{7,6},{8,9},{9,8},{10,11... | collective-permute-start | bytes 786440 | tf_op jit(solution)/shard_map/ppermute | solution.py:552
  74.4 10.6 %collective-permute-start.19 = (bf16[512,256]{1,0:T(8,128)(2,1)S(1)}, bf16[512,256]{1,0:T(8,128)(2,1)S(1)}, u32[]{:S(2)}, u32[]{:S(2)}) collective-permute-start(bf16[512,256]{1,0:T(8,128)(2,1)S(1)} %get-tuple-element.65), channel_id=1, source_target_pairs={{4,0},{8,4},{12,8},{5,1},{9,5},{13,9},{6,2},{10,6},{14,10},{7,3},{... | collective-permute-start | bytes 786440 | tf_op jit(solution)/shard_map/ppermute | solution.py:564
  85.1 2.0 %collective-permute-start.20 = (bf16[128,1024]{1,0:T(8,128)(2,1)S(1)}, bf16[128,1024]{1,0:T(8,128)(2,1)S(1)}, u32[]{:S(2)}, u32[]{:S(2)}) collective-permute-start(bf16[128,1024]{1,0:T(8,128)(2,1)S(1)} %slice.3), channel_id=1, source_target_pairs={{0,1},{1,0},{2,3},{3,2},{4,5},{5,4},{6,7},{7,6},{8,9},{9,8},{10,11... | collective-permute-start | bytes 786440 | tf_op jit(solution)/shard_map/ppermute | solution.py:552
  85.2 3.0 %collective-permute-start.21 = (bf16[128,256]{1,0:T(8,128)(2,1)S(1)}, bf16[128,256]{1,0:T(8,128)(2,1)S(1)}, u32[]{:S(2)}, u32[]{:S(2)}) collective-permute-start(bf16[128,256]{1,0:T(8,128)(2,1)S(1)} %get-tuple-element.67), channel_id=1, source_target_pairs={{0,1},{1,0},{2,3},{3,2},{4,5},{5,4},{6,7},{7,6},{8,9},{9,8},{10,11... | collective-permute-start | bytes 196616 | tf_op jit(solution)/shard_map/ppermute | solution.py:552
  85.7 4.8 %collective-permute-start.22 = (bf16[128,256]{1,0:T(8,128)(2,1)S(1)}, bf16[128,256]{1,0:T(8,128)(2,1)S(1)}, u32[]{:S(2)}, u32[]{:S(2)}) collective-permute-start(bf16[128,256]{1,0:T(8,128)(2,1)S(1)} %get-tuple-element.68), channel_id=1, source_target_pairs={{0,2},{1,3},{2,0},{3,1},{4,6},{5,7},{6,4},{7,5},{8,10},{9,11},{10,... | collective-permute-start | bytes 196616 | tf_op jit(solution)/shard_map/ppermute | solution.py:552
  86.4 4.4 %collective-permute-start.23 = (bf16[128,256]{1,0:T(8,128)(2,1)S(1)}, bf16[128,256]{1,0:T(8,128)(2,1)S(1)}, u32[]{:S(2)}, u32[]{:S(2)}) collective-permute-start(bf16[128,256]{1,0:T(8,128)(2,1)S(1)} %get-tuple-element.69), channel_id=1, source_target_pairs={{0,3},{1,2},{2,1},{3,0},{4,7},{5,6},{6,5},{7,4},{8,11},{9,10},{10,... | collective-permute-start | bytes 196616 | tf_op jit(solution)/shard_map/ppermute | solution.py:552
